TPU v7x, 512 devices: a whole 4x8x8 slice. The times are simulated.
512 devices in a mesh: dp: 32 (over x_hi, z, core), seq: 16 (over x_lo, y).
Axes of the slice: x: 4 (x_hi: 2, x_lo: 2; x = x_hi * 2 + x_lo), y: 8, z: 8, core: 2. Of those that a mesh axis runs over, the one named last changes fastest.
Arguments:
- hidden: bfloat16 [32, 16, 256, 1152], P('dp', 'seq'), may hold values from -6 to 6
- timesteps: int32 [32], P('dp'), may hold values from 0 to 999
- ada_weight: bfloat16 [128, 2304], replicated, may hold values from -0.1796875 to 0.1796875
- master: float32 [1152, 1728], P('dp'), may hold values from -6 to 6
- ema_slow: float32 [1152, 1728], P('dp'), may hold values from -1.8 to 1.8
- ema_fast: float32 [1152, 1728], P('dp'), may hold values from -1.8 to 1.8
- step_count: int32 [1], replicated, may hold values from 20 to 59
- cotangent: bfloat16 [32, 16, 256, 576], P('dp', 'seq'), may hold values from -6 to 6
Outputs:
- hidden_grad: bfloat16 [32, 16, 256, 1152], P('dp', 'seq')
- ema_slow_next: float32 [1152, 1728], P('dp')
- ema_fast_next: float32 [1152, 1728], P('dp')
All inputs are finite; a program needn't handle non-finite values.
Results may differ from a plain program's by a relative error of at most 0.02.
Values may be sent and summed in bfloat16 or wider, within the bound.
No kernel may reach another device: no remote copies, remote signals or barrier semaphores. Data moves between devices by JAX's collectives and lax.ppermute only.
A program may use at most 64 MiB of HBM per device.

v0:
```python
import math

import jax
import jax.numpy as jnp
from jax import lax
from jax.sharding import PartitionSpec as P

HEADS = 8


norm_eps = 1e-06
loss_scale = 128.0
gamma_slow = 16.97
gamma_fast = 6.94


def modulate_table(timesteps, ada_weight):
    half_freq = ada_weight.shape[0] // 2
    frequency = jnp.exp(-math.log(10000.0) * jnp.arange(half_freq, dtype=jnp.float32) / half_freq)
    angles = timesteps.astype(jnp.float32)[:, None] * frequency[None, :]
    embedding = jnp.concatenate([jnp.cos(angles), jnp.sin(angles)], axis=1).astype(jnp.bfloat16)
    return jnp.dot(embedding, ada_weight, preferred_element_type=jnp.float32)


def normalize(inputs, rows_mod):
    model_width = inputs.shape[-1]
    values = inputs.astype(jnp.float32)
    average = jnp.mean(values, axis=-1, keepdims=True)
    variance = jnp.mean((values - average) ** 2, axis=-1, keepdims=True)
    inverse_std = lax.rsqrt(variance + norm_eps)
    centered = (values - average) * inverse_std
    shift_rows = rows_mod[:, None, None, :model_width]
    scale_rows = rows_mod[:, None, None, model_width:]
    normed = (centered * (1.0 + scale_rows) + shift_rows).astype(jnp.bfloat16)
    return (normed, centered, inverse_std, scale_rows)


def normalize_back(normed_grads, centered, inverse_std, scale_rows):
    upstream = normed_grads.astype(jnp.float32) * (1.0 + scale_rows)
    first = jnp.mean(upstream, axis=-1, keepdims=True)
    second = jnp.mean(upstream * centered, axis=-1, keepdims=True)
    return (inverse_std * (upstream - first - centered * second)).astype(jnp.bfloat16)


def attend(projected, cot_block, head_count):
    inner = cot_block.shape[-1]
    head_size = inner // head_count
    factor = 1.0 / math.sqrt(head_size)
    lead = projected.shape[:-1]
    split_shape = lead + (head_count, head_size)
    query = projected[..., :inner].reshape(split_shape)
    keys = projected[..., inner : 2 * inner].reshape(split_shape)
    values = projected[..., 2 * inner :].reshape(split_shape)
    out_grad = cot_block.reshape(split_shape)
    wide = jnp.float32
    scores = jnp.einsum("cfphd,cgphd->cphfg", query, keys, preferred_element_type=wide) * factor
    top = jnp.max(scores, axis=-1, keepdims=True)
    expo = jnp.exp(scores - top)
    attention = expo / jnp.sum(expo, axis=-1, keepdims=True)
    attention_low = attention.astype(jnp.bfloat16)
    value_grad = jnp.einsum(
        "cphfg,cfphd->cgphd", attention_low, out_grad, preferred_element_type=wide
    )
    prob_grad = jnp.einsum("cfphd,cgphd->cphfg", out_grad, values, preferred_element_type=wide)
    row_dot = jnp.sum(attention * prob_grad, axis=-1, keepdims=True)
    score_grad = (attention * (prob_grad - row_dot)).astype(jnp.bfloat16)
    query_grad = (
        jnp.einsum("cphfg,cgphd->cfphd", score_grad, keys, preferred_element_type=wide) * factor
    )
    key_grad = (
        jnp.einsum("cphfg,cfphd->cgphd", score_grad, query, preferred_element_type=wide) * factor
    )
    joined = jnp.concatenate(
        [
            query_grad.reshape(lead + (inner,)),
            key_grad.reshape(lead + (inner,)),
            value_grad.reshape(lead + (inner,)),
        ],
        axis=-1,
    )
    return joined.astype(jnp.bfloat16)


def on_device(hidden, timesteps, ada_weight, master, ema_slow, ema_fast, step_count, cotangent):
    model_width = hidden.shape[3]
    triple = master.shape[1]
    modulation = modulate_table(timesteps, ada_weight)
    normed, centered, inverse_std, scale_rows = normalize(hidden, modulation)
    weights_low = master.astype(jnp.bfloat16)
    project_rows_flat = normed.reshape(-1, model_width)
    columns = project_rows_flat
    projected = jnp.dot(
        columns,
        lax.all_gather(weights_low, "dp", axis=0, tiled=True),
        preferred_element_type=jnp.float32,
    ).astype(jnp.bfloat16)
    projected = projected.reshape(hidden.shape[:3] + (triple,))
    patch_grads = attend(
        lax.all_to_all(projected, "seq", split_axis=2, concat_axis=1, tiled=True),
        lax.all_to_all(cotangent, "seq", split_axis=2, concat_axis=1, tiled=True),
        HEADS,
    )
    projected_grads = lax.all_to_all(patch_grads, "seq", split_axis=1, concat_axis=2, tiled=True)
    project_grads_flat = projected_grads.reshape(-1, triple)
    normed_grads = lax.dot_general(
        project_grads_flat,
        lax.all_gather(weights_low, "dp", axis=0, tiled=True),
        (((1,), (1,)), ((), ())),
        preferred_element_type=jnp.float32,
    ).astype(jnp.bfloat16)
    normed_grads = normed_grads.reshape(hidden.shape)
    hidden_grad = normalize_back(normed_grads, centered, inverse_std, scale_rows)
    rows_flat = normed.reshape(-1, model_width)
    grads_flat = projected_grads.reshape(-1, triple)
    columns = rows_flat
    owned_part = lax.psum_scatter(
        lax.dot_general(
            columns, grads_flat, (((0,), (0,)), ((), ())), preferred_element_type=jnp.float32
        ).astype(jnp.bfloat16),
        "dp",
        scatter_dimension=0,
        tiled=True,
    ).astype(jnp.float32)
    weight_grad = lax.psum(owned_part, "seq") / loss_scale
    base = 1.0 - 1.0 / step_count[0].astype(jnp.float32)
    decay_slow = jnp.power(base, gamma_slow + 1.0)
    decay_fast = jnp.power(base, gamma_fast + 1.0)
    ema_slow_next = decay_slow * ema_slow + (1.0 - decay_slow) * weight_grad
    ema_fast_next = decay_fast * ema_fast + (1.0 - decay_fast) * weight_grad
    return (hidden_grad, ema_slow_next, ema_fast_next)


def solution(mesh):
    placed = (
        P("dp", "seq", None, None),
        P("dp"),
        P(),
        P("dp", None),
        P("dp", None),
        P("dp", None),
        P(),
        P("dp", "seq", None, None),
    )
    return jax.shard_map(
        on_device,
        mesh=mesh,
        in_specs=placed,
        out_specs=(P("dp", "seq", None, None), P("dp", None), P("dp", None)),
        check_vma=False,
    )
```

profile of v0, /device:TPU:4, one launch (start us, length us, event | category | flops | bytes accessed | tf_op | source)
XLA Modules:
  0.0 461.0 jit_solution(8202446510493283849)
XLA Ops:
  7.2 0.0 all-gather.3.cloned.1.call-start
  7.2 1.7 convert_bitcast_fusion
  8.9 0.0 all-gather.3.cloned.1.call-update
  8.9 1.4 copy.28
  10.4 0.5 broadcast.103
  10.9 2.7 reduce.18
  13.6 1.1 reshape.258
  14.7 7.8 %all-to-all-start.1 = ((bf16[16,2,4608]{2,1,0:T(2,128)(2,1)}), bf16[16,2,4608]{2,1,0:T(2,128)(2,1)S(1)}, u32[]{:S(2)}, u32[]{:S(2)}) async-start(bf16[16,2,4608]{2,1,0:T(2,128)(2,1)} %reshape.258), calls=%async_computation.1 | async-start | bytes 589824 | tf_op jit(solution)/shard_map/all_to_all | solution.py:100
  23.2 0.1 sine_convert_fusion
  23.3 0.2 convert_reduce_fusion
  23.4 0.3 fusion.23
  23.7 0.2 fusion.34
  24.0 84.5 %all-gather.3.cloned.1.call-done = bf16[32,36,1728]{2,1,0:T(8,128)(2,1)} async-done(((bf16[1,36,1728]{2,1,0:T(8,128)(2,1)}), bf16[32,36,1728]{2,1,0:T(8,128)(2,1)}) %all-gather.3.cloned.1.call-update) | async-done | bytes 3981328 | tf_op jit(solution)/shard_map/all_gather | solution.py:94
  108.6 7.3 %reshape.248 = bf16[1152,1728]{1,0:T(8,128)(2,1)} reshape(bf16[32,36,1728]{2,1,0:T(8,128)(2,1)} %all-gather.3.cloned.1.call-done) | data formatting | bytes 7962624
  115.9 5.0 %fusion.4 = bf16[1,1,256,1728]{2,3,1,0:T(8,128)(2,1)} fusion(bf16[1152,1728]{1,0:T(8,128)(2,1)} %reshape.248, bf16[1,1,256,1152]{3,2,1,0:T(8,128)(2,1)S(1)} %copy-done.1, f32[1152]{0:T(1024)S(1)} %get-tuple-element.4, f32[1152]{0:T(1024)S(1)} %get-tuple-element.3, f32[256]{0:T(256)S(1)} %add_rsqrt_fusion, f32[256]{0:T(256)S(1)} %broadcast_multiply_fusion.2), kind=kOutput, calls=%fused_computation.6 | convolution fusion | flops 1021427712 | bytes 5467136 | tf_op jit(solution)/shard_map/dot_general | solution.py:92
  120.9 3.9 copy.25
  124.8 7.4 %reduce.17 = bf16[256,1728]{1,0:T(8,128)(2,1)} reduce(bf16[256,1,1,1728]{3,2,1,0:T(2,128)(2,1)S(1)} %bitcast.64, bf16[]{:T(256)} %broadcast.103), dimensions={1,2}, to_apply=%bitcast.52.reduce_sub_computation | reduce | bytes 1769474
  132.2 3.6 reshape.256
  135.8 8.4 %all-to-all-start = ((bf16[16,2,13824]{2,1,0:T(2,128)(2,1)}), bf16[16,2,13824]{2,1,0:T(2,128)(2,1)}, u32[]{:S(2)}, u32[]{:S(2)}) async-start(bf16[16,2,13824]{2,1,0:T(2,128)(2,1)} %reshape.256), calls=%async_computation | async-start | bytes 1769472 | tf_op jit(solution)/shard_map/all_to_all | solution.py:99
  144.2 0.6 reshape.259
  144.8 1.8 bitcast_reduce_fusion
  146.6 1.4 reshape.245
  148.0 20.4 %all-to-all-done = bf16[16,2,13824]{2,1,0:T(2,128)(2,1)} async-done(((bf16[16,2,13824]{2,1,0:T(2,128)(2,1)}), bf16[16,2,13824]{2,1,0:T(2,128)(2,1)}, u32[]{:S(2)}, u32[]{:S(2)}) %all-to-all-start) | async-done | bytes 884768 | tf_op jit(solution)/shard_map/all_to_all | solution.py:99
  168.4 4.7 %reshape.257 = bf16[256,1,1,1728]{3,2,1,0:T(2,128)(2,1)S(1)} reshape(bf16[16,2,13824]{2,1,0:T(2,128)(2,1)} %all-to-all-done) | data formatting | bytes 1769472
  173.0 0.1 copy.40
  173.1 0.2 fusion.50
  173.3 0.6 reshape.242
  173.9 0.6 reshape.243
  174.4 1.3 reshape.244
  175.8 1.0 fusion.51
  176.8 2.0 multiply_reduce_fusion
  178.8 0.3 multiply_convert_fusion
  179.1 0.5 fusion.15
  179.6 0.4 fusion.14
  180.0 0.1 copy-done.3
  180.1 1.3 fusion.16
  181.4 0.1 copy.33
  181.6 0.4 concatenate.26
  181.9 0.1 copy.35
  182.1 0.4 concatenate.27
  182.5 0.1 copy-done.2
  182.6 0.1 copy.37
  182.7 0.4 concatenate.28
  183.1 1.2 concatenate.29
  184.3 4.2 all-to-all-start.2
  188.6 0.3 all-reduce.4.cloned.1.call-start
  189.7 1.3 dynamic-slice.4
  191.6 21.4 %all-to-all-done.2 = bf16[1,16,16,1728]{3,2,0,1:T(8,128)(2,1)S(1)} async-done(((bf16[1,16,16,1728]{3,2,0,1:T(8,128)(2,1)}), bf16[1,16,16,1728]{3,2,0,1:T(8,128)(2,1)S(1)}, u32[]{:S(2)}, u32[]{:S(2)}) %all-to-all-start.2) | async-done | bytes 884768 | tf_op jit(solution)/shard_map/all_to_all | solution.py:103
  213.1 3.6 fusion.19
  216.7 3.4 convolution_convert_fusion
  220.1 80.1 %fusion = bf16[40,1728]{1,0:T(8,128)(2,1)S(1)} fusion(bf16[1152,1728]{1,0:T(8,128)(2,1)} %convolution_convert_fusion), kind=kCustom, calls=%all-reduce-scatter | all-reduce-scatter fusion | flops 2211841 | bytes 4121600
  300.3 1.9 collective-permute-start.2
  302.2 1.9 collective-permute-start.1
  304.1 1.9 collective-permute-start
  306.1 1.9 collective-permute-start.3
  308.0 0.1 reduce_sum.58
  308.1 8.2 %collective-permute-done.3 = bf16[4,1728]{1,0:T(4,128)(2,1)S(1)} collective-permute-done((bf16[4,1728]{1,0:T(4,128)(2,1)S(1)}, bf16[4,1728]{1,0:T(4,128)(2,1)S(1)}, u32[]{:S(2)}, u32[]{:S(2)}) %collective-permute-start.3) | collective-permute-done | bytes 13856
  316.3 0.6 copy-done.6
  316.9 1.6 concatenate.30
  318.5 0.8 dynamic-slice_convert_fusion
  319.2 0.0 all-reduce.4.cloned.1.call-update
  319.3 1.2 fusion.22
  320.5 131.8 %all-reduce.4.cloned.1.call-done = f32[36,1728]{1,0:T(8,128)} async-done(((f32[36,1728]{1,0:T(8,128)}), f32[36,1728]{1,0:T(8,128)}) %all-reduce.4.cloned.1.call-update) | async-done | bytes 248848 | tf_op jit(solution)/shard_map/psum | solution.py:124
  452.3 1.9 multiply_add_fusion
  (21 shorter events, 0.1 us)
Async XLA Ops:
  7.2 16.6 %copy-start = (bf16[128,2304]{1,0:T(8,128)(2,1)S(1)}, bf16[128,2304]{1,0:T(8,128)(2,1)}, u32[]{:S(2)}) copy-start(bf16[128,2304]{1,0:T(8,128)(2,1)} %param.10) | copy-start | bytes 1769476
  7.2 101.4 %all-gather.3.cloned.1.call-start = ((), (), s32[]{:S(2)}) async-start(), calls=%async_computation.4 | async-start | bytes 4730880 | tf_op jit(solution)/shard_map/all_gather | solution.py:94
  10.4 12.9 %copy-start.1 = (bf16[1,1,256,1152]{3,2,1,0:T(8,128)(2,1)S(1)}, bf16[1,1,256,1152]{3,2,1,0:T(8,128)(2,1)}, u32[]{:S(2)}) copy-start(bf16[1,1,256,1152]{3,2,1,0:T(8,128)(2,1)} %param.8) | copy-start | bytes 1769476
  14.7 121.1 %all-to-all-start.1 = ((bf16[16,2,4608]{2,1,0:T(2,128)(2,1)}), bf16[16,2,4608]{2,1,0:T(2,128)(2,1)S(1)}, u32[]{:S(2)}, u32[]{:S(2)}) async-start(bf16[16,2,4608]{2,1,0:T(2,128)(2,1)} %reshape.258), calls=%async_computation.1 | async-start | bytes 589824 | tf_op jit(solution)/shard_map/all_to_all | solution.py:100
  135.8 32.6 %all-to-all-start = ((bf16[16,2,13824]{2,1,0:T(2,128)(2,1)}), bf16[16,2,13824]{2,1,0:T(2,128)(2,1)}, u32[]{:S(2)}, u32[]{:S(2)}) async-start(bf16[16,2,13824]{2,1,0:T(2,128)(2,1)} %reshape.256), calls=%async_computation | async-start | bytes 1769472 | tf_op jit(solution)/shard_map/all_to_all | solution.py:99
  179.1 1.0 copy-start.3
  181.6 1.0 copy-start.2
  184.3 28.7 %all-to-all-start.2 = ((bf16[1,16,16,1728]{3,2,0,1:T(8,128)(2,1)}), bf16[1,16,16,1728]{3,2,0,1:T(8,128)(2,1)S(1)}, u32[]{:S(2)}, u32[]{:S(2)}) async-start(bf16[1,16,16,1728]{3,2,0,1:T(8,128)(2,1)} %bitcast.13), calls=%async_computation.2 | async-start | bytes 1835008 | tf_op jit(solution)/shard_map/all_to_all | solution.py:103
  188.6 263.7 %all-reduce.4.cloned.1.call-start = ((), (), s32[]{:S(2)}) async-start(), calls=%async_computation.3 | async-start | bytes 573440 | tf_op jit(solution)/shard_map/psum | solution.py:124
  300.3 16.1 %collective-permute-start.2 = (bf16[40,1728]{1,0:T(8,128)(2,1)S(1)}, bf16[40,1728]{1,0:T(8,128)(2,1)S(1)}, u32[]{:S(2)}, u32[]{:S(2)}) collective-permute-start(bf16[40,1728]{1,0:T(8,128)(2,1)S(1)} %fusion), channel_id=1, source_target_pairs={{0,48},{16,64},{32,80},{48,96},{64,112},{80,128},{96,144},{112,160... | collective-permute-start | bytes 414728
  302.2 14.1 %collective-permute-start.1 = (bf16[40,1728]{1,0:T(8,128)(2,1)S(1)}, bf16[40,1728]{1,0:T(8,128)(2,1)S(1)}, u32[]{:S(2)}, u32[]{:S(2)}) collective-permute-start(bf16[40,1728]{1,0:T(8,128)(2,1)S(1)} %fusion), channel_id=1, source_target_pairs={{0,32},{16,48},{32,64},{48,80},{64,96},{80,112},{96,128},{112,144}... | collective-permute-start | bytes 414728
  304.1 12.8 %collective-permute-start = (bf16[40,1728]{1,0:T(8,128)(2,1)S(1)}, bf16[40,1728]{1,0:T(8,128)(2,1)S(1)}, u32[]{:S(2)}, u32[]{:S(2)}) collective-permute-start(bf16[40,1728]{1,0:T(8,128)(2,1)S(1)} %fusion), channel_id=1, source_target_pairs={{0,16},{16,32},{32,48},{48,64},{64,80},{80,96},{96,112},{112,128},... | collective-permute-start | bytes 414728
  306.1 10.3 %collective-permute-start.3 = (bf16[4,1728]{1,0:T(4,128)(2,1)S(1)}, bf16[4,1728]{1,0:T(4,128)(2,1)S(1)}, u32[]{:S(2)}, u32[]{:S(2)}) collective-permute-start(bf16[4,1728]{1,0:T(4,128)(2,1)S(1)} %slice.25), channel_id=1, source_target_pairs={{0,64},{16,80},{32,96},{48,112},{64,128},{80,144},{96,160},{112,17... | collective-permute-start | bytes 41480
  316.3 0.6 copy-start.6
  319.2 133.0 %copy-start.4 = (f32[36,1728]{1,0:T(8,128)S(1)}, f32[36,1728]{1,0:T(8,128)}, u32[]{:S(2)}) copy-start(f32[36,1728]{1,0:T(8,128)} %param.13) | copy-start | bytes 746500
  319.3 133.0 %copy-start.5 = (f32[36,1728]{1,0:T(8,128)S(1)}, f32[36,1728]{1,0:T(8,128)}, u32[]{:S(2)}) copy-start(f32[36,1728]{1,0:T(8,128)} %param.12) | copy-start | bytes 746500
Sparse Core Ops, SparseCore 0:
  11.9 96.6 all-gather.2
  319.4 132.8 all-reduce.3
where the time goes:
time: 462 us; the launch traced here: 461 us
  waiting for transfers between devices  266 us (58%)
  blocking collectives  80.1 us (17%)
  local copies, waits for them, and re-layouts  35.4 us (8%)
  starting transfers between devices  28.5 us (6%)
  matrix products  17.5 us (4%)
  other arithmetic  16.5 us (4%)
  between operations  16.4 us (4%)
    psum x1, waiting for transfers between devices, on_device(): weight_grad = lax.psum(owned_part, 'seq') / loss_scale  132 us
    all_gather x1, waiting for transfers between devices, on_device(): lax.all_gather(weights_low, 'dp', axis=0, tiled=True)  84.5 us
    unnamed x1, blocking collectives  80.1 us
    unnamed x25, local copies, waits for them, and re-layouts  23 us
    all_to_all x1, waiting for transfers between devices, on_device(): lax.all_to_all(patch_grads, 'seq', split_axis=1, concat_axis=2, tiled=True)  21.4 us
    all_to_all x1, waiting for transfers between devices, on_device(): lax.all_to_all(projected, 'seq', split_axis=2, concat_axis=1, tiled=True)  20.4 us
    unnamed x3, other arithmetic  11.8 us
  transfers between devices with their start and end apart: 9, of which 5 were waited for; matrix products, arithmetic and copies ran while one was open for 9% of the time, Pallas kernels for 0%

commit v1 on v0

v1 whole, which is shorter than its diff:
```python
import math

import jax
import jax.numpy as jnp
from jax import lax
from jax.experimental import pallas as pl
from jax.experimental.pallas import tpu as pltpu
from jax.sharding import Mesh
from jax.sharding import PartitionSpec as P

HEADS = 8
HDIM = 72
norm_eps = 1e-06
loss_scale = 128.0
gamma_slow = 16.97
gamma_fast = 6.94
AXES = ("xh", "z", "c", "xl", "y")
SEQ = ("xl", "y")
ROWS = ("xh", "z")
F32 = jnp.float32
BF16 = jnp.bfloat16
MIB = 1024 * 1024


def params(mib=48):
    return pltpu.CompilerParams(vmem_limit_bytes=mib * MIB)


def cost(flops, moved):
    return pl.CostEstimate(flops=flops, bytes_accessed=moved, transcendentals=0)


def swap(value, axis):
    return lax.ppermute(value, axis, [(0, 1), (1, 0)])


def modulate_table(timesteps, ada_weight):
    half_freq = ada_weight.shape[0] // 2
    frequency = jnp.exp(-math.log(10000.0) * jnp.arange(half_freq, dtype=F32) / half_freq)
    angles = timesteps.astype(F32)[:, None] * frequency[None, :]
    embedding = jnp.concatenate([jnp.cos(angles), jnp.sin(angles)], axis=1).astype(BF16)
    return jnp.dot(embedding, ada_weight, preferred_element_type=F32)


def pack_kernel(hidden_ref, cot_ref, out_ref):
    width = hidden_ref.shape[1]
    out_ref[:, :width] = hidden_ref[...]
    out_ref[:, width:] = cot_ref[...].T


def stats(values):
    average = jnp.mean(values, axis=-1, keepdims=True)
    moved = values - average
    variance = jnp.mean(moved * moved, axis=-1, keepdims=True)
    inverse_std = lax.rsqrt(variance + norm_eps)
    return moved * inverse_std, inverse_std


def norm_kernel(packed_ref, mod_ref, out_ref):
    width = mod_ref.shape[1] // 2
    centered, _ = stats(packed_ref[:, :width].astype(F32))
    normed = centered * (1.0 + mod_ref[:, width:]) + mod_ref[:, :width]
    out_ref[:, :width] = normed.astype(BF16)
    out_ref[:, width:] = packed_ref[:, width:]


def norm_back_kernel(packed_ref, mod_ref, part_ref, other_ref, out_ref):
    width = mod_ref.shape[1] // 2
    centered, inverse_std = stats(packed_ref[:, :width].astype(F32))
    grads = (part_ref[...].astype(F32) + other_ref[...].astype(F32)).astype(BF16).astype(F32)
    upstream = grads * (1.0 + mod_ref[:, width:])
    first = jnp.mean(upstream, axis=-1, keepdims=True)
    second = jnp.mean(upstream * centered, axis=-1, keepdims=True)
    out_ref[...] = (inverse_std * (upstream - first - centered * second)).astype(BF16)


def dot(left, right, over):
    return lax.dot_general(left, right, ((over[0], over[1]), ((), ())), preferred_element_type=F32)


def attend_block(projected, out_grad, same, lane):
    factor = 1.0 / math.sqrt(HDIM)
    wide = 2 * HDIM
    query = projected[:, :wide]
    keys = projected[:, wide : 2 * wide]
    values = projected[:, 2 * wide :].astype(BF16)
    query_low, keys_low = query.astype(BF16), keys.astype(BF16)
    query_grad = key_grad = value_grad = None
    for head in range(2):
        mine = (lane >= head * HDIM) & (lane < (head + 1) * HDIM)
        own_query = jnp.where(mine, query, 0.0).astype(BF16)
        own_keys = jnp.where(mine, keys, 0.0).astype(BF16)
        own_out = jnp.where(mine, out_grad, 0.0).astype(BF16)
        scores = dot(own_query, keys_low, ((1,), (1,))) * factor
        scores = jnp.where(same, scores, -1e30)
        top = jnp.max(scores, axis=-1, keepdims=True)
        expo = jnp.exp(scores - top)
        attention = expo / jnp.sum(expo, axis=-1, keepdims=True)
        prob_grad = dot(own_out, values, ((1,), (1,)))
        row_dot = jnp.sum(attention * prob_grad, axis=-1, keepdims=True)
        score_grad = (attention * (prob_grad - row_dot)).astype(BF16)
        parts = (
            dot(score_grad, own_keys, ((1,), (0,))),
            dot(score_grad, own_query, ((0,), (0,))),
            dot(attention.astype(BF16), own_out, ((0,), (0,))),
        )
        if head == 0:
            query_grad, key_grad, value_grad = parts
        else:
            query_grad, key_grad, value_grad = (
                query_grad + parts[0],
                key_grad + parts[1],
                value_grad + parts[2],
            )
    return jnp.concatenate([query_grad * factor, key_grad * factor, value_grad], axis=1)


def main_kernel(spot_ref, own_ref, core_ref, side_ref, both_ref, weight_ref, grads_ref, wgrad_ref, total_ref):
    tokens = own_ref.shape[0]
    model_width = weight_ref.shape[0]
    quarter = weight_ref.shape[1] // 3
    spot = spot_ref[0]
    row = lax.broadcasted_iota(jnp.int32, (tokens, tokens), 0)
    col = lax.broadcasted_iota(jnp.int32, (tokens, tokens), 1)
    same = lax.rem(row, 16) == lax.rem(col, 16)
    lane = lax.broadcasted_iota(jnp.int32, (tokens, quarter), 1)
    for index, ref in enumerate((own_ref, core_ref, side_ref, both_ref)):
        projected = dot(ref[:, :model_width], weight_ref[...], ((1,), (0,)))
        projected = projected.astype(BF16).astype(F32)
        cot = ref[:, model_width:].astype(F32)
        out_grad = cot[:, :quarter]
        for other in range(1, 4):
            out_grad = jnp.where(spot == other, cot[:, other * quarter : (other + 1) * quarter], out_grad)
        grads = attend_block(projected, out_grad, same, lane).astype(BF16)
        grads_ref[index * tokens : (index + 1) * tokens, :] = grads
        part = dot(ref[:, :model_width], grads, ((0,), (0,)))
        if index == 0:
            total_ref[...] = part
        elif index < 3:
            total_ref[...] += part
        else:
            wgrad_ref[...] = (total_ref[...] + part).astype(BF16)


def input_kernel(grads_ref, weight_ref, near_ref, far_ref):
    half = near_ref.shape[0] // 2
    for index, (ref, place) in enumerate(((near_ref, 0), (far_ref, 0), (near_ref, 1), (far_ref, 1))):
        part = dot(grads_ref[index * half : (index + 1) * half, :], weight_ref[...], ((1,), (1,)))
        ref[place * half : (place + 1) * half, :] = part.astype(BF16)


def add_kernel(near_ref, got_ref, own_ref, side_ref):
    half = own_ref.shape[0]
    own_ref[...] = (near_ref[:half].astype(F32) + got_ref[:half].astype(F32)).astype(BF16)
    side_ref[...] = (near_ref[half:].astype(F32) + got_ref[half:].astype(F32)).astype(BF16)


def sum_kernel(parts_ref, out_ref):
    total = parts_ref[0].astype(F32)
    for index in range(1, parts_ref.shape[0]):
        total = total + parts_ref[index].astype(F32)
    out_ref[...] = total.astype(out_ref.dtype)


def call(kernel, outs, *args, flops=0, scratch=(), mib=48, smem=0):
    moved = sum(a.size * a.dtype.itemsize for a in args)
    moved += sum(math.prod(shape) * jnp.dtype(kind).itemsize for shape, kind in outs)
    shapes = [jax.ShapeDtypeStruct(shape, kind) for shape, kind in outs]
    specs = [pl.BlockSpec(memory_space=pltpu.SMEM if i < smem else pltpu.VMEM) for i in range(len(args))]
    got = pl.pallas_call(
        kernel,
        out_shape=shapes,
        in_specs=specs,
        out_specs=[pl.BlockSpec(memory_space=pltpu.VMEM)] * len(shapes),
        scratch_shapes=list(scratch),
        compiler_params=params(mib),
        cost_estimate=cost(flops, moved),
    )(*args)
    return got[0] if len(got) == 1 else got


def on_device(hidden, timesteps, ada_weight, master, ema_slow, ema_fast, step_count, cotangent):
    patches, width = hidden.shape[2:]
    inner = cotangent.shape[3]
    own_rows, triple = master.shape
    wide = width + inner
    n_seq = lax.axis_size("xl") * lax.axis_size("y")
    n_rows = lax.axis_size("xh") * lax.axis_size("z")
    n_y = lax.axis_size("y")
    quarter = inner // 4
    core, side = lax.axis_index("c"), lax.axis_index("xl")
    spot = 2 * core + side
    spot_arr = spot.astype(jnp.int32).reshape(1)

    packed = call(pack_kernel, [((patches, wide), BF16)], hidden[0, 0], cotangent[0, 0].T)
    tokens = lax.all_to_all(packed.reshape(n_seq, patches // n_seq, wide), SEQ, 0, 0, tiled=True)
    tokens = tokens.reshape(patches, wide)

    low = master.astype(BF16).reshape(own_rows, 3, 4, quarter)
    mine = lax.dynamic_index_in_dim(low, spot, 2, False).reshape(own_rows, 3 * quarter)
    theirs = lax.dynamic_index_in_dim(low, 2 * (1 - core) + side, 2, False).reshape(own_rows, 3 * quarter)
    theirs = swap(theirs, "c")
    pair = jnp.where(core == 0, jnp.concatenate([mine, theirs]), jnp.concatenate([theirs, mine]))
    copies = jnp.broadcast_to(pair[None], (n_rows,) + pair.shape)
    copies, tokens = lax.optimization_barrier((copies, tokens))
    weights = lax.all_to_all(copies, ROWS, 0, 0, tiled=True).reshape(width, 3 * quarter)

    modulation = modulate_table(timesteps, ada_weight)
    own = call(norm_kernel, [((patches, wide), BF16)], tokens, modulation)
    from_side = swap(own, "xl")
    from_core = swap(own, "c")
    from_both = swap(from_side, "c")

    grads, wgrad = call(
        main_kernel,
        [((4 * patches, 3 * quarter), BF16), ((width, 3 * quarter), BF16)],
        spot_arr, own, from_core, from_side, from_both, weights,
        flops=4 * 4 * patches * width * 3 * quarter,
        scratch=[pltpu.VMEM((width, 3 * quarter), F32)],
        smem=1,
    )

    parts = lax.all_to_all(wgrad.reshape(n_rows, 2 * own_rows, 3 * quarter), ROWS, 0, 0, tiled=True)
    summed = call(sum_kernel, [((2 * own_rows, 3 * quarter), BF16)], parts)
    summed = jnp.broadcast_to(summed[None], (n_y,) + summed.shape)
    parts = lax.all_to_all(summed, "y", 0, 0, tiled=True)
    total = call(sum_kernel, [((2 * own_rows, 3 * quarter), F32)], parts)
    keep = jnp.where(core == 0, total[:own_rows], total[own_rows:])
    give = jnp.where(core == 0, total[own_rows:], total[:own_rows])
    got = swap(give, "c")
    both = jnp.where(core == 0, jnp.stack([keep, got]), jnp.stack([got, keep]))
    over = swap(both, "xl")
    four = jnp.where(side == 0, jnp.stack([both, over], 1), jnp.stack([over, both], 1))
    four = four.reshape(4, own_rows, 3, quarter).transpose(1, 2, 0, 3)
    weight_grad = four.reshape(own_rows, triple) / loss_scale

    near, far = call(
        input_kernel,
        [((2 * patches, width), BF16), ((2 * patches, width), BF16)],
        grads, weights,
        flops=8 * patches * width * 3 * quarter,
    )
    got = swap(far, "c")
    part, give = call(add_kernel, [((patches, width), BF16)] * 2, near, got)
    got = swap(give, "xl")
    back = call(norm_back_kernel, [((patches, width), BF16)], tokens, modulation, part, got)
    back = lax.all_to_all(back.reshape(n_seq, patches // n_seq, width), SEQ, 0, 0, tiled=True)
    hidden_grad = back.reshape(hidden.shape)

    base = 1.0 - 1.0 / step_count[0].astype(F32)
    decay_slow = jnp.power(base, gamma_slow + 1.0)
    decay_fast = jnp.power(base, gamma_fast + 1.0)
    ema_slow_next = decay_slow * ema_slow + (1.0 - decay_slow) * weight_grad
    ema_fast_next = decay_fast * ema_fast + (1.0 - decay_fast) * weight_grad
    return (hidden_grad, ema_slow_next, ema_fast_next)


def solution(mesh):
    fine = Mesh(mesh.devices.reshape(2, 8, 2, 2, 8), AXES)
    dp, seq = ("xh", "z", "c"), SEQ
    placed = (
        P(dp, seq, None, None),
        P(dp),
        P(),
        P(dp, None),
        P(dp, None),
        P(dp, None),
        P(),
        P(dp, seq, None, None),
    )
    return jax.shard_map(
        on_device,
        mesh=fine,
        in_specs=placed,
        out_specs=(P(dp, seq, None, None), P(dp, None), P(dp, None)),
        check_vma=False,
    )
```

time: 462 us -> 198 us (0.43)
  the two profiles are of different devices: /device:TPU:4 before, /device:TPU:1 now
where the time goes in v1:
time: 198 us; the launch traced here: 197 us
  waiting for transfers between devices  78.1 us (39%)
  starting transfers between devices  73.1 us (37%)
  local copies, waits for them, and re-layouts  22.2 us (11%)
  Pallas kernels  19 us (10%)
  between operations  2.46 us (1%)
    ppermute x8, waiting for transfers between devices, swap(): return lax.ppermute(value, axis, [(0, 1), (1, 0)])  41.2 us
    ppermute x8, starting transfers between devices, swap(): return lax.ppermute(value, axis, [(0, 1), (1, 0)])  30 us
    all_to_all x1, waiting for transfers between devices, on_device(): lax.all_to_all(wgrad.reshape(n_rows, 2 * own_rows, 3 * quarter), ROWS, 0,...  21.2 us
    pallas_call x8, Pallas kernels, call(): pl.pallas_call(kernel, out_shape=shapes, in_specs=specs, out_specs=[pl.Bl...  19 us
    all_to_all x1, waiting for transfers between devices, on_device(): lax.all_to_all(packed.reshape(n_seq, patches // n_seq, wide), SEQ, 0, 0,...  15.7 us
    all_to_all x1, starting transfers between devices, on_device(): lax.all_to_all(copies, ROWS, 0, 0, tiled=True).reshape(width, 3 * quarter)  13.1 us
    unnamed x27, local copies, waits for them, and re-layouts  9.52 us
    all_to_all x1, starting transfers between devices, on_device(): lax.all_to_all(packed.reshape(n_seq, patches // n_seq, wide), SEQ, 0, 0,...  8.81 us
  transfers between devices with their start and end apart: 13, of which 6 were waited for; matrix products, arithmetic and copies ran while one was open for 5% of the time, Pallas kernels for 4%

profile of v1, /device:TPU:1, one launch (start us, length us, event | category | flops | bytes accessed | tf_op | source)
XLA Modules:
  0.0 196.8 jit_solution(13048212440896253413)
XLA Ops:
  0.6 0.0 copy-start
  0.7 1.1 copy-done.6
  1.8 1.0 copy-done.7
  2.7 1.1 shard_map.103
  3.8 8.8 %all-to-all-start = ((bf16[16,16,1728]{2,1,0:T(8,128)(2,1)}), bf16[16,16,1728]{2,1,0:T(8,128)(2,1)S(1)}, u32[]{:S(2)}, u32[]{:S(2)}) async-start(bf16[16,16,1728]{2,1,0:T(8,128)(2,1)} %bitcast.3), calls=%async_computation | async-start | bytes 1835008 | tf_op jit(solution)/shard_map/all_to_all | solution.py:196
  12.7 0.3 reshape.169
  12.9 0.8 dynamic-slice_reduce_fusion.1
  13.7 0.1 reshape.170
  13.8 3.7 %collective-permute-start = (bf16[36,432]{1,0:T(8,128)(2,1)S(1)}, bf16[36,432]{1,0:T(8,128)(2,1)S(1)}, u32[]{:S(2)}, u32[]{:S(2)}) collective-permute-start(bf16[36,432]{1,0:T(8,128)(2,1)S(1)} %reshape.170), channel_id=1, source_target_pairs={{0,16},{16,0},{1,17},{17,1},{2,18},{18,2},{3,19},{19,3},{4,20},{20... | collective-permute-start | bytes 93320 | tf_op jit(solution)/shard_map/ppermute | solution.py:34
  18.2 0.1 sine_convert_fusion
  18.3 0.1 concatenate.37
  18.4 0.0 collective-permute-done
  18.4 15.7 %all-to-all-done = bf16[16,16,1728]{2,1,0:T(8,128)(2,1)S(1)} async-done(((bf16[16,16,1728]{2,1,0:T(8,128)(2,1)}), bf16[16,16,1728]{2,1,0:T(8,128)(2,1)S(1)}, u32[]{:S(2)}, u32[]{:S(2)}) %all-to-all-start) | async-done | bytes 884768 | tf_op jit(solution)/shard_map/all_to_all | solution.py:196
  34.1 1.1 broadcast_in_dim.4
  35.2 13.1 %all-to-all-start.1 = ((bf16[16,72,432]{2,1,0:T(8,128)(2,1)}), bf16[16,72,432]{2,1,0:T(8,128)(2,1)}, u32[]{:S(2)}, u32[]{:S(2)}) async-start(bf16[16,72,432]{2,1,0:T(8,128)(2,1)} %broadcast_in_dim.4), calls=%async_computation.1 | async-start | bytes 2359296 | tf_op jit(solution)/shard_map/all_to_all | solution.py:206
  48.3 0.2 fusion.4.mod_ref
  48.6 0.4 shard_map.104.own_ref
  49.0 1.3 copy.23
  50.3 1.9 collective-permute-start.2
  52.2 5.2 %collective-permute-start.1 = (bf16[256,1728]{0,1:T(8,128)(2,1)}, bf16[256,1728]{0,1:T(8,128)(2,1)}, u32[]{:S(2)}, u32[]{:S(2)}) collective-permute-start(bf16[256,1728]{0,1:T(8,128)(2,1)} %copy.23), channel_id=1, source_target_pairs={{0,16},{16,0},{1,17},{17,1},{2,18},{18,2},{3,19},{19,3},{4,20},{20... | collective-permute-start | bytes 2654216 | tf_op jit(solution)/shard_map/ppermute | solution.py:34
  57.4 23.1 %collective-permute-done.2 = bf16[256,1728]{0,1:T(8,128)(2,1)} collective-permute-done((bf16[256,1728]{0,1:T(8,128)(2,1)}, bf16[256,1728]{0,1:T(8,128)(2,1)}, u32[]{:S(2)}, u32[]{:S(2)}) %collective-permute-start.2) | collective-permute-done | bytes 884768 | tf_op jit(solution)/shard_map/ppermute | solution.py:34
  80.5 4.9 %collective-permute-start.3 = (bf16[256,1728]{0,1:T(8,128)(2,1)}, bf16[256,1728]{0,1:T(8,128)(2,1)}, u32[]{:S(2)}, u32[]{:S(2)}) collective-permute-start(bf16[256,1728]{0,1:T(8,128)(2,1)} %collective-permute-done.2), channel_id=1, source_target_pairs={{0,16},{16,0},{1,17},{17,1},{2,18},{18,2},{3,19},{19,3},{4,20},{20... | collective-permute-start | bytes 2654216 | tf_op jit(solution)/shard_map/ppermute | solution.py:34
  85.5 1.5 copy.26.side_ref
  86.9 0.0 collective-permute-done.1
  86.9 2.2 %copy.25.core_ref = bf16[256,1728]{1,0:T(8,128)(2,1)} copy(bf16[256,1728]{0,1:T(8,128)(2,1)} %collective-permute-done.1) | data formatting | bytes 1769472 | tf_op jit(solution)/shard_map/ppermute | solution.py:34
  89.2 2.2 %copy.27.both_ref = bf16[256,1728]{1,0:T(8,128)(2,1)} copy(bf16[256,1728]{0,1:T(8,128)(2,1)} %collective-permute-done.3) | data formatting | bytes 1769472 | tf_op jit(solution)/shard_map/ppermute | solution.py:34
  91.4 0.0 all-to-all-done.1
  91.4 1.2 copy-done.4
  92.5 1.2 copy-done.5
  93.7 10.1 %shard_map.105 = (bf16[1024,432]{1,0:T(8,128)(2,1)S(1)}, bf16[1152,432]{1,0:T(8,128)(2,1)S(1)}) custom-call(s32[1]{0:T(128)} %bitcast.7.spot_ref, bf16[256,1728]{1,0:T(8,128)(2,1)S(1)} %shard_map.104.own_ref, bf16[256,1728]{1,0:T(8,128)(2,1)S(1)} %copy-done.4, bf16[256,1728]{1,0:T(8,128)(2,1)S(1)} %copy.26.side_ref, bf16[256,1728]{1,0:T(8,128)(2,1)S(1)} %copy-done.5, ...), custom_call_target="tpu_custom_call" | custom-call | flops 2038431744 | bytes 6414340 | tf_op jit(solution)/shard_map/pallas_call | solution.py:170
  103.8 1.0 copy-done.3
  104.9 1.0 copy-done.8
  105.8 8.7 %all-to-all-start.3 = ((bf16[16,72,432]{2,1,0:T(8,128)(2,1)}), bf16[16,72,432]{2,1,0:T(8,128)(2,1)S(1)}, u32[]{:S(2)}, u32[]{:S(2)}) async-start(bf16[16,72,432]{2,1,0:T(8,128)(2,1)} %bitcast.33), calls=%async_computation.3 | async-start | bytes 2359296 | tf_op jit(solution)/shard_map/all_to_all | solution.py:223
  114.5 1.2 copy-done.9
  115.8 3.9 %shard_map.106 = (bf16[512,1152]{1,0:T(8,128)(2,1)S(1)}, bf16[512,1152]{1,0:T(8,128)(2,1)}) custom-call(bf16[1024,432]{1,0:T(8,128)(2,1)S(1)} %copy-done.9, bf16[1152,432]{1,0:T(8,128)(2,1)} %bitcast.8.weight_ref), custom_call_target="tpu_custom_call" | custom-call | flops 1019215872 | bytes 4239360 | tf_op jit(solution)/shard_map/pallas_call | solution.py:170
  119.6 1.0 copy-done.1
  120.6 2.2 %collective-permute-start.4 = (bf16[512,1152]{1,0:T(8,128)(2,1)}, bf16[512,1152]{1,0:T(8,128)(2,1)}, u32[]{:S(2)}, u32[]{:S(2)}) collective-permute-start(bf16[512,1152]{1,0:T(8,128)(2,1)} %get-tuple-element.15), channel_id=1, source_target_pairs={{0,16},{16,0},{1,17},{17,1},{2,18},{18,2},{3,19},{19,3},{4,20},{20... | collective-permute-start | bytes 3538952 | tf_op jit(solution)/shard_map/ppermute | solution.py:34
  122.8 21.2 %all-to-all-done.3.parts_ref = bf16[16,72,432]{2,1,0:T(8,128)(2,1)S(1)} async-done(((bf16[16,72,432]{2,1,0:T(8,128)(2,1)}), bf16[16,72,432]{2,1,0:T(8,128)(2,1)S(1)}, u32[]{:S(2)}, u32[]{:S(2)}) %all-to-all-start.3) | async-done | bytes 995360 | tf_op jit(solution)/shard_map/all_to_all | solution.py:223
  144.1 0.2 shard_map.109
  144.2 0.9 broadcast_in_dim.5
  145.1 6.1 %all-to-all-start.4 = ((bf16[8,72,432]{2,1,0:T(8,128)(2,1)}), bf16[8,72,432]{2,1,0:T(8,128)(2,1)S(1)}, u32[]{:S(2)}, u32[]{:S(2)}) async-start(bf16[8,72,432]{2,1,0:T(8,128)(2,1)} %broadcast_in_dim.5), calls=%async_computation.4 | async-start | bytes 1179648 | tf_op jit(solution)/shard_map/all_to_all | solution.py:226
  151.2 1.6 shard_map.107
  152.8 1.9 collective-permute-start.5
  154.8 11.6 %collective-permute-done.5.other_ref = bf16[256,1152]{1,0:T(8,128)(2,1)S(1)} collective-permute-done((bf16[256,1152]{1,0:T(8,128)(2,1)S(1)}, bf16[256,1152]{1,0:T(8,128)(2,1)S(1)}, u32[]{:S(2)}, u32[]{:S(2)}) %collective-permute-start.5) | collective-permute-done | bytes 589856 | tf_op jit(solution)/shard_map/ppermute | solution.py:34
  166.3 1.7 shard_map.108
  168.0 6.5 %all-to-all-start.2 = ((bf16[16,16,1152]{2,1,0:T(8,128)(2,1)}), bf16[16,16,1152]{2,1,0:T(8,128)(2,1)S(1)}, u32[]{:S(2)}, u32[]{:S(2)}) async-start(bf16[16,16,1152]{2,1,0:T(8,128)(2,1)} %bitcast.9), calls=%async_computation.2 | async-start | bytes 1179648 | tf_op jit(solution)/shard_map/all_to_all | solution.py:247
  174.5 0.1 shard_map.110
  174.6 6.6 %collective-permute-start.6 = (f32[36,432]{1,0:T(8,128)S(1)}, f32[36,432]{1,0:T(8,128)S(1)}, u32[]{:S(2)}, u32[]{:S(2)}) collective-permute-start(f32[36,432]{1,0:T(8,128)S(1)} %get-tuple-element.25), channel_id=1, source_target_pairs={{0,16},{16,0},{1,17},{17,1},{2,18},{18,2},{3,19},{19,3},{4,20},{20... | collective-permute-start | bytes 186632 | tf_op jit(solution)/shard_map/ppermute | solution.py:34
  181.2 0.9 collective-permute-done.6
  182.1 3.6 %collective-permute-start.7 = (f32[2,36,432]{2,1,0:T(8,128)S(1)}, f32[2,36,432]{2,1,0:T(8,128)S(1)}, u32[]{:S(2)}, u32[]{:S(2)}) collective-permute-start(f32[2,36,432]{2,1,0:T(8,128)S(1)} %maximum_select_fusion.2), channel_id=1, source_target_pairs={{0,8},{8,0},{1,9},{9,1},{2,10},{10,2},{3,11},{11,3},{4,12},{12,4},... | collective-permute-start | bytes 373256 | tf_op jit(solution)/shard_map/ppermute | solution.py:34
  186.5 5.6 %collective-permute-done.7 = f32[2,36,432]{2,1,0:T(8,128)S(1)} collective-permute-done((f32[2,36,432]{2,1,0:T(8,128)S(1)}, f32[2,36,432]{2,1,0:T(8,128)S(1)}, u32[]{:S(2)}, u32[]{:S(2)}) %collective-permute-start.7) | collective-permute-done | bytes 124448 | tf_op jit(solution)/shard_map/ppermute | solution.py:34
  192.1 0.2 copy.30
  192.4 0.5 mul.91
  192.9 0.1 copy.31
  193.0 0.3 mul.93
  193.3 0.2 copy.28
  193.6 0.0 copy-start.10
  193.6 0.5 mul.83
  194.1 0.0 copy-start.11
  194.1 0.1 copy.29
  194.2 0.3 mul.85
  194.5 0.8 multiply_add_fusion
  195.3 0.7 multiply_add_fusion.1
  196.0 0.8 copy.37
  (25 shorter events, 0.2 us)
Async XLA Ops:
  0.6 47.7 %copy-start = (bf16[128,2304]{1,0:T(8,128)(2,1)S(1)}, bf16[128,2304]{1,0:T(8,128)(2,1)}, u32[]{:S(2)}) copy-start(bf16[128,2304]{1,0:T(8,128)(2,1)} %param.10) | copy-start | bytes 1769476
  0.6 1.1 copy-start.6
  1.8 1.0 copy-start.7
  3.8 8.8 %copy-start.12 = (f32[36,1728]{1,0:T(8,128)S(1)}, f32[36,1728]{1,0:T(8,128)}, u32[]{:S(2)}) copy-start(f32[36,1728]{1,0:T(8,128)} %param.11) | copy-start | bytes 746500
  3.8 30.3 %all-to-all-start = ((bf16[16,16,1728]{2,1,0:T(8,128)(2,1)}), bf16[16,16,1728]{2,1,0:T(8,128)(2,1)S(1)}, u32[]{:S(2)}, u32[]{:S(2)}) async-start(bf16[16,16,1728]{2,1,0:T(8,128)(2,1)} %bitcast.3), calls=%async_computation | async-start | bytes 1835008 | tf_op jit(solution)/shard_map/all_to_all | solution.py:196
  13.8 4.6 %collective-permute-start = (bf16[36,432]{1,0:T(8,128)(2,1)S(1)}, bf16[36,432]{1,0:T(8,128)(2,1)S(1)}, u32[]{:S(2)}, u32[]{:S(2)}) collective-permute-start(bf16[36,432]{1,0:T(8,128)(2,1)S(1)} %reshape.170), channel_id=1, source_target_pairs={{0,16},{16,0},{1,17},{17,1},{2,18},{18,2},{3,19},{19,3},{4,20},{20... | collective-permute-start | bytes 93320 | tf_op jit(solution)/shard_map/ppermute | solution.py:34
  35.2 56.1 %all-to-all-start.1 = ((bf16[16,72,432]{2,1,0:T(8,128)(2,1)}), bf16[16,72,432]{2,1,0:T(8,128)(2,1)}, u32[]{:S(2)}, u32[]{:S(2)}) async-start(bf16[16,72,432]{2,1,0:T(8,128)(2,1)} %broadcast_in_dim.4), calls=%async_computation.1 | async-start | bytes 2359296 | tf_op jit(solution)/shard_map/all_to_all | solution.py:206
  50.3 30.2 %collective-permute-start.2 = (bf16[256,1728]{0,1:T(8,128)(2,1)}, bf16[256,1728]{0,1:T(8,128)(2,1)}, u32[]{:S(2)}, u32[]{:S(2)}) collective-permute-start(bf16[256,1728]{0,1:T(8,128)(2,1)} %copy.23), channel_id=1, source_target_pairs={{0,8},{8,0},{1,9},{9,1},{2,10},{10,2},{3,11},{11,3},{4,12},{12,4},... | collective-permute-start | bytes 2654216 | tf_op jit(solution)/shard_map/ppermute | solution.py:34
  52.2 34.7 %collective-permute-start.1 = (bf16[256,1728]{0,1:T(8,128)(2,1)}, bf16[256,1728]{0,1:T(8,128)(2,1)}, u32[]{:S(2)}, u32[]{:S(2)}) collective-permute-start(bf16[256,1728]{0,1:T(8,128)(2,1)} %copy.23), channel_id=1, source_target_pairs={{0,16},{16,0},{1,17},{17,1},{2,18},{18,2},{3,19},{19,3},{4,20},{20... | collective-permute-start | bytes 2654216 | tf_op jit(solution)/shard_map/ppermute | solution.py:34
  80.5 8.6 %collective-permute-start.3 = (bf16[256,1728]{0,1:T(8,128)(2,1)}, bf16[256,1728]{0,1:T(8,128)(2,1)}, u32[]{:S(2)}, u32[]{:S(2)}) collective-permute-start(bf16[256,1728]{0,1:T(8,128)(2,1)} %collective-permute-done.2), channel_id=1, source_target_pairs={{0,16},{16,0},{1,17},{17,1},{2,18},{18,2},{3,19},{19,3},{4,20},{20... | collective-permute-start | bytes 2654216 | tf_op jit(solution)/shard_map/ppermute | solution.py:34
  91.4 1.2 copy-start.4
  92.5 1.2 copy-start.5
  103.8 1.0 copy-start.3
  104.9 1.0 copy-start.8
  105.8 38.2 %all-to-all-start.3 = ((bf16[16,72,432]{2,1,0:T(8,128)(2,1)}), bf16[16,72,432]{2,1,0:T(8,128)(2,1)S(1)}, u32[]{:S(2)}, u32[]{:S(2)}) async-start(bf16[16,72,432]{2,1,0:T(8,128)(2,1)} %bitcast.33), calls=%async_computation.3 | async-start | bytes 2359296 | tf_op jit(solution)/shard_map/all_to_all | solution.py:223
  114.5 1.2 copy-start.9
  119.6 1.0 copy-start.1
  120.6 30.6 %collective-permute-start.4 = (bf16[512,1152]{1,0:T(8,128)(2,1)}, bf16[512,1152]{1,0:T(8,128)(2,1)}, u32[]{:S(2)}, u32[]{:S(2)}) collective-permute-start(bf16[512,1152]{1,0:T(8,128)(2,1)} %get-tuple-element.15), channel_id=1, source_target_pairs={{0,16},{16,0},{1,17},{17,1},{2,18},{18,2},{3,19},{19,3},{4,20},{20... | collective-permute-start | bytes 3538952 | tf_op jit(solution)/shard_map/ppermute | solution.py:34
  144.2 7.0 %copy-start.2 = (bf16[512,1152]{1,0:T(8,128)(2,1)S(1)}, bf16[512,1152]{1,0:T(8,128)(2,1)}, u32[]{:S(2)}) copy-start(bf16[512,1152]{1,0:T(8,128)(2,1)} %copy-done.1) | copy-start | bytes 3538948
  145.1 22.9 %all-to-all-start.4 = ((bf16[8,72,432]{2,1,0:T(8,128)(2,1)}), bf16[8,72,432]{2,1,0:T(8,128)(2,1)S(1)}, u32[]{:S(2)}, u32[]{:S(2)}) async-start(bf16[8,72,432]{2,1,0:T(8,128)(2,1)} %broadcast_in_dim.5), calls=%async_computation.4 | async-start | bytes 1179648 | tf_op jit(solution)/shard_map/all_to_all | solution.py:226
  152.8 13.5 %collective-permute-start.5 = (bf16[256,1152]{1,0:T(8,128)(2,1)S(1)}, bf16[256,1152]{1,0:T(8,128)(2,1)S(1)}, u32[]{:S(2)}, u32[]{:S(2)}) collective-permute-start(bf16[256,1152]{1,0:T(8,128)(2,1)S(1)} %get-tuple-element.17), channel_id=1, source_target_pairs={{0,8},{8,0},{1,9},{9,1},{2,10},{10,2},{3,11},{11,3},{4,12},{12,4},... | collective-permute-start | bytes 1769480 | tf_op jit(solution)/shard_map/ppermute | solution.py:34
  168.0 18.5 %all-to-all-start.2 = ((bf16[16,16,1152]{2,1,0:T(8,128)(2,1)}), bf16[16,16,1152]{2,1,0:T(8,128)(2,1)S(1)}, u32[]{:S(2)}, u32[]{:S(2)}) async-start(bf16[16,16,1152]{2,1,0:T(8,128)(2,1)} %bitcast.9), calls=%async_computation.2 | async-start | bytes 1179648 | tf_op jit(solution)/shard_map/all_to_all | solution.py:247
  174.6 7.5 %collective-permute-start.6 = (f32[36,432]{1,0:T(8,128)S(1)}, f32[36,432]{1,0:T(8,128)S(1)}, u32[]{:S(2)}, u32[]{:S(2)}) collective-permute-start(f32[36,432]{1,0:T(8,128)S(1)} %get-tuple-element.25), channel_id=1, source_target_pairs={{0,16},{16,0},{1,17},{17,1},{2,18},{18,2},{3,19},{19,3},{4,20},{20... | collective-permute-start | bytes 186632 | tf_op jit(solution)/shard_map/ppermute | solution.py:34
  182.1 10.0 %collective-permute-start.7 = (f32[2,36,432]{2,1,0:T(8,128)S(1)}, f32[2,36,432]{2,1,0:T(8,128)S(1)}, u32[]{:S(2)}, u32[]{:S(2)}) collective-permute-start(f32[2,36,432]{2,1,0:T(8,128)S(1)} %maximum_select_fusion.2), channel_id=1, source_target_pairs={{0,8},{8,0},{1,9},{9,1},{2,10},{10,2},{3,11},{11,3},{4,12},{12,4},... | collective-permute-start | bytes 373256 | tf_op jit(solution)/shard_map/ppermute | solution.py:34
  193.6 1.0 copy-start.10
  194.1 1.2 copy-start.11

commit v2 on v1

v2 whole, which is shorter than its diff:
```python
import math

import jax
import jax.numpy as jnp
from jax import lax
from jax.experimental import pallas as pl
from jax.experimental.pallas import tpu as pltpu
from jax.sharding import Mesh
from jax.sharding import PartitionSpec as P

HEADS = 8
HDIM = 72
norm_eps = 1e-06
loss_scale = 128.0
gamma_slow = 16.97
gamma_fast = 6.94
AXES = ("xh", "z", "c", "xl", "y")
SEQ = ("xl", "y")
F32 = jnp.float32
BF16 = jnp.bfloat16
MIB = 1024 * 1024


def params(mib=48):
    return pltpu.CompilerParams(vmem_limit_bytes=mib * MIB)


def cost(flops, moved):
    return pl.CostEstimate(flops=flops, bytes_accessed=moved, transcendentals=0)


def swap(value, axis):
    return lax.ppermute(value, axis, [(0, 1), (1, 0)])


def shift(value, away):
    count = lax.axis_size("z")
    return lax.ppermute(value, "z", [(i, (i + away) % count) for i in range(count)])


def half_turn(value):
    return shift(value, lax.axis_size("z") // 2)


def both_turn(value):
    count = lax.axis_size("z")
    pairs = [(i, (count - count * (i // count)) + (i % count + count // 2) % count) for i in range(2 * count)]
    return lax.ppermute(value, ("xh", "z"), pairs)


def corner_swap(value):
    return lax.ppermute(value, ("c", "xl"), [(i, 3 - i) for i in range(4)])


def modulate_table(timesteps, ada_weight):
    half_freq = ada_weight.shape[0] // 2
    frequency = jnp.exp(-math.log(10000.0) * jnp.arange(half_freq, dtype=F32) / half_freq)
    angles = timesteps.astype(F32)[:, None] * frequency[None, :]
    embedding = jnp.concatenate([jnp.cos(angles), jnp.sin(angles)], axis=1).astype(BF16)
    return jnp.dot(embedding, ada_weight, preferred_element_type=F32)


def pack_kernel(hidden_ref, cot_ref, out_ref):
    width = hidden_ref.shape[1]
    out_ref[:, :width] = hidden_ref[...]
    out_ref[:, width:] = cot_ref[...].T


def stats(values):
    average = jnp.mean(values, axis=-1, keepdims=True)
    moved = values - average
    variance = jnp.mean(moved * moved, axis=-1, keepdims=True)
    inverse_std = lax.rsqrt(variance + norm_eps)
    return moved * inverse_std, inverse_std


def pick(spot, pieces):
    out = pieces[0]
    for index in range(1, 4):
        out = jnp.where(spot == index, pieces[index], out)
    return out


def norm_kernel(spot_ref, packed_ref, mod_ref, own_ref, core_ref, side_ref):
    width = mod_ref.shape[1] // 2
    quarter = (packed_ref.shape[1] - width) // 4
    centered, _ = stats(packed_ref[:, :width].astype(F32))
    normed = (centered * (1.0 + mod_ref[:, width:]) + mod_ref[:, :width]).astype(BF16)
    cot = packed_ref[:, width:].astype(F32)
    pieces = [cot[:, i * quarter : (i + 1) * quarter] for i in range(4)]
    spot = spot_ref[0]
    own, side, core, both = (pick(spot, [pieces[i ^ flip] for i in range(4)]) for flip in range(4))
    own_ref[:, :width] = normed
    own_ref[:, width : width + quarter] = own.astype(BF16)
    core_ref[:, :width] = normed
    core_ref[:, width : width + quarter] = core.astype(BF16)
    side_ref[:, :width] = normed
    side_ref[:, width : width + 2 * quarter] = jnp.concatenate([side, both], axis=1).astype(BF16)


def norm_back_kernel(packed_ref, mod_ref, *refs):
    out_ref = refs[-1]
    width = mod_ref.shape[1] // 2
    centered, inverse_std = stats(packed_ref[:, :width].astype(F32))
    grads = refs[0][...].astype(F32)
    for ref in refs[1:-1]:
        grads = grads + ref[...].astype(F32)
    grads = grads.astype(BF16).astype(F32)
    upstream = grads * (1.0 + mod_ref[:, width:])
    first = jnp.mean(upstream, axis=-1, keepdims=True)
    second = jnp.mean(upstream * centered, axis=-1, keepdims=True)
    out_ref[...] = (inverse_std * (upstream - first - centered * second)).astype(BF16)


def dot(left, right, over):
    return lax.dot_general(left, right, ((over[0], over[1]), ((), ())), preferred_element_type=F32)


def attend_block(projected, out_grad, same, lane):
    factor = 1.0 / math.sqrt(HDIM)
    wide = 2 * HDIM
    query = projected[:, :wide]
    keys = projected[:, wide : 2 * wide]
    values = projected[:, 2 * wide :].astype(BF16)
    query_low, keys_low = query.astype(BF16), keys.astype(BF16)
    query_grad = key_grad = value_grad = None
    for head in range(2):
        mine = (lane >= head * HDIM) & (lane < (head + 1) * HDIM)
        own_query = jnp.where(mine, query, 0.0).astype(BF16)
        own_keys = jnp.where(mine, keys, 0.0).astype(BF16)
        own_out = jnp.where(mine, out_grad, 0.0).astype(BF16)
        scores = dot(own_query, keys_low, ((1,), (1,))) * factor
        scores = jnp.where(same, scores, -1e30)
        top = jnp.max(scores, axis=-1, keepdims=True)
        expo = jnp.exp(scores - top)
        attention = expo / jnp.sum(expo, axis=-1, keepdims=True)
        prob_grad = dot(own_out, values, ((1,), (1,)))
        row_dot = jnp.sum(attention * prob_grad, axis=-1, keepdims=True)
        score_grad = (attention * (prob_grad - row_dot)).astype(BF16)
        parts = (
            dot(score_grad, own_keys, ((1,), (0,))),
            dot(score_grad, own_query, ((0,), (0,))),
            dot(attention.astype(BF16), own_out, ((0,), (0,))),
        )
        if head == 0:
            query_grad, key_grad, value_grad = parts
        else:
            query_grad, key_grad, value_grad = (
                query_grad + parts[0],
                key_grad + parts[1],
                value_grad + parts[2],
            )
    return jnp.concatenate([query_grad * factor, key_grad * factor, value_grad], axis=1)


def main_kernel(spot_ref, own_ref, core_ref, side_ref, both_ref, weight_ref, grads_ref, near_ref, up_ref, down_ref, low_ref, high_ref, total_ref):
    tokens = own_ref.shape[0]
    model_width = weight_ref.shape[0]
    quarter = weight_ref.shape[1] // 3
    row = lax.broadcasted_iota(jnp.int32, (tokens, tokens), 0)
    col = lax.broadcasted_iota(jnp.int32, (tokens, tokens), 1)
    same = lax.rem(row, 16) == lax.rem(col, 16)
    lane = lax.broadcasted_iota(jnp.int32, (tokens, quarter), 1)
    for index, (ref, skip) in enumerate(((own_ref, 0), (core_ref, 0), (side_ref, 0), (both_ref, 1))):
        projected = dot(ref[:, :model_width], weight_ref[...], ((1,), (0,)))
        projected = projected.astype(BF16).astype(F32)
        cot = ref[:, model_width:].astype(F32)
        out_grad = cot[:, skip * quarter : (skip + 1) * quarter]
        grads = attend_block(projected, out_grad, same, lane).astype(BF16)
        grads_ref[index * tokens : (index + 1) * tokens, :] = grads
        part = dot(ref[:, :model_width], grads, ((0,), (0,)))
        if index == 0:
            total_ref[...] = part
        else:
            total_ref[...] += part
    place = spot_ref[1]
    height = model_width // 16
    for ahead, targets in enumerate(((near_ref,), (up_ref,), (low_ref, high_ref), (down_ref,))):
        lowest = lax.rem(place + ahead, 4)
        for group in range(4):
            ref = targets[group * len(targets) // 4]
            first = pl.multiple_of((4 * group + lowest) * height, 8)
            ref[group % ref.shape[0]] = total_ref[pl.ds(first, height), :].astype(BF16)


def input_kernel(grads_ref, weight_ref, *refs):
    height = refs[0].shape[0]
    for index, ref in enumerate(refs):
        part = dot(grads_ref[index * height : (index + 1) * height, :], weight_ref[...], ((1,), (1,)))
        ref[...] = part.astype(BF16)


def columns_kernel(spot_ref, master_ref, mine_ref, theirs_ref):
    quarter = master_ref.shape[1] // 12
    spot = spot_ref[0]
    for flip, ref in ((0, mine_ref), (2, theirs_ref)):
        parts = []
        for part in range(3):
            pieces = [master_ref[:, (4 * part + i) * quarter : (4 * part + i + 1) * quarter] for i in range(4)]
            parts.append(pick(spot, [pieces[i ^ flip] for i in range(4)]))
        ref[...] = jnp.concatenate(parts, axis=1).astype(BF16)


def pair_kernel(spot_ref, mine_ref, theirs_ref, out_ref):
    mine, theirs = mine_ref[...].astype(F32), theirs_ref[...].astype(F32)
    first = spot_ref[0] < 2
    upper, lower = jnp.where(first, mine, theirs), jnp.where(first, theirs, mine)
    out_ref[...] = jnp.concatenate([upper, lower], axis=0).astype(BF16)


def quad_kernel(spot_ref, own_ref, far_ref, across_ref, both_ref, out_ref):
    place = spot_ref[2]
    out_ref[place] = own_ref[...]
    out_ref[place + 1 - 2 * lax.rem(place, 2)] = far_ref[...]
    out_ref[lax.rem(place + 2, 4)] = across_ref[...]
    out_ref[3 - place] = both_ref[...]


def gather_kernel(spot_ref, near_ref, up_ref, low_ref, high_ref, down_ref, out_ref):
    place = spot_ref[1]
    for ahead, sources in enumerate(((near_ref,), (up_ref,), (low_ref, high_ref), (down_ref,))):
        lowest = lax.rem(place + ahead, 4)
        for group in range(4):
            ref = sources[group * len(sources) // 4]
            out_ref[4 * group + lowest] = ref[group % ref.shape[0]]


def reduce_kernel(spot_ref, near_ref, up_ref, low_ref, high_ref, down_ref, own_ref, far_ref, across_ref, both_ref, total_ref):
    place = spot_ref[2]
    for group in range(4):
        far = low_ref if group < 2 else high_ref
        total = near_ref[group].astype(F32) + up_ref[group].astype(F32)
        total_ref[group] = total + down_ref[group].astype(F32) + far[group % 2].astype(F32)
    own_ref[...] = total_ref[place]
    far_ref[...] = total_ref[place + 1 - 2 * lax.rem(place, 2)].astype(BF16)
    across_ref[...] = total_ref[lax.rem(place + 2, 4)].astype(BF16)
    both_ref[...] = total_ref[3 - place].astype(BF16)


def copies_kernel(own_ref, far_ref, across_ref, both_ref, out_ref):
    total = own_ref[...] + far_ref[...].astype(F32) + across_ref[...].astype(F32) + both_ref[...].astype(F32)
    total = total.astype(BF16)
    for index in range(out_ref.shape[0]):
        out_ref[index] = total


def rows_kernel(spot_ref, parts_ref, own_ref, other_ref):
    total = parts_ref[0].astype(F32)
    for index in range(1, parts_ref.shape[0]):
        total = total + parts_ref[index].astype(F32)
    height = own_ref.shape[0]
    first = spot_ref[0] < 2
    upper, lower = total[:height], total[height:]
    own_ref[...] = jnp.where(first, upper, lower)
    other_ref[...] = jnp.where(first, lower, upper)


def average_kernel(spot_ref, decay_ref, own_ref, side_ref, core_ref, both_ref, slow_ref, fast_ref, slow_out, fast_out):
    quarter = own_ref.shape[1] // 3
    spot = spot_ref[0]
    values = [ref[...] for ref in (own_ref, side_ref, core_ref, both_ref)]
    picked = [pick(spot, [values[i ^ place] for i in range(4)]) for place in range(4)]
    columns = [picked[place][:, part * quarter : (part + 1) * quarter] for part in range(3) for place in range(4)]
    grad = jnp.concatenate(columns, axis=1) / loss_scale
    slow_out[...] = decay_ref[0] * slow_ref[...] + (1.0 - decay_ref[0]) * grad
    fast_out[...] = decay_ref[1] * fast_ref[...] + (1.0 - decay_ref[1]) * grad


def call(kernel, outs, *args, flops=0, scratch=(), mib=48, smem=0):
    moved = sum(a.size * a.dtype.itemsize for a in args)
    moved += sum(math.prod(shape) * jnp.dtype(kind).itemsize for shape, kind in outs)
    shapes = [jax.ShapeDtypeStruct(shape, kind) for shape, kind in outs]
    specs = [pl.BlockSpec(memory_space=pltpu.SMEM if i < smem else pltpu.VMEM) for i in range(len(args))]
    got = pl.pallas_call(
        kernel,
        out_shape=shapes,
        in_specs=specs,
        out_specs=[pl.BlockSpec(memory_space=pltpu.VMEM)] * len(shapes),
        scratch_shapes=list(scratch),
        compiler_params=params(mib),
        cost_estimate=cost(flops, moved),
    )(*args)
    return got[0] if len(got) == 1 else got


def lanes(count):
    return -(-count // 128) * 128


def on_device(hidden, timesteps, ada_weight, master, ema_slow, ema_fast, step_count, cotangent):
    patches, width = hidden.shape[2:]
    inner = cotangent.shape[3]
    own_rows, triple = master.shape
    wide = width + inner
    n_seq = lax.axis_size("xl") * lax.axis_size("y")
    n_y = lax.axis_size("y")
    quarter = inner // 4
    cols = 3 * quarter
    pair_rows = 2 * own_rows
    core, side = lax.axis_index("c"), lax.axis_index("xl")
    across, along = lax.axis_index("xh"), lax.axis_index("z")
    spots = jnp.stack([2 * core + side, lax.rem(along, 4), 2 * across + along // 4]).astype(jnp.int32)

    packed = call(pack_kernel, [((patches, wide), BF16)], hidden[0, 0], cotangent[0, 0].T)
    tokens = lax.all_to_all(packed.reshape(n_seq, patches // n_seq, wide), SEQ, 0, 0, tiled=True)
    tokens = tokens.reshape(patches, wide)

    mine, theirs = call(columns_kernel, [((own_rows, cols), BF16)] * 2, spots, master, smem=1)
    pair = call(pair_kernel, [((pair_rows, cols), BF16)], spots, mine, swap(theirs, "c"), smem=1)
    quad = call(
        quad_kernel,
        [((4, pair_rows, cols), BF16)],
        spots, pair, half_turn(pair), swap(pair, "xh"), both_turn(pair),
        smem=1,
    )
    weights = call(
        gather_kernel,
        [((16, pair_rows, cols), BF16)],
        spots, quad, shift(quad, -1), shift(quad[:2], -2), shift(quad[2:], 2), shift(quad, 1),
        smem=1,
    ).reshape(width, cols)

    modulation = modulate_table(timesteps, ada_weight)
    narrow, broad = lanes(width + quarter), lanes(width + 2 * quarter)
    own, to_core, to_side = call(
        norm_kernel,
        [((patches, narrow), BF16), ((patches, narrow), BF16), ((patches, broad), BF16)],
        spots, tokens, modulation,
        smem=1,
    )
    from_side = swap(to_side, "xl")
    from_core = swap(to_core, "c")
    from_both = swap(from_side, "c")

    quads = ((4, pair_rows, cols), BF16)
    halves = ((2, pair_rows, cols), BF16)
    grads, near, up, down, low, high = call(
        main_kernel,
        [((4 * patches, cols), BF16), quads, quads, quads, halves, halves],
        spots, own, from_core, from_side, from_both, weights,
        flops=4 * 4 * patches * width * cols,
        scratch=[pltpu.VMEM((width, cols), F32)],
        smem=1,
    )

    block = (pair_rows, cols)
    own_part, far, beside, corner = call(
        reduce_kernel,
        [(block, F32), (block, BF16), (block, BF16), (block, BF16)],
        spots, near, shift(up, 1), shift(low, 2), shift(high, -2), shift(down, -1),
        scratch=[pltpu.VMEM((4,) + block, F32)],
        smem=1,
    )
    copies = call(
        copies_kernel,
        [((n_y,) + block, BF16)],
        own_part, half_turn(far), swap(beside, "xh"), both_turn(corner),
    )
    parts = lax.all_to_all(copies, "y", 0, 0, tiled=True)
    own_grad, other_grad = call(rows_kernel, [((own_rows, cols), F32)] * 2, spots, parts, smem=1)
    base = 1.0 - 1.0 / step_count[0].astype(F32)
    decays = jnp.stack([jnp.power(base, gamma_slow + 1.0), jnp.power(base, gamma_fast + 1.0)])
    ema_slow_next, ema_fast_next = call(
        average_kernel,
        [((own_rows, triple), F32)] * 2,
        spots, decays, own_grad, swap(own_grad, "xl"), swap(other_grad, "c"), corner_swap(other_grad), ema_slow, ema_fast,
        smem=2,
    )

    whole = ((patches, width), BF16)
    mine_in, core_in, side_in, both_in = call(
        input_kernel,
        [whole] * 4,
        grads, weights,
        flops=8 * patches * width * cols,
    )
    back = call(
        norm_back_kernel,
        [whole],
        tokens, modulation, mine_in, swap(core_in, "c"), swap(side_in, "xl"), corner_swap(both_in),
    )
    back = lax.all_to_all(back.reshape(n_seq, patches // n_seq, width), SEQ, 0, 0, tiled=True)
    return (back.reshape(hidden.shape), ema_slow_next, ema_fast_next)


def solution(mesh):
    fine = Mesh(mesh.devices.reshape(2, 8, 2, 2, 8), AXES)
    dp, seq = ("xh", "z", "c"), SEQ
    placed = (
        P(dp, seq, None, None),
        P(dp),
        P(),
        P(dp, None),
        P(dp, None),
        P(dp, None),
        P(),
        P(dp, seq, None, None),
    )
    return jax.shard_map(
        on_device,
        mesh=fine,
        in_specs=placed,
        out_specs=(P(dp, seq, None, None), P(dp, None), P(dp, None)),
        check_vma=False,
    )
```

time: 198 us -> 243 us (1.23)
  starting transfers between devices: 73.1 us -> 114 us
  waiting for transfers between devices: 78.1 us -> 94.5 us
  local copies, waits for them, and re-layouts: 22.2 us -> 6.17 us
  Pallas kernels: 19 us -> 22.5 us
    ppermute x0 -> x14, starting transfers between devices: none -> 58.3 us  [the longest x10 42 us: shift(): lax.ppermute(value, 'z', [(i, (i + away) % count) for i in range(count)])]
    ppermute x0 -> x14, waiting for transfers between devices: none -> 41.4 us  [the longest x10 16.3 us: shift(): lax.ppermute(value, 'z', [(i, (i + away) % count) for i in range(count)])]
    all_to_all x3 -> x1, starting transfers between devices: 27.9 us -> 5.41 us  [on_device(): parts = lax.all_to_all(copies, 'y', 0, 0, tiled=True)]
    all_to_all x3 -> x1, waiting for transfers between devices: 21.2 us -> 0.01 us  [on_device(): parts = lax.all_to_all(copies, 'y', 0, 0, tiled=True)]
    ppermute x8 -> x10, waiting for transfers between devices: 41.2 us -> 32.6 us  [swap(): return lax.ppermute(value, axis, [(0, 1), (1, 0)])]
    ppermute x3 -> x0, local copies, waits for them, and re-layouts: 5.88 us -> none  [swap(): return lax.ppermute(value, axis, [(0, 1), (1, 0)])]
    all_to_all x1, waiting for transfers between devices: 15.7 us -> 20.4 us  [on_device(): lax.all_to_all(packed.reshape(n_seq, patches // n_seq, wide), SEQ, 0, 0,...]
    ppermute x8 -> x10, starting transfers between devices: 30 us -> 33.9 us  [swap(): return lax.ppermute(value, axis, [(0, 1), (1, 0)])]
  transfers between devices with their start and end apart: 13 -> 27, of which waited for: 6 -> 13; matrix products, arithmetic and copies ran while one was open for 5% -> 0% of each run, Pallas kernels for 4% -> 3%
where the time goes in v2:
time: 243 us; the launch traced here: 241 us
  starting transfers between devices  114 us (47%)
  waiting for transfers between devices  94.5 us (39%)
  Pallas kernels  22.5 us (9%)
  local copies, waits for them, and re-layouts  6.17 us (3%)
  between operations  2.56 us (1%)
    ppermute x10, starting transfers between devices, shift(): lax.ppermute(value, 'z', [(i, (i + away) % count) for i in range(count)])  42 us
    ppermute x10, starting transfers between devices, swap(): return lax.ppermute(value, axis, [(0, 1), (1, 0)])  33.9 us
    ppermute x10, waiting for transfers between devices, swap(): return lax.ppermute(value, axis, [(0, 1), (1, 0)])  32.6 us
    pallas_call x13, Pallas kernels, call(): pl.pallas_call(kernel, out_shape=shapes, in_specs=specs, out_specs=[pl.Bl...  22.5 us
    all_to_all x1, waiting for transfers between devices, on_device(): lax.all_to_all(packed.reshape(n_seq, patches // n_seq, wide), SEQ, 0, 0,...  20.4 us
    ppermute x10, waiting for transfers between devices, shift(): lax.ppermute(value, 'z', [(i, (i + away) % count) for i in range(count)])  16.3 us
    ppermute x2, waiting for transfers between devices, corner_swap(): return lax.ppermute(value, ('c', 'xl'), [(i, 3 - i) for i in range(4)])  12.7 us
    ppermute x2, waiting for transfers between devices, both_turn(): return lax.ppermute(value, ('xh', 'z'), pairs)  12.4 us
  transfers between devices with their start and end apart: 27, of which 13 were waited for; matrix products, arithmetic and copies ran while one was open for 0% of the time, Pallas kernels for 3%

profile of v2, /device:TPU:1, one launch (start us, length us, event | category | flops | bytes accessed | tf_op | source)
XLA Modules:
  0.0 240.6 jit_solution(8216826616549022564)
XLA Ops:
  0.6 0.0 copy-start
  0.7 1.1 copy-done.3
  1.8 1.0 copy-done.4
  2.7 1.1 shard_map.103
  3.8 8.7 %all-to-all-start = ((bf16[16,16,1728]{2,1,0:T(8,128)(2,1)}), bf16[16,16,1728]{2,1,0:T(8,128)(2,1)S(1)}, u32[]{:S(2)}, u32[]{:S(2)}) async-start(bf16[16,16,1728]{2,1,0:T(8,128)(2,1)} %bitcast.3), calls=%async_computation | async-start | bytes 1835008 | tf_op jit(solution)/shard_map/all_to_all | solution.py:305
  12.5 0.0 copy-start.5
  13.2 0.1 pad_add_fusion.spot_ref
  13.4 0.2 fusion.mod_ref
  13.6 20.4 %all-to-all-done = bf16[16,16,1728]{2,1,0:T(8,128)(2,1)S(1)} async-done(((bf16[16,16,1728]{2,1,0:T(8,128)(2,1)}), bf16[16,16,1728]{2,1,0:T(8,128)(2,1)S(1)}, u32[]{:S(2)}, u32[]{:S(2)}) %all-to-all-start) | async-done | bytes 884768 | tf_op jit(solution)/shard_map/all_to_all | solution.py:305
  34.0 1.8 shard_map.104
  35.8 2.1 collective-permute-start.1
  37.9 15.8 %collective-permute-done.1.side_ref = bf16[256,1536]{1,0:T(8,128)(2,1)S(1)} collective-permute-done((bf16[256,1536]{1,0:T(8,128)(2,1)S(1)}, bf16[256,1536]{1,0:T(8,128)(2,1)S(1)}, u32[]{:S(2)}, u32[]{:S(2)}) %collective-permute-start.1) | collective-permute-done | bytes 786464 | tf_op jit(solution)/shard_map/ppermute | solution.py:33
  53.7 5.9 %collective-permute-start.2 = (bf16[256,1536]{1,0:T(8,128)(2,1)S(1)}, bf16[256,1536]{1,0:T(8,128)(2,1)S(1)}, u32[]{:S(2)}, u32[]{:S(2)}) collective-permute-start(bf16[256,1536]{1,0:T(8,128)(2,1)S(1)} %collective-permute-done.1.side_ref), channel_id=1, source_target_pairs={{0,16},{16,0},{1,17},{17,1},{2,18},{18,2},{3,19},{19,3},{4,20},{20... | collective-permute-start | bytes 2359304 | tf_op jit(solution)/shard_map/ppermute | solution.py:33
  59.6 1.9 collective-permute-start
  61.5 0.9 shard_map.105
  62.4 2.4 %collective-permute-start.3 = (bf16[36,432]{1,0:T(8,128)(2,1)S(1)}, bf16[36,432]{1,0:T(8,128)(2,1)S(1)}, u32[]{:S(2)}, u32[]{:S(2)}) collective-permute-start(bf16[36,432]{1,0:T(8,128)(2,1)S(1)} %get-tuple-element.30), channel_id=1, source_target_pairs={{0,16},{16,0},{1,17},{17,1},{2,18},{18,2},{3,19},{19,3},{4,20},{20... | collective-permute-start | bytes 93320 | tf_op jit(solution)/shard_map/ppermute | solution.py:33
  64.8 0.8 collective-permute-done.3.theirs_ref
  65.6 0.6 shard_map.106.own_ref
  66.2 11.4 %collective-permute-start.4 = (bf16[72,432]{1,0:T(8,128)(2,1)S(1)}, bf16[72,432]{1,0:T(8,128)(2,1)S(1)}, u32[]{:S(2)}, u32[]{:S(2)}) collective-permute-start(bf16[72,432]{1,0:T(8,128)(2,1)S(1)} %shard_map.106.own_ref), channel_id=1, source_target_pairs={{0,128},{32,160},{64,192},{96,224},{128,0},{160,32},{192,64},{224,... | collective-permute-start | bytes 186632 | tf_op jit(solution)/shard_map/ppermute | solution.py:38
  77.6 4.4 %collective-permute-start.5 = (bf16[72,432]{1,0:T(8,128)(2,1)S(1)}, bf16[72,432]{1,0:T(8,128)(2,1)S(1)}, u32[]{:S(2)}, u32[]{:S(2)}) collective-permute-start(bf16[72,432]{1,0:T(8,128)(2,1)S(1)} %shard_map.106.own_ref), channel_id=1, source_target_pairs={{0,256},{256,0},{1,257},{257,1},{2,258},{258,2},{3,259},{259,3},{4... | collective-permute-start | bytes 186632 | tf_op jit(solution)/shard_map/ppermute | solution.py:33
  81.9 2.2 collective-permute-start.6
  84.1 0.1 collective-permute-done.5.across_ref
  84.2 9.5 %collective-permute-done.6.both_ref = bf16[72,432]{1,0:T(8,128)(2,1)S(1)} collective-permute-done((bf16[72,432]{1,0:T(8,128)(2,1)S(1)}, bf16[72,432]{1,0:T(8,128)(2,1)S(1)}, u32[]{:S(2)}, u32[]{:S(2)}) %collective-permute-start.6) | collective-permute-done | bytes 62240 | tf_op jit(solution)/shard_map/ppermute | solution.py:48
  93.6 0.6 shard_map.107.near_ref
  94.2 4.0 %collective-permute-start.8 = (bf16[2,72,432]{2,1,0:T(8,128)(2,1)S(1)}, bf16[2,72,432]{2,1,0:T(8,128)(2,1)S(1)}, u32[]{:S(2)}, u32[]{:S(2)}) collective-permute-start(bf16[2,72,432]{2,1,0:T(8,128)(2,1)S(1)} %get-tuple-element.50), channel_id=1, source_target_pairs={{0,192},{32,224},{64,0},{96,32},{128,64},{160,96},{192,128},{224,1... | collective-permute-start | bytes 373256 | tf_op jit(solution)/shard_map/ppermute | solution.py:38
  98.2 1.9 collective-permute-start.10
  100.2 4.6 %collective-permute-start.7 = (bf16[4,72,432]{2,1,0:T(8,128)(2,1)S(1)}, bf16[4,72,432]{2,1,0:T(8,128)(2,1)S(1)}, u32[]{:S(2)}, u32[]{:S(2)}) collective-permute-start(bf16[4,72,432]{2,1,0:T(8,128)(2,1)S(1)} %shard_map.107.near_ref), channel_id=1, source_target_pairs={{0,224},{32,0},{64,32},{96,64},{128,96},{160,128},{192,160},{224,1... | collective-permute-start | bytes 746504 | tf_op jit(solution)/shard_map/ppermute | solution.py:38
  104.7 3.3 %collective-permute-start.9 = (bf16[2,72,432]{2,1,0:T(8,128)(2,1)S(1)}, bf16[2,72,432]{2,1,0:T(8,128)(2,1)S(1)}, u32[]{:S(2)}, u32[]{:S(2)}) collective-permute-start(bf16[2,72,432]{2,1,0:T(8,128)(2,1)S(1)} %get-tuple-element.49), channel_id=1, source_target_pairs={{0,64},{32,96},{64,128},{96,160},{128,192},{160,224},{192,0},{224,... | collective-permute-start | bytes 373256 | tf_op jit(solution)/shard_map/ppermute | solution.py:38
  108.0 6.3 %collective-permute-done.9.high_ref = bf16[2,72,432]{2,1,0:T(8,128)(2,1)S(1)} collective-permute-done((bf16[2,72,432]{2,1,0:T(8,128)(2,1)S(1)}, bf16[2,72,432]{2,1,0:T(8,128)(2,1)S(1)}, u32[]{:S(2)}, u32[]{:S(2)}) %collective-permute-start.9) | collective-permute-done | bytes 124448 | tf_op jit(solution)/shard_map/ppermute | solution.py:38
  114.3 0.6 shard_map.108
  115.0 1.0 copy-done.1
  116.0 9.7 %shard_map.109 = (bf16[1024,432]{1,0:T(8,128)(2,1)S(1)}, bf16[4,72,432]{2,1,0:T(8,128)(2,1)S(1)}, bf16[4,72,432]{2,1,0:T(8,128)(2,1)S(1)}, bf16[4,72,432]{2,1,0:...) custom-call(s32[3]{0:T(128)S(1)} %pad_add_fusion.spot_ref, ...), custom_call_target="tpu_custom_call" | custom-call | flops 2038431744 | bytes 5890060 | tf_op jit(solution)/shard_map/pallas_call | solution.py:274
  125.8 1.0 copy-done.8
  126.7 1.9 collective-permute-start.14
  128.7 4.5 %collective-permute-start.17 = (bf16[4,72,432]{2,1,0:T(8,128)(2,1)S(1)}, bf16[4,72,432]{2,1,0:T(8,128)(2,1)S(1)}, u32[]{:S(2)}, u32[]{:S(2)}) collective-permute-start(bf16[4,72,432]{2,1,0:T(8,128)(2,1)S(1)} %get-tuple-element.40), channel_id=1, source_target_pairs={{0,224},{32,0},{64,32},{96,64},{128,96},{160,128},{192,160},{224,1... | collective-permute-start | bytes 746504 | tf_op jit(solution)/shard_map/ppermute | solution.py:38
  133.2 3.4 %collective-permute-start.15 = (bf16[2,72,432]{2,1,0:T(8,128)(2,1)S(1)}, bf16[2,72,432]{2,1,0:T(8,128)(2,1)S(1)}, u32[]{:S(2)}, u32[]{:S(2)}) collective-permute-start(bf16[2,72,432]{2,1,0:T(8,128)(2,1)S(1)} %get-tuple-element.38), channel_id=1, source_target_pairs={{0,64},{32,96},{64,128},{96,160},{128,192},{160,224},{192,0},{224,... | collective-permute-start | bytes 373256 | tf_op jit(solution)/shard_map/ppermute | solution.py:38
  136.7 4.0 %collective-permute-start.16 = (bf16[2,72,432]{2,1,0:T(8,128)(2,1)S(1)}, bf16[2,72,432]{2,1,0:T(8,128)(2,1)S(1)}, u32[]{:S(2)}, u32[]{:S(2)}) collective-permute-start(bf16[2,72,432]{2,1,0:T(8,128)(2,1)S(1)} %get-tuple-element.39), channel_id=1, source_target_pairs={{0,192},{32,224},{64,0},{96,32},{128,64},{160,96},{192,128},{224,1... | collective-permute-start | bytes 373256 | tf_op jit(solution)/shard_map/ppermute | solution.py:38
  140.7 2.7 %collective-permute-done.15.low_ref = bf16[2,72,432]{2,1,0:T(8,128)(2,1)S(1)} collective-permute-done((bf16[2,72,432]{2,1,0:T(8,128)(2,1)S(1)}, bf16[2,72,432]{2,1,0:T(8,128)(2,1)S(1)}, u32[]{:S(2)}, u32[]{:S(2)}) %collective-permute-start.15) | collective-permute-done | bytes 124448 | tf_op jit(solution)/shard_map/ppermute | solution.py:38
  143.3 7.3 %collective-permute-done.16.high_ref = bf16[2,72,432]{2,1,0:T(8,128)(2,1)S(1)} collective-permute-done((bf16[2,72,432]{2,1,0:T(8,128)(2,1)S(1)}, bf16[2,72,432]{2,1,0:T(8,128)(2,1)S(1)}, u32[]{:S(2)}, u32[]{:S(2)}) %collective-permute-start.16) | collective-permute-done | bytes 124448 | tf_op jit(solution)/shard_map/ppermute | solution.py:38
  150.6 0.7 shard_map.112
  151.4 3.0 %collective-permute-start.18 = (bf16[72,432]{1,0:T(8,128)(2,1)S(1)}, bf16[72,432]{1,0:T(8,128)(2,1)S(1)}, u32[]{:S(2)}, u32[]{:S(2)}) collective-permute-start(bf16[72,432]{1,0:T(8,128)(2,1)S(1)} %get-tuple-element.42), channel_id=1, source_target_pairs={{0,128},{32,160},{64,192},{96,224},{128,0},{160,32},{192,64},{224,... | collective-permute-start | bytes 186632 | tf_op jit(solution)/shard_map/ppermute | solution.py:38
  154.4 2.4 %collective-permute-start.19 = (bf16[72,432]{1,0:T(8,128)(2,1)S(1)}, bf16[72,432]{1,0:T(8,128)(2,1)S(1)}, u32[]{:S(2)}, u32[]{:S(2)}) collective-permute-start(bf16[72,432]{1,0:T(8,128)(2,1)S(1)} %get-tuple-element.43), channel_id=1, source_target_pairs={{0,256},{256,0},{1,257},{257,1},{2,258},{258,2},{3,259},{259,3},{4... | collective-permute-start | bytes 186632 | tf_op jit(solution)/shard_map/ppermute | solution.py:33
  156.9 8.5 %collective-permute-start.20 = (bf16[72,432]{1,0:T(8,128)(2,1)S(1)}, bf16[72,432]{1,0:T(8,128)(2,1)S(1)}, u32[]{:S(2)}, u32[]{:S(2)}) collective-permute-start(bf16[72,432]{1,0:T(8,128)(2,1)S(1)} %get-tuple-element.44), channel_id=1, source_target_pairs={{0,384},{32,416},{64,448},{96,480},{128,256},{160,288},{192,320},{... | collective-permute-start | bytes 186632 | tf_op jit(solution)/shard_map/ppermute | solution.py:48
  165.4 2.9 %collective-permute-done.20.both_ref = bf16[72,432]{1,0:T(8,128)(2,1)S(1)} collective-permute-done((bf16[72,432]{1,0:T(8,128)(2,1)S(1)}, bf16[72,432]{1,0:T(8,128)(2,1)S(1)}, u32[]{:S(2)}, u32[]{:S(2)}) %collective-permute-start.20) | collective-permute-done | bytes 62240 | tf_op jit(solution)/shard_map/ppermute | solution.py:48
  168.3 0.9 shard_map.113
  169.2 5.4 %all-to-all-start.2 = ((bf16[8,72,432]{2,1,0:T(8,128)(2,1)}), bf16[8,72,432]{2,1,0:T(8,128)(2,1)S(1)}, u32[]{:S(2)}, u32[]{:S(2)}) async-start(bf16[8,72,432]{2,1,0:T(8,128)(2,1)} %shard_map.113), calls=%async_computation.2 | async-start | bytes 1179648 | tf_op jit(solution)/shard_map/all_to_all | solution.py:359
  174.6 1.2 copy-done.9
  175.8 1.6 shard_map.110
  177.4 7.1 %collective-permute-start.11 = (bf16[256,1152]{1,0:T(8,128)(2,1)S(1)}, bf16[256,1152]{1,0:T(8,128)(2,1)S(1)}, u32[]{:S(2)}, u32[]{:S(2)}) collective-permute-start(bf16[256,1152]{1,0:T(8,128)(2,1)S(1)} %get-tuple-element.33), channel_id=1, source_target_pairs={{0,16},{16,0},{1,17},{17,1},{2,18},{18,2},{3,19},{19,3},{4,20},{20... | collective-permute-start | bytes 1769480 | tf_op jit(solution)/shard_map/ppermute | solution.py:33
  184.5 3.2 %collective-permute-start.12 = (bf16[256,1152]{1,0:T(8,128)(2,1)S(1)}, bf16[256,1152]{1,0:T(8,128)(2,1)S(1)}, u32[]{:S(2)}, u32[]{:S(2)}) collective-permute-start(bf16[256,1152]{1,0:T(8,128)(2,1)S(1)} %get-tuple-element.34), channel_id=1, source_target_pairs={{0,8},{8,0},{1,9},{9,1},{2,10},{10,2},{3,11},{11,3},{4,12},{12,4},... | collective-permute-start | bytes 1769480 | tf_op jit(solution)/shard_map/ppermute | solution.py:33
  187.7 2.3 collective-permute-start.13
  190.0 11.4 %collective-permute-done.12.refs_2_ = bf16[256,1152]{1,0:T(8,128)(2,1)S(1)} collective-permute-done((bf16[256,1152]{1,0:T(8,128)(2,1)S(1)}, bf16[256,1152]{1,0:T(8,128)(2,1)S(1)}, u32[]{:S(2)}, u32[]{:S(2)}) %collective-permute-start.12) | collective-permute-done | bytes 589856 | tf_op jit(solution)/shard_map/ppermute | solution.py:33
  201.3 12.7 %collective-permute-done.13.refs_3_ = bf16[256,1152]{1,0:T(8,128)(2,1)S(1)} collective-permute-done((bf16[256,1152]{1,0:T(8,128)(2,1)S(1)}, bf16[256,1152]{1,0:T(8,128)(2,1)S(1)}, u32[]{:S(2)}, u32[]{:S(2)}) %collective-permute-start.13) | collective-permute-done | bytes 589856 | tf_op jit(solution)/shard_map/ppermute | solution.py:52
  214.1 1.8 shard_map.111
  215.9 8.2 %all-to-all-start.1 = ((bf16[16,16,1152]{2,1,0:T(8,128)(2,1)}), bf16[16,16,1152]{2,1,0:T(8,128)(2,1)S(1)}, u32[]{:S(2)}, u32[]{:S(2)}) async-start(bf16[16,16,1152]{2,1,0:T(8,128)(2,1)} %bitcast.11), calls=%async_computation.1 | async-start | bytes 1179648 | tf_op jit(solution)/shard_map/all_to_all | solution.py:382
  224.9 0.6 shard_map.114
  225.5 2.5 %collective-permute-start.22 = (f32[36,432]{1,0:T(8,128)S(1)}, f32[36,432]{1,0:T(8,128)S(1)}, u32[]{:S(2)}, u32[]{:S(2)}) collective-permute-start(f32[36,432]{1,0:T(8,128)S(1)} %get-tuple-element.46), channel_id=1, source_target_pairs={{0,16},{16,0},{1,17},{17,1},{2,18},{18,2},{3,19},{19,3},{4,20},{20... | collective-permute-start | bytes 186632 | tf_op jit(solution)/shard_map/ppermute | solution.py:33
  228.0 3.5 %collective-permute-start.23 = (f32[36,432]{1,0:T(8,128)S(1)}, f32[36,432]{1,0:T(8,128)S(1)}, u32[]{:S(2)}, u32[]{:S(2)}) collective-permute-start(f32[36,432]{1,0:T(8,128)S(1)} %get-tuple-element.46), channel_id=1, source_target_pairs={{0,24},{8,16},{16,8},{24,0},{1,25},{9,17},{17,9},{25,1},{2,26},{10... | collective-permute-start | bytes 186632 | tf_op jit(solution)/shard_map/ppermute | solution.py:52
  231.5 2.0 collective-permute-start.21
  233.5 0.1 pad_maximum_fusion.decay_ref
  233.6 4.6 %collective-permute-done.21.side_ref = f32[36,432]{1,0:T(8,128)S(1)} collective-permute-done((f32[36,432]{1,0:T(8,128)S(1)}, f32[36,432]{1,0:T(8,128)S(1)}, u32[]{:S(2)}, u32[]{:S(2)}) %collective-permute-start.21) | collective-permute-done | bytes 62240 | tf_op jit(solution)/shard_map/ppermute | solution.py:33
  238.2 1.5 shard_map.115
  239.7 0.1 all-to-all-done.1
  239.8 0.8 copy.14
  (29 shorter events, 0.1 us)
Async XLA Ops:
  0.6 12.7 %copy-start = (bf16[128,2304]{1,0:T(8,128)(2,1)S(1)}, bf16[128,2304]{1,0:T(8,128)(2,1)}, u32[]{:S(2)}) copy-start(bf16[128,2304]{1,0:T(8,128)(2,1)} %param.10) | copy-start | bytes 1769476
  0.6 1.1 copy-start.3
  1.8 1.0 copy-start.4
  3.8 30.2 %all-to-all-start = ((bf16[16,16,1728]{2,1,0:T(8,128)(2,1)}), bf16[16,16,1728]{2,1,0:T(8,128)(2,1)S(1)}, u32[]{:S(2)}, u32[]{:S(2)}) async-start(bf16[16,16,1728]{2,1,0:T(8,128)(2,1)} %bitcast.3), calls=%async_computation | async-start | bytes 1835008 | tf_op jit(solution)/shard_map/all_to_all | solution.py:305
  12.5 49.0 %copy-start.5 = (f32[36,1728]{1,0:T(8,128)S(1)}, f32[36,1728]{1,0:T(8,128)}, u32[]{:S(2)}) copy-start(f32[36,1728]{1,0:T(8,128)} %master_ref.1) | copy-start | bytes 746500
  35.8 17.9 %collective-permute-start.1 = (bf16[256,1536]{1,0:T(8,128)(2,1)S(1)}, bf16[256,1536]{1,0:T(8,128)(2,1)S(1)}, u32[]{:S(2)}, u32[]{:S(2)}) collective-permute-start(bf16[256,1536]{1,0:T(8,128)(2,1)S(1)} %get-tuple-element.28), channel_id=1, source_target_pairs={{0,8},{8,0},{1,9},{9,1},{2,10},{10,2},{3,11},{11,3},{4,12},{12,4},... | collective-permute-start | bytes 2359304 | tf_op jit(solution)/shard_map/ppermute | solution.py:33
  53.7 62.3 %collective-permute-start.2 = (bf16[256,1536]{1,0:T(8,128)(2,1)S(1)}, bf16[256,1536]{1,0:T(8,128)(2,1)S(1)}, u32[]{:S(2)}, u32[]{:S(2)}) collective-permute-start(bf16[256,1536]{1,0:T(8,128)(2,1)S(1)} %collective-permute-done.1.side_ref), channel_id=1, source_target_pairs={{0,16},{16,0},{1,17},{17,1},{2,18},{18,2},{3,19},{19,3},{4,20},{20... | collective-permute-start | bytes 2359304 | tf_op jit(solution)/shard_map/ppermute | solution.py:33
  59.6 56.4 %collective-permute-start = (bf16[256,1408]{1,0:T(8,128)(2,1)S(1)}, bf16[256,1408]{1,0:T(8,128)(2,1)S(1)}, u32[]{:S(2)}, u32[]{:S(2)}) collective-permute-start(bf16[256,1408]{1,0:T(8,128)(2,1)S(1)} %get-tuple-element.27), channel_id=1, source_target_pairs={{0,16},{16,0},{1,17},{17,1},{2,18},{18,2},{3,19},{19,3},{4,20},{20... | collective-permute-start | bytes 2162696 | tf_op jit(solution)/shard_map/ppermute | solution.py:33
  62.4 3.3 %collective-permute-start.3 = (bf16[36,432]{1,0:T(8,128)(2,1)S(1)}, bf16[36,432]{1,0:T(8,128)(2,1)S(1)}, u32[]{:S(2)}, u32[]{:S(2)}) collective-permute-start(bf16[36,432]{1,0:T(8,128)(2,1)S(1)} %get-tuple-element.30), channel_id=1, source_target_pairs={{0,16},{16,0},{1,17},{17,1},{2,18},{18,2},{3,19},{19,3},{4,20},{20... | collective-permute-start | bytes 93320 | tf_op jit(solution)/shard_map/ppermute | solution.py:33
  66.2 17.9 %collective-permute-start.4 = (bf16[72,432]{1,0:T(8,128)(2,1)S(1)}, bf16[72,432]{1,0:T(8,128)(2,1)S(1)}, u32[]{:S(2)}, u32[]{:S(2)}) collective-permute-start(bf16[72,432]{1,0:T(8,128)(2,1)S(1)} %shard_map.106.own_ref), channel_id=1, source_target_pairs={{0,128},{32,160},{64,192},{96,224},{128,0},{160,32},{192,64},{224,... | collective-permute-start | bytes 186632 | tf_op jit(solution)/shard_map/ppermute | solution.py:38
  77.6 6.6 %collective-permute-start.5 = (bf16[72,432]{1,0:T(8,128)(2,1)S(1)}, bf16[72,432]{1,0:T(8,128)(2,1)S(1)}, u32[]{:S(2)}, u32[]{:S(2)}) collective-permute-start(bf16[72,432]{1,0:T(8,128)(2,1)S(1)} %shard_map.106.own_ref), channel_id=1, source_target_pairs={{0,256},{256,0},{1,257},{257,1},{2,258},{258,2},{3,259},{259,3},{4... | collective-permute-start | bytes 186632 | tf_op jit(solution)/shard_map/ppermute | solution.py:33
  81.9 11.7 %collective-permute-start.6 = (bf16[72,432]{1,0:T(8,128)(2,1)S(1)}, bf16[72,432]{1,0:T(8,128)(2,1)S(1)}, u32[]{:S(2)}, u32[]{:S(2)}) collective-permute-start(bf16[72,432]{1,0:T(8,128)(2,1)S(1)} %shard_map.106.own_ref), channel_id=1, source_target_pairs={{0,384},{32,416},{64,448},{96,480},{128,256},{160,288},{192,320},{... | collective-permute-start | bytes 186632 | tf_op jit(solution)/shard_map/ppermute | solution.py:48
  94.2 10.5 %collective-permute-start.8 = (bf16[2,72,432]{2,1,0:T(8,128)(2,1)S(1)}, bf16[2,72,432]{2,1,0:T(8,128)(2,1)S(1)}, u32[]{:S(2)}, u32[]{:S(2)}) collective-permute-start(bf16[2,72,432]{2,1,0:T(8,128)(2,1)S(1)} %get-tuple-element.50), channel_id=1, source_target_pairs={{0,192},{32,224},{64,0},{96,32},{128,64},{160,96},{192,128},{224,1... | collective-permute-start | bytes 373256 | tf_op jit(solution)/shard_map/ppermute | solution.py:38
  98.2 16.1 %collective-permute-start.10 = (bf16[4,72,432]{2,1,0:T(8,128)(2,1)S(1)}, bf16[4,72,432]{2,1,0:T(8,128)(2,1)S(1)}, u32[]{:S(2)}, u32[]{:S(2)}) collective-permute-start(bf16[4,72,432]{2,1,0:T(8,128)(2,1)S(1)} %shard_map.107.near_ref), channel_id=1, source_target_pairs={{0,32},{32,64},{64,96},{96,128},{128,160},{160,192},{192,224},{224... | collective-permute-start | bytes 746504 | tf_op jit(solution)/shard_map/ppermute | solution.py:38
  100.2 14.2 %collective-permute-start.7 = (bf16[4,72,432]{2,1,0:T(8,128)(2,1)S(1)}, bf16[4,72,432]{2,1,0:T(8,128)(2,1)S(1)}, u32[]{:S(2)}, u32[]{:S(2)}) collective-permute-start(bf16[4,72,432]{2,1,0:T(8,128)(2,1)S(1)} %shard_map.107.near_ref), channel_id=1, source_target_pairs={{0,224},{32,0},{64,32},{96,64},{128,96},{160,128},{192,160},{224,1... | collective-permute-start | bytes 746504 | tf_op jit(solution)/shard_map/ppermute | solution.py:38
  104.7 9.6 %collective-permute-start.9 = (bf16[2,72,432]{2,1,0:T(8,128)(2,1)S(1)}, bf16[2,72,432]{2,1,0:T(8,128)(2,1)S(1)}, u32[]{:S(2)}, u32[]{:S(2)}) collective-permute-start(bf16[2,72,432]{2,1,0:T(8,128)(2,1)S(1)} %get-tuple-element.49), channel_id=1, source_target_pairs={{0,64},{32,96},{64,128},{96,160},{128,192},{160,224},{192,0},{224,... | collective-permute-start | bytes 373256 | tf_op jit(solution)/shard_map/ppermute | solution.py:38
  115.0 1.0 copy-start.1
  125.8 1.0 copy-start.8
  126.7 23.9 %collective-permute-start.14 = (bf16[4,72,432]{2,1,0:T(8,128)(2,1)S(1)}, bf16[4,72,432]{2,1,0:T(8,128)(2,1)S(1)}, u32[]{:S(2)}, u32[]{:S(2)}) collective-permute-start(bf16[4,72,432]{2,1,0:T(8,128)(2,1)S(1)} %get-tuple-element.37), channel_id=1, source_target_pairs={{0,32},{32,64},{64,96},{96,128},{128,160},{160,192},{192,224},{224... | collective-permute-start | bytes 746504 | tf_op jit(solution)/shard_map/ppermute | solution.py:38
  128.7 21.9 %collective-permute-start.17 = (bf16[4,72,432]{2,1,0:T(8,128)(2,1)S(1)}, bf16[4,72,432]{2,1,0:T(8,128)(2,1)S(1)}, u32[]{:S(2)}, u32[]{:S(2)}) collective-permute-start(bf16[4,72,432]{2,1,0:T(8,128)(2,1)S(1)} %get-tuple-element.40), channel_id=1, source_target_pairs={{0,224},{32,0},{64,32},{96,64},{128,96},{160,128},{192,160},{224,1... | collective-permute-start | bytes 746504 | tf_op jit(solution)/shard_map/ppermute | solution.py:38
  133.2 10.1 %collective-permute-start.15 = (bf16[2,72,432]{2,1,0:T(8,128)(2,1)S(1)}, bf16[2,72,432]{2,1,0:T(8,128)(2,1)S(1)}, u32[]{:S(2)}, u32[]{:S(2)}) collective-permute-start(bf16[2,72,432]{2,1,0:T(8,128)(2,1)S(1)} %get-tuple-element.38), channel_id=1, source_target_pairs={{0,64},{32,96},{64,128},{96,160},{128,192},{160,224},{192,0},{224,... | collective-permute-start | bytes 373256 | tf_op jit(solution)/shard_map/ppermute | solution.py:38
  136.7 13.9 %collective-permute-start.16 = (bf16[2,72,432]{2,1,0:T(8,128)(2,1)S(1)}, bf16[2,72,432]{2,1,0:T(8,128)(2,1)S(1)}, u32[]{:S(2)}, u32[]{:S(2)}) collective-permute-start(bf16[2,72,432]{2,1,0:T(8,128)(2,1)S(1)} %get-tuple-element.39), channel_id=1, source_target_pairs={{0,192},{32,224},{64,0},{96,32},{128,64},{160,96},{192,128},{224,1... | collective-permute-start | bytes 373256 | tf_op jit(solution)/shard_map/ppermute | solution.py:38
  151.4 23.2 %copy-start.2 = (bf16[16,72,432]{2,1,0:T(8,128)(2,1)S(1)}, bf16[16,72,432]{2,1,0:T(8,128)(2,1)}, u32[]{:S(2)}) copy-start(bf16[16,72,432]{2,1,0:T(8,128)(2,1)} %copy-done.1) | copy-start | bytes 2985988
  151.4 13.9 %collective-permute-start.18 = (bf16[72,432]{1,0:T(8,128)(2,1)S(1)}, bf16[72,432]{1,0:T(8,128)(2,1)S(1)}, u32[]{:S(2)}, u32[]{:S(2)}) collective-permute-start(bf16[72,432]{1,0:T(8,128)(2,1)S(1)} %get-tuple-element.42), channel_id=1, source_target_pairs={{0,128},{32,160},{64,192},{96,224},{128,0},{160,32},{192,64},{224,... | collective-permute-start | bytes 186632 | tf_op jit(solution)/shard_map/ppermute | solution.py:38
  154.4 10.9 %collective-permute-start.19 = (bf16[72,432]{1,0:T(8,128)(2,1)S(1)}, bf16[72,432]{1,0:T(8,128)(2,1)S(1)}, u32[]{:S(2)}, u32[]{:S(2)}) collective-permute-start(bf16[72,432]{1,0:T(8,128)(2,1)S(1)} %get-tuple-element.43), channel_id=1, source_target_pairs={{0,256},{256,0},{1,257},{257,1},{2,258},{258,2},{3,259},{259,3},{4... | collective-permute-start | bytes 186632 | tf_op jit(solution)/shard_map/ppermute | solution.py:33
  156.9 11.4 %collective-permute-start.20 = (bf16[72,432]{1,0:T(8,128)(2,1)S(1)}, bf16[72,432]{1,0:T(8,128)(2,1)S(1)}, u32[]{:S(2)}, u32[]{:S(2)}) collective-permute-start(bf16[72,432]{1,0:T(8,128)(2,1)S(1)} %get-tuple-element.44), channel_id=1, source_target_pairs={{0,384},{32,416},{64,448},{96,480},{128,256},{160,288},{192,320},{... | collective-permute-start | bytes 186632 | tf_op jit(solution)/shard_map/ppermute | solution.py:48
  169.2 46.7 %all-to-all-start.2 = ((bf16[8,72,432]{2,1,0:T(8,128)(2,1)}), bf16[8,72,432]{2,1,0:T(8,128)(2,1)S(1)}, u32[]{:S(2)}, u32[]{:S(2)}) async-start(bf16[8,72,432]{2,1,0:T(8,128)(2,1)} %shard_map.113), calls=%async_computation.2 | async-start | bytes 1179648 | tf_op jit(solution)/shard_map/all_to_all | solution.py:359
  174.6 1.2 copy-start.9
  177.4 12.6 %collective-permute-start.11 = (bf16[256,1152]{1,0:T(8,128)(2,1)S(1)}, bf16[256,1152]{1,0:T(8,128)(2,1)S(1)}, u32[]{:S(2)}, u32[]{:S(2)}) collective-permute-start(bf16[256,1152]{1,0:T(8,128)(2,1)S(1)} %get-tuple-element.33), channel_id=1, source_target_pairs={{0,16},{16,0},{1,17},{17,1},{2,18},{18,2},{3,19},{19,3},{4,20},{20... | collective-permute-start | bytes 1769480 | tf_op jit(solution)/shard_map/ppermute | solution.py:33
  184.5 16.8 %collective-permute-start.12 = (bf16[256,1152]{1,0:T(8,128)(2,1)S(1)}, bf16[256,1152]{1,0:T(8,128)(2,1)S(1)}, u32[]{:S(2)}, u32[]{:S(2)}) collective-permute-start(bf16[256,1152]{1,0:T(8,128)(2,1)S(1)} %get-tuple-element.34), channel_id=1, source_target_pairs={{0,8},{8,0},{1,9},{9,1},{2,10},{10,2},{3,11},{11,3},{4,12},{12,4},... | collective-permute-start | bytes 1769480 | tf_op jit(solution)/shard_map/ppermute | solution.py:33
  187.7 26.4 %collective-permute-start.13 = (bf16[256,1152]{1,0:T(8,128)(2,1)S(1)}, bf16[256,1152]{1,0:T(8,128)(2,1)S(1)}, u32[]{:S(2)}, u32[]{:S(2)}) collective-permute-start(bf16[256,1152]{1,0:T(8,128)(2,1)S(1)} %get-tuple-element.35), channel_id=1, source_target_pairs={{0,24},{8,16},{16,8},{24,0},{1,25},{9,17},{17,9},{25,1},{2,26},{10... | collective-permute-start | bytes 1769480 | tf_op jit(solution)/shard_map/ppermute | solution.py:52
  215.9 22.3 %copy-start.6 = (f32[36,1728]{1,0:T(8,128)S(1)}, f32[36,1728]{1,0:T(8,128)}, u32[]{:S(2)}) copy-start(f32[36,1728]{1,0:T(8,128)} %slow_ref.1) | copy-start | bytes 746500
  215.9 22.3 %copy-start.7 = (f32[36,1728]{1,0:T(8,128)S(1)}, f32[36,1728]{1,0:T(8,128)}, u32[]{:S(2)}) copy-start(f32[36,1728]{1,0:T(8,128)} %fast_ref.1) | copy-start | bytes 746500
  215.9 23.9 %all-to-all-start.1 = ((bf16[16,16,1152]{2,1,0:T(8,128)(2,1)}), bf16[16,16,1152]{2,1,0:T(8,128)(2,1)S(1)}, u32[]{:S(2)}, u32[]{:S(2)}) async-start(bf16[16,16,1152]{2,1,0:T(8,128)(2,1)} %bitcast.11), calls=%async_computation.1 | async-start | bytes 1179648 | tf_op jit(solution)/shard_map/all_to_all | solution.py:382
  225.5 12.6 %collective-permute-start.22 = (f32[36,432]{1,0:T(8,128)S(1)}, f32[36,432]{1,0:T(8,128)S(1)}, u32[]{:S(2)}, u32[]{:S(2)}) collective-permute-start(f32[36,432]{1,0:T(8,128)S(1)} %get-tuple-element.46), channel_id=1, source_target_pairs={{0,16},{16,0},{1,17},{17,1},{2,18},{18,2},{3,19},{19,3},{4,20},{20... | collective-permute-start | bytes 186632 | tf_op jit(solution)/shard_map/ppermute | solution.py:33
  228.0 10.1 %collective-permute-start.23 = (f32[36,432]{1,0:T(8,128)S(1)}, f32[36,432]{1,0:T(8,128)S(1)}, u32[]{:S(2)}, u32[]{:S(2)}) collective-permute-start(f32[36,432]{1,0:T(8,128)S(1)} %get-tuple-element.46), channel_id=1, source_target_pairs={{0,24},{8,16},{16,8},{24,0},{1,25},{9,17},{17,9},{25,1},{2,26},{10... | collective-permute-start | bytes 186632 | tf_op jit(solution)/shard_map/ppermute | solution.py:52
  231.5 6.7 %collective-permute-start.21 = (f32[36,432]{1,0:T(8,128)S(1)}, f32[36,432]{1,0:T(8,128)S(1)}, u32[]{:S(2)}, u32[]{:S(2)}) collective-permute-start(f32[36,432]{1,0:T(8,128)S(1)} %get-tuple-element.45.own_ref), channel_id=1, source_target_pairs={{0,8},{8,0},{1,9},{9,1},{2,10},{10,2},{3,11},{11,3},{4,12},{12,4},... | collective-permute-start | bytes 186632 | tf_op jit(solution)/shard_map/ppermute | solution.py:33

commit v3 on v2

--- a/solution.py
+++ b/solution.py
@@ -16,6 +16,7 @@
 gamma_fast = 6.94
 AXES = ("xh", "z", "c", "xl", "y")
 SEQ = ("xl", "y")
+ROWS = ("xh", "z")
 F32 = jnp.float32
 BF16 = jnp.bfloat16
 MIB = 1024 * 1024
@@ -31,21 +32,6 @@
 
 def swap(value, axis):
     return lax.ppermute(value, axis, [(0, 1), (1, 0)])
-
-
-def shift(value, away):
-    count = lax.axis_size("z")
-    return lax.ppermute(value, "z", [(i, (i + away) % count) for i in range(count)])
-
-
-def half_turn(value):
-    return shift(value, lax.axis_size("z") // 2)
-
-
-def both_turn(value):
-    count = lax.axis_size("z")
-    pairs = [(i, (count - count * (i // count)) + (i % count + count // 2) % count) for i in range(2 * count)]
-    return lax.ppermute(value, ("xh", "z"), pairs)
 
 
 def corner_swap(value):
@@ -153,16 +139,34 @@
     return jnp.concatenate([query_grad * factor, key_grad * factor, value_grad], axis=1)
 
 
-def main_kernel(spot_ref, own_ref, core_ref, side_ref, both_ref, weight_ref, grads_ref, near_ref, up_ref, down_ref, low_ref, high_ref, total_ref):
+def tiles_of(block):
+    rows = [block[8 * i : 8 * i + 8] for i in range(block.shape[0] // 8)]
+    tiles = [row[:, 128 * k : 128 * k + 128] for row in rows for k in range(3)]
+    rest = [row[:, 384:] for row in rows] + [jnp.zeros_like(rows[0][:, 384:])]
+    pad = jnp.zeros((8, 128 - 2 * rest[0].shape[1]), block.dtype)
+    tiles += [jnp.concatenate([rest[i], rest[i + 1], pad], axis=1) for i in range(0, len(rest), 2)]
+    return tiles
+
+
+def block_of(tiles, height):
+    count = height // 8
+    rows = []
+    for i in range(count):
+        last = tiles[3 * count + i // 2][:, 48 * (i % 2) : 48 * (i % 2) + 48]
+        rows.append(jnp.concatenate(tiles[3 * i : 3 * i + 3] + [last], axis=1))
+    return jnp.concatenate(rows, axis=0)
+
+
+def main_kernel(own_ref, core_ref, side_ref, both_ref, weight_ref, grads_ref, packed_ref, total_ref):
     tokens = own_ref.shape[0]
-    model_width = weight_ref.shape[0]
-    quarter = weight_ref.shape[1] // 3
+    model_width, cols = total_ref.shape
+    quarter = cols // 3
     row = lax.broadcasted_iota(jnp.int32, (tokens, tokens), 0)
     col = lax.broadcasted_iota(jnp.int32, (tokens, tokens), 1)
     same = lax.rem(row, 16) == lax.rem(col, 16)
     lane = lax.broadcasted_iota(jnp.int32, (tokens, quarter), 1)
     for index, (ref, skip) in enumerate(((own_ref, 0), (core_ref, 0), (side_ref, 0), (both_ref, 1))):
-        projected = dot(ref[:, :model_width], weight_ref[...], ((1,), (0,)))
+        projected = dot(ref[:, :model_width], weight_ref[:, :cols], ((1,), (0,)))
         projected = projected.astype(BF16).astype(F32)
         cot = ref[:, model_width:].astype(F32)
         out_grad = cot[:, skip * quarter : (skip + 1) * quarter]
@@ -173,20 +177,19 @@
             total_ref[...] = part
         else:
             total_ref[...] += part
-    place = spot_ref[1]
     height = model_width // 16
-    for ahead, targets in enumerate(((near_ref,), (up_ref,), (low_ref, high_ref), (down_ref,))):
-        lowest = lax.rem(place + ahead, 4)
-        for group in range(4):
-            ref = targets[group * len(targets) // 4]
-            first = pl.multiple_of((4 * group + lowest) * height, 8)
-            ref[group % ref.shape[0]] = total_ref[pl.ds(first, height), :].astype(BF16)
+    pieces = packed_ref.shape[0] // 16
+    for owner in range(16):
+        tiles = tiles_of(total_ref[owner * height : (owner + 1) * height, :])
+        each = len(tiles) // pieces
+        for piece in range(pieces):
+            packed_ref[owner * pieces + piece] = jnp.concatenate(tiles[each * piece : each * piece + each], axis=0).astype(BF16)
 
 
 def input_kernel(grads_ref, weight_ref, *refs):
     height = refs[0].shape[0]
     for index, ref in enumerate(refs):
-        part = dot(grads_ref[index * height : (index + 1) * height, :], weight_ref[...], ((1,), (1,)))
+        part = dot(grads_ref[index * height : (index + 1) * height, :], weight_ref[:, : grads_ref.shape[1]], ((1,), (1,)))
         ref[...] = part.astype(BF16)
 
 
@@ -205,68 +208,51 @@
     mine, theirs = mine_ref[...].astype(F32), theirs_ref[...].astype(F32)
     first = spot_ref[0] < 2
     upper, lower = jnp.where(first, mine, theirs), jnp.where(first, theirs, mine)
-    out_ref[...] = jnp.concatenate([upper, lower], axis=0).astype(BF16)
-
-
-def quad_kernel(spot_ref, own_ref, far_ref, across_ref, both_ref, out_ref):
-    place = spot_ref[2]
-    out_ref[place] = own_ref[...]
-    out_ref[place + 1 - 2 * lax.rem(place, 2)] = far_ref[...]
-    out_ref[lax.rem(place + 2, 4)] = across_ref[...]
-    out_ref[3 - place] = both_ref[...]
-
-
-def gather_kernel(spot_ref, near_ref, up_ref, low_ref, high_ref, down_ref, out_ref):
-    place = spot_ref[1]
-    for ahead, sources in enumerate(((near_ref,), (up_ref,), (low_ref, high_ref), (down_ref,))):
-        lowest = lax.rem(place + ahead, 4)
-        for group in range(4):
-            ref = sources[group * len(sources) // 4]
-            out_ref[4 * group + lowest] = ref[group % ref.shape[0]]
-
-
-def reduce_kernel(spot_ref, near_ref, up_ref, low_ref, high_ref, down_ref, own_ref, far_ref, across_ref, both_ref, total_ref):
-    place = spot_ref[2]
-    for group in range(4):
-        far = low_ref if group < 2 else high_ref
-        total = near_ref[group].astype(F32) + up_ref[group].astype(F32)
-        total_ref[group] = total + down_ref[group].astype(F32) + far[group % 2].astype(F32)
-    own_ref[...] = total_ref[place]
-    far_ref[...] = total_ref[place + 1 - 2 * lax.rem(place, 2)].astype(BF16)
-    across_ref[...] = total_ref[lax.rem(place + 2, 4)].astype(BF16)
-    both_ref[...] = total_ref[3 - place].astype(BF16)
-
-
-def copies_kernel(own_ref, far_ref, across_ref, both_ref, out_ref):
-    total = own_ref[...] + far_ref[...].astype(F32) + across_ref[...].astype(F32) + both_ref[...].astype(F32)
-    total = total.astype(BF16)
-    for index in range(out_ref.shape[0]):
-        out_ref[index] = total
-
-
-def rows_kernel(spot_ref, parts_ref, own_ref, other_ref):
+    pair = jnp.concatenate([upper, lower], axis=0)
+    rest = jnp.zeros((pair.shape[0], out_ref.shape[1] - pair.shape[1]), F32)
+    out_ref[...] = jnp.concatenate([pair, rest], axis=1).astype(BF16)
+
+
+def payload_kernel(parts_ref, back_ref, out_ref):
     total = parts_ref[0].astype(F32)
     for index in range(1, parts_ref.shape[0]):
         total = total + parts_ref[index].astype(F32)
-    height = own_ref.shape[0]
+    half = total.shape[0] // 2
+    piece = jnp.concatenate([total[:half], total[half:]], axis=1).astype(BF16)
+    width = back_ref.shape[1]
+    out_ref[:, :width] = back_ref[...]
+    for index in range(out_ref.shape[0] // half):
+        out_ref[index * half : (index + 1) * half, width:] = piece
+
+
+def rows_kernel(spot_ref, pieces_ref, own_ref, other_ref):
+    width = pieces_ref.shape[2] - 256
+    count = pieces_ref.shape[0] // 2
+    height = own_ref.shape[1]
     first = spot_ref[0] < 2
-    upper, lower = total[:height], total[height:]
-    own_ref[...] = jnp.where(first, upper, lower)
-    other_ref[...] = jnp.where(first, lower, upper)
-
-
-def average_kernel(spot_ref, decay_ref, own_ref, side_ref, core_ref, both_ref, slow_ref, fast_ref, slow_out, fast_out):
-    quarter = own_ref.shape[1] // 3
-    spot = spot_ref[0]
-    values = [ref[...] for ref in (own_ref, side_ref, core_ref, both_ref)]
-    picked = [pick(spot, [values[i ^ place] for i in range(4)]) for place in range(4)]
-    columns = [picked[place][:, part * quarter : (part + 1) * quarter] for part in range(3) for place in range(4)]
+    for side in range(2):
+        tiles = []
+        for index in range(count):
+            piece = pieces_ref[side * count + index][:, width:].astype(F32)
+            tiles += [piece[:8, :128], piece[8:, :128], piece[:8, 128:], piece[8:, 128:]]
+        total = block_of(tiles, 2 * height)
+        upper, lower = total[:height], total[height:]
+        own_ref[side] = jnp.where(first, upper, lower)
+        other_ref[side] = jnp.where(first, lower, upper)
+
+
+def average_kernel(spot_ref, decay_ref, own_ref, core_ref, slow_ref, fast_ref, slow_out, fast_out):
+    quarter = own_ref.shape[2] // 3
+    first = spot_ref[0] < 2
+    own, other = [own_ref[0], own_ref[1]], [core_ref[0], core_ref[1]]
+    places = [jnp.where(first, a, b) for a, b in zip(own + other, other + own)]
+    columns = [place[:, part * quarter : (part + 1) * quarter] for part in range(3) for place in places]
     grad = jnp.concatenate(columns, axis=1) / loss_scale
     slow_out[...] = decay_ref[0] * slow_ref[...] + (1.0 - decay_ref[0]) * grad
     fast_out[...] = decay_ref[1] * fast_ref[...] + (1.0 - decay_ref[1]) * grad
 
 
-def call(kernel, outs, *args, flops=0, scratch=(), mib=48, smem=0):
+def call(kernel, outs, *args, flops=0, scratch=(), mib=16, smem=0):
     moved = sum(a.size * a.dtype.itemsize for a in args)
     moved += sum(math.prod(shape) * jnp.dtype(kind).itemsize for shape, kind in outs)
     shapes = [jax.ShapeDtypeStruct(shape, kind) for shape, kind in outs]
@@ -293,32 +279,21 @@
     own_rows, triple = master.shape
     wide = width + inner
     n_seq = lax.axis_size("xl") * lax.axis_size("y")
+    n_rows = lax.axis_size("xh") * lax.axis_size("z")
     n_y = lax.axis_size("y")
     quarter = inner // 4
     cols = 3 * quarter
     pair_rows = 2 * own_rows
     core, side = lax.axis_index("c"), lax.axis_index("xl")
-    across, along = lax.axis_index("xh"), lax.axis_index("z")
-    spots = jnp.stack([2 * core + side, lax.rem(along, 4), 2 * across + along // 4]).astype(jnp.int32)
+    spots = jnp.stack([2 * core + side]).astype(jnp.int32)
 
     packed = call(pack_kernel, [((patches, wide), BF16)], hidden[0, 0], cotangent[0, 0].T)
     tokens = lax.all_to_all(packed.reshape(n_seq, patches // n_seq, wide), SEQ, 0, 0, tiled=True)
     tokens = tokens.reshape(patches, wide)
 
     mine, theirs = call(columns_kernel, [((own_rows, cols), BF16)] * 2, spots, master, smem=1)
-    pair = call(pair_kernel, [((pair_rows, cols), BF16)], spots, mine, swap(theirs, "c"), smem=1)
-    quad = call(
-        quad_kernel,
-        [((4, pair_rows, cols), BF16)],
-        spots, pair, half_turn(pair), swap(pair, "xh"), both_turn(pair),
-        smem=1,
-    )
-    weights = call(
-        gather_kernel,
-        [((16, pair_rows, cols), BF16)],
-        spots, quad, shift(quad, -1), shift(quad[:2], -2), shift(quad[2:], 2), shift(quad, 1),
-        smem=1,
-    ).reshape(width, cols)
+    pair = call(pair_kernel, [((pair_rows, lanes(cols)), BF16)], spots, mine, swap(theirs, "c"), smem=1)
+    weights = lax.all_gather(pair, ROWS, axis=0, tiled=True)
 
     modulation = modulate_table(timesteps, ada_weight)
     narrow, broad = lanes(width + quarter), lanes(width + 2 * quarter)
@@ -330,41 +305,16 @@
     )
     from_side = swap(to_side, "xl")
     from_core = swap(to_core, "c")
+    from_side, from_core = lax.optimization_barrier((from_side, from_core))
     from_both = swap(from_side, "c")
 
-    quads = ((4, pair_rows, cols), BF16)
-    halves = ((2, pair_rows, cols), BF16)
-    grads, near, up, down, low, high = call(
+    pieces = n_rows * n_y
+    grads, packed = call(
         main_kernel,
-        [((4 * patches, cols), BF16), quads, quads, quads, halves, halves],
-        spots, own, from_core, from_side, from_both, weights,
+        [((4 * patches, cols), BF16), ((pieces, 32, 128), BF16)],
+        own, from_core, from_side, from_both, weights,
         flops=4 * 4 * patches * width * cols,
         scratch=[pltpu.VMEM((width, cols), F32)],
-        smem=1,
-    )
-
-    block = (pair_rows, cols)
-    own_part, far, beside, corner = call(
-        reduce_kernel,
-        [(block, F32), (block, BF16), (block, BF16), (block, BF16)],
-        spots, near, shift(up, 1), shift(low, 2), shift(high, -2), shift(down, -1),
-        scratch=[pltpu.VMEM((4,) + block, F32)],
-        smem=1,
-    )
-    copies = call(
-        copies_kernel,
-        [((n_y,) + block, BF16)],
-        own_part, half_turn(far), swap(beside, "xh"), both_turn(corner),
-    )
-    parts = lax.all_to_all(copies, "y", 0, 0, tiled=True)
-    own_grad, other_grad = call(rows_kernel, [((own_rows, cols), F32)] * 2, spots, parts, smem=1)
-    base = 1.0 - 1.0 / step_count[0].astype(F32)
-    decays = jnp.stack([jnp.power(base, gamma_slow + 1.0), jnp.power(base, gamma_fast + 1.0)])
-    ema_slow_next, ema_fast_next = call(
-        average_kernel,
-        [((own_rows, triple), F32)] * 2,
-        spots, decays, own_grad, swap(own_grad, "xl"), swap(other_grad, "c"), corner_swap(other_grad), ema_slow, ema_fast,
-        smem=2,
     )
 
     whole = ((patches, width), BF16)
@@ -379,8 +329,20 @@
         [whole],
         tokens, modulation, mine_in, swap(core_in, "c"), swap(side_in, "xl"), corner_swap(both_in),
     )
-    back = lax.all_to_all(back.reshape(n_seq, patches // n_seq, width), SEQ, 0, 0, tiled=True)
-    return (back.reshape(hidden.shape), ema_slow_next, ema_fast_next)
+
+    parts = lax.all_to_all(packed, ROWS + ("y",), 0, 0, tiled=True)
+    joint = call(payload_kernel, [((patches, width + 256), BF16)], parts, back)
+    joint = lax.all_to_all(joint.reshape(n_seq, patches // n_seq, width + 256), SEQ, 0, 0, tiled=True)
+    own_grad, other_grad = call(rows_kernel, [((2, own_rows, cols), F32)] * 2, spots, joint, smem=1)
+    base = 1.0 - 1.0 / step_count[0].astype(F32)
+    decays = jnp.stack([jnp.power(base, gamma_slow + 1.0), jnp.power(base, gamma_fast + 1.0)])
+    ema_slow_next, ema_fast_next = call(
+        average_kernel,
+        [((own_rows, triple), F32)] * 2,
+        spots, decays, own_grad, swap(other_grad, "c"), ema_slow, ema_fast,
+        smem=2,
+    )
+    return (joint[:, :, :width].reshape(hidden.shape), ema_slow_next, ema_fast_next)
 
 
 def solution(mesh):

time: 243 us -> 224 us (0.922)
  starting transfers between devices: 114 us -> 54.5 us
  blocking collectives: 0 us -> 24.4 us
  between operations: 2.56 us -> 15.7 us
  Pallas kernels: 22.5 us -> 16 us
  local copies, waits for them, and re-layouts: 6.17 us -> 12.6 us
  waiting for transfers between devices: 94.5 us -> 98.9 us
    ppermute x12 -> x0, starting transfers between devices: 52.6 us -> none  [the longest x10 42 us: shift(): lax.ppermute(value, 'z', [(i, (i + away) % count) for i in range(count)])]
    all_gather x0 -> x1, waiting for transfers between devices: none -> 44 us  [on_device(): weights = lax.all_gather(pair, ROWS, axis=0, tiled=True)]
    ppermute x12 -> x0, waiting for transfers between devices: 28.7 us -> none  [the longest x10 16.3 us: shift(): lax.ppermute(value, 'z', [(i, (i + away) % count) for i in range(count)])]
    all_to_all x0 -> x1, blocking collectives: none -> 24.4 us  [on_device(): lax.all_to_all(joint.reshape(n_seq, patches // n_seq, width + 256), SEQ,...]
    pallas_call x13 -> x10, Pallas kernels: 22.5 us -> 16 us  [call(): pl.pallas_call(kernel, out_shape=shapes, in_specs=specs, out_specs=[pl.Bl...]
    unnamed x21 -> x30, local copies, waits for them, and re-layouts: 6.15 us -> 11.8 us
    all_to_all x1, waiting for transfers between devices: 20.4 us -> 14.8 us  [on_device(): lax.all_to_all(packed.reshape(n_seq, patches // n_seq, wide), SEQ, 0, 0,...]
    ppermute x10 -> x7, waiting for transfers between devices: 32.6 us -> 27.4 us  [swap(): return lax.ppermute(value, axis, [(0, 1), (1, 0)])]
  transfers between devices with their start and end apart: 27 -> 11, of which waited for: 13 -> 7; matrix products, arithmetic and copies ran while one was open for 0% -> 1% of each run, Pallas kernels for 3% -> 2%
where the time goes in v3:
time: 224 us; the launch traced here: 223 us
  waiting for transfers between devices  98.9 us (44%)
  starting transfers between devices  54.5 us (24%)
  blocking collectives  24.4 us (11%)
  Pallas kernels  16 us (7%)
  between operations  15.7 us (7%)
  local copies, waits for them, and re-layouts  12.6 us (6%)
    all_gather x1, waiting for transfers between devices, on_device(): weights = lax.all_gather(pair, ROWS, axis=0, tiled=True)  44 us
    ppermute x7, starting transfers between devices, swap(): return lax.ppermute(value, axis, [(0, 1), (1, 0)])  31.5 us
    ppermute x7, waiting for transfers between devices, swap(): return lax.ppermute(value, axis, [(0, 1), (1, 0)])  27.4 us
    all_to_all x1, blocking collectives, on_device(): lax.all_to_all(joint.reshape(n_seq, patches // n_seq, width + 256), SEQ,...  24.4 us
    pallas_call x10, Pallas kernels, call(): pl.pallas_call(kernel, out_shape=shapes, in_specs=specs, out_specs=[pl.Bl...  16 us
    all_to_all x1, waiting for transfers between devices, on_device(): lax.all_to_all(packed.reshape(n_seq, patches // n_seq, wide), SEQ, 0, 0,...  14.8 us
    ppermute x1, waiting for transfers between devices, corner_swap(): return lax.ppermute(value, ('c', 'xl'), [(i, 3 - i) for i in range(4)])  12.6 us
    unnamed x30, local copies, waits for them, and re-layouts  11.8 us
  transfers between devices with their start and end apart: 11, of which 7 were waited for; matrix products, arithmetic and copies ran while one was open for 1% of the time, Pallas kernels for 2%

profile of v3, /device:TPU:1, one launch (start us, length us, event | category | flops | bytes accessed | tf_op | source)
XLA Modules:
  0.0 222.5 jit_solution(7933310021190054725)
XLA Ops:
  7.2 0.0 copy-start
  7.2 0.0 copy-start.2
  7.2 1.1 copy-done.2
  8.3 0.0 copy-start.3
  8.3 1.0 copy-done.3
  9.3 1.1 shard_map.103
  10.3 0.0 copy-start.4
  10.3 8.8 %all-to-all-start = ((bf16[16,16,1728]{2,1,0:T(8,128)(2,1)}), bf16[16,16,1728]{2,1,0:T(8,128)(2,1)S(1)}, u32[]{:S(2)}, u32[]{:S(2)}) async-start(bf16[16,16,1728]{2,1,0:T(8,128)(2,1)} %bitcast.4), calls=%async_computation | async-start | bytes 1835008 | tf_op jit(solution)/shard_map/all_to_all | solution.py:291
  19.1 0.0 all-gather.2.cloned.1.call-start
  19.2 0.0 copy-done.4
  19.2 0.3 shard_map.105
  19.5 3.7 %collective-permute-start.3 = (bf16[36,432]{1,0:T(8,128)(2,1)S(1)}, bf16[36,432]{1,0:T(8,128)(2,1)S(1)}, u32[]{:S(2)}, u32[]{:S(2)}) collective-permute-start(bf16[36,432]{1,0:T(8,128)(2,1)S(1)} %get-tuple-element.26), channel_id=1, source_target_pairs={{0,16},{16,0},{1,17},{17,1},{2,18},{18,2},{3,19},{19,3},{4,20},{20... | collective-permute-start | bytes 93320 | tf_op jit(solution)/shard_map/ppermute | solution.py:34
  23.3 0.8 collective-permute-done.3.theirs_ref
  24.1 0.7 shard_map.106
  24.8 0.0 all-gather.2.cloned.1.call-update
  25.5 0.1 sine_convert_fusion
  25.5 0.0 copy-done
  25.5 0.2 fusion.mod_ref
  25.8 14.8 %all-to-all-done = bf16[16,16,1728]{2,1,0:T(8,128)(2,1)S(1)} async-done(((bf16[16,16,1728]{2,1,0:T(8,128)(2,1)}), bf16[16,16,1728]{2,1,0:T(8,128)(2,1)S(1)}, u32[]{:S(2)}, u32[]{:S(2)}) %all-to-all-start) | async-done | bytes 884768 | tf_op jit(solution)/shard_map/all_to_all | solution.py:291
  40.6 1.3 shard_map.104
  41.9 0.0 copy-start.9
  41.9 0.9 copy-done.9
  42.8 2.0 collective-permute-start
  44.8 6.0 %collective-permute-start.1 = (bf16[256,1408]{1,0:T(8,128)(2,1)S(1)}, bf16[256,1408]{1,0:T(8,128)(2,1)S(1)}, u32[]{:S(2)}, u32[]{:S(2)}) collective-permute-start(bf16[256,1408]{1,0:T(8,128)(2,1)S(1)} %get-tuple-element.22), channel_id=1, source_target_pairs={{0,16},{16,0},{1,17},{17,1},{2,18},{18,2},{3,19},{19,3},{4,20},{20... | collective-permute-start | bytes 2162696 | tf_op jit(solution)/shard_map/ppermute | solution.py:34
  50.8 1.8 collective-permute-done.1.core_ref
  52.6 0.0 copy-start.11
  52.6 0.9 copy-done.11
  53.5 7.3 %collective-permute-done.side_ref = bf16[256,1536]{1,0:T(8,128)(2,1)S(1)} collective-permute-done((bf16[256,1536]{1,0:T(8,128)(2,1)S(1)}, bf16[256,1536]{1,0:T(8,128)(2,1)S(1)}, u32[]{:S(2)}, u32[]{:S(2)}) %collective-permute-start) | collective-permute-done | bytes 786464 | tf_op jit(solution)/shard_map/ppermute | solution.py:34
  60.8 5.7 %collective-permute-start.2 = (bf16[256,1536]{1,0:T(8,128)(2,1)S(1)}, bf16[256,1536]{1,0:T(8,128)(2,1)S(1)}, u32[]{:S(2)}, u32[]{:S(2)}) collective-permute-start(bf16[256,1536]{1,0:T(8,128)(2,1)S(1)} %collective-permute-done.side_ref), channel_id=1, source_target_pairs={{0,16},{16,0},{1,17},{17,1},{2,18},{18,2},{3,19},{19,3},{4,20},{20... | collective-permute-start | bytes 2359304 | tf_op jit(solution)/shard_map/ppermute | solution.py:34
  66.5 44.0 %all-gather.2.cloned.1.call-done.weight_ref = bf16[1152,512]{1,0:T(8,128)(2,1)} async-done(((bf16[72,512]{1,0:T(8,128)(2,1)}), bf16[1152,512]{1,0:T(8,128)(2,1)}) %all-gather.2.cloned.1.call-update) | async-done | bytes 1179664 | tf_op jit(solution)/shard_map/all_gather | solution.py:296
  110.5 0.0 collective-permute-done.2.both_ref
  110.5 0.0 copy-start.7
  110.5 1.3 copy-done.7
  111.8 1.1 copy-done.10
  112.9 0.0 copy-start.12
  112.9 1.1 copy-done.12
  114.0 8.3 %shard_map.107 = (bf16[1024,432]{1,0:T(8,128)(2,1)S(1)}, bf16[128,32,128]{2,1,0:T(8,128)(2,1)S(1)}) custom-call(bf16[256,1408]{1,0:T(8,128)(2,1)S(1)} %copy-done.10, bf16[256,1408]{1,0:T(8,128)(2,1)S(1)} %copy-done.12, bf16[256,1536]{1,0:T(8,128)(2,1)S(1)} %collective-permute-done.side_ref, bf16[256,1536]{1,0:T(8,128)(2,1)S(1)} %collective-permute-done.2.both_ref, ...), custom_call_target="tpu_custom_call" | custom-call | flops 2038431744 | bytes 6127616 | tf_op jit(solution)/shard_map/pallas_call | solution.py:260
  122.4 0.0 copy-start.1
  122.4 1.0 copy-done.1
  123.3 0.0 copy-start.13
  123.3 1.0 copy-done.13
  124.3 11.7 %all-to-all-start.1 = ((bf16[128,32,128]{2,1,0:T(8,128)(2,1)}), bf16[128,32,128]{2,1,0:T(8,128)(2,1)S(1)}, u32[]{:S(2)}, u32[]{:S(2)}) async-start(bf16[128,32,128]{2,1,0:T(8,128)(2,1)} %copy-done.1), calls=%async_computation.1 | async-start | bytes 2097152 | tf_op jit(solution)/shard_map/all_to_all | solution.py:333
  136.1 0.0 copy-start.8
  136.1 1.3 copy-done.8
  137.3 1.2 copy-done.14
  138.6 1.6 shard_map.108
  140.1 6.3 %collective-permute-start.4 = (bf16[256,1152]{1,0:T(8,128)(2,1)S(1)}, bf16[256,1152]{1,0:T(8,128)(2,1)S(1)}, u32[]{:S(2)}, u32[]{:S(2)}) collective-permute-start(bf16[256,1152]{1,0:T(8,128)(2,1)S(1)} %get-tuple-element.30), channel_id=1, source_target_pairs={{0,16},{16,0},{1,17},{17,1},{2,18},{18,2},{3,19},{19,3},{4,20},{20... | collective-permute-start | bytes 1769480 | tf_op jit(solution)/shard_map/ppermute | solution.py:34
  146.4 3.1 %collective-permute-start.5 = (bf16[256,1152]{1,0:T(8,128)(2,1)S(1)}, bf16[256,1152]{1,0:T(8,128)(2,1)S(1)}, u32[]{:S(2)}, u32[]{:S(2)}) collective-permute-start(bf16[256,1152]{1,0:T(8,128)(2,1)S(1)} %get-tuple-element.31), channel_id=1, source_target_pairs={{0,8},{8,0},{1,9},{9,1},{2,10},{10,2},{3,11},{11,3},{4,12},{12,4},... | collective-permute-start | bytes 1769480 | tf_op jit(solution)/shard_map/ppermute | solution.py:34
  149.5 2.4 %collective-permute-start.6 = (bf16[256,1152]{1,0:T(8,128)(2,1)S(1)}, bf16[256,1152]{1,0:T(8,128)(2,1)S(1)}, u32[]{:S(2)}, u32[]{:S(2)}) collective-permute-start(bf16[256,1152]{1,0:T(8,128)(2,1)S(1)} %get-tuple-element.32), channel_id=1, source_target_pairs={{0,24},{8,16},{16,8},{24,0},{1,25},{9,17},{17,9},{25,1},{2,26},{10... | collective-permute-start | bytes 1769480 | tf_op jit(solution)/shard_map/ppermute | solution.py:38
  151.9 0.0 collective-permute-done.4.refs_1_
  151.9 17.5 %collective-permute-done.5.refs_2_ = bf16[256,1152]{1,0:T(8,128)(2,1)S(1)} collective-permute-done((bf16[256,1152]{1,0:T(8,128)(2,1)S(1)}, bf16[256,1152]{1,0:T(8,128)(2,1)S(1)}, u32[]{:S(2)}, u32[]{:S(2)}) %collective-permute-start.5) | collective-permute-done | bytes 589856 | tf_op jit(solution)/shard_map/ppermute | solution.py:34
  169.4 12.6 %collective-permute-done.6.refs_3_ = bf16[256,1152]{1,0:T(8,128)(2,1)S(1)} collective-permute-done((bf16[256,1152]{1,0:T(8,128)(2,1)S(1)}, bf16[256,1152]{1,0:T(8,128)(2,1)S(1)}, u32[]{:S(2)}, u32[]{:S(2)}) %collective-permute-start.6) | collective-permute-done | bytes 589856 | tf_op jit(solution)/shard_map/ppermute | solution.py:38
  182.0 1.0 shard_map.109.back_ref
  183.0 0.0 all-to-all-done.1.parts_ref
  183.0 0.2 shard_map.110
  183.3 24.4 %all_to_all.15.pieces_ref = bf16[16,16,1408]{2,1,0:T(8,128)(2,1)S(1)} all-to-all(bf16[16,16,1408]{2,1,0:T(8,128)(2,1)S(1)} %bitcast.16), channel_id=1, replica_groups=mesh['xh'=2,'z'=8,'c'=2,'xl'=2,'y'=8] {'xl','y'}, dimensions={0} | all-to-all | bytes 1441792 | tf_op jit(solution)/shard_map/all_to_all | solution.py:335
  207.7 0.1 shard_map.111
  207.8 4.7 %collective-permute-start.7 = (f32[2,36,432]{2,1,0:T(8,128)S(1)}, f32[2,36,432]{2,1,0:T(8,128)S(1)}, u32[]{:S(2)}, u32[]{:S(2)}) collective-permute-start(f32[2,36,432]{2,1,0:T(8,128)S(1)} %get-tuple-element.34), channel_id=1, source_target_pairs={{0,16},{16,0},{1,17},{17,1},{2,18},{18,2},{3,19},{19,3},{4,20},{20... | collective-permute-start | bytes 373256 | tf_op jit(solution)/shard_map/ppermute | solution.py:34
  213.2 0.1 pad_maximum_fusion.decay_ref
  213.3 0.9 slice.4
  214.2 0.0 collective-permute-done.7.core_ref
  214.2 0.0 copy-done.5
  214.2 0.0 copy-done.6
  214.2 1.5 shard_map.112
  (4 shorter events, 0.0 us)
Async XLA Ops:
  7.2 18.4 %copy-start = (bf16[128,2304]{1,0:T(8,128)(2,1)S(1)}, bf16[128,2304]{1,0:T(8,128)(2,1)}, u32[]{:S(2)}) copy-start(bf16[128,2304]{1,0:T(8,128)(2,1)} %param.10) | copy-start | bytes 1769476
  7.2 1.1 copy-start.2
  8.3 1.0 copy-start.3
  10.3 8.9 %copy-start.4 = (f32[36,1728]{1,0:T(8,128)S(1)}, f32[36,1728]{1,0:T(8,128)}, u32[]{:S(2)}) copy-start(f32[36,1728]{1,0:T(8,128)} %master_ref.1) | copy-start | bytes 746500
  10.3 30.3 %all-to-all-start = ((bf16[16,16,1728]{2,1,0:T(8,128)(2,1)}), bf16[16,16,1728]{2,1,0:T(8,128)(2,1)S(1)}, u32[]{:S(2)}, u32[]{:S(2)}) async-start(bf16[16,16,1728]{2,1,0:T(8,128)(2,1)} %bitcast.4), calls=%async_computation | async-start | bytes 1835008 | tf_op jit(solution)/shard_map/all_to_all | solution.py:291
  19.1 91.4 %all-gather.2.cloned.1.call-start = ((), (), s32[]{:S(2)}) async-start(), calls=%async_computation.3 | async-start | bytes 1253376 | tf_op jit(solution)/shard_map/all_gather | solution.py:296
  19.5 4.6 %collective-permute-start.3 = (bf16[36,432]{1,0:T(8,128)(2,1)S(1)}, bf16[36,432]{1,0:T(8,128)(2,1)S(1)}, u32[]{:S(2)}, u32[]{:S(2)}) collective-permute-start(bf16[36,432]{1,0:T(8,128)(2,1)S(1)} %get-tuple-element.26), channel_id=1, source_target_pairs={{0,16},{16,0},{1,17},{17,1},{2,18},{18,2},{3,19},{19,3},{4,20},{20... | collective-permute-start | bytes 93320 | tf_op jit(solution)/shard_map/ppermute | solution.py:34
  41.9 0.9 copy-start.9
  42.8 18.0 %collective-permute-start = (bf16[256,1536]{1,0:T(8,128)(2,1)S(1)}, bf16[256,1536]{1,0:T(8,128)(2,1)S(1)}, u32[]{:S(2)}, u32[]{:S(2)}) collective-permute-start(bf16[256,1536]{1,0:T(8,128)(2,1)S(1)} %get-tuple-element.21), channel_id=1, source_target_pairs={{0,8},{8,0},{1,9},{9,1},{2,10},{10,2},{3,11},{11,3},{4,12},{12,4},... | collective-permute-start | bytes 2359304 | tf_op jit(solution)/shard_map/ppermute | solution.py:34
  44.8 7.8 %collective-permute-start.1 = (bf16[256,1408]{1,0:T(8,128)(2,1)S(1)}, bf16[256,1408]{1,0:T(8,128)(2,1)S(1)}, u32[]{:S(2)}, u32[]{:S(2)}) collective-permute-start(bf16[256,1408]{1,0:T(8,128)(2,1)S(1)} %get-tuple-element.22), channel_id=1, source_target_pairs={{0,16},{16,0},{1,17},{17,1},{2,18},{18,2},{3,19},{19,3},{4,20},{20... | collective-permute-start | bytes 2162696 | tf_op jit(solution)/shard_map/ppermute | solution.py:34
  52.6 0.9 copy-start.11
  60.8 49.8 %collective-permute-start.2 = (bf16[256,1536]{1,0:T(8,128)(2,1)S(1)}, bf16[256,1536]{1,0:T(8,128)(2,1)S(1)}, u32[]{:S(2)}, u32[]{:S(2)}) collective-permute-start(bf16[256,1536]{1,0:T(8,128)(2,1)S(1)} %collective-permute-done.side_ref), channel_id=1, source_target_pairs={{0,16},{16,0},{1,17},{17,1},{2,18},{18,2},{3,19},{19,3},{4,20},{20... | collective-permute-start | bytes 2359304 | tf_op jit(solution)/shard_map/ppermute | solution.py:34
  110.5 1.3 copy-start.7
  111.8 1.1 copy-start.10
  112.9 1.1 copy-start.12
  122.4 1.0 copy-start.1
  123.3 1.0 copy-start.13
  124.3 58.7 %all-to-all-start.1 = ((bf16[128,32,128]{2,1,0:T(8,128)(2,1)}), bf16[128,32,128]{2,1,0:T(8,128)(2,1)S(1)}, u32[]{:S(2)}, u32[]{:S(2)}) async-start(bf16[128,32,128]{2,1,0:T(8,128)(2,1)} %copy-done.1), calls=%async_computation.1 | async-start | bytes 2097152 | tf_op jit(solution)/shard_map/all_to_all | solution.py:333
  136.1 1.3 copy-start.8
  137.3 1.2 copy-start.14
  140.1 11.7 %collective-permute-start.4 = (bf16[256,1152]{1,0:T(8,128)(2,1)S(1)}, bf16[256,1152]{1,0:T(8,128)(2,1)S(1)}, u32[]{:S(2)}, u32[]{:S(2)}) collective-permute-start(bf16[256,1152]{1,0:T(8,128)(2,1)S(1)} %get-tuple-element.30), channel_id=1, source_target_pairs={{0,16},{16,0},{1,17},{17,1},{2,18},{18,2},{3,19},{19,3},{4,20},{20... | collective-permute-start | bytes 1769480 | tf_op jit(solution)/shard_map/ppermute | solution.py:34
  146.4 23.0 %collective-permute-start.5 = (bf16[256,1152]{1,0:T(8,128)(2,1)S(1)}, bf16[256,1152]{1,0:T(8,128)(2,1)S(1)}, u32[]{:S(2)}, u32[]{:S(2)}) collective-permute-start(bf16[256,1152]{1,0:T(8,128)(2,1)S(1)} %get-tuple-element.31), channel_id=1, source_target_pairs={{0,8},{8,0},{1,9},{9,1},{2,10},{10,2},{3,11},{11,3},{4,12},{12,4},... | collective-permute-start | bytes 1769480 | tf_op jit(solution)/shard_map/ppermute | solution.py:34
  149.5 32.5 %collective-permute-start.6 = (bf16[256,1152]{1,0:T(8,128)(2,1)S(1)}, bf16[256,1152]{1,0:T(8,128)(2,1)S(1)}, u32[]{:S(2)}, u32[]{:S(2)}) collective-permute-start(bf16[256,1152]{1,0:T(8,128)(2,1)S(1)} %get-tuple-element.32), channel_id=1, source_target_pairs={{0,24},{8,16},{16,8},{24,0},{1,25},{9,17},{17,9},{25,1},{2,26},{10... | collective-permute-start | bytes 1769480 | tf_op jit(solution)/shard_map/ppermute | solution.py:38
  207.7 6.5 %copy-start.5 = (f32[36,1728]{1,0:T(8,128)S(1)}, f32[36,1728]{1,0:T(8,128)}, u32[]{:S(2)}) copy-start(f32[36,1728]{1,0:T(8,128)} %slow_ref.1) | copy-start | bytes 746500
  207.7 6.5 %copy-start.6 = (f32[36,1728]{1,0:T(8,128)S(1)}, f32[36,1728]{1,0:T(8,128)}, u32[]{:S(2)}) copy-start(f32[36,1728]{1,0:T(8,128)} %fast_ref.1) | copy-start | bytes 746500
  207.8 6.4 %collective-permute-start.7 = (f32[2,36,432]{2,1,0:T(8,128)S(1)}, f32[2,36,432]{2,1,0:T(8,128)S(1)}, u32[]{:S(2)}, u32[]{:S(2)}) collective-permute-start(f32[2,36,432]{2,1,0:T(8,128)S(1)} %get-tuple-element.34), channel_id=1, source_target_pairs={{0,16},{16,0},{1,17},{17,1},{2,18},{18,2},{3,19},{19,3},{4,20},{20... | collective-permute-start | bytes 373256 | tf_op jit(solution)/shard_map/ppermute | solution.py:34
Sparse Core Ops, SparseCore 0:
  24.9 85.5 all-gather.1

commit v4 on v3

--- a/solution.py
+++ b/solution.py
@@ -34,8 +34,19 @@
     return lax.ppermute(value, axis, [(0, 1), (1, 0)])
 
 
-def corner_swap(value):
-    return lax.ppermute(value, ("c", "xl"), [(i, 3 - i) for i in range(4)])
+def shift(value, away):
+    count = lax.axis_size("z")
+    return lax.ppermute(value, "z", [(i, (i + away) % count) for i in range(count)])
+
+
+def half_turn(value):
+    return shift(value, lax.axis_size("z") // 2)
+
+
+def both_turn(value):
+    count = lax.axis_size("z")
+    pairs = [(i, (count - count * (i // count)) + (i % count + count // 2) % count) for i in range(2 * count)]
+    return lax.ppermute(value, ("xh", "z"), pairs)
 
 
 def modulate_table(timesteps, ada_weight):
@@ -67,7 +78,7 @@
     return out
 
 
-def norm_kernel(spot_ref, packed_ref, mod_ref, own_ref, core_ref, side_ref):
+def norm_kernel(spot_ref, packed_ref, mod_ref, own_ref, core_ref, side_ref, held_ref, sem):
     width = mod_ref.shape[1] // 2
     quarter = (packed_ref.shape[1] - width) // 4
     centered, _ = stats(packed_ref[:, :width].astype(F32))
@@ -76,12 +87,15 @@
     pieces = [cot[:, i * quarter : (i + 1) * quarter] for i in range(4)]
     spot = spot_ref[0]
     own, side, core, both = (pick(spot, [pieces[i ^ flip] for i in range(4)]) for flip in range(4))
-    own_ref[:, :width] = normed
-    own_ref[:, width : width + quarter] = own.astype(BF16)
+    held_ref[:, :width] = normed
+    held_ref[:, width : width + quarter] = own.astype(BF16)
+    copy = pltpu.make_async_copy(held_ref, own_ref, sem)
+    copy.start()
     core_ref[:, :width] = normed
     core_ref[:, width : width + quarter] = core.astype(BF16)
     side_ref[:, :width] = normed
     side_ref[:, width : width + 2 * quarter] = jnp.concatenate([side, both], axis=1).astype(BF16)
+    copy.wait()
 
 
 def norm_back_kernel(packed_ref, mod_ref, *refs):
@@ -157,26 +171,46 @@
     return jnp.concatenate(rows, axis=0)
 
 
-def main_kernel(own_ref, core_ref, side_ref, both_ref, weight_ref, grads_ref, packed_ref, total_ref):
+def main_kernel(
+    weight_hbm, own_hbm, core_hbm, side_hbm, both_hbm, packed_hbm, near_hbm, far_hbm,
+    weight_ref, own_ref, core_ref, side_ref, both_ref, packed_ref, parts_ref, total_ref, in_sems, out_sems,
+):
     tokens = own_ref.shape[0]
     model_width, cols = total_ref.shape
     quarter = cols // 3
+    pairs = (
+        (weight_hbm, weight_ref), (own_hbm, own_ref), (core_hbm, core_ref), (side_hbm, side_ref), (both_hbm, both_ref),
+    )
+    loads = [pltpu.make_async_copy(source, target, in_sems.at[i]) for i, (source, target) in enumerate(pairs)]
+    for load in loads:
+        load.start()
     row = lax.broadcasted_iota(jnp.int32, (tokens, tokens), 0)
     col = lax.broadcasted_iota(jnp.int32, (tokens, tokens), 1)
     same = lax.rem(row, 16) == lax.rem(col, 16)
     lane = lax.broadcasted_iota(jnp.int32, (tokens, quarter), 1)
-    for index, (ref, skip) in enumerate(((own_ref, 0), (core_ref, 0), (side_ref, 0), (both_ref, 1))):
-        projected = dot(ref[:, :model_width], weight_ref[:, :cols], ((1,), (0,)))
+    stores = []
+    loads[0].wait()
+    places = ((near_hbm, 0, 0), (far_hbm, 0, 0), (near_hbm, 1, 0), (far_hbm, 1, 1))
+    for index, (target, place, skip) in enumerate(places):
+        ref = pairs[index + 1][1]
+        loads[index + 1].wait()
+        projected = dot(ref[:, :model_width], weight_ref[...], ((1,), (0,)))
         projected = projected.astype(BF16).astype(F32)
         cot = ref[:, model_width:].astype(F32)
         out_grad = cot[:, skip * quarter : (skip + 1) * quarter]
         grads = attend_block(projected, out_grad, same, lane).astype(BF16)
-        grads_ref[index * tokens : (index + 1) * tokens, :] = grads
         part = dot(ref[:, :model_width], grads, ((0,), (0,)))
         if index == 0:
             total_ref[...] = part
         else:
             total_ref[...] += part
+        parts_ref[index] = dot(grads, weight_ref[...], ((1,), (1,))).astype(BF16)
+        stores.append(
+            pltpu.make_async_copy(
+                parts_ref.at[index], target.at[pl.ds(place * tokens, tokens)], out_sems.at[index]
+            )
+        )
+        stores[-1].start()
     height = model_width // 16
     pieces = packed_ref.shape[0] // 16
     for owner in range(16):
@@ -184,13 +218,18 @@
         each = len(tiles) // pieces
         for piece in range(pieces):
             packed_ref[owner * pieces + piece] = jnp.concatenate(tiles[each * piece : each * piece + each], axis=0).astype(BF16)
-
-
-def input_kernel(grads_ref, weight_ref, *refs):
-    height = refs[0].shape[0]
-    for index, ref in enumerate(refs):
-        part = dot(grads_ref[index * height : (index + 1) * height, :], weight_ref[:, : grads_ref.shape[1]], ((1,), (1,)))
-        ref[...] = part.astype(BF16)
+        if owner % 4 == 3:
+            part = pl.ds((owner - 3) * pieces, 4 * pieces)
+            stores.append(pltpu.make_async_copy(packed_ref.at[part], packed_hbm.at[part], out_sems.at[4 + owner // 4]))
+            stores[-1].start()
+    for store in stores:
+        store.wait()
+
+
+def add_kernel(near_ref, got_ref, own_ref, side_ref):
+    half = own_ref.shape[0]
+    side_ref[...] = (near_ref[half:].astype(F32) + got_ref[half:].astype(F32)).astype(BF16)
+    own_ref[...] = (near_ref[:half].astype(F32) + got_ref[:half].astype(F32)).astype(BF16)
 
 
 def columns_kernel(spot_ref, master_ref, mine_ref, theirs_ref):
@@ -208,9 +247,24 @@
     mine, theirs = mine_ref[...].astype(F32), theirs_ref[...].astype(F32)
     first = spot_ref[0] < 2
     upper, lower = jnp.where(first, mine, theirs), jnp.where(first, theirs, mine)
-    pair = jnp.concatenate([upper, lower], axis=0)
-    rest = jnp.zeros((pair.shape[0], out_ref.shape[1] - pair.shape[1]), F32)
-    out_ref[...] = jnp.concatenate([pair, rest], axis=1).astype(BF16)
+    out_ref[...] = jnp.concatenate([upper, lower], axis=0).astype(BF16)
+
+
+def quad_kernel(spot_ref, own_ref, far_ref, across_ref, both_ref, out_ref):
+    place = spot_ref[2]
+    out_ref[place] = own_ref[...]
+    out_ref[place + 1 - 2 * lax.rem(place, 2)] = far_ref[...]
+    out_ref[lax.rem(place + 2, 4)] = across_ref[...]
+    out_ref[3 - place] = both_ref[...]
+
+
+def gather_kernel(spot_ref, near_ref, up_ref, low_ref, high_ref, down_ref, out_ref):
+    place = spot_ref[1]
+    for ahead, sources in enumerate(((near_ref,), (up_ref,), (low_ref, high_ref), (down_ref,))):
+        lowest = lax.rem(place + ahead, 4)
+        for group in range(4):
+            ref = sources[group * len(sources) // 4]
+            out_ref[4 * group + lowest] = ref[group % ref.shape[0]]
 
 
 def payload_kernel(parts_ref, back_ref, out_ref):
@@ -252,16 +306,17 @@
     fast_out[...] = decay_ref[1] * fast_ref[...] + (1.0 - decay_ref[1]) * grad
 
 
-def call(kernel, outs, *args, flops=0, scratch=(), mib=16, smem=0):
+def call(kernel, outs, *args, flops=0, scratch=(), mib=16, smem=0, hbm_in=False, hbm_out=()):
     moved = sum(a.size * a.dtype.itemsize for a in args)
     moved += sum(math.prod(shape) * jnp.dtype(kind).itemsize for shape, kind in outs)
     shapes = [jax.ShapeDtypeStruct(shape, kind) for shape, kind in outs]
-    specs = [pl.BlockSpec(memory_space=pltpu.SMEM if i < smem else pltpu.VMEM) for i in range(len(args))]
+    body = pltpu.HBM if hbm_in else pltpu.VMEM
+    specs = [pl.BlockSpec(memory_space=pltpu.SMEM if i < smem else body) for i in range(len(args))]
     got = pl.pallas_call(
         kernel,
         out_shape=shapes,
         in_specs=specs,
-        out_specs=[pl.BlockSpec(memory_space=pltpu.VMEM)] * len(shapes),
+        out_specs=[pl.BlockSpec(memory_space=pltpu.HBM if i in hbm_out else pltpu.VMEM) for i in range(len(shapes))],
         scratch_shapes=list(scratch),
         compiler_params=params(mib),
         cost_estimate=cost(flops, moved),
@@ -285,15 +340,22 @@
     cols = 3 * quarter
     pair_rows = 2 * own_rows
     core, side = lax.axis_index("c"), lax.axis_index("xl")
-    spots = jnp.stack([2 * core + side]).astype(jnp.int32)
+    across, along = lax.axis_index("xh"), lax.axis_index("z")
+    spots = jnp.stack([2 * core + side, lax.rem(along, 4), 2 * across + along // 4]).astype(jnp.int32)
 
     packed = call(pack_kernel, [((patches, wide), BF16)], hidden[0, 0], cotangent[0, 0].T)
     tokens = lax.all_to_all(packed.reshape(n_seq, patches // n_seq, wide), SEQ, 0, 0, tiled=True)
     tokens = tokens.reshape(patches, wide)
 
     mine, theirs = call(columns_kernel, [((own_rows, cols), BF16)] * 2, spots, master, smem=1)
-    pair = call(pair_kernel, [((pair_rows, lanes(cols)), BF16)], spots, mine, swap(theirs, "c"), smem=1)
-    weights = lax.all_gather(pair, ROWS, axis=0, tiled=True)
+    pair = call(pair_kernel, [((pair_rows, cols), BF16)], spots, mine, swap(theirs, "c"), smem=1)
+    quad = call(
+        quad_kernel,
+        [((4, pair_rows, cols), BF16)],
+        spots, pair, half_turn(pair), swap(pair, "xh"), both_turn(pair),
+        smem=1,
+    )
+    quad, tokens = lax.optimization_barrier((quad, tokens))
 
     modulation = modulate_table(timesteps, ada_weight)
     narrow, broad = lanes(width + quarter), lanes(width + 2 * quarter)
@@ -301,34 +363,44 @@
         norm_kernel,
         [((patches, narrow), BF16), ((patches, narrow), BF16), ((patches, broad), BF16)],
         spots, tokens, modulation,
+        scratch=[pltpu.VMEM((patches, narrow), BF16), pltpu.SemaphoreType.DMA(())],
         smem=1,
+        hbm_out=(0,),
     )
     from_side = swap(to_side, "xl")
     from_core = swap(to_core, "c")
-    from_side, from_core = lax.optimization_barrier((from_side, from_core))
+    up, low, high, down = shift(quad, -1), shift(quad[:2], -2), shift(quad[2:], 2), shift(quad, 1)
+    from_side, from_core, up, low, high, down = lax.optimization_barrier((from_side, from_core, up, low, high, down))
     from_both = swap(from_side, "c")
+    weights = call(
+        gather_kernel, [((16, pair_rows, cols), BF16)], spots, quad, up, low, high, down, smem=1
+    ).reshape(width, cols)
 
     pieces = n_rows * n_y
-    grads, packed = call(
+    packed, near, far = call(
         main_kernel,
-        [((4 * patches, cols), BF16), ((pieces, 32, 128), BF16)],
-        own, from_core, from_side, from_both, weights,
-        flops=4 * 4 * patches * width * cols,
-        scratch=[pltpu.VMEM((width, cols), F32)],
-    )
-
-    whole = ((patches, width), BF16)
-    mine_in, core_in, side_in, both_in = call(
-        input_kernel,
-        [whole] * 4,
-        grads, weights,
-        flops=8 * patches * width * cols,
-    )
-    back = call(
-        norm_back_kernel,
-        [whole],
-        tokens, modulation, mine_in, swap(core_in, "c"), swap(side_in, "xl"), corner_swap(both_in),
-    )
+        [((pieces, 32, 128), BF16), ((2 * patches, width), BF16), ((2 * patches, width), BF16)],
+        weights, own, from_core, from_side, from_both,
+        flops=6 * 4 * patches * width * cols,
+        scratch=[
+            pltpu.VMEM((width, cols), BF16),
+            pltpu.VMEM((patches, narrow), BF16),
+            pltpu.VMEM((patches, narrow), BF16),
+            pltpu.VMEM((patches, broad), BF16),
+            pltpu.VMEM((patches, broad), BF16),
+            pltpu.VMEM((pieces, 32, 128), BF16),
+            pltpu.VMEM((4, patches, width), BF16),
+            pltpu.VMEM((width, cols), F32),
+            pltpu.SemaphoreType.DMA((5,)),
+            pltpu.SemaphoreType.DMA((8,)),
+        ],
+        mib=58,
+        hbm_in=True,
+        hbm_out=(0, 1, 2),
+    )
+
+    part, give = call(add_kernel, [((patches, width), BF16)] * 2, near, swap(far, "c"))
+    back = call(norm_back_kernel, [((patches, width), BF16)], tokens, modulation, part, swap(give, "xl"))
 
     parts = lax.all_to_all(packed, ROWS + ("y",), 0, 0, tiled=True)
     joint = call(payload_kernel, [((patches, width + 256), BF16)], parts, back)

time: 224 us -> 177 us (0.79)
  waiting for transfers between devices: 98.9 us -> 44.2 us
  starting transfers between devices: 54.5 us -> 76 us
  between operations: 15.7 us -> 2.41 us
  Pallas kernels: 16 us -> 21.8 us
  local copies, waits for them, and re-layouts: 12.6 us -> 7.05 us
    all_gather x1 -> x0, waiting for transfers between devices: 44 us -> none  [on_device(): weights = lax.all_gather(pair, ROWS, axis=0, tiled=True)]
    ppermute x1 -> x6, starting transfers between devices: 2.39 us -> 22 us  [the longest x5 19.8 us: shift(): lax.ppermute(value, 'z', [(i, (i + away) % count) for i in range(count)])]
    all_to_all x1, waiting for transfers between devices: 14.8 us -> 0.01 us  [on_device(): lax.all_to_all(packed.reshape(n_seq, patches // n_seq, wide), SEQ, 0, 0,...]
    ppermute x1 -> x6, waiting for transfers between devices: 12.6 us -> 18.8 us  [the longest x5 10.2 us: shift(): lax.ppermute(value, 'z', [(i, (i + away) % count) for i in range(count)])]
    pallas_call x10 -> x12, Pallas kernels: 16 us -> 21.8 us  [call(): pl.pallas_call(kernel, out_shape=shapes, in_specs=specs, out_specs=[pl.Bl...]
    unnamed x30 -> x24, local copies, waits for them, and re-layouts: 11.8 us -> 6.17 us
    all_to_all x1, starting transfers between devices: 11.7 us -> 15.6 us  [on_device(): parts = lax.all_to_all(packed, ROWS + ('y',), 0, 0, tiled=True)]
    ppermute x7 -> x8, waiting for transfers between devices: 27.4 us -> 25.4 us  [swap(): return lax.ppermute(value, axis, [(0, 1), (1, 0)])]
  transfers between devices with their start and end apart: 11 -> 16, of which waited for: 7 -> 8; matrix products, arithmetic and copies ran while one was open for 1% -> 1% of each run, Pallas kernels for 2% -> 2%
where the time goes in v4:
time: 177 us; the launch traced here: 176 us
  starting transfers between devices  76 us (43%)
  waiting for transfers between devices  44.2 us (25%)
  blocking collectives  24.5 us (14%)
  Pallas kernels  21.8 us (12%)
  local copies, waits for them, and re-layouts  7.05 us (4%)
  between operations  2.41 us (1%)
    ppermute x8, starting transfers between devices, swap(): return lax.ppermute(value, axis, [(0, 1), (1, 0)])  29.5 us
    ppermute x8, waiting for transfers between devices, swap(): return lax.ppermute(value, axis, [(0, 1), (1, 0)])  25.4 us
    all_to_all x1, blocking collectives, on_device(): lax.all_to_all(joint.reshape(n_seq, patches // n_seq, width + 256), SEQ,...  24.5 us
    pallas_call x12, Pallas kernels, call(): pl.pallas_call(kernel, out_shape=shapes, in_specs=specs, out_specs=[pl.Bl...  21.8 us
    ppermute x5, starting transfers between devices, shift(): lax.ppermute(value, 'z', [(i, (i + away) % count) for i in range(count)])  19.8 us
    all_to_all x1, starting transfers between devices, on_device(): parts = lax.all_to_all(packed, ROWS + ('y',), 0, 0, tiled=True)  15.6 us
    ppermute x5, waiting for transfers between devices, shift(): lax.ppermute(value, 'z', [(i, (i + away) % count) for i in range(count)])  10.2 us
    all_to_all x1, starting transfers between devices, on_device(): lax.all_to_all(packed.reshape(n_seq, patches // n_seq, wide), SEQ, 0, 0,...  8.81 us
  transfers between devices with their start and end apart: 16, of which 8 were waited for; matrix products, arithmetic and copies ran while one was open for 1% of the time, Pallas kernels for 2%

profile of v4, /device:TPU:1, one launch (start us, length us, event | category | flops | bytes accessed | tf_op | source)
XLA Modules:
  0.0 176.3 jit_solution(6144868962685256103)
XLA Ops:
  0.6 0.0 copy-start
  0.6 0.0 copy-start.3
  0.7 1.1 copy-done.3
  1.8 1.0 copy-done.4
  2.7 1.1 shard_map.106
  3.8 8.8 %all-to-all-start = ((bf16[16,16,1728]{2,1,0:T(8,128)(2,1)}), bf16[16,16,1728]{2,1,0:T(8,128)(2,1)S(1)}, u32[]{:S(2)}, u32[]{:S(2)}) async-start(bf16[16,16,1728]{2,1,0:T(8,128)(2,1)} %bitcast.6), calls=%async_computation | async-start | bytes 1835008 | tf_op jit(solution)/shard_map/all_to_all | solution.py:347
  12.7 0.1 pad_add_fusion.spot_ref
  12.7 0.0 copy-done.5
  12.7 0.9 shard_map.103
  13.6 3.7 %collective-permute-start = (bf16[36,432]{1,0:T(8,128)(2,1)S(1)}, bf16[36,432]{1,0:T(8,128)(2,1)S(1)}, u32[]{:S(2)}, u32[]{:S(2)}) collective-permute-start(bf16[36,432]{1,0:T(8,128)(2,1)S(1)} %get-tuple-element.26), channel_id=1, source_target_pairs={{0,16},{16,0},{1,17},{17,1},{2,18},{18,2},{3,19},{19,3},{4,20},{20... | collective-permute-start | bytes 93320 | tf_op jit(solution)/shard_map/ppermute | solution.py:34
  18.0 0.1 sine_convert_fusion
  18.0 0.1 collective-permute-done.theirs_ref
  18.2 0.6 shard_map.104.own_ref
  18.8 9.8 %collective-permute-start.1 = (bf16[72,432]{1,0:T(8,128)(2,1)S(1)}, bf16[72,432]{1,0:T(8,128)(2,1)S(1)}, u32[]{:S(2)}, u32[]{:S(2)}) collective-permute-start(bf16[72,432]{1,0:T(8,128)(2,1)S(1)} %shard_map.104.own_ref), channel_id=1, source_target_pairs={{0,128},{32,160},{64,192},{96,224},{128,0},{160,32},{192,64},{224,... | collective-permute-start | bytes 186632 | tf_op jit(solution)/shard_map/ppermute | solution.py:39
  28.5 4.4 %collective-permute-start.2 = (bf16[72,432]{1,0:T(8,128)(2,1)S(1)}, bf16[72,432]{1,0:T(8,128)(2,1)S(1)}, u32[]{:S(2)}, u32[]{:S(2)}) collective-permute-start(bf16[72,432]{1,0:T(8,128)(2,1)S(1)} %shard_map.104.own_ref), channel_id=1, source_target_pairs={{0,256},{256,0},{1,257},{257,1},{2,258},{258,2},{3,259},{259,3},{4... | collective-permute-start | bytes 186632 | tf_op jit(solution)/shard_map/ppermute | solution.py:34
  32.9 2.2 %collective-permute-start.3 = (bf16[72,432]{1,0:T(8,128)(2,1)S(1)}, bf16[72,432]{1,0:T(8,128)(2,1)S(1)}, u32[]{:S(2)}, u32[]{:S(2)}) collective-permute-start(bf16[72,432]{1,0:T(8,128)(2,1)S(1)} %shard_map.104.own_ref), channel_id=1, source_target_pairs={{0,384},{32,416},{64,448},{96,480},{128,256},{160,288},{192,320},{... | collective-permute-start | bytes 186632 | tf_op jit(solution)/shard_map/ppermute | solution.py:49
  35.1 0.0 copy-done
  35.1 0.2 fusion.mod_ref
  35.3 0.0 collective-permute-done.1.far_ref
  35.3 0.7 collective-permute-done.2.across_ref
  36.0 8.6 %collective-permute-done.3.both_ref = bf16[72,432]{1,0:T(8,128)(2,1)S(1)} collective-permute-done((bf16[72,432]{1,0:T(8,128)(2,1)S(1)}, bf16[72,432]{1,0:T(8,128)(2,1)S(1)}, u32[]{:S(2)}, u32[]{:S(2)}) %collective-permute-start.3) | collective-permute-done | bytes 62240 | tf_op jit(solution)/shard_map/ppermute | solution.py:49
  44.6 0.6 shard_map.105.near_ref
  45.2 0.0 all-to-all-done
  45.2 2.3 %shard_map.107 = (bf16[256,1408]{1,0:T(8,128)(2,1)S(1)}, bf16[256,1408]{1,0:T(8,128)(2,1)S(1)}, bf16[256,1536]{1,0:T(8,128)(2,1)S(1)}) custom-call(s32[3]{0:T(128)S(1)} %pad_add_fusion.spot_ref, bf16[256,1728]{1,0:T(8,128)(2,1)S(1)} %bitcast.17, f32[1,2304]{1,0:T(1,128)S(1)} %fusion.mod_ref), custom_call_target="tpu_custom_call" | custom-call | bytes 3122188 | tf_op jit(solution)/shard_map/pallas_call | solution.py:315
  47.5 0.9 copy-done.8
  48.3 2.9 %collective-permute-start.4 = (bf16[256,1536]{1,0:T(8,128)(2,1)S(1)}, bf16[256,1536]{1,0:T(8,128)(2,1)S(1)}, u32[]{:S(2)}, u32[]{:S(2)}) collective-permute-start(bf16[256,1536]{1,0:T(8,128)(2,1)S(1)} %get-tuple-element.29), channel_id=1, source_target_pairs={{0,8},{8,0},{1,9},{9,1},{2,10},{10,2},{3,11},{11,3},{4,12},{12,4},... | collective-permute-start | bytes 2359304 | tf_op jit(solution)/shard_map/ppermute | solution.py:34
  51.3 5.3 %collective-permute-start.5 = (bf16[256,1408]{1,0:T(8,128)(2,1)S(1)}, bf16[256,1408]{1,0:T(8,128)(2,1)S(1)}, u32[]{:S(2)}, u32[]{:S(2)}) collective-permute-start(bf16[256,1408]{1,0:T(8,128)(2,1)S(1)} %get-tuple-element.30), channel_id=1, source_target_pairs={{0,16},{16,0},{1,17},{17,1},{2,18},{18,2},{3,19},{19,3},{4,20},{20... | collective-permute-start | bytes 2162696 | tf_op jit(solution)/shard_map/ppermute | solution.py:34
  56.6 2.2 %collective-permute-start.7 = (bf16[2,72,432]{2,1,0:T(8,128)(2,1)S(1)}, bf16[2,72,432]{2,1,0:T(8,128)(2,1)S(1)}, u32[]{:S(2)}, u32[]{:S(2)}) collective-permute-start(bf16[2,72,432]{2,1,0:T(8,128)(2,1)S(1)} %get-tuple-element.48), channel_id=1, source_target_pairs={{0,192},{32,224},{64,0},{96,32},{128,64},{160,96},{192,128},{224,1... | collective-permute-start | bytes 373256 | tf_op jit(solution)/shard_map/ppermute | solution.py:39
  58.9 1.9 %collective-permute-start.6 = (bf16[4,72,432]{2,1,0:T(8,128)(2,1)S(1)}, bf16[4,72,432]{2,1,0:T(8,128)(2,1)S(1)}, u32[]{:S(2)}, u32[]{:S(2)}) collective-permute-start(bf16[4,72,432]{2,1,0:T(8,128)(2,1)S(1)} %shard_map.105.near_ref), channel_id=1, source_target_pairs={{0,224},{32,0},{64,32},{96,64},{128,96},{160,128},{192,160},{224,1... | collective-permute-start | bytes 746504 | tf_op jit(solution)/shard_map/ppermute | solution.py:39
  60.8 3.4 %collective-permute-start.9 = (bf16[4,72,432]{2,1,0:T(8,128)(2,1)S(1)}, bf16[4,72,432]{2,1,0:T(8,128)(2,1)S(1)}, u32[]{:S(2)}, u32[]{:S(2)}) collective-permute-start(bf16[4,72,432]{2,1,0:T(8,128)(2,1)S(1)} %shard_map.105.near_ref), channel_id=1, source_target_pairs={{0,32},{32,64},{64,96},{96,128},{128,160},{160,192},{192,224},{224... | collective-permute-start | bytes 746504 | tf_op jit(solution)/shard_map/ppermute | solution.py:39
  64.2 2.7 %collective-permute-done.7.low_ref = bf16[2,72,432]{2,1,0:T(8,128)(2,1)S(1)} collective-permute-done((bf16[2,72,432]{2,1,0:T(8,128)(2,1)S(1)}, bf16[2,72,432]{2,1,0:T(8,128)(2,1)S(1)}, u32[]{:S(2)}, u32[]{:S(2)}) %collective-permute-start.7) | collective-permute-done | bytes 124448 | tf_op jit(solution)/shard_map/ppermute | solution.py:39
  66.9 2.5 %collective-permute-start.8 = (bf16[2,72,432]{2,1,0:T(8,128)(2,1)S(1)}, bf16[2,72,432]{2,1,0:T(8,128)(2,1)S(1)}, u32[]{:S(2)}, u32[]{:S(2)}) collective-permute-start(bf16[2,72,432]{2,1,0:T(8,128)(2,1)S(1)} %get-tuple-element.47), channel_id=1, source_target_pairs={{0,64},{32,96},{64,128},{96,160},{128,192},{160,224},{192,0},{224,... | collective-permute-start | bytes 373256 | tf_op jit(solution)/shard_map/ppermute | solution.py:39
  69.4 7.5 %collective-permute-done.8.high_ref = bf16[2,72,432]{2,1,0:T(8,128)(2,1)S(1)} collective-permute-done((bf16[2,72,432]{2,1,0:T(8,128)(2,1)S(1)}, bf16[2,72,432]{2,1,0:T(8,128)(2,1)S(1)}, u32[]{:S(2)}, u32[]{:S(2)}) %collective-permute-start.8) | collective-permute-done | bytes 124448 | tf_op jit(solution)/shard_map/ppermute | solution.py:39
  76.9 0.0 collective-permute-done.6.up_ref
  76.9 0.0 collective-permute-done.9.down_ref
  76.9 0.0 collective-permute-done.5.core_hbm
  76.9 0.0 copy-start.11
  76.9 0.0 collective-permute-done.4.side_hbm
  76.9 3.7 %collective-permute-start.10 = (bf16[256,1536]{1,0:T(8,128)(2,1)S(1)}, bf16[256,1536]{1,0:T(8,128)(2,1)S(1)}, u32[]{:S(2)}, u32[]{:S(2)}) collective-permute-start(bf16[256,1536]{1,0:T(8,128)(2,1)S(1)} %collective-permute-done.4.side_hbm), channel_id=1, source_target_pairs={{0,16},{16,0},{1,17},{17,1},{2,18},{18,2},{3,19},{19,3},{4,20},{20... | collective-permute-start | bytes 2359304 | tf_op jit(solution)/shard_map/ppermute | solution.py:34
  80.7 0.6 shard_map.108
  81.3 0.0 copy-done.11
  81.3 0.0 copy-done.9
  81.3 0.0 copy-start.1
  81.3 1.0 copy-done.1
  82.4 0.2 collective-permute-done.10.both_hbm
  82.6 0.9 copy-done.10
  83.5 12.3 %shard_map.109 = (bf16[128,32,128]{2,1,0:T(8,128)(2,1)}, bf16[512,1152]{1,0:T(8,128)(2,1)}, bf16[512,1152]{1,0:T(8,128)(2,1)}) custom-call(bf16[1152,432]{1,0:T(8,128)(2,1)} %bitcast.20, bf16[256,1408]{1,0:T(8,128)(2,1)} %copy-done.8, bf16[256,1408]{1,0:T(8,128)(2,1)} %copy-done.11, bf16[256,1536]{1,0:T(8,128)(2,1)} %copy-done.9, bf16[256,1536]{1,0:T(8,128)(2,1)} %copy-done.10), custom_call_target="tpu_custom_call" | custom-call | flops 3057647616 | bytes 7417856 | tf_op jit(solution)/shard_map/pallas_call | solution.py:315
  95.8 15.6 %all-to-all-start.1 = ((bf16[128,32,128]{2,1,0:T(8,128)(2,1)}), bf16[128,32,128]{2,1,0:T(8,128)(2,1)S(1)}, u32[]{:S(2)}, u32[]{:S(2)}) async-start(bf16[128,32,128]{2,1,0:T(8,128)(2,1)} %get-tuple-element.38), calls=%async_computation.1 | async-start | bytes 2097152 | tf_op jit(solution)/shard_map/all_to_all | solution.py:405
  111.5 2.6 %collective-permute-start.11 = (bf16[512,1152]{1,0:T(8,128)(2,1)}, bf16[512,1152]{1,0:T(8,128)(2,1)S(1)}, u32[]{:S(2)}, u32[]{:S(2)}) collective-permute-start(bf16[512,1152]{1,0:T(8,128)(2,1)} %get-tuple-element.40), channel_id=1, source_target_pairs={{0,16},{16,0},{1,17},{17,1},{2,18},{18,2},{3,19},{19,3},{4,20},{20... | collective-permute-start | bytes 3538952 | tf_op jit(solution)/shard_map/ppermute | solution.py:34
  114.0 2.7 %collective-permute-done.11.got_ref = bf16[512,1152]{1,0:T(8,128)(2,1)S(1)} collective-permute-done((bf16[512,1152]{1,0:T(8,128)(2,1)}, bf16[512,1152]{1,0:T(8,128)(2,1)S(1)}, u32[]{:S(2)}, u32[]{:S(2)}) %collective-permute-start.11) | collective-permute-done | bytes 1179680 | tf_op jit(solution)/shard_map/ppermute | solution.py:34
  116.7 1.3 copy-done.2
  118.0 0.3 shard_map.110
  118.3 1.9 %collective-permute-start.12 = (bf16[256,1152]{1,0:T(8,128)(2,1)S(1)}, bf16[256,1152]{1,0:T(8,128)(2,1)S(1)}, u32[]{:S(2)}, u32[]{:S(2)}) collective-permute-start(bf16[256,1152]{1,0:T(8,128)(2,1)S(1)} %get-tuple-element.42), channel_id=1, source_target_pairs={{0,8},{8,0},{1,9},{9,1},{2,10},{10,2},{3,11},{11,3},{4,12},{12,4},... | collective-permute-start | bytes 1769480 | tf_op jit(solution)/shard_map/ppermute | solution.py:34
  120.2 21.7 %collective-permute-done.12.refs_1_ = bf16[256,1152]{1,0:T(8,128)(2,1)S(1)} collective-permute-done((bf16[256,1152]{1,0:T(8,128)(2,1)S(1)}, bf16[256,1152]{1,0:T(8,128)(2,1)S(1)}, u32[]{:S(2)}, u32[]{:S(2)}) %collective-permute-start.12) | collective-permute-done | bytes 589856 | tf_op jit(solution)/shard_map/ppermute | solution.py:34
  141.9 0.9 shard_map.111.back_ref
  142.7 0.0 all-to-all-done.1.parts_ref
  142.7 0.2 shard_map.112
  143.0 24.5 %all_to_all.15.pieces_ref = bf16[16,16,1408]{2,1,0:T(8,128)(2,1)S(1)} all-to-all(bf16[16,16,1408]{2,1,0:T(8,128)(2,1)S(1)} %bitcast.19), channel_id=1, replica_groups=mesh['xh'=2,'z'=8,'c'=2,'xl'=2,'y'=8] {'xl','y'}, dimensions={0} | all-to-all | bytes 1441792 | tf_op jit(solution)/shard_map/all_to_all | solution.py:407
  167.4 0.6 shard_map.113
  168.1 5.0 %collective-permute-start.13 = (f32[2,36,432]{2,1,0:T(8,128)S(1)}, f32[2,36,432]{2,1,0:T(8,128)S(1)}, u32[]{:S(2)}, u32[]{:S(2)}) collective-permute-start(f32[2,36,432]{2,1,0:T(8,128)S(1)} %get-tuple-element.44), channel_id=1, source_target_pairs={{0,16},{16,0},{1,17},{17,1},{2,18},{18,2},{3,19},{19,3},{4,20},{20... | collective-permute-start | bytes 373256 | tf_op jit(solution)/shard_map/ppermute | solution.py:34
  173.8 0.1 pad_maximum_fusion.decay_ref
  173.9 0.9 slice.12
  174.8 0.0 collective-permute-done.13.core_ref
  174.8 1.5 shard_map.114
  (11 shorter events, 0.0 us)
Async XLA Ops:
  0.6 34.4 %copy-start = (bf16[128,2304]{1,0:T(8,128)(2,1)S(1)}, bf16[128,2304]{1,0:T(8,128)(2,1)}, u32[]{:S(2)}) copy-start(bf16[128,2304]{1,0:T(8,128)(2,1)} %param.10) | copy-start | bytes 1769476
  0.6 1.1 copy-start.3
  1.8 1.0 copy-start.4
  3.8 8.9 %copy-start.5 = (f32[36,1728]{1,0:T(8,128)S(1)}, f32[36,1728]{1,0:T(8,128)}, u32[]{:S(2)}) copy-start(f32[36,1728]{1,0:T(8,128)} %master_ref.1) | copy-start | bytes 746500
  3.8 41.4 %all-to-all-start = ((bf16[16,16,1728]{2,1,0:T(8,128)(2,1)}), bf16[16,16,1728]{2,1,0:T(8,128)(2,1)S(1)}, u32[]{:S(2)}, u32[]{:S(2)}) async-start(bf16[16,16,1728]{2,1,0:T(8,128)(2,1)} %bitcast.6), calls=%async_computation | async-start | bytes 1835008 | tf_op jit(solution)/shard_map/all_to_all | solution.py:347
  13.6 4.6 %collective-permute-start = (bf16[36,432]{1,0:T(8,128)(2,1)S(1)}, bf16[36,432]{1,0:T(8,128)(2,1)S(1)}, u32[]{:S(2)}, u32[]{:S(2)}) collective-permute-start(bf16[36,432]{1,0:T(8,128)(2,1)S(1)} %get-tuple-element.26), channel_id=1, source_target_pairs={{0,16},{16,0},{1,17},{17,1},{2,18},{18,2},{3,19},{19,3},{4,20},{20... | collective-permute-start | bytes 93320 | tf_op jit(solution)/shard_map/ppermute | solution.py:34
  18.8 16.6 %collective-permute-start.1 = (bf16[72,432]{1,0:T(8,128)(2,1)S(1)}, bf16[72,432]{1,0:T(8,128)(2,1)S(1)}, u32[]{:S(2)}, u32[]{:S(2)}) collective-permute-start(bf16[72,432]{1,0:T(8,128)(2,1)S(1)} %shard_map.104.own_ref), channel_id=1, source_target_pairs={{0,128},{32,160},{64,192},{96,224},{128,0},{160,32},{192,64},{224,... | collective-permute-start | bytes 186632 | tf_op jit(solution)/shard_map/ppermute | solution.py:39
  28.5 7.5 %collective-permute-start.2 = (bf16[72,432]{1,0:T(8,128)(2,1)S(1)}, bf16[72,432]{1,0:T(8,128)(2,1)S(1)}, u32[]{:S(2)}, u32[]{:S(2)}) collective-permute-start(bf16[72,432]{1,0:T(8,128)(2,1)S(1)} %shard_map.104.own_ref), channel_id=1, source_target_pairs={{0,256},{256,0},{1,257},{257,1},{2,258},{258,2},{3,259},{259,3},{4... | collective-permute-start | bytes 186632 | tf_op jit(solution)/shard_map/ppermute | solution.py:34
  32.9 11.7 %collective-permute-start.3 = (bf16[72,432]{1,0:T(8,128)(2,1)S(1)}, bf16[72,432]{1,0:T(8,128)(2,1)S(1)}, u32[]{:S(2)}, u32[]{:S(2)}) collective-permute-start(bf16[72,432]{1,0:T(8,128)(2,1)S(1)} %shard_map.104.own_ref), channel_id=1, source_target_pairs={{0,384},{32,416},{64,448},{96,480},{128,256},{160,288},{192,320},{... | collective-permute-start | bytes 186632 | tf_op jit(solution)/shard_map/ppermute | solution.py:49
  47.5 0.9 copy-start.8
  48.3 28.6 %collective-permute-start.4 = (bf16[256,1536]{1,0:T(8,128)(2,1)S(1)}, bf16[256,1536]{1,0:T(8,128)(2,1)S(1)}, u32[]{:S(2)}, u32[]{:S(2)}) collective-permute-start(bf16[256,1536]{1,0:T(8,128)(2,1)S(1)} %get-tuple-element.29), channel_id=1, source_target_pairs={{0,8},{8,0},{1,9},{9,1},{2,10},{10,2},{3,11},{11,3},{4,12},{12,4},... | collective-permute-start | bytes 2359304 | tf_op jit(solution)/shard_map/ppermute | solution.py:34
  51.3 25.6 %collective-permute-start.5 = (bf16[256,1408]{1,0:T(8,128)(2,1)S(1)}, bf16[256,1408]{1,0:T(8,128)(2,1)S(1)}, u32[]{:S(2)}, u32[]{:S(2)}) collective-permute-start(bf16[256,1408]{1,0:T(8,128)(2,1)S(1)} %get-tuple-element.30), channel_id=1, source_target_pairs={{0,16},{16,0},{1,17},{17,1},{2,18},{18,2},{3,19},{19,3},{4,20},{20... | collective-permute-start | bytes 2162696 | tf_op jit(solution)/shard_map/ppermute | solution.py:34
  56.6 10.2 %collective-permute-start.7 = (bf16[2,72,432]{2,1,0:T(8,128)(2,1)S(1)}, bf16[2,72,432]{2,1,0:T(8,128)(2,1)S(1)}, u32[]{:S(2)}, u32[]{:S(2)}) collective-permute-start(bf16[2,72,432]{2,1,0:T(8,128)(2,1)S(1)} %get-tuple-element.48), channel_id=1, source_target_pairs={{0,192},{32,224},{64,0},{96,32},{128,64},{160,96},{192,128},{224,1... | collective-permute-start | bytes 373256 | tf_op jit(solution)/shard_map/ppermute | solution.py:39
  58.9 18.0 %collective-permute-start.6 = (bf16[4,72,432]{2,1,0:T(8,128)(2,1)S(1)}, bf16[4,72,432]{2,1,0:T(8,128)(2,1)S(1)}, u32[]{:S(2)}, u32[]{:S(2)}) collective-permute-start(bf16[4,72,432]{2,1,0:T(8,128)(2,1)S(1)} %shard_map.105.near_ref), channel_id=1, source_target_pairs={{0,224},{32,0},{64,32},{96,64},{128,96},{160,128},{192,160},{224,1... | collective-permute-start | bytes 746504 | tf_op jit(solution)/shard_map/ppermute | solution.py:39
  60.8 16.1 %collective-permute-start.9 = (bf16[4,72,432]{2,1,0:T(8,128)(2,1)S(1)}, bf16[4,72,432]{2,1,0:T(8,128)(2,1)S(1)}, u32[]{:S(2)}, u32[]{:S(2)}) collective-permute-start(bf16[4,72,432]{2,1,0:T(8,128)(2,1)S(1)} %shard_map.105.near_ref), channel_id=1, source_target_pairs={{0,32},{32,64},{64,96},{96,128},{128,160},{160,192},{192,224},{224... | collective-permute-start | bytes 746504 | tf_op jit(solution)/shard_map/ppermute | solution.py:39
  66.9 10.0 %collective-permute-start.8 = (bf16[2,72,432]{2,1,0:T(8,128)(2,1)S(1)}, bf16[2,72,432]{2,1,0:T(8,128)(2,1)S(1)}, u32[]{:S(2)}, u32[]{:S(2)}) collective-permute-start(bf16[2,72,432]{2,1,0:T(8,128)(2,1)S(1)} %get-tuple-element.47), channel_id=1, source_target_pairs={{0,64},{32,96},{64,128},{96,160},{128,192},{160,224},{192,0},{224,... | collective-permute-start | bytes 373256 | tf_op jit(solution)/shard_map/ppermute | solution.py:39
  76.9 4.4 %copy-start.11 = (bf16[256,1408]{1,0:T(8,128)(2,1)}, bf16[256,1408]{1,0:T(8,128)(2,1)S(1)}, u32[]{:S(2)}) copy-start(bf16[256,1408]{1,0:T(8,128)(2,1)S(1)} %collective-permute-done.5.core_hbm) | copy-start | bytes 2162692
  76.9 4.4 %copy-start.9 = (bf16[256,1536]{1,0:T(8,128)(2,1)}, bf16[256,1536]{1,0:T(8,128)(2,1)S(1)}, u32[]{:S(2)}) copy-start(bf16[256,1536]{1,0:T(8,128)(2,1)S(1)} %collective-permute-done.4.side_hbm) | copy-start | bytes 2359300
  76.9 5.6 %collective-permute-start.10 = (bf16[256,1536]{1,0:T(8,128)(2,1)S(1)}, bf16[256,1536]{1,0:T(8,128)(2,1)S(1)}, u32[]{:S(2)}, u32[]{:S(2)}) collective-permute-start(bf16[256,1536]{1,0:T(8,128)(2,1)S(1)} %collective-permute-done.4.side_hbm), channel_id=1, source_target_pairs={{0,16},{16,0},{1,17},{17,1},{2,18},{18,2},{3,19},{19,3},{4,20},{20... | collective-permute-start | bytes 2359304 | tf_op jit(solution)/shard_map/ppermute | solution.py:34
  81.3 1.0 copy-start.1
  82.6 0.9 copy-start.10
  95.8 46.9 %all-to-all-start.1 = ((bf16[128,32,128]{2,1,0:T(8,128)(2,1)}), bf16[128,32,128]{2,1,0:T(8,128)(2,1)S(1)}, u32[]{:S(2)}, u32[]{:S(2)}) async-start(bf16[128,32,128]{2,1,0:T(8,128)(2,1)} %get-tuple-element.38), calls=%async_computation.1 | async-start | bytes 2097152 | tf_op jit(solution)/shard_map/all_to_all | solution.py:405
  111.5 5.2 %collective-permute-start.11 = (bf16[512,1152]{1,0:T(8,128)(2,1)}, bf16[512,1152]{1,0:T(8,128)(2,1)S(1)}, u32[]{:S(2)}, u32[]{:S(2)}) collective-permute-start(bf16[512,1152]{1,0:T(8,128)(2,1)} %get-tuple-element.40), channel_id=1, source_target_pairs={{0,16},{16,0},{1,17},{17,1},{2,18},{18,2},{3,19},{19,3},{4,20},{20... | collective-permute-start | bytes 3538952 | tf_op jit(solution)/shard_map/ppermute | solution.py:34
  116.7 1.3 copy-start.2
  118.3 23.6 %collective-permute-start.12 = (bf16[256,1152]{1,0:T(8,128)(2,1)S(1)}, bf16[256,1152]{1,0:T(8,128)(2,1)S(1)}, u32[]{:S(2)}, u32[]{:S(2)}) collective-permute-start(bf16[256,1152]{1,0:T(8,128)(2,1)S(1)} %get-tuple-element.42), channel_id=1, source_target_pairs={{0,8},{8,0},{1,9},{9,1},{2,10},{10,2},{3,11},{11,3},{4,12},{12,4},... | collective-permute-start | bytes 1769480 | tf_op jit(solution)/shard_map/ppermute | solution.py:34
  167.4 7.4 %copy-start.6 = (f32[36,1728]{1,0:T(8,128)S(1)}, f32[36,1728]{1,0:T(8,128)}, u32[]{:S(2)}) copy-start(f32[36,1728]{1,0:T(8,128)} %slow_ref.1) | copy-start | bytes 746500
  167.4 7.4 %copy-start.7 = (f32[36,1728]{1,0:T(8,128)S(1)}, f32[36,1728]{1,0:T(8,128)}, u32[]{:S(2)}) copy-start(f32[36,1728]{1,0:T(8,128)} %fast_ref.1) | copy-start | bytes 746500
  168.1 6.7 %collective-permute-start.13 = (f32[2,36,432]{2,1,0:T(8,128)S(1)}, f32[2,36,432]{2,1,0:T(8,128)S(1)}, u32[]{:S(2)}, u32[]{:S(2)}) collective-permute-start(f32[2,36,432]{2,1,0:T(8,128)S(1)} %get-tuple-element.44), channel_id=1, source_target_pairs={{0,16},{16,0},{1,17},{17,1},{2,18},{18,2},{3,19},{19,3},{4,20},{20... | collective-permute-start | bytes 373256 | tf_op jit(solution)/shard_map/ppermute | solution.py:34

commit v5 on v4

--- a/solution.py
+++ b/solution.py
@@ -14,9 +14,9 @@
 loss_scale = 128.0
 gamma_slow = 16.97
 gamma_fast = 6.94
-AXES = ("xh", "z", "c", "xl", "y")
+AXES = ("xh", "zh", "zl", "c", "xl", "y")
 SEQ = ("xl", "y")
-ROWS = ("xh", "z")
+ROWS = ("xh", "zh", "zl")
 F32 = jnp.float32
 BF16 = jnp.bfloat16
 MIB = 1024 * 1024
@@ -32,21 +32,6 @@
 
 def swap(value, axis):
     return lax.ppermute(value, axis, [(0, 1), (1, 0)])
-
-
-def shift(value, away):
-    count = lax.axis_size("z")
-    return lax.ppermute(value, "z", [(i, (i + away) % count) for i in range(count)])
-
-
-def half_turn(value):
-    return shift(value, lax.axis_size("z") // 2)
-
-
-def both_turn(value):
-    count = lax.axis_size("z")
-    pairs = [(i, (count - count * (i // count)) + (i % count + count // 2) % count) for i in range(2 * count)]
-    return lax.ppermute(value, ("xh", "z"), pairs)
 
 
 def modulate_table(timesteps, ada_weight):
@@ -78,7 +63,7 @@
     return out
 
 
-def norm_kernel(spot_ref, packed_ref, mod_ref, own_ref, core_ref, side_ref, held_ref, sem):
+def norm_kernel(spot_ref, packed_ref, mod_ref, core_ref, side_ref):
     width = mod_ref.shape[1] // 2
     quarter = (packed_ref.shape[1] - width) // 4
     centered, _ = stats(packed_ref[:, :width].astype(F32))
@@ -87,15 +72,10 @@
     pieces = [cot[:, i * quarter : (i + 1) * quarter] for i in range(4)]
     spot = spot_ref[0]
     own, side, core, both = (pick(spot, [pieces[i ^ flip] for i in range(4)]) for flip in range(4))
-    held_ref[:, :width] = normed
-    held_ref[:, width : width + quarter] = own.astype(BF16)
-    copy = pltpu.make_async_copy(held_ref, own_ref, sem)
-    copy.start()
-    core_ref[:, :width] = normed
-    core_ref[:, width : width + quarter] = core.astype(BF16)
     side_ref[:, :width] = normed
     side_ref[:, width : width + 2 * quarter] = jnp.concatenate([side, both], axis=1).astype(BF16)
-    copy.wait()
+    core_ref[:, :width] = normed
+    core_ref[:, width : width + 2 * quarter] = jnp.concatenate([core, own], axis=1).astype(BF16)
 
 
 def norm_back_kernel(packed_ref, mod_ref, *refs):
@@ -173,13 +153,13 @@
 
 def main_kernel(
     weight_hbm, own_hbm, core_hbm, side_hbm, both_hbm, packed_hbm, near_hbm, far_hbm,
-    weight_ref, own_ref, core_ref, side_ref, both_ref, packed_ref, parts_ref, total_ref, in_sems, out_sems,
+    raw_ref, own_ref, core_ref, side_ref, both_ref, weight_ref, packed_ref, parts_ref, total_ref, in_sems, out_sems,
 ):
     tokens = own_ref.shape[0]
     model_width, cols = total_ref.shape
     quarter = cols // 3
     pairs = (
-        (weight_hbm, weight_ref), (own_hbm, own_ref), (core_hbm, core_ref), (side_hbm, side_ref), (both_hbm, both_ref),
+        (weight_hbm, raw_ref), (own_hbm, own_ref), (core_hbm, core_ref), (side_hbm, side_ref), (both_hbm, both_ref),
     )
     loads = [pltpu.make_async_copy(source, target, in_sems.at[i]) for i, (source, target) in enumerate(pairs)]
     for load in loads:
@@ -190,7 +170,9 @@
     lane = lax.broadcasted_iota(jnp.int32, (tokens, quarter), 1)
     stores = []
     loads[0].wait()
-    places = ((near_hbm, 0, 0), (far_hbm, 0, 0), (near_hbm, 1, 0), (far_hbm, 1, 1))
+    blocks = [raw_ref[low, group][:, :cols].astype(F32) for group in range(4) for low in range(4)]
+    weight_ref[...] = jnp.concatenate(blocks, axis=0).astype(BF16)
+    places = ((near_hbm, 0, 1), (far_hbm, 0, 0), (near_hbm, 1, 0), (far_hbm, 1, 1))
     for index, (target, place, skip) in enumerate(places):
         ref = pairs[index + 1][1]
         loads[index + 1].wait()
@@ -247,24 +229,20 @@
     mine, theirs = mine_ref[...].astype(F32), theirs_ref[...].astype(F32)
     first = spot_ref[0] < 2
     upper, lower = jnp.where(first, mine, theirs), jnp.where(first, theirs, mine)
-    out_ref[...] = jnp.concatenate([upper, lower], axis=0).astype(BF16)
-
-
-def quad_kernel(spot_ref, own_ref, far_ref, across_ref, both_ref, out_ref):
-    place = spot_ref[2]
-    out_ref[place] = own_ref[...]
-    out_ref[place + 1 - 2 * lax.rem(place, 2)] = far_ref[...]
-    out_ref[lax.rem(place + 2, 4)] = across_ref[...]
-    out_ref[3 - place] = both_ref[...]
-
-
-def gather_kernel(spot_ref, near_ref, up_ref, low_ref, high_ref, down_ref, out_ref):
-    place = spot_ref[1]
-    for ahead, sources in enumerate(((near_ref,), (up_ref,), (low_ref, high_ref), (down_ref,))):
-        lowest = lax.rem(place + ahead, 4)
-        for group in range(4):
-            ref = sources[group * len(sources) // 4]
-            out_ref[4 * group + lowest] = ref[group % ref.shape[0]]
+    pair = jnp.concatenate([upper, lower], axis=0)
+    rest = jnp.zeros((pair.shape[0], out_ref.shape[1] - pair.shape[1]), F32)
+    out_ref[...] = jnp.concatenate([pair, rest], axis=1).astype(BF16)
+
+
+def double_kernel(spot_ref, own_ref, got_ref, out_ref):
+    out_ref[spot_ref[1]] = own_ref[...]
+    out_ref[1 - spot_ref[1]] = got_ref[...]
+
+
+def quad_kernel(spot_ref, own_ref, got_ref, out_ref):
+    for across in range(2):
+        out_ref[2 * across + spot_ref[2]] = own_ref[across]
+        out_ref[2 * across + 1 - spot_ref[2]] = got_ref[across]
 
 
 def payload_kernel(parts_ref, back_ref, out_ref):
@@ -334,60 +312,47 @@
     own_rows, triple = master.shape
     wide = width + inner
     n_seq = lax.axis_size("xl") * lax.axis_size("y")
-    n_rows = lax.axis_size("xh") * lax.axis_size("z")
+    n_rows = lax.axis_size("xh") * lax.axis_size("zh") * lax.axis_size("zl")
     n_y = lax.axis_size("y")
     quarter = inner // 4
     cols = 3 * quarter
     pair_rows = 2 * own_rows
     core, side = lax.axis_index("c"), lax.axis_index("xl")
-    across, along = lax.axis_index("xh"), lax.axis_index("z")
-    spots = jnp.stack([2 * core + side, lax.rem(along, 4), 2 * across + along // 4]).astype(jnp.int32)
+    spots = jnp.stack([2 * core + side, lax.axis_index("xh"), lax.axis_index("zh")]).astype(jnp.int32)
 
     packed = call(pack_kernel, [((patches, wide), BF16)], hidden[0, 0], cotangent[0, 0].T)
     tokens = lax.all_to_all(packed.reshape(n_seq, patches // n_seq, wide), SEQ, 0, 0, tiled=True)
     tokens = tokens.reshape(patches, wide)
 
     mine, theirs = call(columns_kernel, [((own_rows, cols), BF16)] * 2, spots, master, smem=1)
-    pair = call(pair_kernel, [((pair_rows, cols), BF16)], spots, mine, swap(theirs, "c"), smem=1)
-    quad = call(
-        quad_kernel,
-        [((4, pair_rows, cols), BF16)],
-        spots, pair, half_turn(pair), swap(pair, "xh"), both_turn(pair),
-        smem=1,
-    )
-    quad, tokens = lax.optimization_barrier((quad, tokens))
+    padded = lanes(cols)
+    pair = call(pair_kernel, [((pair_rows, padded), BF16)], spots, mine, swap(theirs, "c"), smem=1)
+    double = call(double_kernel, [((2, pair_rows, padded), BF16)], spots, pair, swap(pair, "xh"), smem=1)
+    quad = call(quad_kernel, [((4, pair_rows, padded), BF16)], spots, double, swap(double, "zh"), smem=1)
+    weights = lax.all_gather(quad.reshape(4 * pair_rows, padded), "zl", axis=0, tiled=True)
+    weights = weights.reshape(4, 4, pair_rows, padded)
 
     modulation = modulate_table(timesteps, ada_weight)
-    narrow, broad = lanes(width + quarter), lanes(width + 2 * quarter)
-    own, to_core, to_side = call(
-        norm_kernel,
-        [((patches, narrow), BF16), ((patches, narrow), BF16), ((patches, broad), BF16)],
-        spots, tokens, modulation,
-        scratch=[pltpu.VMEM((patches, narrow), BF16), pltpu.SemaphoreType.DMA(())],
-        smem=1,
-        hbm_out=(0,),
-    )
+    broad = lanes(width + 2 * quarter)
+    to_core, to_side = call(norm_kernel, [((patches, broad), BF16)] * 2, spots, tokens, modulation, smem=1)
     from_side = swap(to_side, "xl")
     from_core = swap(to_core, "c")
-    up, low, high, down = shift(quad, -1), shift(quad[:2], -2), shift(quad[2:], 2), shift(quad, 1)
-    from_side, from_core, up, low, high, down = lax.optimization_barrier((from_side, from_core, up, low, high, down))
+    from_side, from_core = lax.optimization_barrier((from_side, from_core))
     from_both = swap(from_side, "c")
-    weights = call(
-        gather_kernel, [((16, pair_rows, cols), BF16)], spots, quad, up, low, high, down, smem=1
-    ).reshape(width, cols)
 
     pieces = n_rows * n_y
     packed, near, far = call(
         main_kernel,
         [((pieces, 32, 128), BF16), ((2 * patches, width), BF16), ((2 * patches, width), BF16)],
-        weights, own, from_core, from_side, from_both,
+        weights, to_core, from_core, from_side, from_both,
         flops=6 * 4 * patches * width * cols,
         scratch=[
-            pltpu.VMEM((width, cols), BF16),
-            pltpu.VMEM((patches, narrow), BF16),
-            pltpu.VMEM((patches, narrow), BF16),
+            pltpu.VMEM((4, 4, pair_rows, padded), BF16),
             pltpu.VMEM((patches, broad), BF16),
             pltpu.VMEM((patches, broad), BF16),
+            pltpu.VMEM((patches, broad), BF16),
+            pltpu.VMEM((patches, broad), BF16),
+            pltpu.VMEM((width, cols), BF16),
             pltpu.VMEM((pieces, 32, 128), BF16),
             pltpu.VMEM((4, patches, width), BF16),
             pltpu.VMEM((width, cols), F32),
@@ -418,8 +383,8 @@
 
 
 def solution(mesh):
-    fine = Mesh(mesh.devices.reshape(2, 8, 2, 2, 8), AXES)
-    dp, seq = ("xh", "z", "c"), SEQ
+    fine = Mesh(mesh.devices.reshape(2, 2, 4, 2, 2, 8), AXES)
+    dp, seq = ROWS + ("c",), SEQ
     placed = (
         P(dp, seq, None, None),
         P(dp),

time: 177 us -> 194 us (1.096)
  waiting for transfers between devices: 44.2 us -> 63.9 us
  between operations: 2.41 us -> 15.7 us
  starting transfers between devices: 76 us -> 63.3 us
  local copies, waits for them, and re-layouts: 7.05 us -> 4.24 us
    ppermute x8 -> x9, waiting for transfers between devices: 25.4 us -> 49.4 us  [swap(): return lax.ppermute(value, axis, [(0, 1), (1, 0)])]
    ppermute x6 -> x0, starting transfers between devices: 22 us -> none  [the longest x5 19.8 us: shift(): lax.ppermute(value, 'z', [(i, (i + away) % count) for i in range(count)])]
    ppermute x6 -> x0, waiting for transfers between devices: 18.8 us -> none  [the longest x5 10.2 us: shift(): lax.ppermute(value, 'z', [(i, (i + away) % count) for i in range(count)])]
    all_gather x0 -> x1, waiting for transfers between devices: none -> 14.5 us  [on_device(): lax.all_gather(quad.reshape(4 * pair_rows, padded), 'zl', axis=0, tiled=T...]
    ppermute x8 -> x9, starting transfers between devices: 29.5 us -> 39.8 us  [swap(): return lax.ppermute(value, axis, [(0, 1), (1, 0)])]
    unnamed x24 -> x18, local copies, waits for them, and re-layouts: 6.17 us -> 3.38 us
  transfers between devices with their start and end apart: 16 -> 12, of which waited for: 8 -> 7; matrix products, arithmetic and copies ran while one was open for 1% -> 1% of each run, Pallas kernels for 2% -> 3%
where the time goes in v5:
time: 194 us
  waiting for transfers between devices  63.9 us (33%)
  starting transfers between devices  63.3 us (33%)
  blocking collectives  24 us (12%)
  Pallas kernels  22 us (11%)
  between operations  15.7 us (8%)
  local copies, waits for them, and re-layouts  4.24 us (2%)
    ppermute x9, waiting for transfers between devices, swap(): return lax.ppermute(value, axis, [(0, 1), (1, 0)])  49.4 us
    ppermute x9, starting transfers between devices, swap(): return lax.ppermute(value, axis, [(0, 1), (1, 0)])  39.8 us
    all_to_all x1, blocking collectives, on_device(): lax.all_to_all(joint.reshape(n_seq, patches // n_seq, width + 256), SEQ,...  24 us
    pallas_call x12, Pallas kernels, call(): pl.pallas_call(kernel, out_shape=shapes, in_specs=specs, out_specs=[pl.Bl...  22 us
    all_to_all x1, starting transfers between devices, on_device(): parts = lax.all_to_all(packed, ROWS + ('y',), 0, 0, tiled=True)  14.6 us
    all_gather x1, waiting for transfers between devices, on_device(): lax.all_gather(quad.reshape(4 * pair_rows, padded), 'zl', axis=0, tiled=T...  14.5 us
    all_to_all x1, starting transfers between devices, on_device(): lax.all_to_all(packed.reshape(n_seq, patches // n_seq, wide), SEQ, 0, 0,...  8.81 us
  transfers between devices with their start and end apart: 12, of which 7 were waited for; matrix products, arithmetic and copies ran while one was open for 1% of the time, Pallas kernels for 3%

profile of v5, /device:TPU:1, one launch (start us, length us, event | category | flops | bytes accessed | tf_op | source)
XLA Modules:
  0.0 193.6 jit_solution(130554517492622245)
XLA Ops:
  7.2 0.0 copy-start
  7.2 0.0 copy-start.2
  7.2 1.1 copy-done.2
  8.3 0.0 copy-start.3
  8.3 1.0 copy-done.3
  9.3 1.1 shard_map.107
  10.3 0.0 copy-start.4
  10.3 8.8 %all-to-all-start = ((bf16[16,16,1728]{2,1,0:T(8,128)(2,1)}), bf16[16,16,1728]{2,1,0:T(8,128)(2,1)S(1)}, u32[]{:S(2)}, u32[]{:S(2)}) async-start(bf16[16,16,1728]{2,1,0:T(8,128)(2,1)} %bitcast.8), calls=%async_computation | async-start | bytes 1835008 | tf_op jit(solution)/shard_map/all_to_all | solution.py:324
  19.2 0.0 all-gather.2.cloned.1.call-start
  19.2 0.1 pad_add_fusion.spot_ref
  19.3 0.0 copy-done.4
  19.3 0.9 shard_map.103
  20.2 3.7 %collective-permute-start = (bf16[36,432]{1,0:T(8,128)(2,1)S(1)}, bf16[36,432]{1,0:T(8,128)(2,1)S(1)}, u32[]{:S(2)}, u32[]{:S(2)}) collective-permute-start(bf16[36,432]{1,0:T(8,128)(2,1)S(1)} %get-tuple-element.19), channel_id=1, source_target_pairs={{0,16},{16,0},{1,17},{17,1},{2,18},{18,2},{3,19},{19,3},{4,20},{20... | collective-permute-start | bytes 93320 | tf_op jit(solution)/shard_map/ppermute | solution.py:34
  23.9 0.8 collective-permute-done.theirs_ref
  24.7 0.6 shard_map.104.own_ref
  25.3 3.5 %collective-permute-start.1 = (bf16[72,512]{1,0:T(8,128)(2,1)S(1)}, bf16[72,512]{1,0:T(8,128)(2,1)S(1)}, u32[]{:S(2)}, u32[]{:S(2)}) collective-permute-start(bf16[72,512]{1,0:T(8,128)(2,1)S(1)} %shard_map.104.own_ref), channel_id=1, source_target_pairs={{0,256},{256,0},{1,257},{257,1},{2,258},{258,2},{3,259},{259,3},{4... | collective-permute-start | bytes 221192 | tf_op jit(solution)/shard_map/ppermute | solution.py:34
  28.8 4.5 %collective-permute-done.1.got_ref = bf16[72,512]{1,0:T(8,128)(2,1)S(1)} collective-permute-done((bf16[72,512]{1,0:T(8,128)(2,1)S(1)}, bf16[72,512]{1,0:T(8,128)(2,1)S(1)}, u32[]{:S(2)}, u32[]{:S(2)}) %collective-permute-start.1) | collective-permute-done | bytes 73760 | tf_op jit(solution)/shard_map/ppermute | solution.py:34
  33.3 0.6 shard_map.105.own_ref
  33.9 9.4 %collective-permute-start.2 = (bf16[2,72,512]{2,1,0:T(8,128)(2,1)S(1)}, bf16[2,72,512]{2,1,0:T(8,128)(2,1)S(1)}, u32[]{:S(2)}, u32[]{:S(2)}) collective-permute-start(bf16[2,72,512]{2,1,0:T(8,128)(2,1)S(1)} %shard_map.105.own_ref), channel_id=1, source_target_pairs={{0,128},{128,0},{1,129},{129,1},{2,130},{130,2},{3,131},{131,3},{4... | collective-permute-start | bytes 442376 | tf_op jit(solution)/shard_map/ppermute | solution.py:34
  43.9 0.1 sine_convert_fusion
  43.9 1.9 collective-permute-done.2.got_ref
  45.9 1.3 shard_map.106
  47.1 0.0 all-gather.2.cloned.1.call-update
  47.2 0.0 copy-done
  47.2 0.2 fusion.mod_ref
  47.4 0.0 all-to-all-done
  47.4 1.8 shard_map.108
  49.3 0.0 copy-start.7
  49.3 6.8 %collective-permute-start.4 = (bf16[256,1536]{1,0:T(8,128)(2,1)S(1)}, bf16[256,1536]{1,0:T(8,128)(2,1)S(1)}, u32[]{:S(2)}, u32[]{:S(2)}) collective-permute-start(bf16[256,1536]{1,0:T(8,128)(2,1)S(1)} %get-tuple-element.20.own_hbm), channel_id=1, source_target_pairs={{0,16},{16,0},{1,17},{17,1},{2,18},{18,2},{3,19},{19,3},{4,20},{20... | collective-permute-start | bytes 2359304 | tf_op jit(solution)/shard_map/ppermute | solution.py:34
  56.1 3.7 %collective-permute-start.3 = (bf16[256,1536]{1,0:T(8,128)(2,1)S(1)}, bf16[256,1536]{1,0:T(8,128)(2,1)}, u32[]{:S(2)}, u32[]{:S(2)}) collective-permute-start(bf16[256,1536]{1,0:T(8,128)(2,1)S(1)} %get-tuple-element.21), channel_id=1, source_target_pairs={{0,8},{8,0},{1,9},{9,1},{2,10},{10,2},{3,11},{11,3},{4,12},{12,4},... | collective-permute-start | bytes 2359304 | tf_op jit(solution)/shard_map/ppermute | solution.py:34
  59.8 0.0 collective-permute-done.4.core_hbm
  59.8 0.0 copy-start.8
  59.8 18.0 %collective-permute-done.3.side_hbm = bf16[256,1536]{1,0:T(8,128)(2,1)} collective-permute-done((bf16[256,1536]{1,0:T(8,128)(2,1)S(1)}, bf16[256,1536]{1,0:T(8,128)(2,1)}, u32[]{:S(2)}, u32[]{:S(2)}) %collective-permute-start.3) | collective-permute-done | bytes 786464 | tf_op jit(solution)/shard_map/ppermute | solution.py:34
  77.8 2.5 %collective-permute-start.5 = (bf16[256,1536]{1,0:T(8,128)(2,1)}, bf16[256,1536]{1,0:T(8,128)(2,1)}, u32[]{:S(2)}, u32[]{:S(2)}) collective-permute-start(bf16[256,1536]{1,0:T(8,128)(2,1)} %collective-permute-done.3.side_hbm), channel_id=1, source_target_pairs={{0,16},{16,0},{1,17},{17,1},{2,18},{18,2},{3,19},{19,3},{4,20},{20... | collective-permute-start | bytes 2359304 | tf_op jit(solution)/shard_map/ppermute | solution.py:34
  80.3 14.5 %all-gather.2.cloned.1.call-done = bf16[1152,512]{1,0:T(8,128)(2,1)} async-done(((bf16[288,512]{1,0:T(8,128)(2,1)}), bf16[1152,512]{1,0:T(8,128)(2,1)}) %all-gather.2.cloned.1.call-update) | async-done | bytes 1179664 | tf_op jit(solution)/shard_map/all_gather | solution.py:332
  94.8 0.0 collective-permute-done.5.both_hbm
  94.8 0.0 copy-done.7
  94.8 0.0 copy-done.8
  94.8 12.4 %shard_map.109 = (bf16[128,32,128]{2,1,0:T(8,128)(2,1)}, bf16[512,1152]{1,0:T(8,128)(2,1)}, bf16[512,1152]{1,0:T(8,128)(2,1)}) custom-call(bf16[4,4,72,512]{3,2,1,0:T(8,128)(2,1)} %bitcast.24, bf16[256,1536]{1,0:T(8,128)(2,1)} %copy-done.7, bf16[256,1536]{1,0:T(8,128)(2,1)} %copy-done.8, bf16[256,1536]{1,0:T(8,128)(2,1)} %collective-permute-done.3.side_hbm, ...), custom_call_target="tpu_custom_call" | custom-call | flops 3057647616 | bytes 7733248 | tf_op jit(solution)/shard_map/pallas_call | solution.py:293
  107.2 14.6 %all-to-all-start.1 = ((bf16[128,32,128]{2,1,0:T(8,128)(2,1)}), bf16[128,32,128]{2,1,0:T(8,128)(2,1)S(1)}, u32[]{:S(2)}, u32[]{:S(2)}) async-start(bf16[128,32,128]{2,1,0:T(8,128)(2,1)} %get-tuple-element.24), calls=%async_computation.1 | async-start | bytes 2097152 | tf_op jit(solution)/shard_map/all_to_all | solution.py:370
  121.8 2.8 %collective-permute-start.6 = (bf16[512,1152]{1,0:T(8,128)(2,1)}, bf16[512,1152]{1,0:T(8,128)(2,1)S(1)}, u32[]{:S(2)}, u32[]{:S(2)}) collective-permute-start(bf16[512,1152]{1,0:T(8,128)(2,1)} %get-tuple-element.26), channel_id=1, source_target_pairs={{0,16},{16,0},{1,17},{17,1},{2,18},{18,2},{3,19},{19,3},{4,20},{20... | collective-permute-start | bytes 3538952 | tf_op jit(solution)/shard_map/ppermute | solution.py:34
  124.6 2.7 %collective-permute-done.6.got_ref = bf16[512,1152]{1,0:T(8,128)(2,1)S(1)} collective-permute-done((bf16[512,1152]{1,0:T(8,128)(2,1)}, bf16[512,1152]{1,0:T(8,128)(2,1)S(1)}, u32[]{:S(2)}, u32[]{:S(2)}) %collective-permute-start.6) | collective-permute-done | bytes 1179680 | tf_op jit(solution)/shard_map/ppermute | solution.py:34
  127.2 0.0 copy-start.1
  127.2 1.3 copy-done.1
  128.5 0.3 shard_map.110
  128.8 2.2 %collective-permute-start.7 = (bf16[256,1152]{1,0:T(8,128)(2,1)S(1)}, bf16[256,1152]{1,0:T(8,128)(2,1)S(1)}, u32[]{:S(2)}, u32[]{:S(2)}) collective-permute-start(bf16[256,1152]{1,0:T(8,128)(2,1)S(1)} %get-tuple-element.28), channel_id=1, source_target_pairs={{0,8},{8,0},{1,9},{9,1},{2,10},{10,2},{3,11},{11,3},{4,12},{12,4},... | collective-permute-start | bytes 1769480 | tf_op jit(solution)/shard_map/ppermute | solution.py:34
  131.0 21.5 %collective-permute-done.7.refs_1_ = bf16[256,1152]{1,0:T(8,128)(2,1)S(1)} collective-permute-done((bf16[256,1152]{1,0:T(8,128)(2,1)S(1)}, bf16[256,1152]{1,0:T(8,128)(2,1)S(1)}, u32[]{:S(2)}, u32[]{:S(2)}) %collective-permute-start.7) | collective-permute-done | bytes 589856 | tf_op jit(solution)/shard_map/ppermute | solution.py:34
  152.4 0.9 shard_map.111.back_ref
  153.3 0.0 all-to-all-done.1.parts_ref
  153.3 0.2 shard_map.112
  153.5 24.0 %all_to_all.15.pieces_ref = bf16[16,16,1408]{2,1,0:T(8,128)(2,1)S(1)} all-to-all(bf16[16,16,1408]{2,1,0:T(8,128)(2,1)S(1)} %bitcast.20), channel_id=1, replica_groups=mesh['xh'=2,'zh'=2,'zl'=4,'c'=2,'xl'=2,'y'=8] {'xl','y'}, dimensions={0} | all-to-all | bytes 1441792 | tf_op jit(solution)/shard_map/all_to_all | solution.py:372
  177.5 0.0 copy-start.5
  177.5 0.0 copy-start.6
  177.6 0.6 shard_map.113
  178.2 5.3 %collective-permute-start.8 = (f32[2,36,432]{2,1,0:T(8,128)S(1)}, f32[2,36,432]{2,1,0:T(8,128)S(1)}, u32[]{:S(2)}, u32[]{:S(2)}) collective-permute-start(f32[2,36,432]{2,1,0:T(8,128)S(1)} %get-tuple-element.30), channel_id=1, source_target_pairs={{0,16},{16,0},{1,17},{17,1},{2,18},{18,2},{3,19},{19,3},{4,20},{20... | collective-permute-start | bytes 373256 | tf_op jit(solution)/shard_map/ppermute | solution.py:34
  184.3 0.1 pad_maximum_fusion.decay_ref
  184.3 0.9 slice.4
  185.2 0.0 collective-permute-done.8.core_ref
  185.2 0.0 copy-done.5
  185.2 0.0 copy-done.6
  185.2 1.5 shard_map.114
Async XLA Ops:
  7.2 40.0 %copy-start = (bf16[128,2304]{1,0:T(8,128)(2,1)S(1)}, bf16[128,2304]{1,0:T(8,128)(2,1)}, u32[]{:S(2)}) copy-start(bf16[128,2304]{1,0:T(8,128)(2,1)} %param.10) | copy-start | bytes 1769476
  7.2 1.1 copy-start.2
  8.3 1.0 copy-start.3
  10.3 9.0 %copy-start.4 = (f32[36,1728]{1,0:T(8,128)S(1)}, f32[36,1728]{1,0:T(8,128)}, u32[]{:S(2)}) copy-start(f32[36,1728]{1,0:T(8,128)} %master_ref.1) | copy-start | bytes 746500
  10.3 37.1 %all-to-all-start = ((bf16[16,16,1728]{2,1,0:T(8,128)(2,1)}), bf16[16,16,1728]{2,1,0:T(8,128)(2,1)S(1)}, u32[]{:S(2)}, u32[]{:S(2)}) async-start(bf16[16,16,1728]{2,1,0:T(8,128)(2,1)} %bitcast.8), calls=%async_computation | async-start | bytes 1835008 | tf_op jit(solution)/shard_map/all_to_all | solution.py:324
  19.2 75.6 %all-gather.2.cloned.1.call-start = ((), (), s32[]{:S(2)}) async-start(), calls=%async_computation.3 | async-start | bytes 1474560 | tf_op jit(solution)/shard_map/all_gather | solution.py:332
  20.2 4.6 %collective-permute-start = (bf16[36,432]{1,0:T(8,128)(2,1)S(1)}, bf16[36,432]{1,0:T(8,128)(2,1)S(1)}, u32[]{:S(2)}, u32[]{:S(2)}) collective-permute-start(bf16[36,432]{1,0:T(8,128)(2,1)S(1)} %get-tuple-element.19), channel_id=1, source_target_pairs={{0,16},{16,0},{1,17},{17,1},{2,18},{18,2},{3,19},{19,3},{4,20},{20... | collective-permute-start | bytes 93320 | tf_op jit(solution)/shard_map/ppermute | solution.py:34
  25.3 8.0 %collective-permute-start.1 = (bf16[72,512]{1,0:T(8,128)(2,1)S(1)}, bf16[72,512]{1,0:T(8,128)(2,1)S(1)}, u32[]{:S(2)}, u32[]{:S(2)}) collective-permute-start(bf16[72,512]{1,0:T(8,128)(2,1)S(1)} %shard_map.104.own_ref), channel_id=1, source_target_pairs={{0,256},{256,0},{1,257},{257,1},{2,258},{258,2},{3,259},{259,3},{4... | collective-permute-start | bytes 221192 | tf_op jit(solution)/shard_map/ppermute | solution.py:34
  33.9 12.0 %collective-permute-start.2 = (bf16[2,72,512]{2,1,0:T(8,128)(2,1)S(1)}, bf16[2,72,512]{2,1,0:T(8,128)(2,1)S(1)}, u32[]{:S(2)}, u32[]{:S(2)}) collective-permute-start(bf16[2,72,512]{2,1,0:T(8,128)(2,1)S(1)} %shard_map.105.own_ref), channel_id=1, source_target_pairs={{0,128},{128,0},{1,129},{129,1},{2,130},{130,2},{3,131},{131,3},{4... | collective-permute-start | bytes 442376 | tf_op jit(solution)/shard_map/ppermute | solution.py:34
  49.3 45.5 %copy-start.7 = (bf16[256,1536]{1,0:T(8,128)(2,1)}, bf16[256,1536]{1,0:T(8,128)(2,1)S(1)}, u32[]{:S(2)}) copy-start(bf16[256,1536]{1,0:T(8,128)(2,1)S(1)} %get-tuple-element.20.own_hbm) | copy-start | bytes 2359300
  49.3 10.5 %collective-permute-start.4 = (bf16[256,1536]{1,0:T(8,128)(2,1)S(1)}, bf16[256,1536]{1,0:T(8,128)(2,1)S(1)}, u32[]{:S(2)}, u32[]{:S(2)}) collective-permute-start(bf16[256,1536]{1,0:T(8,128)(2,1)S(1)} %get-tuple-element.20.own_hbm), channel_id=1, source_target_pairs={{0,16},{16,0},{1,17},{17,1},{2,18},{18,2},{3,19},{19,3},{4,20},{20... | collective-permute-start | bytes 2359304 | tf_op jit(solution)/shard_map/ppermute | solution.py:34
  56.1 21.7 %collective-permute-start.3 = (bf16[256,1536]{1,0:T(8,128)(2,1)S(1)}, bf16[256,1536]{1,0:T(8,128)(2,1)}, u32[]{:S(2)}, u32[]{:S(2)}) collective-permute-start(bf16[256,1536]{1,0:T(8,128)(2,1)S(1)} %get-tuple-element.21), channel_id=1, source_target_pairs={{0,8},{8,0},{1,9},{9,1},{2,10},{10,2},{3,11},{11,3},{4,12},{12,4},... | collective-permute-start | bytes 2359304 | tf_op jit(solution)/shard_map/ppermute | solution.py:34
  59.8 35.0 %copy-start.8 = (bf16[256,1536]{1,0:T(8,128)(2,1)}, bf16[256,1536]{1,0:T(8,128)(2,1)S(1)}, u32[]{:S(2)}) copy-start(bf16[256,1536]{1,0:T(8,128)(2,1)S(1)} %collective-permute-done.4.core_hbm) | copy-start | bytes 2359300
  77.8 17.0 %collective-permute-start.5 = (bf16[256,1536]{1,0:T(8,128)(2,1)}, bf16[256,1536]{1,0:T(8,128)(2,1)}, u32[]{:S(2)}, u32[]{:S(2)}) collective-permute-start(bf16[256,1536]{1,0:T(8,128)(2,1)} %collective-permute-done.3.side_hbm), channel_id=1, source_target_pairs={{0,16},{16,0},{1,17},{17,1},{2,18},{18,2},{3,19},{19,3},{4,20},{20... | collective-permute-start | bytes 2359304 | tf_op jit(solution)/shard_map/ppermute | solution.py:34
  107.2 46.1 %all-to-all-start.1 = ((bf16[128,32,128]{2,1,0:T(8,128)(2,1)}), bf16[128,32,128]{2,1,0:T(8,128)(2,1)S(1)}, u32[]{:S(2)}, u32[]{:S(2)}) async-start(bf16[128,32,128]{2,1,0:T(8,128)(2,1)} %get-tuple-element.24), calls=%async_computation.1 | async-start | bytes 2097152 | tf_op jit(solution)/shard_map/all_to_all | solution.py:370
  121.8 5.5 %collective-permute-start.6 = (bf16[512,1152]{1,0:T(8,128)(2,1)}, bf16[512,1152]{1,0:T(8,128)(2,1)S(1)}, u32[]{:S(2)}, u32[]{:S(2)}) collective-permute-start(bf16[512,1152]{1,0:T(8,128)(2,1)} %get-tuple-element.26), channel_id=1, source_target_pairs={{0,16},{16,0},{1,17},{17,1},{2,18},{18,2},{3,19},{19,3},{4,20},{20... | collective-permute-start | bytes 3538952 | tf_op jit(solution)/shard_map/ppermute | solution.py:34
  127.2 1.3 copy-start.1
  128.8 23.7 %collective-permute-start.7 = (bf16[256,1152]{1,0:T(8,128)(2,1)S(1)}, bf16[256,1152]{1,0:T(8,128)(2,1)S(1)}, u32[]{:S(2)}, u32[]{:S(2)}) collective-permute-start(bf16[256,1152]{1,0:T(8,128)(2,1)S(1)} %get-tuple-element.28), channel_id=1, source_target_pairs={{0,8},{8,0},{1,9},{9,1},{2,10},{10,2},{3,11},{11,3},{4,12},{12,4},... | collective-permute-start | bytes 1769480 | tf_op jit(solution)/shard_map/ppermute | solution.py:34
  177.5 7.7 %copy-start.5 = (f32[36,1728]{1,0:T(8,128)S(1)}, f32[36,1728]{1,0:T(8,128)}, u32[]{:S(2)}) copy-start(f32[36,1728]{1,0:T(8,128)} %slow_ref.1) | copy-start | bytes 746500
  177.5 7.7 %copy-start.6 = (f32[36,1728]{1,0:T(8,128)S(1)}, f32[36,1728]{1,0:T(8,128)}, u32[]{:S(2)}) copy-start(f32[36,1728]{1,0:T(8,128)} %fast_ref.1) | copy-start | bytes 746500
  178.2 7.0 %collective-permute-start.8 = (f32[2,36,432]{2,1,0:T(8,128)S(1)}, f32[2,36,432]{2,1,0:T(8,128)S(1)}, u32[]{:S(2)}, u32[]{:S(2)}) collective-permute-start(f32[2,36,432]{2,1,0:T(8,128)S(1)} %get-tuple-element.30), channel_id=1, source_target_pairs={{0,16},{16,0},{1,17},{17,1},{2,18},{18,2},{3,19},{19,3},{4,20},{20... | collective-permute-start | bytes 373256 | tf_op jit(solution)/shard_map/ppermute | solution.py:34
Sparse Core Ops, SparseCore 0:
  47.3 47.4 all-gather.1

commit v6 on v4

--- a/solution.py
+++ b/solution.py
@@ -57,10 +57,19 @@
     return jnp.dot(embedding, ada_weight, preferred_element_type=F32)
 
 
-def pack_kernel(hidden_ref, cot_ref, out_ref):
-    width = hidden_ref.shape[1]
-    out_ref[:, :width] = hidden_ref[...]
-    out_ref[:, width:] = cot_ref[...].T
+def pack_kernel(hidden_hbm, cot_hbm, out_hbm, cot_ref, turned_ref, sems):
+    width = hidden_hbm.shape[1]
+    whole = pltpu.make_async_copy(hidden_hbm, out_hbm.at[:, pl.ds(0, width)], sems.at[0])
+    whole.start()
+    load = pltpu.make_async_copy(cot_hbm, cot_ref, sems.at[1])
+    load.start()
+    load.wait()
+    inner = cot_ref.shape[0]
+    turned_ref[:, :inner] = cot_ref[...].T
+    store = pltpu.make_async_copy(turned_ref, out_hbm.at[:, pl.ds(width, turned_ref.shape[1])], sems.at[2])
+    store.start()
+    store.wait()
+    whole.wait()
 
 
 def stats(values):
@@ -78,24 +87,19 @@
     return out
 
 
-def norm_kernel(spot_ref, packed_ref, mod_ref, own_ref, core_ref, side_ref, held_ref, sem):
+def norm_kernel(spot_ref, packed_ref, mod_ref, core_ref, side_ref):
     width = mod_ref.shape[1] // 2
-    quarter = (packed_ref.shape[1] - width) // 4
+    quarter = width // 8
     centered, _ = stats(packed_ref[:, :width].astype(F32))
     normed = (centered * (1.0 + mod_ref[:, width:]) + mod_ref[:, :width]).astype(BF16)
-    cot = packed_ref[:, width:].astype(F32)
+    cot = packed_ref[:, width : width + 4 * quarter].astype(F32)
     pieces = [cot[:, i * quarter : (i + 1) * quarter] for i in range(4)]
     spot = spot_ref[0]
     own, side, core, both = (pick(spot, [pieces[i ^ flip] for i in range(4)]) for flip in range(4))
-    held_ref[:, :width] = normed
-    held_ref[:, width : width + quarter] = own.astype(BF16)
-    copy = pltpu.make_async_copy(held_ref, own_ref, sem)
-    copy.start()
-    core_ref[:, :width] = normed
-    core_ref[:, width : width + quarter] = core.astype(BF16)
     side_ref[:, :width] = normed
     side_ref[:, width : width + 2 * quarter] = jnp.concatenate([side, both], axis=1).astype(BF16)
-    copy.wait()
+    core_ref[:, :width] = normed
+    core_ref[:, width : width + 2 * quarter] = jnp.concatenate([core, own], axis=1).astype(BF16)
 
 
 def norm_back_kernel(packed_ref, mod_ref, *refs):
@@ -172,15 +176,22 @@
 
 
 def main_kernel(
-    weight_hbm, own_hbm, core_hbm, side_hbm, both_hbm, packed_hbm, near_hbm, far_hbm,
-    weight_ref, own_ref, core_ref, side_ref, both_ref, packed_ref, parts_ref, total_ref, in_sems, out_sems,
+    spot_ref, near_hbm, up_hbm, low_hbm, high_hbm, down_hbm, own_hbm, core_hbm, side_hbm, both_hbm, packed_hbm, inner_hbm, outer_hbm,
+    raw_ref, own_ref, core_ref, side_ref, both_ref, weight_ref, packed_ref, parts_ref, total_ref, in_sems, out_sems,
 ):
     tokens = own_ref.shape[0]
     model_width, cols = total_ref.shape
     quarter = cols // 3
+    lows = [lax.rem(spot_ref[1] + ahead, 4) for ahead in range(4)]
+    half = raw_ref.shape[1] // 2
+    tokens_in = ((own_hbm, own_ref), (core_hbm, core_ref), (side_hbm, side_ref), (both_hbm, both_ref))
     pairs = (
-        (weight_hbm, weight_ref), (own_hbm, own_ref), (core_hbm, core_ref), (side_hbm, side_ref), (both_hbm, both_ref),
-    )
+        (near_hbm, raw_ref.at[lows[0]]),
+        (up_hbm, raw_ref.at[lows[1]]),
+        (low_hbm, raw_ref.at[lows[2], pl.ds(0, half)]),
+        (high_hbm, raw_ref.at[lows[2], pl.ds(half, half)]),
+        (down_hbm, raw_ref.at[lows[3]]),
+    ) + tokens_in
     loads = [pltpu.make_async_copy(source, target, in_sems.at[i]) for i, (source, target) in enumerate(pairs)]
     for load in loads:
         load.start()
@@ -189,11 +200,14 @@
     same = lax.rem(row, 16) == lax.rem(col, 16)
     lane = lax.broadcasted_iota(jnp.int32, (tokens, quarter), 1)
     stores = []
-    loads[0].wait()
-    places = ((near_hbm, 0, 0), (far_hbm, 0, 0), (near_hbm, 1, 0), (far_hbm, 1, 1))
+    for load in loads[:5]:
+        load.wait()
+    blocks = [raw_ref[low, group].astype(F32) for group in range(4) for low in range(4)]
+    weight_ref[...] = jnp.concatenate(blocks, axis=0).astype(BF16)
+    places = ((inner_hbm, 0, 1), (outer_hbm, 0, 0), (inner_hbm, 1, 0), (outer_hbm, 1, 1))
     for index, (target, place, skip) in enumerate(places):
-        ref = pairs[index + 1][1]
-        loads[index + 1].wait()
+        ref = tokens_in[index][1]
+        loads[index + 5].wait()
         projected = dot(ref[:, :model_width], weight_ref[...], ((1,), (0,)))
         projected = projected.astype(BF16).astype(F32)
         cot = ref[:, model_width:].astype(F32)
@@ -258,15 +272,6 @@
     out_ref[3 - place] = both_ref[...]
 
 
-def gather_kernel(spot_ref, near_ref, up_ref, low_ref, high_ref, down_ref, out_ref):
-    place = spot_ref[1]
-    for ahead, sources in enumerate(((near_ref,), (up_ref,), (low_ref, high_ref), (down_ref,))):
-        lowest = lax.rem(place + ahead, 4)
-        for group in range(4):
-            ref = sources[group * len(sources) // 4]
-            out_ref[4 * group + lowest] = ref[group % ref.shape[0]]
-
-
 def payload_kernel(parts_ref, back_ref, out_ref):
     total = parts_ref[0].astype(F32)
     for index in range(1, parts_ref.shape[0]):
@@ -332,7 +337,6 @@
     patches, width = hidden.shape[2:]
     inner = cotangent.shape[3]
     own_rows, triple = master.shape
-    wide = width + inner
     n_seq = lax.axis_size("xl") * lax.axis_size("y")
     n_rows = lax.axis_size("xh") * lax.axis_size("z")
     n_y = lax.axis_size("y")
@@ -343,9 +347,18 @@
     across, along = lax.axis_index("xh"), lax.axis_index("z")
     spots = jnp.stack([2 * core + side, lax.rem(along, 4), 2 * across + along // 4]).astype(jnp.int32)
 
-    packed = call(pack_kernel, [((patches, wide), BF16)], hidden[0, 0], cotangent[0, 0].T)
-    tokens = lax.all_to_all(packed.reshape(n_seq, patches // n_seq, wide), SEQ, 0, 0, tiled=True)
-    tokens = tokens.reshape(patches, wide)
+    loose = lanes(inner)
+    packed = call(
+        pack_kernel,
+        [((patches, width + loose), BF16)],
+        hidden[0, 0], cotangent[0, 0].T,
+        scratch=[pltpu.VMEM((inner, patches), BF16), pltpu.VMEM((patches, loose), BF16), pltpu.SemaphoreType.DMA((3,))],
+        mib=58,
+        hbm_in=True,
+        hbm_out=(0,),
+    )
+    tokens = lax.all_to_all(packed.reshape(n_seq, patches // n_seq, width + loose), SEQ, 0, 0, tiled=True)
+    tokens = tokens.reshape(patches, width + loose)
 
     mine, theirs = call(columns_kernel, [((own_rows, cols), BF16)] * 2, spots, master, smem=1)
     pair = call(pair_kernel, [((pair_rows, cols), BF16)], spots, mine, swap(theirs, "c"), smem=1)
@@ -358,43 +371,36 @@
     quad, tokens = lax.optimization_barrier((quad, tokens))
 
     modulation = modulate_table(timesteps, ada_weight)
-    narrow, broad = lanes(width + quarter), lanes(width + 2 * quarter)
-    own, to_core, to_side = call(
-        norm_kernel,
-        [((patches, narrow), BF16), ((patches, narrow), BF16), ((patches, broad), BF16)],
-        spots, tokens, modulation,
-        scratch=[pltpu.VMEM((patches, narrow), BF16), pltpu.SemaphoreType.DMA(())],
-        smem=1,
-        hbm_out=(0,),
-    )
+    broad = lanes(width + 2 * quarter)
+    to_core, to_side = call(norm_kernel, [((patches, broad), BF16)] * 2, spots, tokens, modulation, smem=1)
     from_side = swap(to_side, "xl")
+    up, low, high, down = shift(quad, -1), shift(quad[:2], -2), shift(quad[2:], 2), shift(quad, 1)
+    to_core, low = lax.optimization_barrier((to_core, low))
     from_core = swap(to_core, "c")
-    up, low, high, down = shift(quad, -1), shift(quad[:2], -2), shift(quad[2:], 2), shift(quad, 1)
-    from_side, from_core, up, low, high, down = lax.optimization_barrier((from_side, from_core, up, low, high, down))
+    from_side, up, low, high, down = lax.optimization_barrier((from_side, up, low, high, down))
     from_both = swap(from_side, "c")
-    weights = call(
-        gather_kernel, [((16, pair_rows, cols), BF16)], spots, quad, up, low, high, down, smem=1
-    ).reshape(width, cols)
 
     pieces = n_rows * n_y
     packed, near, far = call(
         main_kernel,
         [((pieces, 32, 128), BF16), ((2 * patches, width), BF16), ((2 * patches, width), BF16)],
-        weights, own, from_core, from_side, from_both,
+        spots, quad, up, low, high, down, to_core, from_core, from_side, from_both,
         flops=6 * 4 * patches * width * cols,
         scratch=[
-            pltpu.VMEM((width, cols), BF16),
-            pltpu.VMEM((patches, narrow), BF16),
-            pltpu.VMEM((patches, narrow), BF16),
+            pltpu.VMEM((4, 4, pair_rows, cols), BF16),
             pltpu.VMEM((patches, broad), BF16),
             pltpu.VMEM((patches, broad), BF16),
+            pltpu.VMEM((patches, broad), BF16),
+            pltpu.VMEM((patches, broad), BF16),
+            pltpu.VMEM((width, cols), BF16),
             pltpu.VMEM((pieces, 32, 128), BF16),
             pltpu.VMEM((4, patches, width), BF16),
             pltpu.VMEM((width, cols), F32),
-            pltpu.SemaphoreType.DMA((5,)),
+            pltpu.SemaphoreType.DMA((9,)),
             pltpu.SemaphoreType.DMA((8,)),
         ],
         mib=58,
+        smem=1,
         hbm_in=True,
         hbm_out=(0, 1, 2),
     )
@@ -419,7 +425,7 @@
 
 def solution(mesh):
     fine = Mesh(mesh.devices.reshape(2, 8, 2, 2, 8), AXES)
-    dp, seq = ("xh", "z", "c"), SEQ
+    dp, seq = ROWS + ("c",), SEQ
     placed = (
         P(dp, seq, None, None),
         P(dp),

time: 177 us -> 187 us (1.056)
  Pallas kernels: 21.8 us -> 39.4 us
  waiting for transfers between devices: 44.2 us -> 39 us
  local copies, waits for them, and re-layouts: 7.05 us -> 3.11 us
    pallas_call x12 -> x11, Pallas kernels: 21.8 us -> 39.4 us  [call(): pl.pallas_call(kernel, out_shape=shapes, in_specs=specs, out_specs=[pl.Bl...]
    ppermute x5, waiting for transfers between devices: 10.2 us -> 3.43 us  [shift(): lax.ppermute(value, 'z', [(i, (i + away) % count) for i in range(count)])]
    unnamed x24 -> x32, local copies, waits for them, and re-layouts: 6.17 us -> 2.23 us
    ppermute x5, starting transfers between devices: 19.8 us -> 22.3 us  [shift(): lax.ppermute(value, 'z', [(i, (i + away) % count) for i in range(count)])]
  transfers between devices with their start and end apart: 16 -> 16, of which waited for: 8 -> 7; matrix products, arithmetic and copies ran while one was open for 1% -> 1% of each run, Pallas kernels for 2% -> 2%
where the time goes in v6:
time: 187 us; the launch traced here: 186 us
  starting transfers between devices  77.2 us (41%)
  Pallas kernels  39.4 us (21%)
  waiting for transfers between devices  39 us (21%)
  blocking collectives  24.5 us (13%)
  local copies, waits for them, and re-layouts  3.11 us (2%)
  between operations  2.49 us (1%)
    pallas_call x11, Pallas kernels, call(): pl.pallas_call(kernel, out_shape=shapes, in_specs=specs, out_specs=[pl.Bl...  39.4 us
    ppermute x8, starting transfers between devices, swap(): return lax.ppermute(value, axis, [(0, 1), (1, 0)])  29.7 us
    ppermute x8, waiting for transfers between devices, swap(): return lax.ppermute(value, axis, [(0, 1), (1, 0)])  27 us
    all_to_all x1, blocking collectives, on_device(): lax.all_to_all(joint.reshape(n_seq, patches // n_seq, width + 256), SEQ,...  24.5 us
    ppermute x5, starting transfers between devices, shift(): lax.ppermute(value, 'z', [(i, (i + away) % count) for i in range(count)])  22.3 us
    all_to_all x1, starting transfers between devices, on_device(): parts = lax.all_to_all(packed, ROWS + ('y',), 0, 0, tiled=True)  14.3 us
    all_to_all x1, starting transfers between devices, on_device(): lax.all_to_all(packed.reshape(n_seq, patches // n_seq, width + loose), SE...  8.83 us
    ppermute x1, waiting for transfers between devices, both_turn(): return lax.ppermute(value, ('xh', 'z'), pairs)  8.6 us
  transfers between devices with their start and end apart: 16, of which 7 were waited for; matrix products, arithmetic and copies ran while one was open for 1% of the time, Pallas kernels for 2%

profile of v6, /device:TPU:1, one launch (start us, length us, event | category | flops | bytes accessed | tf_op | source)
XLA Modules:
  0.0 186.2 jit_solution(3426161300688864760)
XLA Ops:
  0.6 0.0 copy-start
  0.6 19.0 %shard_map.106 = bf16[256,1792]{1,0:T(8,128)(2,1)} custom-call(bf16[256,1152]{1,0:T(8,128)(2,1)} %bitcast.20, bf16[576,256]{1,0:T(8,128)(2,1)} %bitcast.22), custom_call_target="tpu_custom_call" | custom-call | bytes 1802240 | tf_op jit(solution)/shard_map/pallas_call | solution.py:320
  19.6 0.0 copy-start.3
  19.7 8.8 %all-to-all-start = ((bf16[16,16,1792]{2,1,0:T(8,128)(2,1)}), bf16[16,16,1792]{2,1,0:T(8,128)(2,1)S(1)}, u32[]{:S(2)}, u32[]{:S(2)}) async-start(bf16[16,16,1792]{2,1,0:T(8,128)(2,1)} %bitcast.19), calls=%async_computation | async-start | bytes 1835008 | tf_op jit(solution)/shard_map/all_to_all | solution.py:360
  28.5 0.1 pad_add_fusion.spot_ref
  28.6 0.0 copy-done.3
  28.6 0.9 shard_map.103
  29.5 3.7 %collective-permute-start = (bf16[36,432]{1,0:T(8,128)(2,1)S(1)}, bf16[36,432]{1,0:T(8,128)(2,1)S(1)}, u32[]{:S(2)}, u32[]{:S(2)}) collective-permute-start(bf16[36,432]{1,0:T(8,128)(2,1)S(1)} %get-tuple-element.26), channel_id=1, source_target_pairs={{0,16},{16,0},{1,17},{17,1},{2,18},{18,2},{3,19},{19,3},{4,20},{20... | collective-permute-start | bytes 93320 | tf_op jit(solution)/shard_map/ppermute | solution.py:34
  33.9 0.1 sine_convert_fusion
  33.9 0.1 collective-permute-done.theirs_ref
  34.1 0.6 shard_map.104.own_ref
  34.6 9.8 %collective-permute-start.1 = (bf16[72,432]{1,0:T(8,128)(2,1)S(1)}, bf16[72,432]{1,0:T(8,128)(2,1)S(1)}, u32[]{:S(2)}, u32[]{:S(2)}) collective-permute-start(bf16[72,432]{1,0:T(8,128)(2,1)S(1)} %shard_map.104.own_ref), channel_id=1, source_target_pairs={{0,128},{32,160},{64,192},{96,224},{128,0},{160,32},{192,64},{224,... | collective-permute-start | bytes 186632 | tf_op jit(solution)/shard_map/ppermute | solution.py:39
  44.4 4.4 %collective-permute-start.2 = (bf16[72,432]{1,0:T(8,128)(2,1)S(1)}, bf16[72,432]{1,0:T(8,128)(2,1)S(1)}, u32[]{:S(2)}, u32[]{:S(2)}) collective-permute-start(bf16[72,432]{1,0:T(8,128)(2,1)S(1)} %shard_map.104.own_ref), channel_id=1, source_target_pairs={{0,256},{256,0},{1,257},{257,1},{2,258},{258,2},{3,259},{259,3},{4... | collective-permute-start | bytes 186632 | tf_op jit(solution)/shard_map/ppermute | solution.py:34
  48.8 2.2 %collective-permute-start.3 = (bf16[72,432]{1,0:T(8,128)(2,1)S(1)}, bf16[72,432]{1,0:T(8,128)(2,1)S(1)}, u32[]{:S(2)}, u32[]{:S(2)}) collective-permute-start(bf16[72,432]{1,0:T(8,128)(2,1)S(1)} %shard_map.104.own_ref), channel_id=1, source_target_pairs={{0,384},{32,416},{64,448},{96,480},{128,256},{160,288},{192,320},{... | collective-permute-start | bytes 186632 | tf_op jit(solution)/shard_map/ppermute | solution.py:49
  50.9 0.0 copy-done
  50.9 0.2 fusion.mod_ref
  51.2 0.0 collective-permute-done.1.far_ref
  51.2 0.7 collective-permute-done.2.across_ref
  51.9 8.6 %collective-permute-done.3.both_ref = bf16[72,432]{1,0:T(8,128)(2,1)S(1)} collective-permute-done((bf16[72,432]{1,0:T(8,128)(2,1)S(1)}, bf16[72,432]{1,0:T(8,128)(2,1)S(1)}, u32[]{:S(2)}, u32[]{:S(2)}) %collective-permute-start.3) | collective-permute-done | bytes 62240 | tf_op jit(solution)/shard_map/ppermute | solution.py:49
  60.5 0.6 shard_map.105.near_hbm
  61.0 0.0 copy-start.2
  61.0 0.0 all-to-all-done
  61.0 1.8 shard_map.107
  62.9 0.0 copy-done.6
  62.9 0.0 copy-start.8
  62.9 2.9 %collective-permute-start.4 = (bf16[256,1536]{1,0:T(8,128)(2,1)S(1)}, bf16[256,1536]{1,0:T(8,128)(2,1)S(1)}, u32[]{:S(2)}, u32[]{:S(2)}) collective-permute-start(bf16[256,1536]{1,0:T(8,128)(2,1)S(1)} %get-tuple-element.29), channel_id=1, source_target_pairs={{0,8},{8,0},{1,9},{9,1},{2,10},{10,2},{3,11},{11,3},{4,12},{12,4},... | collective-permute-start | bytes 2359304 | tf_op jit(solution)/shard_map/ppermute | solution.py:34
  65.8 1.9 %collective-permute-start.5 = (bf16[4,72,432]{2,1,0:T(8,128)(2,1)S(1)}, bf16[4,72,432]{2,1,0:T(8,128)(2,1)S(1)}, u32[]{:S(2)}, u32[]{:S(2)}) collective-permute-start(bf16[4,72,432]{2,1,0:T(8,128)(2,1)S(1)} %shard_map.105.near_hbm), channel_id=1, source_target_pairs={{0,224},{32,0},{64,32},{96,64},{128,96},{160,128},{192,160},{224,1... | collective-permute-start | bytes 746504 | tf_op jit(solution)/shard_map/ppermute | solution.py:39
  67.8 3.4 %collective-permute-start.8 = (bf16[4,72,432]{2,1,0:T(8,128)(2,1)S(1)}, bf16[4,72,432]{2,1,0:T(8,128)(2,1)S(1)}, u32[]{:S(2)}, u32[]{:S(2)}) collective-permute-start(bf16[4,72,432]{2,1,0:T(8,128)(2,1)S(1)} %shard_map.105.near_hbm), channel_id=1, source_target_pairs={{0,32},{32,64},{64,96},{96,128},{128,160},{160,192},{192,224},{224... | collective-permute-start | bytes 746504 | tf_op jit(solution)/shard_map/ppermute | solution.py:39
  71.2 4.3 %collective-permute-start.6 = (bf16[2,72,432]{2,1,0:T(8,128)(2,1)S(1)}, bf16[2,72,432]{2,1,0:T(8,128)(2,1)S(1)}, u32[]{:S(2)}, u32[]{:S(2)}) collective-permute-start(bf16[2,72,432]{2,1,0:T(8,128)(2,1)S(1)} %get-tuple-element.48), channel_id=1, source_target_pairs={{0,192},{32,224},{64,0},{96,32},{128,64},{160,96},{192,128},{224,1... | collective-permute-start | bytes 373256 | tf_op jit(solution)/shard_map/ppermute | solution.py:39
  75.5 2.9 %collective-permute-start.7 = (bf16[2,72,432]{2,1,0:T(8,128)(2,1)S(1)}, bf16[2,72,432]{2,1,0:T(8,128)(2,1)S(1)}, u32[]{:S(2)}, u32[]{:S(2)}) collective-permute-start(bf16[2,72,432]{2,1,0:T(8,128)(2,1)S(1)} %get-tuple-element.47), channel_id=1, source_target_pairs={{0,64},{32,96},{64,128},{96,160},{128,192},{160,224},{192,0},{224,... | collective-permute-start | bytes 373256 | tf_op jit(solution)/shard_map/ppermute | solution.py:39
  78.4 3.4 %collective-permute-done.6.low_hbm = bf16[2,72,432]{2,1,0:T(8,128)(2,1)S(1)} collective-permute-done((bf16[2,72,432]{2,1,0:T(8,128)(2,1)S(1)}, bf16[2,72,432]{2,1,0:T(8,128)(2,1)S(1)}, u32[]{:S(2)}, u32[]{:S(2)}) %collective-permute-start.6) | collective-permute-done | bytes 124448 | tf_op jit(solution)/shard_map/ppermute | solution.py:39
  81.8 5.1 %collective-permute-start.9 = (bf16[256,1536]{1,0:T(8,128)(2,1)S(1)}, bf16[256,1536]{1,0:T(8,128)(2,1)S(1)}, u32[]{:S(2)}, u32[]{:S(2)}) collective-permute-start(bf16[256,1536]{1,0:T(8,128)(2,1)S(1)} %get-tuple-element.36.own_hbm), channel_id=1, source_target_pairs={{0,16},{16,0},{1,17},{17,1},{2,18},{18,2},{3,19},{19,3},{4,20},{20... | collective-permute-start | bytes 2359304 | tf_op jit(solution)/shard_map/ppermute | solution.py:34
  86.9 0.0 collective-permute-done.7.high_hbm
  86.9 0.0 copy-start.15
  86.9 0.0 collective-permute-done.5.up_hbm
  86.9 0.0 copy-start.12
  86.9 0.0 collective-permute-done.8.down_hbm
  87.0 0.0 copy-start.13
  87.0 0.0 collective-permute-done.4.side_hbm
  87.0 0.0 copy-start.9
  87.0 4.1 %collective-permute-start.10 = (bf16[256,1536]{1,0:T(8,128)(2,1)S(1)}, bf16[256,1536]{1,0:T(8,128)(2,1)S(1)}, u32[]{:S(2)}, u32[]{:S(2)}) collective-permute-start(bf16[256,1536]{1,0:T(8,128)(2,1)S(1)} %collective-permute-done.4.side_hbm), channel_id=1, source_target_pairs={{0,16},{16,0},{1,17},{17,1},{2,18},{18,2},{3,19},{19,3},{4,20},{20... | collective-permute-start | bytes 2359304 | tf_op jit(solution)/shard_map/ppermute | solution.py:34
  91.1 0.0 collective-permute-done.9.core_hbm
  91.2 1.9 collective-permute-done.10.both_hbm
  93.0 0.0 copy-done.14
  93.1 0.9 copy-done.11
  94.0 13.0 %shard_map.108 = (bf16[128,32,128]{2,1,0:T(8,128)(2,1)}, bf16[512,1152]{1,0:T(8,128)(2,1)}, bf16[512,1152]{1,0:T(8,128)(2,1)}) custom-call(s32[3]{0:T(128)} %copy-done.6, bf16[4,72,432]{2,1,0:T(8,128)(2,1)} %copy-done.2, bf16[4,72,432]{2,1,0:T(8,128)(2,1)} %copy-done.12, bf16[2,72,432]{2,1,0:T(8,128)(2,1)} %copy-done.14, bf16[2,72,432]{2,1,0:T(8,128)(2,1)} %copy-done.15, ...), custom_call_target="tpu_custom_call" | custom-call | flops 3057647616 | bytes 7548940 | tf_op jit(solution)/shard_map/pallas_call | solution.py:320
  107.0 14.3 %all-to-all-start.1 = ((bf16[128,32,128]{2,1,0:T(8,128)(2,1)}), bf16[128,32,128]{2,1,0:T(8,128)(2,1)S(1)}, u32[]{:S(2)}, u32[]{:S(2)}) async-start(bf16[128,32,128]{2,1,0:T(8,128)(2,1)} %get-tuple-element.38), calls=%async_computation.1 | async-start | bytes 2097152 | tf_op jit(solution)/shard_map/all_to_all | solution.py:411
  121.3 2.6 %collective-permute-start.11 = (bf16[512,1152]{1,0:T(8,128)(2,1)}, bf16[512,1152]{1,0:T(8,128)(2,1)S(1)}, u32[]{:S(2)}, u32[]{:S(2)}) collective-permute-start(bf16[512,1152]{1,0:T(8,128)(2,1)} %get-tuple-element.40), channel_id=1, source_target_pairs={{0,16},{16,0},{1,17},{17,1},{2,18},{18,2},{3,19},{19,3},{4,20},{20... | collective-permute-start | bytes 3538952 | tf_op jit(solution)/shard_map/ppermute | solution.py:34
  123.9 2.7 %collective-permute-done.11.got_ref = bf16[512,1152]{1,0:T(8,128)(2,1)S(1)} collective-permute-done((bf16[512,1152]{1,0:T(8,128)(2,1)}, bf16[512,1152]{1,0:T(8,128)(2,1)S(1)}, u32[]{:S(2)}, u32[]{:S(2)}) %collective-permute-start.11) | collective-permute-done | bytes 1179680 | tf_op jit(solution)/shard_map/ppermute | solution.py:34
  126.5 1.3 copy-done.1
  127.8 0.3 shard_map.109
  128.1 1.9 %collective-permute-start.12 = (bf16[256,1152]{1,0:T(8,128)(2,1)S(1)}, bf16[256,1152]{1,0:T(8,128)(2,1)S(1)}, u32[]{:S(2)}, u32[]{:S(2)}) collective-permute-start(bf16[256,1152]{1,0:T(8,128)(2,1)S(1)} %get-tuple-element.42), channel_id=1, source_target_pairs={{0,8},{8,0},{1,9},{9,1},{2,10},{10,2},{3,11},{11,3},{4,12},{12,4},... | collective-permute-start | bytes 1769480 | tf_op jit(solution)/shard_map/ppermute | solution.py:34
  130.0 21.7 %collective-permute-done.12.refs_1_ = bf16[256,1152]{1,0:T(8,128)(2,1)S(1)} collective-permute-done((bf16[256,1152]{1,0:T(8,128)(2,1)S(1)}, bf16[256,1152]{1,0:T(8,128)(2,1)S(1)}, u32[]{:S(2)}, u32[]{:S(2)}) %collective-permute-start.12) | collective-permute-done | bytes 589856 | tf_op jit(solution)/shard_map/ppermute | solution.py:34
  151.7 0.9 shard_map.110.back_ref
  152.5 0.0 all-to-all-done.1.parts_ref
  152.5 0.2 shard_map.111
  152.8 24.5 %all_to_all.15.pieces_ref = bf16[16,16,1408]{2,1,0:T(8,128)(2,1)S(1)} all-to-all(bf16[16,16,1408]{2,1,0:T(8,128)(2,1)S(1)} %bitcast.18), channel_id=1, replica_groups=mesh['xh'=2,'z'=8,'c'=2,'xl'=2,'y'=8] {'xl','y'}, dimensions={0} | all-to-all | bytes 1441792 | tf_op jit(solution)/shard_map/all_to_all | solution.py:413
  177.3 0.6 shard_map.112
  177.9 5.0 %collective-permute-start.13 = (f32[2,36,432]{2,1,0:T(8,128)S(1)}, f32[2,36,432]{2,1,0:T(8,128)S(1)}, u32[]{:S(2)}, u32[]{:S(2)}) collective-permute-start(f32[2,36,432]{2,1,0:T(8,128)S(1)} %get-tuple-element.44), channel_id=1, source_target_pairs={{0,16},{16,0},{1,17},{17,1},{2,18},{18,2},{3,19},{19,3},{4,20},{20... | collective-permute-start | bytes 373256 | tf_op jit(solution)/shard_map/ppermute | solution.py:34
  183.7 0.1 pad_maximum_fusion.decay_ref
  183.8 0.9 slice.12
  184.6 0.0 collective-permute-done.13.core_ref
  184.6 0.0 copy-done.4
  184.6 1.5 shard_map.113
  (18 shorter events, 0.1 us)
Async XLA Ops:
  0.6 50.3 %copy-start = (bf16[128,2304]{1,0:T(8,128)(2,1)S(1)}, bf16[128,2304]{1,0:T(8,128)(2,1)}, u32[]{:S(2)}) copy-start(bf16[128,2304]{1,0:T(8,128)(2,1)} %param.10) | copy-start | bytes 1769476
  19.6 8.9 %copy-start.3 = (f32[36,1728]{1,0:T(8,128)S(1)}, f32[36,1728]{1,0:T(8,128)}, u32[]{:S(2)}) copy-start(f32[36,1728]{1,0:T(8,128)} %master_ref.1) | copy-start | bytes 746500
  19.7 41.4 %all-to-all-start = ((bf16[16,16,1792]{2,1,0:T(8,128)(2,1)}), bf16[16,16,1792]{2,1,0:T(8,128)(2,1)S(1)}, u32[]{:S(2)}, u32[]{:S(2)}) async-start(bf16[16,16,1792]{2,1,0:T(8,128)(2,1)} %bitcast.19), calls=%async_computation | async-start | bytes 1835008 | tf_op jit(solution)/shard_map/all_to_all | solution.py:360
  28.6 34.3 %copy-start.6 = (s32[3]{0:T(128)}, s32[3]{0:T(128)S(1)}, u32[]{:S(2)}) copy-start(s32[3]{0:T(128)S(1)} %pad_add_fusion.spot_ref) | copy-start | bytes 40
  29.5 4.6 %collective-permute-start = (bf16[36,432]{1,0:T(8,128)(2,1)S(1)}, bf16[36,432]{1,0:T(8,128)(2,1)S(1)}, u32[]{:S(2)}, u32[]{:S(2)}) collective-permute-start(bf16[36,432]{1,0:T(8,128)(2,1)S(1)} %get-tuple-element.26), channel_id=1, source_target_pairs={{0,16},{16,0},{1,17},{17,1},{2,18},{18,2},{3,19},{19,3},{4,20},{20... | collective-permute-start | bytes 93320 | tf_op jit(solution)/shard_map/ppermute | solution.py:34
  34.6 16.6 %collective-permute-start.1 = (bf16[72,432]{1,0:T(8,128)(2,1)S(1)}, bf16[72,432]{1,0:T(8,128)(2,1)S(1)}, u32[]{:S(2)}, u32[]{:S(2)}) collective-permute-start(bf16[72,432]{1,0:T(8,128)(2,1)S(1)} %shard_map.104.own_ref), channel_id=1, source_target_pairs={{0,128},{32,160},{64,192},{96,224},{128,0},{160,32},{192,64},{224,... | collective-permute-start | bytes 186632 | tf_op jit(solution)/shard_map/ppermute | solution.py:39
  44.4 7.5 %collective-permute-start.2 = (bf16[72,432]{1,0:T(8,128)(2,1)S(1)}, bf16[72,432]{1,0:T(8,128)(2,1)S(1)}, u32[]{:S(2)}, u32[]{:S(2)}) collective-permute-start(bf16[72,432]{1,0:T(8,128)(2,1)S(1)} %shard_map.104.own_ref), channel_id=1, source_target_pairs={{0,256},{256,0},{1,257},{257,1},{2,258},{258,2},{3,259},{259,3},{4... | collective-permute-start | bytes 186632 | tf_op jit(solution)/shard_map/ppermute | solution.py:34
  48.8 11.7 %collective-permute-start.3 = (bf16[72,432]{1,0:T(8,128)(2,1)S(1)}, bf16[72,432]{1,0:T(8,128)(2,1)S(1)}, u32[]{:S(2)}, u32[]{:S(2)}) collective-permute-start(bf16[72,432]{1,0:T(8,128)(2,1)S(1)} %shard_map.104.own_ref), channel_id=1, source_target_pairs={{0,384},{32,416},{64,448},{96,480},{128,256},{160,288},{192,320},{... | collective-permute-start | bytes 186632 | tf_op jit(solution)/shard_map/ppermute | solution.py:49
  61.0 32.0 %copy-start.2 = (bf16[4,72,432]{2,1,0:T(8,128)(2,1)}, bf16[4,72,432]{2,1,0:T(8,128)(2,1)S(1)}, u32[]{:S(2)}) copy-start(bf16[4,72,432]{2,1,0:T(8,128)(2,1)S(1)} %shard_map.105.near_hbm) | copy-start | bytes 746500
  62.9 30.1 %copy-start.8 = (bf16[256,1536]{1,0:T(8,128)(2,1)}, bf16[256,1536]{1,0:T(8,128)(2,1)S(1)}, u32[]{:S(2)}) copy-start(bf16[256,1536]{1,0:T(8,128)(2,1)S(1)} %get-tuple-element.36.own_hbm) | copy-start | bytes 2359300
  62.9 24.1 %collective-permute-start.4 = (bf16[256,1536]{1,0:T(8,128)(2,1)S(1)}, bf16[256,1536]{1,0:T(8,128)(2,1)S(1)}, u32[]{:S(2)}, u32[]{:S(2)}) collective-permute-start(bf16[256,1536]{1,0:T(8,128)(2,1)S(1)} %get-tuple-element.29), channel_id=1, source_target_pairs={{0,8},{8,0},{1,9},{9,1},{2,10},{10,2},{3,11},{11,3},{4,12},{12,4},... | collective-permute-start | bytes 2359304 | tf_op jit(solution)/shard_map/ppermute | solution.py:34
  65.8 21.1 %collective-permute-start.5 = (bf16[4,72,432]{2,1,0:T(8,128)(2,1)S(1)}, bf16[4,72,432]{2,1,0:T(8,128)(2,1)S(1)}, u32[]{:S(2)}, u32[]{:S(2)}) collective-permute-start(bf16[4,72,432]{2,1,0:T(8,128)(2,1)S(1)} %shard_map.105.near_hbm), channel_id=1, source_target_pairs={{0,224},{32,0},{64,32},{96,64},{128,96},{160,128},{192,160},{224,1... | collective-permute-start | bytes 746504 | tf_op jit(solution)/shard_map/ppermute | solution.py:39
  67.8 19.2 %collective-permute-start.8 = (bf16[4,72,432]{2,1,0:T(8,128)(2,1)S(1)}, bf16[4,72,432]{2,1,0:T(8,128)(2,1)S(1)}, u32[]{:S(2)}, u32[]{:S(2)}) collective-permute-start(bf16[4,72,432]{2,1,0:T(8,128)(2,1)S(1)} %shard_map.105.near_hbm), channel_id=1, source_target_pairs={{0,32},{32,64},{64,96},{96,128},{128,160},{160,192},{192,224},{224... | collective-permute-start | bytes 746504 | tf_op jit(solution)/shard_map/ppermute | solution.py:39
  71.2 10.7 %collective-permute-start.6 = (bf16[2,72,432]{2,1,0:T(8,128)(2,1)S(1)}, bf16[2,72,432]{2,1,0:T(8,128)(2,1)S(1)}, u32[]{:S(2)}, u32[]{:S(2)}) collective-permute-start(bf16[2,72,432]{2,1,0:T(8,128)(2,1)S(1)} %get-tuple-element.48), channel_id=1, source_target_pairs={{0,192},{32,224},{64,0},{96,32},{128,64},{160,96},{192,128},{224,1... | collective-permute-start | bytes 373256 | tf_op jit(solution)/shard_map/ppermute | solution.py:39
  75.5 11.4 %collective-permute-start.7 = (bf16[2,72,432]{2,1,0:T(8,128)(2,1)S(1)}, bf16[2,72,432]{2,1,0:T(8,128)(2,1)S(1)}, u32[]{:S(2)}, u32[]{:S(2)}) collective-permute-start(bf16[2,72,432]{2,1,0:T(8,128)(2,1)S(1)} %get-tuple-element.47), channel_id=1, source_target_pairs={{0,64},{32,96},{64,128},{96,160},{128,192},{160,224},{192,0},{224,... | collective-permute-start | bytes 373256 | tf_op jit(solution)/shard_map/ppermute | solution.py:39
  81.8 11.2 %copy-start.14 = (bf16[2,72,432]{2,1,0:T(8,128)(2,1)}, bf16[2,72,432]{2,1,0:T(8,128)(2,1)S(1)}, u32[]{:S(2)}) copy-start(bf16[2,72,432]{2,1,0:T(8,128)(2,1)S(1)} %collective-permute-done.6.low_hbm) | copy-start | bytes 373252
  81.8 9.3 %collective-permute-start.9 = (bf16[256,1536]{1,0:T(8,128)(2,1)S(1)}, bf16[256,1536]{1,0:T(8,128)(2,1)S(1)}, u32[]{:S(2)}, u32[]{:S(2)}) collective-permute-start(bf16[256,1536]{1,0:T(8,128)(2,1)S(1)} %get-tuple-element.36.own_hbm), channel_id=1, source_target_pairs={{0,16},{16,0},{1,17},{17,1},{2,18},{18,2},{3,19},{19,3},{4,20},{20... | collective-permute-start | bytes 2359304 | tf_op jit(solution)/shard_map/ppermute | solution.py:34
  86.9 4.2 %copy-start.15 = (bf16[2,72,432]{2,1,0:T(8,128)(2,1)}, bf16[2,72,432]{2,1,0:T(8,128)(2,1)S(1)}, u32[]{:S(2)}) copy-start(bf16[2,72,432]{2,1,0:T(8,128)(2,1)S(1)} %collective-permute-done.7.high_hbm) | copy-start | bytes 373252
  86.9 6.1 %copy-start.12 = (bf16[4,72,432]{2,1,0:T(8,128)(2,1)}, bf16[4,72,432]{2,1,0:T(8,128)(2,1)S(1)}, u32[]{:S(2)}) copy-start(bf16[4,72,432]{2,1,0:T(8,128)(2,1)S(1)} %collective-permute-done.5.up_hbm) | copy-start | bytes 746500
  87.0 6.1 %copy-start.13 = (bf16[4,72,432]{2,1,0:T(8,128)(2,1)}, bf16[4,72,432]{2,1,0:T(8,128)(2,1)S(1)}, u32[]{:S(2)}) copy-start(bf16[4,72,432]{2,1,0:T(8,128)(2,1)S(1)} %collective-permute-done.8.down_hbm) | copy-start | bytes 746500
  87.0 6.1 %copy-start.9 = (bf16[256,1536]{1,0:T(8,128)(2,1)}, bf16[256,1536]{1,0:T(8,128)(2,1)S(1)}, u32[]{:S(2)}) copy-start(bf16[256,1536]{1,0:T(8,128)(2,1)S(1)} %collective-permute-done.4.side_hbm) | copy-start | bytes 2359300
  87.0 6.0 %collective-permute-start.10 = (bf16[256,1536]{1,0:T(8,128)(2,1)S(1)}, bf16[256,1536]{1,0:T(8,128)(2,1)S(1)}, u32[]{:S(2)}, u32[]{:S(2)}) collective-permute-start(bf16[256,1536]{1,0:T(8,128)(2,1)S(1)} %collective-permute-done.4.side_hbm), channel_id=1, source_target_pairs={{0,16},{16,0},{1,17},{17,1},{2,18},{18,2},{3,19},{19,3},{4,20},{20... | collective-permute-start | bytes 2359304 | tf_op jit(solution)/shard_map/ppermute | solution.py:34
  91.2 1.9 %copy-start.10 = (bf16[256,1536]{1,0:T(8,128)(2,1)}, bf16[256,1536]{1,0:T(8,128)(2,1)S(1)}, u32[]{:S(2)}) copy-start(bf16[256,1536]{1,0:T(8,128)(2,1)S(1)} %collective-permute-done.9.core_hbm) | copy-start | bytes 2359300
  93.1 0.9 copy-start.11
  107.0 45.5 %all-to-all-start.1 = ((bf16[128,32,128]{2,1,0:T(8,128)(2,1)}), bf16[128,32,128]{2,1,0:T(8,128)(2,1)S(1)}, u32[]{:S(2)}, u32[]{:S(2)}) async-start(bf16[128,32,128]{2,1,0:T(8,128)(2,1)} %get-tuple-element.38), calls=%async_computation.1 | async-start | bytes 2097152 | tf_op jit(solution)/shard_map/all_to_all | solution.py:411
  121.3 5.2 %collective-permute-start.11 = (bf16[512,1152]{1,0:T(8,128)(2,1)}, bf16[512,1152]{1,0:T(8,128)(2,1)S(1)}, u32[]{:S(2)}, u32[]{:S(2)}) collective-permute-start(bf16[512,1152]{1,0:T(8,128)(2,1)} %get-tuple-element.40), channel_id=1, source_target_pairs={{0,16},{16,0},{1,17},{17,1},{2,18},{18,2},{3,19},{19,3},{4,20},{20... | collective-permute-start | bytes 3538952 | tf_op jit(solution)/shard_map/ppermute | solution.py:34
  126.5 1.3 copy-start.1
  128.1 23.6 %collective-permute-start.12 = (bf16[256,1152]{1,0:T(8,128)(2,1)S(1)}, bf16[256,1152]{1,0:T(8,128)(2,1)S(1)}, u32[]{:S(2)}, u32[]{:S(2)}) collective-permute-start(bf16[256,1152]{1,0:T(8,128)(2,1)S(1)} %get-tuple-element.42), channel_id=1, source_target_pairs={{0,8},{8,0},{1,9},{9,1},{2,10},{10,2},{3,11},{11,3},{4,12},{12,4},... | collective-permute-start | bytes 1769480 | tf_op jit(solution)/shard_map/ppermute | solution.py:34
  152.8 24.5 %copy-start.7 = (s32[3]{0:T(128)S(1)}, s32[3]{0:T(128)}, u32[]{:S(2)}) copy-start(s32[3]{0:T(128)} %copy-done.6) | copy-start | bytes 40
  177.3 7.4 %copy-start.4 = (f32[36,1728]{1,0:T(8,128)S(1)}, f32[36,1728]{1,0:T(8,128)}, u32[]{:S(2)}) copy-start(f32[36,1728]{1,0:T(8,128)} %slow_ref.1) | copy-start | bytes 746500
  177.3 7.4 %copy-start.5 = (f32[36,1728]{1,0:T(8,128)S(1)}, f32[36,1728]{1,0:T(8,128)}, u32[]{:S(2)}) copy-start(f32[36,1728]{1,0:T(8,128)} %fast_ref.1) | copy-start | bytes 746500
  177.9 6.7 %collective-permute-start.13 = (f32[2,36,432]{2,1,0:T(8,128)S(1)}, f32[2,36,432]{2,1,0:T(8,128)S(1)}, u32[]{:S(2)}, u32[]{:S(2)}) collective-permute-start(f32[2,36,432]{2,1,0:T(8,128)S(1)} %get-tuple-element.44), channel_id=1, source_target_pairs={{0,16},{16,0},{1,17},{17,1},{2,18},{18,2},{3,19},{19,3},{4,20},{20... | collective-permute-start | bytes 373256 | tf_op jit(solution)/shard_map/ppermute | solution.py:34

commit v7 on v6

--- a/solution.py
+++ b/solution.py
@@ -57,19 +57,22 @@
     return jnp.dot(embedding, ada_weight, preferred_element_type=F32)
 
 
-def pack_kernel(hidden_hbm, cot_hbm, out_hbm, cot_ref, turned_ref, sems):
+def pack_kernel(hidden_hbm, cot_hbm, out_hbm, hidden_ref, cot_ref, turned_ref, sems):
     width = hidden_hbm.shape[1]
-    whole = pltpu.make_async_copy(hidden_hbm, out_hbm.at[:, pl.ds(0, width)], sems.at[0])
-    whole.start()
-    load = pltpu.make_async_copy(cot_hbm, cot_ref, sems.at[1])
-    load.start()
-    load.wait()
+    first = pltpu.make_async_copy(cot_hbm, cot_ref, sems.at[0])
+    second = pltpu.make_async_copy(hidden_hbm, hidden_ref, sems.at[1])
+    first.start()
+    second.start()
+    first.wait()
     inner = cot_ref.shape[0]
     turned_ref[:, :inner] = cot_ref[...].T
-    store = pltpu.make_async_copy(turned_ref, out_hbm.at[:, pl.ds(width, turned_ref.shape[1])], sems.at[2])
-    store.start()
-    store.wait()
-    whole.wait()
+    right = pltpu.make_async_copy(turned_ref, out_hbm.at[:, pl.ds(width, turned_ref.shape[1])], sems.at[2])
+    right.start()
+    second.wait()
+    left = pltpu.make_async_copy(hidden_ref, out_hbm.at[:, pl.ds(0, width)], sems.at[3])
+    left.start()
+    right.wait()
+    left.wait()
 
 
 def stats(values):
@@ -352,7 +355,12 @@
         pack_kernel,
         [((patches, width + loose), BF16)],
         hidden[0, 0], cotangent[0, 0].T,
-        scratch=[pltpu.VMEM((inner, patches), BF16), pltpu.VMEM((patches, loose), BF16), pltpu.SemaphoreType.DMA((3,))],
+        scratch=[
+            pltpu.VMEM((patches, width), BF16),
+            pltpu.VMEM((inner, patches), BF16),
+            pltpu.VMEM((patches, loose), BF16),
+            pltpu.SemaphoreType.DMA((4,)),
+        ],
         mib=58,
         hbm_in=True,
         hbm_out=(0,),
@@ -374,9 +382,10 @@
     broad = lanes(width + 2 * quarter)
     to_core, to_side = call(norm_kernel, [((patches, broad), BF16)] * 2, spots, tokens, modulation, smem=1)
     from_side = swap(to_side, "xl")
-    up, low, high, down = shift(quad, -1), shift(quad[:2], -2), shift(quad[2:], 2), shift(quad, 1)
-    to_core, low = lax.optimization_barrier((to_core, low))
     from_core = swap(to_core, "c")
+    up, down, low = shift(quad, -1), shift(quad, 1), shift(quad[:2], -2)
+    upper, from_core = lax.optimization_barrier((quad[2:], from_core))
+    high = shift(upper, 2)
     from_side, up, low, high, down = lax.optimization_barrier((from_side, up, low, high, down))
     from_both = swap(from_side, "c")
 

time: 187 us -> 173 us (0.925)
  Pallas kernels: 39.4 us -> 22.5 us
  waiting for transfers between devices: 39 us -> 42.1 us
    pallas_call x11, Pallas kernels: 39.4 us -> 22.5 us  [call(): pl.pallas_call(kernel, out_shape=shapes, in_specs=specs, out_specs=[pl.Bl...]
    ppermute x8, waiting for transfers between devices: 27 us -> 29.3 us  [swap(): return lax.ppermute(value, axis, [(0, 1), (1, 0)])]
    all_to_all x1, starting transfers between devices: 14.3 us -> 16.2 us  [on_device(): parts = lax.all_to_all(packed, ROWS + ('y',), 0, 0, tiled=True)]
  transfers between devices with their start and end apart: 16 -> 16, of which waited for: 7 -> 8; matrix products, arithmetic and copies ran while one was open for 1% -> 1% of each run, Pallas kernels for 2% -> 2%
where the time goes in v7:
time: 173 us; the launch traced here: 172 us
  starting transfers between devices  76.6 us (44%)
  waiting for transfers between devices  42.1 us (24%)
  blocking collectives  24.5 us (14%)
  Pallas kernels  22.5 us (13%)
  local copies, waits for them, and re-layouts  3.79 us (2%)
  between operations  2.44 us (1%)
    ppermute x8, waiting for transfers between devices, swap(): return lax.ppermute(value, axis, [(0, 1), (1, 0)])  29.3 us
    ppermute x8, starting transfers between devices, swap(): return lax.ppermute(value, axis, [(0, 1), (1, 0)])  28.2 us
    all_to_all x1, blocking collectives, on_device(): lax.all_to_all(joint.reshape(n_seq, patches // n_seq, width + 256), SEQ,...  24.5 us
    pallas_call x11, Pallas kernels, call(): pl.pallas_call(kernel, out_shape=shapes, in_specs=specs, out_specs=[pl.Bl...  22.5 us
    ppermute x5, starting transfers between devices, shift(): lax.ppermute(value, 'z', [(i, (i + away) % count) for i in range(count)])  21.2 us
    all_to_all x1, starting transfers between devices, on_device(): parts = lax.all_to_all(packed, ROWS + ('y',), 0, 0, tiled=True)  16.2 us
    all_to_all x1, starting transfers between devices, on_device(): lax.all_to_all(packed.reshape(n_seq, patches // n_seq, width + loose), SE...  8.83 us
    ppermute x1, waiting for transfers between devices, both_turn(): return lax.ppermute(value, ('xh', 'z'), pairs)  8.6 us
  transfers between devices with their start and end apart: 16, of which 8 were waited for; matrix products, arithmetic and copies ran while one was open for 1% of the time, Pallas kernels for 2%

profile of v7, /device:TPU:1, one launch (start us, length us, event | category | flops | bytes accessed | tf_op | source)
XLA Modules:
  0.0 172.4 jit_solution(2470406724708411736)
XLA Ops:
  0.6 0.0 copy-start
  0.6 2.2 %shard_map.106 = bf16[256,1792]{1,0:T(8,128)(2,1)} custom-call(bf16[256,1152]{1,0:T(8,128)(2,1)} %bitcast.20, bf16[576,256]{1,0:T(8,128)(2,1)} %bitcast.22), custom_call_target="tpu_custom_call" | custom-call | bytes 1802240 | tf_op jit(solution)/shard_map/pallas_call | solution.py:323
  2.8 0.0 copy-start.3
  2.8 8.8 %all-to-all-start = ((bf16[16,16,1792]{2,1,0:T(8,128)(2,1)}), bf16[16,16,1792]{2,1,0:T(8,128)(2,1)S(1)}, u32[]{:S(2)}, u32[]{:S(2)}) async-start(bf16[16,16,1792]{2,1,0:T(8,128)(2,1)} %bitcast.19), calls=%async_computation | async-start | bytes 1835008 | tf_op jit(solution)/shard_map/all_to_all | solution.py:368
  11.7 0.1 pad_add_fusion.spot_ref
  11.7 0.0 copy-done.3
  11.8 0.9 shard_map.103
  12.6 3.7 %collective-permute-start = (bf16[36,432]{1,0:T(8,128)(2,1)S(1)}, bf16[36,432]{1,0:T(8,128)(2,1)S(1)}, u32[]{:S(2)}, u32[]{:S(2)}) collective-permute-start(bf16[36,432]{1,0:T(8,128)(2,1)S(1)} %get-tuple-element.26), channel_id=1, source_target_pairs={{0,16},{16,0},{1,17},{17,1},{2,18},{18,2},{3,19},{19,3},{4,20},{20... | collective-permute-start | bytes 93320 | tf_op jit(solution)/shard_map/ppermute | solution.py:34
  17.0 0.1 sine_convert_fusion
  17.1 0.1 collective-permute-done.theirs_ref
  17.2 0.6 shard_map.104.own_ref
  17.8 9.8 %collective-permute-start.1 = (bf16[72,432]{1,0:T(8,128)(2,1)S(1)}, bf16[72,432]{1,0:T(8,128)(2,1)S(1)}, u32[]{:S(2)}, u32[]{:S(2)}) collective-permute-start(bf16[72,432]{1,0:T(8,128)(2,1)S(1)} %shard_map.104.own_ref), channel_id=1, source_target_pairs={{0,128},{32,160},{64,192},{96,224},{128,0},{160,32},{192,64},{224,... | collective-permute-start | bytes 186632 | tf_op jit(solution)/shard_map/ppermute | solution.py:39
  27.6 4.4 %collective-permute-start.2 = (bf16[72,432]{1,0:T(8,128)(2,1)S(1)}, bf16[72,432]{1,0:T(8,128)(2,1)S(1)}, u32[]{:S(2)}, u32[]{:S(2)}) collective-permute-start(bf16[72,432]{1,0:T(8,128)(2,1)S(1)} %shard_map.104.own_ref), channel_id=1, source_target_pairs={{0,256},{256,0},{1,257},{257,1},{2,258},{258,2},{3,259},{259,3},{4... | collective-permute-start | bytes 186632 | tf_op jit(solution)/shard_map/ppermute | solution.py:34
  31.9 2.2 %collective-permute-start.3 = (bf16[72,432]{1,0:T(8,128)(2,1)S(1)}, bf16[72,432]{1,0:T(8,128)(2,1)S(1)}, u32[]{:S(2)}, u32[]{:S(2)}) collective-permute-start(bf16[72,432]{1,0:T(8,128)(2,1)S(1)} %shard_map.104.own_ref), channel_id=1, source_target_pairs={{0,384},{32,416},{64,448},{96,480},{128,256},{160,288},{192,320},{... | collective-permute-start | bytes 186632 | tf_op jit(solution)/shard_map/ppermute | solution.py:49
  34.1 0.0 copy-done
  34.1 0.2 fusion.mod_ref
  34.3 0.0 collective-permute-done.1.far_ref
  34.3 0.7 collective-permute-done.2.across_ref
  35.0 8.6 %collective-permute-done.3.both_ref = bf16[72,432]{1,0:T(8,128)(2,1)S(1)} collective-permute-done((bf16[72,432]{1,0:T(8,128)(2,1)S(1)}, bf16[72,432]{1,0:T(8,128)(2,1)S(1)}, u32[]{:S(2)}, u32[]{:S(2)}) %collective-permute-start.3) | collective-permute-done | bytes 62240 | tf_op jit(solution)/shard_map/ppermute | solution.py:49
  43.6 0.6 shard_map.105.near_hbm
  44.2 0.0 copy-start.2
  44.2 0.0 all-to-all-done
  44.2 1.8 %shard_map.107 = (bf16[256,1536]{1,0:T(8,128)(2,1)S(1)}, bf16[256,1536]{1,0:T(8,128)(2,1)S(1)}) custom-call(s32[3]{0:T(128)S(1)} %pad_add_fusion.spot_ref, bf16[256,1792]{1,0:T(8,128)(2,1)S(1)} %bitcast.16, f32[1,2304]{1,0:T(1,128)S(1)} %fusion.mod_ref), custom_call_target="tpu_custom_call" | custom-call | bytes 2499596 | tf_op jit(solution)/shard_map/pallas_call | solution.py:323
  46.0 0.0 copy-done.6
  46.1 0.0 copy-start.8
  46.1 5.0 %collective-permute-start.7 = (bf16[256,1536]{1,0:T(8,128)(2,1)S(1)}, bf16[256,1536]{1,0:T(8,128)(2,1)S(1)}, u32[]{:S(2)}, u32[]{:S(2)}) collective-permute-start(bf16[256,1536]{1,0:T(8,128)(2,1)S(1)} %get-tuple-element.30.own_hbm), channel_id=1, source_target_pairs={{0,16},{16,0},{1,17},{17,1},{2,18},{18,2},{3,19},{19,3},{4,20},{20... | collective-permute-start | bytes 2359304 | tf_op jit(solution)/shard_map/ppermute | solution.py:34
  51.0 3.0 %collective-permute-start.4 = (bf16[256,1536]{1,0:T(8,128)(2,1)S(1)}, bf16[256,1536]{1,0:T(8,128)(2,1)S(1)}, u32[]{:S(2)}, u32[]{:S(2)}) collective-permute-start(bf16[256,1536]{1,0:T(8,128)(2,1)S(1)} %get-tuple-element.29), channel_id=1, source_target_pairs={{0,8},{8,0},{1,9},{9,1},{2,10},{10,2},{3,11},{11,3},{4,12},{12,4},... | collective-permute-start | bytes 2359304 | tf_op jit(solution)/shard_map/ppermute | solution.py:34
  54.0 1.9 %collective-permute-start.5 = (bf16[4,72,432]{2,1,0:T(8,128)(2,1)S(1)}, bf16[4,72,432]{2,1,0:T(8,128)(2,1)S(1)}, u32[]{:S(2)}, u32[]{:S(2)}) collective-permute-start(bf16[4,72,432]{2,1,0:T(8,128)(2,1)S(1)} %shard_map.105.near_hbm), channel_id=1, source_target_pairs={{0,224},{32,0},{64,32},{96,64},{128,96},{160,128},{192,160},{224,1... | collective-permute-start | bytes 746504 | tf_op jit(solution)/shard_map/ppermute | solution.py:39
  56.0 3.4 %collective-permute-start.9 = (bf16[4,72,432]{2,1,0:T(8,128)(2,1)S(1)}, bf16[4,72,432]{2,1,0:T(8,128)(2,1)S(1)}, u32[]{:S(2)}, u32[]{:S(2)}) collective-permute-start(bf16[4,72,432]{2,1,0:T(8,128)(2,1)S(1)} %shard_map.105.near_hbm), channel_id=1, source_target_pairs={{0,32},{32,64},{64,96},{96,128},{128,160},{160,192},{192,224},{224... | collective-permute-start | bytes 746504 | tf_op jit(solution)/shard_map/ppermute | solution.py:39
  59.4 2.2 %collective-permute-start.6 = (bf16[2,72,432]{2,1,0:T(8,128)(2,1)S(1)}, bf16[2,72,432]{2,1,0:T(8,128)(2,1)S(1)}, u32[]{:S(2)}, u32[]{:S(2)}) collective-permute-start(bf16[2,72,432]{2,1,0:T(8,128)(2,1)S(1)} %get-tuple-element.48), channel_id=1, source_target_pairs={{0,192},{32,224},{64,0},{96,32},{128,64},{160,96},{192,128},{224,1... | collective-permute-start | bytes 373256 | tf_op jit(solution)/shard_map/ppermute | solution.py:39
  61.6 0.0 collective-permute-done.7.core_hbm
  61.6 0.0 copy-start.9
  61.6 3.9 %collective-permute-start.8 = (bf16[2,72,432]{2,1,0:T(8,128)(2,1)S(1)}, bf16[2,72,432]{2,1,0:T(8,128)(2,1)S(1)}, u32[]{:S(2)}, u32[]{:S(2)}) collective-permute-start(bf16[2,72,432]{2,1,0:T(8,128)(2,1)S(1)} %get-tuple-element.31), channel_id=1, source_target_pairs={{0,64},{32,96},{64,128},{96,160},{128,192},{160,224},{192,0},{224,... | collective-permute-start | bytes 373256 | tf_op jit(solution)/shard_map/ppermute | solution.py:39
  65.6 4.2 %collective-permute-done.6.low_hbm = bf16[2,72,432]{2,1,0:T(8,128)(2,1)S(1)} collective-permute-done((bf16[2,72,432]{2,1,0:T(8,128)(2,1)S(1)}, bf16[2,72,432]{2,1,0:T(8,128)(2,1)S(1)}, u32[]{:S(2)}, u32[]{:S(2)}) %collective-permute-start.6) | collective-permute-done | bytes 124448 | tf_op jit(solution)/shard_map/ppermute | solution.py:39
  69.8 0.0 collective-permute-done.5.up_hbm
  69.8 0.0 collective-permute-done.9.down_hbm
  69.8 0.0 copy-start.13
  69.8 2.3 %collective-permute-done.4.side_hbm = bf16[256,1536]{1,0:T(8,128)(2,1)S(1)} collective-permute-done((bf16[256,1536]{1,0:T(8,128)(2,1)S(1)}, bf16[256,1536]{1,0:T(8,128)(2,1)S(1)}, u32[]{:S(2)}, u32[]{:S(2)}) %collective-permute-start.4) | collective-permute-done | bytes 786464 | tf_op jit(solution)/shard_map/ppermute | solution.py:34
  72.1 0.0 collective-permute-done.8.high_hbm
  72.1 0.7 copy-done.15
  72.8 2.7 %collective-permute-start.10 = (bf16[256,1536]{1,0:T(8,128)(2,1)S(1)}, bf16[256,1536]{1,0:T(8,128)(2,1)S(1)}, u32[]{:S(2)}, u32[]{:S(2)}) collective-permute-start(bf16[256,1536]{1,0:T(8,128)(2,1)S(1)} %collective-permute-done.4.side_hbm), channel_id=1, source_target_pairs={{0,16},{16,0},{1,17},{17,1},{2,18},{18,2},{3,19},{19,3},{4,20},{20... | collective-permute-start | bytes 2359304 | tf_op jit(solution)/shard_map/ppermute | solution.py:34
  75.5 1.9 %collective-permute-done.10.both_hbm = bf16[256,1536]{1,0:T(8,128)(2,1)S(1)} collective-permute-done((bf16[256,1536]{1,0:T(8,128)(2,1)S(1)}, bf16[256,1536]{1,0:T(8,128)(2,1)S(1)}, u32[]{:S(2)}, u32[]{:S(2)}) %collective-permute-start.10) | collective-permute-done | bytes 786464 | tf_op jit(solution)/shard_map/ppermute | solution.py:34
  77.4 0.0 copy-done.9
  77.4 0.9 copy-done.11
  78.3 13.0 %shard_map.108 = (bf16[128,32,128]{2,1,0:T(8,128)(2,1)}, bf16[512,1152]{1,0:T(8,128)(2,1)}, bf16[512,1152]{1,0:T(8,128)(2,1)}) custom-call(s32[3]{0:T(128)} %copy-done.6, bf16[4,72,432]{2,1,0:T(8,128)(2,1)} %copy-done.2, bf16[4,72,432]{2,1,0:T(8,128)(2,1)} %copy-done.12, bf16[2,72,432]{2,1,0:T(8,128)(2,1)} %copy-done.14, bf16[2,72,432]{2,1,0:T(8,128)(2,1)} %copy-done.15, ...), custom_call_target="tpu_custom_call" | custom-call | flops 3057647616 | bytes 7548940 | tf_op jit(solution)/shard_map/pallas_call | solution.py:323
  91.4 16.2 %all-to-all-start.1 = ((bf16[128,32,128]{2,1,0:T(8,128)(2,1)}), bf16[128,32,128]{2,1,0:T(8,128)(2,1)S(1)}, u32[]{:S(2)}, u32[]{:S(2)}) async-start(bf16[128,32,128]{2,1,0:T(8,128)(2,1)} %get-tuple-element.38), calls=%async_computation.1 | async-start | bytes 2097152 | tf_op jit(solution)/shard_map/all_to_all | solution.py:420
  107.5 2.6 %collective-permute-start.11 = (bf16[512,1152]{1,0:T(8,128)(2,1)}, bf16[512,1152]{1,0:T(8,128)(2,1)S(1)}, u32[]{:S(2)}, u32[]{:S(2)}) collective-permute-start(bf16[512,1152]{1,0:T(8,128)(2,1)} %get-tuple-element.40), channel_id=1, source_target_pairs={{0,16},{16,0},{1,17},{17,1},{2,18},{18,2},{3,19},{19,3},{4,20},{20... | collective-permute-start | bytes 3538952 | tf_op jit(solution)/shard_map/ppermute | solution.py:34
  110.1 2.7 %collective-permute-done.11.got_ref = bf16[512,1152]{1,0:T(8,128)(2,1)S(1)} collective-permute-done((bf16[512,1152]{1,0:T(8,128)(2,1)}, bf16[512,1152]{1,0:T(8,128)(2,1)S(1)}, u32[]{:S(2)}, u32[]{:S(2)}) %collective-permute-start.11) | collective-permute-done | bytes 1179680 | tf_op jit(solution)/shard_map/ppermute | solution.py:34
  112.8 1.3 copy-done.1
  114.1 0.3 shard_map.109
  114.3 1.9 %collective-permute-start.12 = (bf16[256,1152]{1,0:T(8,128)(2,1)S(1)}, bf16[256,1152]{1,0:T(8,128)(2,1)S(1)}, u32[]{:S(2)}, u32[]{:S(2)}) collective-permute-start(bf16[256,1152]{1,0:T(8,128)(2,1)S(1)} %get-tuple-element.42), channel_id=1, source_target_pairs={{0,8},{8,0},{1,9},{9,1},{2,10},{10,2},{3,11},{11,3},{4,12},{12,4},... | collective-permute-start | bytes 1769480 | tf_op jit(solution)/shard_map/ppermute | solution.py:34
  116.3 21.7 %collective-permute-done.12.refs_1_ = bf16[256,1152]{1,0:T(8,128)(2,1)S(1)} collective-permute-done((bf16[256,1152]{1,0:T(8,128)(2,1)S(1)}, bf16[256,1152]{1,0:T(8,128)(2,1)S(1)}, u32[]{:S(2)}, u32[]{:S(2)}) %collective-permute-start.12) | collective-permute-done | bytes 589856 | tf_op jit(solution)/shard_map/ppermute | solution.py:34
  137.9 0.9 shard_map.110.back_ref
  138.8 0.0 all-to-all-done.1.parts_ref
  138.8 0.2 shard_map.111
  139.0 0.0 copy-start.7
  139.0 24.5 %all_to_all.15.pieces_ref = bf16[16,16,1408]{2,1,0:T(8,128)(2,1)S(1)} all-to-all(bf16[16,16,1408]{2,1,0:T(8,128)(2,1)S(1)} %bitcast.18), channel_id=1, replica_groups=mesh['xh'=2,'z'=8,'c'=2,'xl'=2,'y'=8] {'xl','y'}, dimensions={0} | all-to-all | bytes 1441792 | tf_op jit(solution)/shard_map/all_to_all | solution.py:422
  163.5 0.6 shard_map.112
  164.1 5.0 %collective-permute-start.13 = (f32[2,36,432]{2,1,0:T(8,128)S(1)}, f32[2,36,432]{2,1,0:T(8,128)S(1)}, u32[]{:S(2)}, u32[]{:S(2)}) collective-permute-start(f32[2,36,432]{2,1,0:T(8,128)S(1)} %get-tuple-element.44), channel_id=1, source_target_pairs={{0,16},{16,0},{1,17},{17,1},{2,18},{18,2},{3,19},{19,3},{4,20},{20... | collective-permute-start | bytes 373256 | tf_op jit(solution)/shard_map/ppermute | solution.py:34
  169.9 0.1 pad_maximum_fusion.decay_ref
  170.0 0.9 slice.12
  170.9 0.0 collective-permute-done.13.core_ref
  170.9 0.0 copy-done.5
  170.9 1.5 shard_map.113
  (18 shorter events, 0.1 us)
Async XLA Ops:
  0.6 33.5 %copy-start = (bf16[128,2304]{1,0:T(8,128)(2,1)S(1)}, bf16[128,2304]{1,0:T(8,128)(2,1)}, u32[]{:S(2)}) copy-start(bf16[128,2304]{1,0:T(8,128)(2,1)} %param.10) | copy-start | bytes 1769476
  2.8 8.9 %copy-start.3 = (f32[36,1728]{1,0:T(8,128)S(1)}, f32[36,1728]{1,0:T(8,128)}, u32[]{:S(2)}) copy-start(f32[36,1728]{1,0:T(8,128)} %master_ref.1) | copy-start | bytes 746500
  2.8 41.4 %all-to-all-start = ((bf16[16,16,1792]{2,1,0:T(8,128)(2,1)}), bf16[16,16,1792]{2,1,0:T(8,128)(2,1)S(1)}, u32[]{:S(2)}, u32[]{:S(2)}) async-start(bf16[16,16,1792]{2,1,0:T(8,128)(2,1)} %bitcast.19), calls=%async_computation | async-start | bytes 1835008 | tf_op jit(solution)/shard_map/all_to_all | solution.py:368
  11.8 34.3 %copy-start.6 = (s32[3]{0:T(128)}, s32[3]{0:T(128)S(1)}, u32[]{:S(2)}) copy-start(s32[3]{0:T(128)S(1)} %pad_add_fusion.spot_ref) | copy-start | bytes 40
  12.6 4.6 %collective-permute-start = (bf16[36,432]{1,0:T(8,128)(2,1)S(1)}, bf16[36,432]{1,0:T(8,128)(2,1)S(1)}, u32[]{:S(2)}, u32[]{:S(2)}) collective-permute-start(bf16[36,432]{1,0:T(8,128)(2,1)S(1)} %get-tuple-element.26), channel_id=1, source_target_pairs={{0,16},{16,0},{1,17},{17,1},{2,18},{18,2},{3,19},{19,3},{4,20},{20... | collective-permute-start | bytes 93320 | tf_op jit(solution)/shard_map/ppermute | solution.py:34
  17.8 16.6 %collective-permute-start.1 = (bf16[72,432]{1,0:T(8,128)(2,1)S(1)}, bf16[72,432]{1,0:T(8,128)(2,1)S(1)}, u32[]{:S(2)}, u32[]{:S(2)}) collective-permute-start(bf16[72,432]{1,0:T(8,128)(2,1)S(1)} %shard_map.104.own_ref), channel_id=1, source_target_pairs={{0,128},{32,160},{64,192},{96,224},{128,0},{160,32},{192,64},{224,... | collective-permute-start | bytes 186632 | tf_op jit(solution)/shard_map/ppermute | solution.py:39
  27.6 7.5 %collective-permute-start.2 = (bf16[72,432]{1,0:T(8,128)(2,1)S(1)}, bf16[72,432]{1,0:T(8,128)(2,1)S(1)}, u32[]{:S(2)}, u32[]{:S(2)}) collective-permute-start(bf16[72,432]{1,0:T(8,128)(2,1)S(1)} %shard_map.104.own_ref), channel_id=1, source_target_pairs={{0,256},{256,0},{1,257},{257,1},{2,258},{258,2},{3,259},{259,3},{4... | collective-permute-start | bytes 186632 | tf_op jit(solution)/shard_map/ppermute | solution.py:34
  31.9 11.7 %collective-permute-start.3 = (bf16[72,432]{1,0:T(8,128)(2,1)S(1)}, bf16[72,432]{1,0:T(8,128)(2,1)S(1)}, u32[]{:S(2)}, u32[]{:S(2)}) collective-permute-start(bf16[72,432]{1,0:T(8,128)(2,1)S(1)} %shard_map.104.own_ref), channel_id=1, source_target_pairs={{0,384},{32,416},{64,448},{96,480},{128,256},{160,288},{192,320},{... | collective-permute-start | bytes 186632 | tf_op jit(solution)/shard_map/ppermute | solution.py:49
  44.2 33.2 %copy-start.2 = (bf16[4,72,432]{2,1,0:T(8,128)(2,1)}, bf16[4,72,432]{2,1,0:T(8,128)(2,1)S(1)}, u32[]{:S(2)}) copy-start(bf16[4,72,432]{2,1,0:T(8,128)(2,1)S(1)} %shard_map.105.near_hbm) | copy-start | bytes 746500
  46.1 31.3 %copy-start.8 = (bf16[256,1536]{1,0:T(8,128)(2,1)}, bf16[256,1536]{1,0:T(8,128)(2,1)S(1)}, u32[]{:S(2)}) copy-start(bf16[256,1536]{1,0:T(8,128)(2,1)S(1)} %get-tuple-element.30.own_hbm) | copy-start | bytes 2359300
  46.1 15.6 %collective-permute-start.7 = (bf16[256,1536]{1,0:T(8,128)(2,1)S(1)}, bf16[256,1536]{1,0:T(8,128)(2,1)S(1)}, u32[]{:S(2)}, u32[]{:S(2)}) collective-permute-start(bf16[256,1536]{1,0:T(8,128)(2,1)S(1)} %get-tuple-element.30.own_hbm), channel_id=1, source_target_pairs={{0,16},{16,0},{1,17},{17,1},{2,18},{18,2},{3,19},{19,3},{4,20},{20... | collective-permute-start | bytes 2359304 | tf_op jit(solution)/shard_map/ppermute | solution.py:34
  51.0 21.1 %collective-permute-start.4 = (bf16[256,1536]{1,0:T(8,128)(2,1)S(1)}, bf16[256,1536]{1,0:T(8,128)(2,1)S(1)}, u32[]{:S(2)}, u32[]{:S(2)}) collective-permute-start(bf16[256,1536]{1,0:T(8,128)(2,1)S(1)} %get-tuple-element.29), channel_id=1, source_target_pairs={{0,8},{8,0},{1,9},{9,1},{2,10},{10,2},{3,11},{11,3},{4,12},{12,4},... | collective-permute-start | bytes 2359304 | tf_op jit(solution)/shard_map/ppermute | solution.py:34
  54.0 15.7 %collective-permute-start.5 = (bf16[4,72,432]{2,1,0:T(8,128)(2,1)S(1)}, bf16[4,72,432]{2,1,0:T(8,128)(2,1)S(1)}, u32[]{:S(2)}, u32[]{:S(2)}) collective-permute-start(bf16[4,72,432]{2,1,0:T(8,128)(2,1)S(1)} %shard_map.105.near_hbm), channel_id=1, source_target_pairs={{0,224},{32,0},{64,32},{96,64},{128,96},{160,128},{192,160},{224,1... | collective-permute-start | bytes 746504 | tf_op jit(solution)/shard_map/ppermute | solution.py:39
  56.0 13.8 %collective-permute-start.9 = (bf16[4,72,432]{2,1,0:T(8,128)(2,1)S(1)}, bf16[4,72,432]{2,1,0:T(8,128)(2,1)S(1)}, u32[]{:S(2)}, u32[]{:S(2)}) collective-permute-start(bf16[4,72,432]{2,1,0:T(8,128)(2,1)S(1)} %shard_map.105.near_hbm), channel_id=1, source_target_pairs={{0,32},{32,64},{64,96},{96,128},{128,160},{160,192},{192,224},{224... | collective-permute-start | bytes 746504 | tf_op jit(solution)/shard_map/ppermute | solution.py:39
  59.4 10.4 %collective-permute-start.6 = (bf16[2,72,432]{2,1,0:T(8,128)(2,1)S(1)}, bf16[2,72,432]{2,1,0:T(8,128)(2,1)S(1)}, u32[]{:S(2)}, u32[]{:S(2)}) collective-permute-start(bf16[2,72,432]{2,1,0:T(8,128)(2,1)S(1)} %get-tuple-element.48), channel_id=1, source_target_pairs={{0,192},{32,224},{64,0},{96,32},{128,64},{160,96},{192,128},{224,1... | collective-permute-start | bytes 373256 | tf_op jit(solution)/shard_map/ppermute | solution.py:39
  61.6 15.8 %copy-start.9 = (bf16[256,1536]{1,0:T(8,128)(2,1)}, bf16[256,1536]{1,0:T(8,128)(2,1)S(1)}, u32[]{:S(2)}) copy-start(bf16[256,1536]{1,0:T(8,128)(2,1)S(1)} %collective-permute-done.7.core_hbm) | copy-start | bytes 2359300
  61.6 10.5 %collective-permute-start.8 = (bf16[2,72,432]{2,1,0:T(8,128)(2,1)S(1)}, bf16[2,72,432]{2,1,0:T(8,128)(2,1)S(1)}, u32[]{:S(2)}, u32[]{:S(2)}) collective-permute-start(bf16[2,72,432]{2,1,0:T(8,128)(2,1)S(1)} %get-tuple-element.31), channel_id=1, source_target_pairs={{0,64},{32,96},{64,128},{96,160},{128,192},{160,224},{192,0},{224,... | collective-permute-start | bytes 373256 | tf_op jit(solution)/shard_map/ppermute | solution.py:39
  69.8 7.6 %copy-start.14 = (bf16[2,72,432]{2,1,0:T(8,128)(2,1)}, bf16[2,72,432]{2,1,0:T(8,128)(2,1)S(1)}, u32[]{:S(2)}) copy-start(bf16[2,72,432]{2,1,0:T(8,128)(2,1)S(1)} %collective-permute-done.6.low_hbm) | copy-start | bytes 373252
  69.8 7.6 %copy-start.12 = (bf16[4,72,432]{2,1,0:T(8,128)(2,1)}, bf16[4,72,432]{2,1,0:T(8,128)(2,1)S(1)}, u32[]{:S(2)}) copy-start(bf16[4,72,432]{2,1,0:T(8,128)(2,1)S(1)} %collective-permute-done.5.up_hbm) | copy-start | bytes 746500
  69.8 7.6 %copy-start.13 = (bf16[4,72,432]{2,1,0:T(8,128)(2,1)}, bf16[4,72,432]{2,1,0:T(8,128)(2,1)S(1)}, u32[]{:S(2)}) copy-start(bf16[4,72,432]{2,1,0:T(8,128)(2,1)S(1)} %collective-permute-done.9.down_hbm) | copy-start | bytes 746500
  72.1 5.3 %copy-start.10 = (bf16[256,1536]{1,0:T(8,128)(2,1)}, bf16[256,1536]{1,0:T(8,128)(2,1)S(1)}, u32[]{:S(2)}) copy-start(bf16[256,1536]{1,0:T(8,128)(2,1)S(1)} %collective-permute-done.4.side_hbm) | copy-start | bytes 2359300
  72.1 0.7 copy-start.15
  72.8 4.6 %collective-permute-start.10 = (bf16[256,1536]{1,0:T(8,128)(2,1)S(1)}, bf16[256,1536]{1,0:T(8,128)(2,1)S(1)}, u32[]{:S(2)}, u32[]{:S(2)}) collective-permute-start(bf16[256,1536]{1,0:T(8,128)(2,1)S(1)} %collective-permute-done.4.side_hbm), channel_id=1, source_target_pairs={{0,16},{16,0},{1,17},{17,1},{2,18},{18,2},{3,19},{19,3},{4,20},{20... | collective-permute-start | bytes 2359304 | tf_op jit(solution)/shard_map/ppermute | solution.py:34
  77.4 0.9 copy-start.11
  91.4 47.4 %all-to-all-start.1 = ((bf16[128,32,128]{2,1,0:T(8,128)(2,1)}), bf16[128,32,128]{2,1,0:T(8,128)(2,1)S(1)}, u32[]{:S(2)}, u32[]{:S(2)}) async-start(bf16[128,32,128]{2,1,0:T(8,128)(2,1)} %get-tuple-element.38), calls=%async_computation.1 | async-start | bytes 2097152 | tf_op jit(solution)/shard_map/all_to_all | solution.py:420
  107.5 5.2 %collective-permute-start.11 = (bf16[512,1152]{1,0:T(8,128)(2,1)}, bf16[512,1152]{1,0:T(8,128)(2,1)S(1)}, u32[]{:S(2)}, u32[]{:S(2)}) collective-permute-start(bf16[512,1152]{1,0:T(8,128)(2,1)} %get-tuple-element.40), channel_id=1, source_target_pairs={{0,16},{16,0},{1,17},{17,1},{2,18},{18,2},{3,19},{19,3},{4,20},{20... | collective-permute-start | bytes 3538952 | tf_op jit(solution)/shard_map/ppermute | solution.py:34
  112.8 1.3 copy-start.1
  114.3 23.6 %collective-permute-start.12 = (bf16[256,1152]{1,0:T(8,128)(2,1)S(1)}, bf16[256,1152]{1,0:T(8,128)(2,1)S(1)}, u32[]{:S(2)}, u32[]{:S(2)}) collective-permute-start(bf16[256,1152]{1,0:T(8,128)(2,1)S(1)} %get-tuple-element.42), channel_id=1, source_target_pairs={{0,8},{8,0},{1,9},{9,1},{2,10},{10,2},{3,11},{11,3},{4,12},{12,4},... | collective-permute-start | bytes 1769480 | tf_op jit(solution)/shard_map/ppermute | solution.py:34
  139.0 24.5 %copy-start.7 = (s32[3]{0:T(128)S(1)}, s32[3]{0:T(128)}, u32[]{:S(2)}) copy-start(s32[3]{0:T(128)} %copy-done.6) | copy-start | bytes 40
  163.5 7.4 %copy-start.4 = (f32[36,1728]{1,0:T(8,128)S(1)}, f32[36,1728]{1,0:T(8,128)}, u32[]{:S(2)}) copy-start(f32[36,1728]{1,0:T(8,128)} %slow_ref.1) | copy-start | bytes 746500
  163.5 7.4 %copy-start.5 = (f32[36,1728]{1,0:T(8,128)S(1)}, f32[36,1728]{1,0:T(8,128)}, u32[]{:S(2)}) copy-start(f32[36,1728]{1,0:T(8,128)} %fast_ref.1) | copy-start | bytes 746500
  164.1 6.7 %collective-permute-start.13 = (f32[2,36,432]{2,1,0:T(8,128)S(1)}, f32[2,36,432]{2,1,0:T(8,128)S(1)}, u32[]{:S(2)}, u32[]{:S(2)}) collective-permute-start(f32[2,36,432]{2,1,0:T(8,128)S(1)} %get-tuple-element.44), channel_id=1, source_target_pairs={{0,16},{16,0},{1,17},{17,1},{2,18},{18,2},{3,19},{19,3},{4,20},{20... | collective-permute-start | bytes 373256 | tf_op jit(solution)/shard_map/ppermute | solution.py:34

commit v8 on v7

--- a/solution.py
+++ b/solution.py
@@ -47,6 +47,14 @@
     count = lax.axis_size("z")
     pairs = [(i, (count - count * (i // count)) + (i % count + count // 2) % count) for i in range(2 * count)]
     return lax.ppermute(value, ("xh", "z"), pairs)
+
+
+def corner_swap(value):
+    return lax.ppermute(value, ("c", "xl"), [(i, 3 - i) for i in range(4)])
+
+
+def flip(value, bit):
+    return lax.ppermute(value, "y", [(i, i ^ bit) for i in range(lax.axis_size("y"))])
 
 
 def modulate_table(timesteps, ada_weight):
@@ -229,14 +237,11 @@
         )
         stores[-1].start()
     height = model_width // 16
-    pieces = packed_ref.shape[0] // 16
     for owner in range(16):
         tiles = tiles_of(total_ref[owner * height : (owner + 1) * height, :])
-        each = len(tiles) // pieces
-        for piece in range(pieces):
-            packed_ref[owner * pieces + piece] = jnp.concatenate(tiles[each * piece : each * piece + each], axis=0).astype(BF16)
+        packed_ref[owner] = jnp.concatenate(tiles, axis=0).astype(BF16)
         if owner % 4 == 3:
-            part = pl.ds((owner - 3) * pieces, 4 * pieces)
+            part = pl.ds(owner - 3, 4)
             stores.append(pltpu.make_async_copy(packed_ref.at[part], packed_hbm.at[part], out_sems.at[4 + owner // 4]))
             stores[-1].start()
     for store in stores:
@@ -275,40 +280,33 @@
     out_ref[3 - place] = both_ref[...]
 
 
-def payload_kernel(parts_ref, back_ref, out_ref):
+def sum_kernel(parts_ref, out_ref):
     total = parts_ref[0].astype(F32)
     for index in range(1, parts_ref.shape[0]):
         total = total + parts_ref[index].astype(F32)
-    half = total.shape[0] // 2
-    piece = jnp.concatenate([total[:half], total[half:]], axis=1).astype(BF16)
-    width = back_ref.shape[1]
-    out_ref[:, :width] = back_ref[...]
-    for index in range(out_ref.shape[0] // half):
-        out_ref[index * half : (index + 1) * half, width:] = piece
-
-
-def rows_kernel(spot_ref, pieces_ref, own_ref, other_ref):
-    width = pieces_ref.shape[2] - 256
-    count = pieces_ref.shape[0] // 2
-    height = own_ref.shape[1]
+    out_ref[...] = total.astype(out_ref.dtype)
+
+
+def join_kernel(left_ref, right_ref, out_ref):
+    out_ref[...] = (left_ref[...].astype(F32) + right_ref[...].astype(F32)).astype(BF16)
+
+
+def rows_kernel(spot_ref, left_ref, right_ref, own_ref, other_ref):
+    total = left_ref[...].astype(F32) + right_ref[...].astype(F32)
+    height = own_ref.shape[0]
+    block = block_of([total[8 * i : 8 * i + 8] for i in range(total.shape[0] // 8)], 2 * height)
     first = spot_ref[0] < 2
-    for side in range(2):
-        tiles = []
-        for index in range(count):
-            piece = pieces_ref[side * count + index][:, width:].astype(F32)
-            tiles += [piece[:8, :128], piece[8:, :128], piece[:8, 128:], piece[8:, 128:]]
-        total = block_of(tiles, 2 * height)
-        upper, lower = total[:height], total[height:]
-        own_ref[side] = jnp.where(first, upper, lower)
-        other_ref[side] = jnp.where(first, lower, upper)
-
-
-def average_kernel(spot_ref, decay_ref, own_ref, core_ref, slow_ref, fast_ref, slow_out, fast_out):
-    quarter = own_ref.shape[2] // 3
-    first = spot_ref[0] < 2
-    own, other = [own_ref[0], own_ref[1]], [core_ref[0], core_ref[1]]
-    places = [jnp.where(first, a, b) for a, b in zip(own + other, other + own)]
-    columns = [place[:, part * quarter : (part + 1) * quarter] for part in range(3) for place in places]
+    upper, lower = block[:height], block[height:]
+    own_ref[...] = jnp.where(first, upper, lower)
+    other_ref[...] = jnp.where(first, lower, upper)
+
+
+def average_kernel(spot_ref, decay_ref, own_ref, side_ref, core_ref, both_ref, slow_ref, fast_ref, slow_out, fast_out):
+    quarter = own_ref.shape[1] // 3
+    spot = spot_ref[0]
+    values = [ref[...] for ref in (own_ref, side_ref, core_ref, both_ref)]
+    picked = [pick(spot, [values[i ^ place] for i in range(4)]) for place in range(4)]
+    columns = [picked[place][:, part * quarter : (part + 1) * quarter] for part in range(3) for place in range(4)]
     grad = jnp.concatenate(columns, axis=1) / loss_scale
     slow_out[...] = decay_ref[0] * slow_ref[...] + (1.0 - decay_ref[0]) * grad
     fast_out[...] = decay_ref[1] * fast_ref[...] + (1.0 - decay_ref[1]) * grad
@@ -342,7 +340,6 @@
     own_rows, triple = master.shape
     n_seq = lax.axis_size("xl") * lax.axis_size("y")
     n_rows = lax.axis_size("xh") * lax.axis_size("z")
-    n_y = lax.axis_size("y")
     quarter = inner // 4
     cols = 3 * quarter
     pair_rows = 2 * own_rows
@@ -382,17 +379,15 @@
     broad = lanes(width + 2 * quarter)
     to_core, to_side = call(norm_kernel, [((patches, broad), BF16)] * 2, spots, tokens, modulation, smem=1)
     from_side = swap(to_side, "xl")
+    up, low, high, down = shift(quad, -1), shift(quad[:2], -2), shift(quad[2:], 2), shift(quad, 1)
+    to_core, low = lax.optimization_barrier((to_core, low))
     from_core = swap(to_core, "c")
-    up, down, low = shift(quad, -1), shift(quad, 1), shift(quad[:2], -2)
-    upper, from_core = lax.optimization_barrier((quad[2:], from_core))
-    high = shift(upper, 2)
     from_side, up, low, high, down = lax.optimization_barrier((from_side, up, low, high, down))
     from_both = swap(from_side, "c")
 
-    pieces = n_rows * n_y
     packed, near, far = call(
         main_kernel,
-        [((pieces, 32, 128), BF16), ((2 * patches, width), BF16), ((2 * patches, width), BF16)],
+        [((n_rows, 256, 128), BF16), ((2 * patches, width), BF16), ((2 * patches, width), BF16)],
         spots, quad, up, low, high, down, to_core, from_core, from_side, from_both,
         flops=6 * 4 * patches * width * cols,
         scratch=[
@@ -402,7 +397,7 @@
             pltpu.VMEM((patches, broad), BF16),
             pltpu.VMEM((patches, broad), BF16),
             pltpu.VMEM((width, cols), BF16),
-            pltpu.VMEM((pieces, 32, 128), BF16),
+            pltpu.VMEM((n_rows, 256, 128), BF16),
             pltpu.VMEM((4, patches, width), BF16),
             pltpu.VMEM((width, cols), F32),
             pltpu.SemaphoreType.DMA((9,)),
@@ -417,19 +412,23 @@
     part, give = call(add_kernel, [((patches, width), BF16)] * 2, near, swap(far, "c"))
     back = call(norm_back_kernel, [((patches, width), BF16)], tokens, modulation, part, swap(give, "xl"))
 
-    parts = lax.all_to_all(packed, ROWS + ("y",), 0, 0, tiled=True)
-    joint = call(payload_kernel, [((patches, width + 256), BF16)], parts, back)
-    joint = lax.all_to_all(joint.reshape(n_seq, patches // n_seq, width + 256), SEQ, 0, 0, tiled=True)
-    own_grad, other_grad = call(rows_kernel, [((2, own_rows, cols), F32)] * 2, spots, joint, smem=1)
+    back = lax.all_to_all(back.reshape(n_seq, patches // n_seq, width), SEQ, 0, 0, tiled=True)
+
+    parts = lax.all_to_all(packed, ROWS, 0, 0, tiled=True)
+    piece = ((256, 128), BF16)
+    summed = call(sum_kernel, [piece], parts)
+    for bit in (1, 2):
+        summed = call(join_kernel, [piece], summed, flip(summed, bit))
+    own_grad, other_grad = call(rows_kernel, [((own_rows, cols), F32)] * 2, spots, summed, flip(summed, 4), smem=1)
     base = 1.0 - 1.0 / step_count[0].astype(F32)
     decays = jnp.stack([jnp.power(base, gamma_slow + 1.0), jnp.power(base, gamma_fast + 1.0)])
     ema_slow_next, ema_fast_next = call(
         average_kernel,
         [((own_rows, triple), F32)] * 2,
-        spots, decays, own_grad, swap(other_grad, "c"), ema_slow, ema_fast,
+        spots, decays, own_grad, swap(own_grad, "xl"), swap(other_grad, "c"), corner_swap(other_grad), ema_slow, ema_fast,
         smem=2,
     )
-    return (joint[:, :, :width].reshape(hidden.shape), ema_slow_next, ema_fast_next)
+    return (back.reshape(hidden.shape), ema_slow_next, ema_fast_next)
 
 
 def solution(mesh):

time: 173 us -> 185 us (1.069)
  blocking collectives: 24.5 us -> 0 us
  starting transfers between devices: 76.6 us -> 95.8 us
  waiting for transfers between devices: 42.1 us -> 59 us
    all_to_all x1 -> x0, blocking collectives: 24.5 us -> none  [on_device(): lax.all_to_all(joint.reshape(n_seq, patches // n_seq, width + 256), SEQ,...]
    ppermute x0 -> x4, waiting for transfers between devices: none -> 17.6 us  [the longest x3 17.6 us: flip(): lax.ppermute(value, 'y', [(i, i ^ bit) for i in range(lax.axis_size('y'))])]
    ppermute x0 -> x4, starting transfers between devices: none -> 15.6 us  [the longest x3 12.3 us: flip(): lax.ppermute(value, 'y', [(i, i ^ bit) for i in range(lax.axis_size('y'))])]
    ppermute x8 -> x9, starting transfers between devices: 28.2 us -> 32.6 us  [swap(): return lax.ppermute(value, axis, [(0, 1), (1, 0)])]
    all_to_all x1 -> x2, starting transfers between devices: 16.2 us -> 14.4 us  [the longest x1 7.23 us: on_device(): lax.all_to_all(back.reshape(n_seq, patches // n_seq, width), SEQ, 0, 0, t...]
    pallas_call x11 -> x13, Pallas kernels: 22.5 us -> 23.3 us  [call(): pl.pallas_call(kernel, out_shape=shapes, in_specs=specs, out_specs=[pl.Bl...]
    ppermute x8 -> x9, waiting for transfers between devices: 29.3 us -> 29.3 us  [swap(): return lax.ppermute(value, axis, [(0, 1), (1, 0)])]
  transfers between devices with their start and end apart: 16 -> 22, of which waited for: 8 -> 11; matrix products, arithmetic and copies ran while one was open for 1% -> 0% of each run, Pallas kernels for 2% -> 3%
where the time goes in v8:
time: 185 us; the launch traced here: 184 us
  starting transfers between devices  95.8 us (52%)
  waiting for transfers between devices  59 us (32%)
  Pallas kernels  23.3 us (13%)
  local copies, waits for them, and re-layouts  3.07 us (2%)
  between operations  2.54 us (1%)
    ppermute x9, starting transfers between devices, swap(): return lax.ppermute(value, axis, [(0, 1), (1, 0)])  32.6 us
    ppermute x9, waiting for transfers between devices, swap(): return lax.ppermute(value, axis, [(0, 1), (1, 0)])  29.3 us
    pallas_call x13, Pallas kernels, call(): pl.pallas_call(kernel, out_shape=shapes, in_specs=specs, out_specs=[pl.Bl...  23.3 us
    ppermute x5, starting transfers between devices, shift(): lax.ppermute(value, 'z', [(i, (i + away) % count) for i in range(count)])  22.3 us
    ppermute x3, waiting for transfers between devices, flip(): lax.ppermute(value, 'y', [(i, i ^ bit) for i in range(lax.axis_size('y'))])  17.6 us
    ppermute x3, starting transfers between devices, flip(): lax.ppermute(value, 'y', [(i, i ^ bit) for i in range(lax.axis_size('y'))])  12.3 us
    all_to_all x1, starting transfers between devices, on_device(): lax.all_to_all(packed.reshape(n_seq, patches // n_seq, width + loose), SE...  8.83 us
    ppermute x1, waiting for transfers between devices, both_turn(): return lax.ppermute(value, ('xh', 'z'), pairs)  8.6 us
  transfers between devices with their start and end apart: 22, of which 11 were waited for; matrix products, arithmetic and copies ran while one was open for 0% of the time, Pallas kernels for 3%

profile of v8, /device:TPU:1, one launch (start us, length us, event | category | flops | bytes accessed | tf_op | source)
XLA Modules:
  0.0 184.2 jit_solution(4252099166212489295)
XLA Ops:
  0.6 0.0 copy-start
  0.6 2.1 %shard_map.106 = bf16[256,1792]{1,0:T(8,128)(2,1)} custom-call(bf16[256,1152]{1,0:T(8,128)(2,1)} %bitcast.20, bf16[576,256]{1,0:T(8,128)(2,1)} %bitcast.21), custom_call_target="tpu_custom_call" | custom-call | bytes 1802240 | tf_op jit(solution)/shard_map/pallas_call | solution.py:321
  2.8 0.0 copy-start.3
  2.8 8.8 %all-to-all-start = ((bf16[16,16,1792]{2,1,0:T(8,128)(2,1)}), bf16[16,16,1792]{2,1,0:T(8,128)(2,1)S(1)}, u32[]{:S(2)}, u32[]{:S(2)}) async-start(bf16[16,16,1792]{2,1,0:T(8,128)(2,1)} %bitcast.18), calls=%async_computation | async-start | bytes 1835008 | tf_op jit(solution)/shard_map/all_to_all | solution.py:365
  11.6 0.1 pad_add_fusion.spot_ref
  11.7 0.9 shard_map.103
  12.6 3.7 %collective-permute-start = (bf16[36,432]{1,0:T(8,128)(2,1)S(1)}, bf16[36,432]{1,0:T(8,128)(2,1)S(1)}, u32[]{:S(2)}, u32[]{:S(2)}) collective-permute-start(bf16[36,432]{1,0:T(8,128)(2,1)S(1)} %get-tuple-element.26), channel_id=1, source_target_pairs={{0,16},{16,0},{1,17},{17,1},{2,18},{18,2},{3,19},{19,3},{4,20},{20... | collective-permute-start | bytes 93320 | tf_op jit(solution)/shard_map/ppermute | solution.py:34
  17.0 0.1 sine_convert_fusion
  17.0 0.1 collective-permute-done.theirs_ref
  17.2 0.6 shard_map.104.own_ref
  17.8 9.8 %collective-permute-start.1 = (bf16[72,432]{1,0:T(8,128)(2,1)S(1)}, bf16[72,432]{1,0:T(8,128)(2,1)S(1)}, u32[]{:S(2)}, u32[]{:S(2)}) collective-permute-start(bf16[72,432]{1,0:T(8,128)(2,1)S(1)} %shard_map.104.own_ref), channel_id=1, source_target_pairs={{0,128},{32,160},{64,192},{96,224},{128,0},{160,32},{192,64},{224,... | collective-permute-start | bytes 186632 | tf_op jit(solution)/shard_map/ppermute | solution.py:39
  27.5 4.4 %collective-permute-start.2 = (bf16[72,432]{1,0:T(8,128)(2,1)S(1)}, bf16[72,432]{1,0:T(8,128)(2,1)S(1)}, u32[]{:S(2)}, u32[]{:S(2)}) collective-permute-start(bf16[72,432]{1,0:T(8,128)(2,1)S(1)} %shard_map.104.own_ref), channel_id=1, source_target_pairs={{0,256},{256,0},{1,257},{257,1},{2,258},{258,2},{3,259},{259,3},{4... | collective-permute-start | bytes 186632 | tf_op jit(solution)/shard_map/ppermute | solution.py:34
  31.9 2.2 %collective-permute-start.3 = (bf16[72,432]{1,0:T(8,128)(2,1)S(1)}, bf16[72,432]{1,0:T(8,128)(2,1)S(1)}, u32[]{:S(2)}, u32[]{:S(2)}) collective-permute-start(bf16[72,432]{1,0:T(8,128)(2,1)S(1)} %shard_map.104.own_ref), channel_id=1, source_target_pairs={{0,384},{32,416},{64,448},{96,480},{128,256},{160,288},{192,320},{... | collective-permute-start | bytes 186632 | tf_op jit(solution)/shard_map/ppermute | solution.py:49
  34.1 0.2 fusion.mod_ref
  34.3 0.7 collective-permute-done.2.across_ref
  35.0 8.6 %collective-permute-done.3.both_ref = bf16[72,432]{1,0:T(8,128)(2,1)S(1)} collective-permute-done((bf16[72,432]{1,0:T(8,128)(2,1)S(1)}, bf16[72,432]{1,0:T(8,128)(2,1)S(1)}, u32[]{:S(2)}, u32[]{:S(2)}) %collective-permute-start.3) | collective-permute-done | bytes 62240 | tf_op jit(solution)/shard_map/ppermute | solution.py:49
  43.6 0.6 shard_map.105.near_hbm
  44.2 0.0 copy-start.2
  44.2 0.0 all-to-all-done
  44.2 1.8 shard_map.107
  46.0 2.9 %collective-permute-start.4 = (bf16[256,1536]{1,0:T(8,128)(2,1)S(1)}, bf16[256,1536]{1,0:T(8,128)(2,1)S(1)}, u32[]{:S(2)}, u32[]{:S(2)}) collective-permute-start(bf16[256,1536]{1,0:T(8,128)(2,1)S(1)} %get-tuple-element.29), channel_id=1, source_target_pairs={{0,8},{8,0},{1,9},{9,1},{2,10},{10,2},{3,11},{11,3},{4,12},{12,4},... | collective-permute-start | bytes 2359304 | tf_op jit(solution)/shard_map/ppermute | solution.py:34
  49.0 1.9 %collective-permute-start.5 = (bf16[4,72,432]{2,1,0:T(8,128)(2,1)S(1)}, bf16[4,72,432]{2,1,0:T(8,128)(2,1)S(1)}, u32[]{:S(2)}, u32[]{:S(2)}) collective-permute-start(bf16[4,72,432]{2,1,0:T(8,128)(2,1)S(1)} %shard_map.105.near_hbm), channel_id=1, source_target_pairs={{0,224},{32,0},{64,32},{96,64},{128,96},{160,128},{192,160},{224,1... | collective-permute-start | bytes 746504 | tf_op jit(solution)/shard_map/ppermute | solution.py:39
  50.9 3.4 %collective-permute-start.8 = (bf16[4,72,432]{2,1,0:T(8,128)(2,1)S(1)}, bf16[4,72,432]{2,1,0:T(8,128)(2,1)S(1)}, u32[]{:S(2)}, u32[]{:S(2)}) collective-permute-start(bf16[4,72,432]{2,1,0:T(8,128)(2,1)S(1)} %shard_map.105.near_hbm), channel_id=1, source_target_pairs={{0,32},{32,64},{64,96},{96,128},{128,160},{160,192},{192,224},{224... | collective-permute-start | bytes 746504 | tf_op jit(solution)/shard_map/ppermute | solution.py:39
  54.3 4.3 %collective-permute-start.6 = (bf16[2,72,432]{2,1,0:T(8,128)(2,1)S(1)}, bf16[2,72,432]{2,1,0:T(8,128)(2,1)S(1)}, u32[]{:S(2)}, u32[]{:S(2)}) collective-permute-start(bf16[2,72,432]{2,1,0:T(8,128)(2,1)S(1)} %get-tuple-element.48), channel_id=1, source_target_pairs={{0,192},{32,224},{64,0},{96,32},{128,64},{160,96},{192,128},{224,1... | collective-permute-start | bytes 373256 | tf_op jit(solution)/shard_map/ppermute | solution.py:39
  58.7 2.9 %collective-permute-start.7 = (bf16[2,72,432]{2,1,0:T(8,128)(2,1)S(1)}, bf16[2,72,432]{2,1,0:T(8,128)(2,1)S(1)}, u32[]{:S(2)}, u32[]{:S(2)}) collective-permute-start(bf16[2,72,432]{2,1,0:T(8,128)(2,1)S(1)} %get-tuple-element.47), channel_id=1, source_target_pairs={{0,64},{32,96},{64,128},{96,160},{128,192},{160,224},{192,0},{224,... | collective-permute-start | bytes 373256 | tf_op jit(solution)/shard_map/ppermute | solution.py:39
  61.5 3.4 %collective-permute-done.6.low_hbm = bf16[2,72,432]{2,1,0:T(8,128)(2,1)S(1)} collective-permute-done((bf16[2,72,432]{2,1,0:T(8,128)(2,1)S(1)}, bf16[2,72,432]{2,1,0:T(8,128)(2,1)S(1)}, u32[]{:S(2)}, u32[]{:S(2)}) %collective-permute-start.6) | collective-permute-done | bytes 124448 | tf_op jit(solution)/shard_map/ppermute | solution.py:39
  65.0 5.1 %collective-permute-start.9 = (bf16[256,1536]{1,0:T(8,128)(2,1)S(1)}, bf16[256,1536]{1,0:T(8,128)(2,1)S(1)}, u32[]{:S(2)}, u32[]{:S(2)}) collective-permute-start(bf16[256,1536]{1,0:T(8,128)(2,1)S(1)} %get-tuple-element.36.own_hbm), channel_id=1, source_target_pairs={{0,16},{16,0},{1,17},{17,1},{2,18},{18,2},{3,19},{19,3},{4,20},{20... | collective-permute-start | bytes 2359304 | tf_op jit(solution)/shard_map/ppermute | solution.py:34
  70.0 0.0 collective-permute-done.7.high_hbm
  70.0 0.0 copy-start.15
  70.1 0.0 collective-permute-done.8.down_hbm
  70.1 0.0 collective-permute-done.4.side_hbm
  70.1 4.1 %collective-permute-start.10 = (bf16[256,1536]{1,0:T(8,128)(2,1)S(1)}, bf16[256,1536]{1,0:T(8,128)(2,1)S(1)}, u32[]{:S(2)}, u32[]{:S(2)}) collective-permute-start(bf16[256,1536]{1,0:T(8,128)(2,1)S(1)} %collective-permute-done.4.side_hbm), channel_id=1, source_target_pairs={{0,16},{16,0},{1,17},{17,1},{2,18},{18,2},{3,19},{19,3},{4,20},{20... | collective-permute-start | bytes 2359304 | tf_op jit(solution)/shard_map/ppermute | solution.py:34
  74.3 0.0 collective-permute-done.9.core_hbm
  74.3 1.9 %collective-permute-done.10.both_hbm = bf16[256,1536]{1,0:T(8,128)(2,1)S(1)} collective-permute-done((bf16[256,1536]{1,0:T(8,128)(2,1)S(1)}, bf16[256,1536]{1,0:T(8,128)(2,1)S(1)}, u32[]{:S(2)}, u32[]{:S(2)}) %collective-permute-start.10) | collective-permute-done | bytes 786464 | tf_op jit(solution)/shard_map/ppermute | solution.py:34
  76.2 0.9 copy-done.11
  77.1 13.0 %shard_map.108 = (bf16[16,256,128]{2,1,0:T(8,128)(2,1)}, bf16[512,1152]{1,0:T(8,128)(2,1)}, bf16[512,1152]{1,0:T(8,128)(2,1)}) custom-call(s32[3]{0:T(128)} %copy-done.6, bf16[4,72,432]{2,1,0:T(8,128)(2,1)} %copy-done.2, bf16[4,72,432]{2,1,0:T(8,128)(2,1)} %copy-done.12, bf16[2,72,432]{2,1,0:T(8,128)(2,1)} %copy-done.14, bf16[2,72,432]{2,1,0:T(8,128)(2,1)} %copy-done.15, ...), custom_call_target="tpu_custom_call" | custom-call | flops 3057647616 | bytes 7548940 | tf_op jit(solution)/shard_map/pallas_call | solution.py:321
  90.2 7.2 %all-to-all-start.2 = ((bf16[16,256,128]{2,1,0:T(8,128)(2,1)}), bf16[16,256,128]{2,1,0:T(8,128)(2,1)S(1)}, u32[]{:S(2)}, u32[]{:S(2)}) async-start(bf16[16,256,128]{2,1,0:T(8,128)(2,1)} %get-tuple-element.42), calls=%async_computation.2 | async-start | bytes 2097152 | tf_op jit(solution)/shard_map/all_to_all | solution.py:417
  97.3 2.6 %collective-permute-start.11 = (bf16[512,1152]{1,0:T(8,128)(2,1)}, bf16[512,1152]{1,0:T(8,128)(2,1)S(1)}, u32[]{:S(2)}, u32[]{:S(2)}) collective-permute-start(bf16[512,1152]{1,0:T(8,128)(2,1)} %get-tuple-element.39), channel_id=1, source_target_pairs={{0,16},{16,0},{1,17},{17,1},{2,18},{18,2},{3,19},{19,3},{4,20},{20... | collective-permute-start | bytes 3538952 | tf_op jit(solution)/shard_map/ppermute | solution.py:34
  99.9 2.7 %collective-permute-done.11.got_ref = bf16[512,1152]{1,0:T(8,128)(2,1)S(1)} collective-permute-done((bf16[512,1152]{1,0:T(8,128)(2,1)}, bf16[512,1152]{1,0:T(8,128)(2,1)S(1)}, u32[]{:S(2)}, u32[]{:S(2)}) %collective-permute-start.11) | collective-permute-done | bytes 1179680 | tf_op jit(solution)/shard_map/ppermute | solution.py:34
  102.6 1.3 copy-done.1
  103.8 0.3 shard_map.109
  104.1 1.9 %collective-permute-start.12 = (bf16[256,1152]{1,0:T(8,128)(2,1)S(1)}, bf16[256,1152]{1,0:T(8,128)(2,1)S(1)}, u32[]{:S(2)}, u32[]{:S(2)}) collective-permute-start(bf16[256,1152]{1,0:T(8,128)(2,1)S(1)} %get-tuple-element.41), channel_id=1, source_target_pairs={{0,8},{8,0},{1,9},{9,1},{2,10},{10,2},{3,11},{11,3},{4,12},{12,4},... | collective-permute-start | bytes 1769480 | tf_op jit(solution)/shard_map/ppermute | solution.py:34
  106.0 20.9 %collective-permute-done.12.refs_1_ = bf16[256,1152]{1,0:T(8,128)(2,1)S(1)} collective-permute-done((bf16[256,1152]{1,0:T(8,128)(2,1)S(1)}, bf16[256,1152]{1,0:T(8,128)(2,1)S(1)}, u32[]{:S(2)}, u32[]{:S(2)}) %collective-permute-start.12) | collective-permute-done | bytes 589856 | tf_op jit(solution)/shard_map/ppermute | solution.py:34
  126.9 1.7 shard_map.110
  128.6 0.0 all-to-all-done.2.parts_ref
  128.6 7.2 %all-to-all-start.1 = ((bf16[16,16,1152]{2,1,0:T(8,128)(2,1)}), bf16[16,16,1152]{2,1,0:T(8,128)(2,1)S(1)}, u32[]{:S(2)}, u32[]{:S(2)}) async-start(bf16[16,16,1152]{2,1,0:T(8,128)(2,1)} %bitcast.10), calls=%async_computation.1 | async-start | bytes 1179648 | tf_op jit(solution)/shard_map/all_to_all | solution.py:415
  135.8 0.1 shard_map.111.left_ref
  136.0 3.3 %collective-permute-start.13 = (bf16[256,128]{1,0:T(8,128)(2,1)S(1)}, bf16[256,128]{1,0:T(8,128)(2,1)S(1)}, u32[]{:S(2)}, u32[]{:S(2)}) collective-permute-start(bf16[256,128]{1,0:T(8,128)(2,1)S(1)} %shard_map.111.left_ref), channel_id=1, source_target_pairs={{0,1},{1,0},{2,3},{3,2},{4,5},{5,4},{6,7},{7,6},{8,9},{9,8},{10,11... | collective-permute-start | bytes 196616 | tf_op jit(solution)/shard_map/ppermute | solution.py:57
  139.3 12.0 %collective-permute-done.13.right_ref = bf16[256,128]{1,0:T(8,128)(2,1)S(1)} collective-permute-done((bf16[256,128]{1,0:T(8,128)(2,1)S(1)}, bf16[256,128]{1,0:T(8,128)(2,1)S(1)}, u32[]{:S(2)}, u32[]{:S(2)}) %collective-permute-start.13) | collective-permute-done | bytes 65568 | tf_op jit(solution)/shard_map/ppermute | solution.py:57
  151.3 3.0 %collective-permute-start.14 = (bf16[256,128]{1,0:T(8,128)(2,1)S(1)}, bf16[256,128]{1,0:T(8,128)(2,1)S(1)}, u32[]{:S(2)}, u32[]{:S(2)}) collective-permute-start(bf16[256,128]{1,0:T(8,128)(2,1)S(1)} %shard_map.112.left_ref), channel_id=1, source_target_pairs={{0,2},{1,3},{2,0},{3,1},{4,6},{5,7},{6,4},{7,5},{8,10},{9,11},{10,... | collective-permute-start | bytes 196616 | tf_op jit(solution)/shard_map/ppermute | solution.py:57
  154.3 3.6 %collective-permute-done.14.right_ref = bf16[256,128]{1,0:T(8,128)(2,1)S(1)} collective-permute-done((bf16[256,128]{1,0:T(8,128)(2,1)S(1)}, bf16[256,128]{1,0:T(8,128)(2,1)S(1)}, u32[]{:S(2)}, u32[]{:S(2)}) %collective-permute-start.14) | collective-permute-done | bytes 65568 | tf_op jit(solution)/shard_map/ppermute | solution.py:57
  157.9 6.0 %collective-permute-start.15 = (bf16[256,128]{1,0:T(8,128)(2,1)S(1)}, bf16[256,128]{1,0:T(8,128)(2,1)S(1)}, u32[]{:S(2)}, u32[]{:S(2)}) collective-permute-start(bf16[256,128]{1,0:T(8,128)(2,1)S(1)} %shard_map.113.left_ref), channel_id=1, source_target_pairs={{0,4},{1,5},{2,6},{3,7},{4,0},{5,1},{6,2},{7,3},{8,12},{9,13},{10,... | collective-permute-start | bytes 196616 | tf_op jit(solution)/shard_map/ppermute | solution.py:57
  164.7 2.1 %collective-permute-done.15.right_ref = bf16[256,128]{1,0:T(8,128)(2,1)S(1)} collective-permute-done((bf16[256,128]{1,0:T(8,128)(2,1)S(1)}, bf16[256,128]{1,0:T(8,128)(2,1)S(1)}, u32[]{:S(2)}, u32[]{:S(2)}) %collective-permute-start.15) | collective-permute-done | bytes 65568 | tf_op jit(solution)/shard_map/ppermute | solution.py:57
  166.8 0.6 shard_map.114
  167.4 5.9 %collective-permute-start.17 = (f32[36,432]{1,0:T(8,128)S(1)}, f32[36,432]{1,0:T(8,128)S(1)}, u32[]{:S(2)}, u32[]{:S(2)}) collective-permute-start(f32[36,432]{1,0:T(8,128)S(1)} %get-tuple-element.44), channel_id=1, source_target_pairs={{0,16},{16,0},{1,17},{17,1},{2,18},{18,2},{3,19},{19,3},{4,20},{20... | collective-permute-start | bytes 186632 | tf_op jit(solution)/shard_map/ppermute | solution.py:34
  173.3 3.3 %collective-permute-start.18 = (f32[36,432]{1,0:T(8,128)S(1)}, f32[36,432]{1,0:T(8,128)S(1)}, u32[]{:S(2)}, u32[]{:S(2)}) collective-permute-start(f32[36,432]{1,0:T(8,128)S(1)} %get-tuple-element.44), channel_id=1, source_target_pairs={{0,24},{8,16},{16,8},{24,0},{1,25},{9,17},{17,9},{25,1},{2,26},{10... | collective-permute-start | bytes 186632 | tf_op jit(solution)/shard_map/ppermute | solution.py:53
  176.6 2.0 %collective-permute-start.16 = (f32[36,432]{1,0:T(8,128)S(1)}, f32[36,432]{1,0:T(8,128)S(1)}, u32[]{:S(2)}, u32[]{:S(2)}) collective-permute-start(f32[36,432]{1,0:T(8,128)S(1)} %get-tuple-element.43.own_ref), channel_id=1, source_target_pairs={{0,8},{8,0},{1,9},{9,1},{2,10},{10,2},{3,11},{11,3},{4,12},{12,4},... | collective-permute-start | bytes 186632 | tf_op jit(solution)/shard_map/ppermute | solution.py:34
  178.6 0.1 pad_maximum_fusion.decay_ref
  178.7 3.1 %collective-permute-done.16.side_ref = f32[36,432]{1,0:T(8,128)S(1)} collective-permute-done((f32[36,432]{1,0:T(8,128)S(1)}, f32[36,432]{1,0:T(8,128)S(1)}, u32[]{:S(2)}, u32[]{:S(2)}) %collective-permute-start.16) | collective-permute-done | bytes 62240 | tf_op jit(solution)/shard_map/ppermute | solution.py:34
  181.8 0.0 collective-permute-done.17.core_ref
  181.8 0.0 collective-permute-done.18.both_ref
  181.8 1.5 shard_map.115
  183.4 0.0 all-to-all-done.1
  183.4 0.8 copy.14
  (31 shorter events, 0.1 us)
Async XLA Ops:
  0.6 33.4 %copy-start = (bf16[128,2304]{1,0:T(8,128)(2,1)S(1)}, bf16[128,2304]{1,0:T(8,128)(2,1)}, u32[]{:S(2)}) copy-start(bf16[128,2304]{1,0:T(8,128)(2,1)} %param.10) | copy-start | bytes 1769476
  2.8 8.9 %copy-start.3 = (f32[36,1728]{1,0:T(8,128)S(1)}, f32[36,1728]{1,0:T(8,128)}, u32[]{:S(2)}) copy-start(f32[36,1728]{1,0:T(8,128)} %master_ref.1) | copy-start | bytes 746500
  2.8 41.4 %all-to-all-start = ((bf16[16,16,1792]{2,1,0:T(8,128)(2,1)}), bf16[16,16,1792]{2,1,0:T(8,128)(2,1)S(1)}, u32[]{:S(2)}, u32[]{:S(2)}) async-start(bf16[16,16,1792]{2,1,0:T(8,128)(2,1)} %bitcast.18), calls=%async_computation | async-start | bytes 1835008 | tf_op jit(solution)/shard_map/all_to_all | solution.py:365
  11.7 34.3 %copy-start.6 = (s32[3]{0:T(128)}, s32[3]{0:T(128)S(1)}, u32[]{:S(2)}) copy-start(s32[3]{0:T(128)S(1)} %pad_add_fusion.spot_ref) | copy-start | bytes 40
  12.6 4.6 %collective-permute-start = (bf16[36,432]{1,0:T(8,128)(2,1)S(1)}, bf16[36,432]{1,0:T(8,128)(2,1)S(1)}, u32[]{:S(2)}, u32[]{:S(2)}) collective-permute-start(bf16[36,432]{1,0:T(8,128)(2,1)S(1)} %get-tuple-element.26), channel_id=1, source_target_pairs={{0,16},{16,0},{1,17},{17,1},{2,18},{18,2},{3,19},{19,3},{4,20},{20... | collective-permute-start | bytes 93320 | tf_op jit(solution)/shard_map/ppermute | solution.py:34
  17.8 16.6 %collective-permute-start.1 = (bf16[72,432]{1,0:T(8,128)(2,1)S(1)}, bf16[72,432]{1,0:T(8,128)(2,1)S(1)}, u32[]{:S(2)}, u32[]{:S(2)}) collective-permute-start(bf16[72,432]{1,0:T(8,128)(2,1)S(1)} %shard_map.104.own_ref), channel_id=1, source_target_pairs={{0,128},{32,160},{64,192},{96,224},{128,0},{160,32},{192,64},{224,... | collective-permute-start | bytes 186632 | tf_op jit(solution)/shard_map/ppermute | solution.py:39
  27.5 7.5 %collective-permute-start.2 = (bf16[72,432]{1,0:T(8,128)(2,1)S(1)}, bf16[72,432]{1,0:T(8,128)(2,1)S(1)}, u32[]{:S(2)}, u32[]{:S(2)}) collective-permute-start(bf16[72,432]{1,0:T(8,128)(2,1)S(1)} %shard_map.104.own_ref), channel_id=1, source_target_pairs={{0,256},{256,0},{1,257},{257,1},{2,258},{258,2},{3,259},{259,3},{4... | collective-permute-start | bytes 186632 | tf_op jit(solution)/shard_map/ppermute | solution.py:34
  31.9 11.7 %collective-permute-start.3 = (bf16[72,432]{1,0:T(8,128)(2,1)S(1)}, bf16[72,432]{1,0:T(8,128)(2,1)S(1)}, u32[]{:S(2)}, u32[]{:S(2)}) collective-permute-start(bf16[72,432]{1,0:T(8,128)(2,1)S(1)} %shard_map.104.own_ref), channel_id=1, source_target_pairs={{0,384},{32,416},{64,448},{96,480},{128,256},{160,288},{192,320},{... | collective-permute-start | bytes 186632 | tf_op jit(solution)/shard_map/ppermute | solution.py:49
  44.2 32.0 %copy-start.2 = (bf16[4,72,432]{2,1,0:T(8,128)(2,1)}, bf16[4,72,432]{2,1,0:T(8,128)(2,1)S(1)}, u32[]{:S(2)}) copy-start(bf16[4,72,432]{2,1,0:T(8,128)(2,1)S(1)} %shard_map.105.near_hbm) | copy-start | bytes 746500
  46.0 30.1 %copy-start.8 = (bf16[256,1536]{1,0:T(8,128)(2,1)}, bf16[256,1536]{1,0:T(8,128)(2,1)S(1)}, u32[]{:S(2)}) copy-start(bf16[256,1536]{1,0:T(8,128)(2,1)S(1)} %get-tuple-element.36.own_hbm) | copy-start | bytes 2359300
  46.0 24.1 %collective-permute-start.4 = (bf16[256,1536]{1,0:T(8,128)(2,1)S(1)}, bf16[256,1536]{1,0:T(8,128)(2,1)S(1)}, u32[]{:S(2)}, u32[]{:S(2)}) collective-permute-start(bf16[256,1536]{1,0:T(8,128)(2,1)S(1)} %get-tuple-element.29), channel_id=1, source_target_pairs={{0,8},{8,0},{1,9},{9,1},{2,10},{10,2},{3,11},{11,3},{4,12},{12,4},... | collective-permute-start | bytes 2359304 | tf_op jit(solution)/shard_map/ppermute | solution.py:34
  49.0 21.1 %collective-permute-start.5 = (bf16[4,72,432]{2,1,0:T(8,128)(2,1)S(1)}, bf16[4,72,432]{2,1,0:T(8,128)(2,1)S(1)}, u32[]{:S(2)}, u32[]{:S(2)}) collective-permute-start(bf16[4,72,432]{2,1,0:T(8,128)(2,1)S(1)} %shard_map.105.near_hbm), channel_id=1, source_target_pairs={{0,224},{32,0},{64,32},{96,64},{128,96},{160,128},{192,160},{224,1... | collective-permute-start | bytes 746504 | tf_op jit(solution)/shard_map/ppermute | solution.py:39
  50.9 19.2 %collective-permute-start.8 = (bf16[4,72,432]{2,1,0:T(8,128)(2,1)S(1)}, bf16[4,72,432]{2,1,0:T(8,128)(2,1)S(1)}, u32[]{:S(2)}, u32[]{:S(2)}) collective-permute-start(bf16[4,72,432]{2,1,0:T(8,128)(2,1)S(1)} %shard_map.105.near_hbm), channel_id=1, source_target_pairs={{0,32},{32,64},{64,96},{96,128},{128,160},{160,192},{192,224},{224... | collective-permute-start | bytes 746504 | tf_op jit(solution)/shard_map/ppermute | solution.py:39
  54.3 10.7 %collective-permute-start.6 = (bf16[2,72,432]{2,1,0:T(8,128)(2,1)S(1)}, bf16[2,72,432]{2,1,0:T(8,128)(2,1)S(1)}, u32[]{:S(2)}, u32[]{:S(2)}) collective-permute-start(bf16[2,72,432]{2,1,0:T(8,128)(2,1)S(1)} %get-tuple-element.48), channel_id=1, source_target_pairs={{0,192},{32,224},{64,0},{96,32},{128,64},{160,96},{192,128},{224,1... | collective-permute-start | bytes 373256 | tf_op jit(solution)/shard_map/ppermute | solution.py:39
  58.7 11.4 %collective-permute-start.7 = (bf16[2,72,432]{2,1,0:T(8,128)(2,1)S(1)}, bf16[2,72,432]{2,1,0:T(8,128)(2,1)S(1)}, u32[]{:S(2)}, u32[]{:S(2)}) collective-permute-start(bf16[2,72,432]{2,1,0:T(8,128)(2,1)S(1)} %get-tuple-element.47), channel_id=1, source_target_pairs={{0,64},{32,96},{64,128},{96,160},{128,192},{160,224},{192,0},{224,... | collective-permute-start | bytes 373256 | tf_op jit(solution)/shard_map/ppermute | solution.py:39
  65.0 11.2 %copy-start.14 = (bf16[2,72,432]{2,1,0:T(8,128)(2,1)}, bf16[2,72,432]{2,1,0:T(8,128)(2,1)S(1)}, u32[]{:S(2)}) copy-start(bf16[2,72,432]{2,1,0:T(8,128)(2,1)S(1)} %collective-permute-done.6.low_hbm) | copy-start | bytes 373252
  65.0 9.3 %collective-permute-start.9 = (bf16[256,1536]{1,0:T(8,128)(2,1)S(1)}, bf16[256,1536]{1,0:T(8,128)(2,1)S(1)}, u32[]{:S(2)}, u32[]{:S(2)}) collective-permute-start(bf16[256,1536]{1,0:T(8,128)(2,1)S(1)} %get-tuple-element.36.own_hbm), channel_id=1, source_target_pairs={{0,16},{16,0},{1,17},{17,1},{2,18},{18,2},{3,19},{19,3},{4,20},{20... | collective-permute-start | bytes 2359304 | tf_op jit(solution)/shard_map/ppermute | solution.py:34
  70.0 4.2 %copy-start.15 = (bf16[2,72,432]{2,1,0:T(8,128)(2,1)}, bf16[2,72,432]{2,1,0:T(8,128)(2,1)S(1)}, u32[]{:S(2)}) copy-start(bf16[2,72,432]{2,1,0:T(8,128)(2,1)S(1)} %collective-permute-done.7.high_hbm) | copy-start | bytes 373252
  70.1 6.1 %copy-start.12 = (bf16[4,72,432]{2,1,0:T(8,128)(2,1)}, bf16[4,72,432]{2,1,0:T(8,128)(2,1)S(1)}, u32[]{:S(2)}) copy-start(bf16[4,72,432]{2,1,0:T(8,128)(2,1)S(1)} %collective-permute-done.5.up_hbm) | copy-start | bytes 746500
  70.1 6.1 %copy-start.13 = (bf16[4,72,432]{2,1,0:T(8,128)(2,1)}, bf16[4,72,432]{2,1,0:T(8,128)(2,1)S(1)}, u32[]{:S(2)}) copy-start(bf16[4,72,432]{2,1,0:T(8,128)(2,1)S(1)} %collective-permute-done.8.down_hbm) | copy-start | bytes 746500
  70.1 6.1 %copy-start.9 = (bf16[256,1536]{1,0:T(8,128)(2,1)}, bf16[256,1536]{1,0:T(8,128)(2,1)S(1)}, u32[]{:S(2)}) copy-start(bf16[256,1536]{1,0:T(8,128)(2,1)S(1)} %collective-permute-done.4.side_hbm) | copy-start | bytes 2359300
  70.1 6.0 %collective-permute-start.10 = (bf16[256,1536]{1,0:T(8,128)(2,1)S(1)}, bf16[256,1536]{1,0:T(8,128)(2,1)S(1)}, u32[]{:S(2)}, u32[]{:S(2)}) collective-permute-start(bf16[256,1536]{1,0:T(8,128)(2,1)S(1)} %collective-permute-done.4.side_hbm), channel_id=1, source_target_pairs={{0,16},{16,0},{1,17},{17,1},{2,18},{18,2},{3,19},{19,3},{4,20},{20... | collective-permute-start | bytes 2359304 | tf_op jit(solution)/shard_map/ppermute | solution.py:34
  74.3 1.9 %copy-start.10 = (bf16[256,1536]{1,0:T(8,128)(2,1)}, bf16[256,1536]{1,0:T(8,128)(2,1)S(1)}, u32[]{:S(2)}) copy-start(bf16[256,1536]{1,0:T(8,128)(2,1)S(1)} %collective-permute-done.9.core_hbm) | copy-start | bytes 2359300
  76.2 0.9 copy-start.11
  90.2 38.4 %all-to-all-start.2 = ((bf16[16,256,128]{2,1,0:T(8,128)(2,1)}), bf16[16,256,128]{2,1,0:T(8,128)(2,1)S(1)}, u32[]{:S(2)}, u32[]{:S(2)}) async-start(bf16[16,256,128]{2,1,0:T(8,128)(2,1)} %get-tuple-element.42), calls=%async_computation.2 | async-start | bytes 2097152 | tf_op jit(solution)/shard_map/all_to_all | solution.py:417
  97.3 5.2 %collective-permute-start.11 = (bf16[512,1152]{1,0:T(8,128)(2,1)}, bf16[512,1152]{1,0:T(8,128)(2,1)S(1)}, u32[]{:S(2)}, u32[]{:S(2)}) collective-permute-start(bf16[512,1152]{1,0:T(8,128)(2,1)} %get-tuple-element.39), channel_id=1, source_target_pairs={{0,16},{16,0},{1,17},{17,1},{2,18},{18,2},{3,19},{19,3},{4,20},{20... | collective-permute-start | bytes 3538952 | tf_op jit(solution)/shard_map/ppermute | solution.py:34
  102.6 1.3 copy-start.1
  104.1 22.8 %collective-permute-start.12 = (bf16[256,1152]{1,0:T(8,128)(2,1)S(1)}, bf16[256,1152]{1,0:T(8,128)(2,1)S(1)}, u32[]{:S(2)}, u32[]{:S(2)}) collective-permute-start(bf16[256,1152]{1,0:T(8,128)(2,1)S(1)} %get-tuple-element.41), channel_id=1, source_target_pairs={{0,8},{8,0},{1,9},{9,1},{2,10},{10,2},{3,11},{11,3},{4,12},{12,4},... | collective-permute-start | bytes 1769480 | tf_op jit(solution)/shard_map/ppermute | solution.py:34
  128.6 38.2 %copy-start.7 = (s32[3]{0:T(128)S(1)}, s32[3]{0:T(128)}, u32[]{:S(2)}) copy-start(s32[3]{0:T(128)} %copy-done.6) | copy-start | bytes 40
  128.6 53.2 %copy-start.4 = (f32[36,1728]{1,0:T(8,128)S(1)}, f32[36,1728]{1,0:T(8,128)}, u32[]{:S(2)}) copy-start(f32[36,1728]{1,0:T(8,128)} %slow_ref.1) | copy-start | bytes 746500
  128.6 53.2 %copy-start.5 = (f32[36,1728]{1,0:T(8,128)S(1)}, f32[36,1728]{1,0:T(8,128)}, u32[]{:S(2)}) copy-start(f32[36,1728]{1,0:T(8,128)} %fast_ref.1) | copy-start | bytes 746500
  128.6 54.8 %all-to-all-start.1 = ((bf16[16,16,1152]{2,1,0:T(8,128)(2,1)}), bf16[16,16,1152]{2,1,0:T(8,128)(2,1)S(1)}, u32[]{:S(2)}, u32[]{:S(2)}) async-start(bf16[16,16,1152]{2,1,0:T(8,128)(2,1)} %bitcast.10), calls=%async_computation.1 | async-start | bytes 1179648 | tf_op jit(solution)/shard_map/all_to_all | solution.py:415
  136.0 15.2 %collective-permute-start.13 = (bf16[256,128]{1,0:T(8,128)(2,1)S(1)}, bf16[256,128]{1,0:T(8,128)(2,1)S(1)}, u32[]{:S(2)}, u32[]{:S(2)}) collective-permute-start(bf16[256,128]{1,0:T(8,128)(2,1)S(1)} %shard_map.111.left_ref), channel_id=1, source_target_pairs={{0,1},{1,0},{2,3},{3,2},{4,5},{5,4},{6,7},{7,6},{8,9},{9,8},{10,11... | collective-permute-start | bytes 196616 | tf_op jit(solution)/shard_map/ppermute | solution.py:57
  151.3 6.6 %collective-permute-start.14 = (bf16[256,128]{1,0:T(8,128)(2,1)S(1)}, bf16[256,128]{1,0:T(8,128)(2,1)S(1)}, u32[]{:S(2)}, u32[]{:S(2)}) collective-permute-start(bf16[256,128]{1,0:T(8,128)(2,1)S(1)} %shard_map.112.left_ref), channel_id=1, source_target_pairs={{0,2},{1,3},{2,0},{3,1},{4,6},{5,7},{6,4},{7,5},{8,10},{9,11},{10,... | collective-permute-start | bytes 196616 | tf_op jit(solution)/shard_map/ppermute | solution.py:57
  157.9 8.9 %collective-permute-start.15 = (bf16[256,128]{1,0:T(8,128)(2,1)S(1)}, bf16[256,128]{1,0:T(8,128)(2,1)S(1)}, u32[]{:S(2)}, u32[]{:S(2)}) collective-permute-start(bf16[256,128]{1,0:T(8,128)(2,1)S(1)} %shard_map.113.left_ref), channel_id=1, source_target_pairs={{0,4},{1,5},{2,6},{3,7},{4,0},{5,1},{6,2},{7,3},{8,12},{9,13},{10,... | collective-permute-start | bytes 196616 | tf_op jit(solution)/shard_map/ppermute | solution.py:57
  167.4 14.3 %collective-permute-start.17 = (f32[36,432]{1,0:T(8,128)S(1)}, f32[36,432]{1,0:T(8,128)S(1)}, u32[]{:S(2)}, u32[]{:S(2)}) collective-permute-start(f32[36,432]{1,0:T(8,128)S(1)} %get-tuple-element.44), channel_id=1, source_target_pairs={{0,16},{16,0},{1,17},{17,1},{2,18},{18,2},{3,19},{19,3},{4,20},{20... | collective-permute-start | bytes 186632 | tf_op jit(solution)/shard_map/ppermute | solution.py:34
  173.3 8.5 %collective-permute-start.18 = (f32[36,432]{1,0:T(8,128)S(1)}, f32[36,432]{1,0:T(8,128)S(1)}, u32[]{:S(2)}, u32[]{:S(2)}) collective-permute-start(f32[36,432]{1,0:T(8,128)S(1)} %get-tuple-element.44), channel_id=1, source_target_pairs={{0,24},{8,16},{16,8},{24,0},{1,25},{9,17},{17,9},{25,1},{2,26},{10... | collective-permute-start | bytes 186632 | tf_op jit(solution)/shard_map/ppermute | solution.py:53
  176.6 5.2 %collective-permute-start.16 = (f32[36,432]{1,0:T(8,128)S(1)}, f32[36,432]{1,0:T(8,128)S(1)}, u32[]{:S(2)}, u32[]{:S(2)}) collective-permute-start(f32[36,432]{1,0:T(8,128)S(1)} %get-tuple-element.43.own_ref), channel_id=1, source_target_pairs={{0,8},{8,0},{1,9},{9,1},{2,10},{10,2},{3,11},{11,3},{4,12},{12,4},... | collective-permute-start | bytes 186632 | tf_op jit(solution)/shard_map/ppermute | solution.py:34

commit v9 on v7

--- a/solution.py
+++ b/solution.py
@@ -382,10 +382,9 @@
     broad = lanes(width + 2 * quarter)
     to_core, to_side = call(norm_kernel, [((patches, broad), BF16)] * 2, spots, tokens, modulation, smem=1)
     from_side = swap(to_side, "xl")
+    up, low, high, down = shift(quad, -1), shift(quad[:2], -2), shift(quad[2:], 2), shift(quad, 1)
+    to_core, low = lax.optimization_barrier((to_core, low))
     from_core = swap(to_core, "c")
-    up, down, low = shift(quad, -1), shift(quad, 1), shift(quad[:2], -2)
-    upper, from_core = lax.optimization_barrier((quad[2:], from_core))
-    high = shift(upper, 2)
     from_side, up, low, high, down = lax.optimization_barrier((from_side, up, low, high, down))
     from_both = swap(from_side, "c")
 

time: 173 us -> 170 us (0.983)
  waiting for transfers between devices: 42.1 us -> 39.1 us
    ppermute x8, waiting for transfers between devices: 29.3 us -> 27 us  [swap(): return lax.ppermute(value, axis, [(0, 1), (1, 0)])]
    all_to_all x1, starting transfers between devices: 16.2 us -> 14.3 us  [on_device(): parts = lax.all_to_all(packed, ROWS + ('y',), 0, 0, tiled=True)]
  transfers between devices with their start and end apart: 16 -> 16, of which waited for: 8 -> 7; matrix products, arithmetic and copies ran while one was open for 1% -> 1% of each run, Pallas kernels for 2% -> 2%
where the time goes in v9:
time: 170 us; the launch traced here: 169 us
  starting transfers between devices  77.2 us (45%)
  waiting for transfers between devices  39.1 us (23%)
  blocking collectives  24.5 us (14%)
  Pallas kernels  22.5 us (13%)
  local copies, waits for them, and re-layouts  3.11 us (2%)
  between operations  2.49 us (1%)
    ppermute x8, starting transfers between devices, swap(): return lax.ppermute(value, axis, [(0, 1), (1, 0)])  29.7 us
    ppermute x8, waiting for transfers between devices, swap(): return lax.ppermute(value, axis, [(0, 1), (1, 0)])  27 us
    all_to_all x1, blocking collectives, on_device(): lax.all_to_all(joint.reshape(n_seq, patches // n_seq, width + 256), SEQ,...  24.5 us
    pallas_call x11, Pallas kernels, call(): pl.pallas_call(kernel, out_shape=shapes, in_specs=specs, out_specs=[pl.Bl...  22.5 us
    ppermute x5, starting transfers between devices, shift(): lax.ppermute(value, 'z', [(i, (i + away) % count) for i in range(count)])  22.3 us
    all_to_all x1, starting transfers between devices, on_device(): parts = lax.all_to_all(packed, ROWS + ('y',), 0, 0, tiled=True)  14.3 us
    all_to_all x1, starting transfers between devices, on_device(): lax.all_to_all(packed.reshape(n_seq, patches // n_seq, width + loose), SE...  8.83 us
    ppermute x1, waiting for transfers between devices, both_turn(): return lax.ppermute(value, ('xh', 'z'), pairs)  8.6 us
  transfers between devices with their start and end apart: 16, of which 7 were waited for; matrix products, arithmetic and copies ran while one was open for 1% of the time, Pallas kernels for 2%

profile of v9, /device:TPU:1, one launch (start us, length us, event | category | flops | bytes accessed | tf_op | source)
XLA Modules:
  0.0 169.3 jit_solution(10112789792329050429)
XLA Ops:
  0.6 0.0 copy-start
  0.6 2.2 %shard_map.106 = bf16[256,1792]{1,0:T(8,128)(2,1)} custom-call(bf16[256,1152]{1,0:T(8,128)(2,1)} %bitcast.20, bf16[576,256]{1,0:T(8,128)(2,1)} %bitcast.22), custom_call_target="tpu_custom_call" | custom-call | bytes 1802240 | tf_op jit(solution)/shard_map/pallas_call | solution.py:323
  2.8 0.0 copy-start.3
  2.8 8.8 %all-to-all-start = ((bf16[16,16,1792]{2,1,0:T(8,128)(2,1)}), bf16[16,16,1792]{2,1,0:T(8,128)(2,1)S(1)}, u32[]{:S(2)}, u32[]{:S(2)}) async-start(bf16[16,16,1792]{2,1,0:T(8,128)(2,1)} %bitcast.19), calls=%async_computation | async-start | bytes 1835008 | tf_op jit(solution)/shard_map/all_to_all | solution.py:368
  11.7 0.1 pad_add_fusion.spot_ref
  11.8 0.9 shard_map.103
  12.6 3.7 %collective-permute-start = (bf16[36,432]{1,0:T(8,128)(2,1)S(1)}, bf16[36,432]{1,0:T(8,128)(2,1)S(1)}, u32[]{:S(2)}, u32[]{:S(2)}) collective-permute-start(bf16[36,432]{1,0:T(8,128)(2,1)S(1)} %get-tuple-element.26), channel_id=1, source_target_pairs={{0,16},{16,0},{1,17},{17,1},{2,18},{18,2},{3,19},{19,3},{4,20},{20... | collective-permute-start | bytes 93320 | tf_op jit(solution)/shard_map/ppermute | solution.py:34
  17.0 0.1 sine_convert_fusion
  17.1 0.1 collective-permute-done.theirs_ref
  17.2 0.6 shard_map.104.own_ref
  17.8 9.8 %collective-permute-start.1 = (bf16[72,432]{1,0:T(8,128)(2,1)S(1)}, bf16[72,432]{1,0:T(8,128)(2,1)S(1)}, u32[]{:S(2)}, u32[]{:S(2)}) collective-permute-start(bf16[72,432]{1,0:T(8,128)(2,1)S(1)} %shard_map.104.own_ref), channel_id=1, source_target_pairs={{0,128},{32,160},{64,192},{96,224},{128,0},{160,32},{192,64},{224,... | collective-permute-start | bytes 186632 | tf_op jit(solution)/shard_map/ppermute | solution.py:39
  27.6 4.4 %collective-permute-start.2 = (bf16[72,432]{1,0:T(8,128)(2,1)S(1)}, bf16[72,432]{1,0:T(8,128)(2,1)S(1)}, u32[]{:S(2)}, u32[]{:S(2)}) collective-permute-start(bf16[72,432]{1,0:T(8,128)(2,1)S(1)} %shard_map.104.own_ref), channel_id=1, source_target_pairs={{0,256},{256,0},{1,257},{257,1},{2,258},{258,2},{3,259},{259,3},{4... | collective-permute-start | bytes 186632 | tf_op jit(solution)/shard_map/ppermute | solution.py:34
  31.9 2.2 %collective-permute-start.3 = (bf16[72,432]{1,0:T(8,128)(2,1)S(1)}, bf16[72,432]{1,0:T(8,128)(2,1)S(1)}, u32[]{:S(2)}, u32[]{:S(2)}) collective-permute-start(bf16[72,432]{1,0:T(8,128)(2,1)S(1)} %shard_map.104.own_ref), channel_id=1, source_target_pairs={{0,384},{32,416},{64,448},{96,480},{128,256},{160,288},{192,320},{... | collective-permute-start | bytes 186632 | tf_op jit(solution)/shard_map/ppermute | solution.py:49
  34.1 0.0 copy-done
  34.1 0.2 fusion.mod_ref
  34.3 0.0 collective-permute-done.1.far_ref
  34.3 0.7 collective-permute-done.2.across_ref
  35.0 8.6 %collective-permute-done.3.both_ref = bf16[72,432]{1,0:T(8,128)(2,1)S(1)} collective-permute-done((bf16[72,432]{1,0:T(8,128)(2,1)S(1)}, bf16[72,432]{1,0:T(8,128)(2,1)S(1)}, u32[]{:S(2)}, u32[]{:S(2)}) %collective-permute-start.3) | collective-permute-done | bytes 62240 | tf_op jit(solution)/shard_map/ppermute | solution.py:49
  43.6 0.6 shard_map.105.near_hbm
  44.2 0.0 copy-start.2
  44.2 0.0 all-to-all-done
  44.2 1.8 %shard_map.107 = (bf16[256,1536]{1,0:T(8,128)(2,1)S(1)}, bf16[256,1536]{1,0:T(8,128)(2,1)S(1)}) custom-call(s32[3]{0:T(128)S(1)} %pad_add_fusion.spot_ref, bf16[256,1792]{1,0:T(8,128)(2,1)S(1)} %bitcast.16, f32[1,2304]{1,0:T(1,128)S(1)} %fusion.mod_ref), custom_call_target="tpu_custom_call" | custom-call | bytes 2499596 | tf_op jit(solution)/shard_map/pallas_call | solution.py:323
  46.0 0.0 copy-done.6
  46.1 0.0 copy-start.8
  46.1 2.9 %collective-permute-start.4 = (bf16[256,1536]{1,0:T(8,128)(2,1)S(1)}, bf16[256,1536]{1,0:T(8,128)(2,1)S(1)}, u32[]{:S(2)}, u32[]{:S(2)}) collective-permute-start(bf16[256,1536]{1,0:T(8,128)(2,1)S(1)} %get-tuple-element.29), channel_id=1, source_target_pairs={{0,8},{8,0},{1,9},{9,1},{2,10},{10,2},{3,11},{11,3},{4,12},{12,4},... | collective-permute-start | bytes 2359304 | tf_op jit(solution)/shard_map/ppermute | solution.py:34
  49.0 1.9 %collective-permute-start.5 = (bf16[4,72,432]{2,1,0:T(8,128)(2,1)S(1)}, bf16[4,72,432]{2,1,0:T(8,128)(2,1)S(1)}, u32[]{:S(2)}, u32[]{:S(2)}) collective-permute-start(bf16[4,72,432]{2,1,0:T(8,128)(2,1)S(1)} %shard_map.105.near_hbm), channel_id=1, source_target_pairs={{0,224},{32,0},{64,32},{96,64},{128,96},{160,128},{192,160},{224,1... | collective-permute-start | bytes 746504 | tf_op jit(solution)/shard_map/ppermute | solution.py:39
  50.9 3.4 %collective-permute-start.8 = (bf16[4,72,432]{2,1,0:T(8,128)(2,1)S(1)}, bf16[4,72,432]{2,1,0:T(8,128)(2,1)S(1)}, u32[]{:S(2)}, u32[]{:S(2)}) collective-permute-start(bf16[4,72,432]{2,1,0:T(8,128)(2,1)S(1)} %shard_map.105.near_hbm), channel_id=1, source_target_pairs={{0,32},{32,64},{64,96},{96,128},{128,160},{160,192},{192,224},{224... | collective-permute-start | bytes 746504 | tf_op jit(solution)/shard_map/ppermute | solution.py:39
  54.3 4.3 %collective-permute-start.6 = (bf16[2,72,432]{2,1,0:T(8,128)(2,1)S(1)}, bf16[2,72,432]{2,1,0:T(8,128)(2,1)S(1)}, u32[]{:S(2)}, u32[]{:S(2)}) collective-permute-start(bf16[2,72,432]{2,1,0:T(8,128)(2,1)S(1)} %get-tuple-element.48), channel_id=1, source_target_pairs={{0,192},{32,224},{64,0},{96,32},{128,64},{160,96},{192,128},{224,1... | collective-permute-start | bytes 373256 | tf_op jit(solution)/shard_map/ppermute | solution.py:39
  58.7 2.9 %collective-permute-start.7 = (bf16[2,72,432]{2,1,0:T(8,128)(2,1)S(1)}, bf16[2,72,432]{2,1,0:T(8,128)(2,1)S(1)}, u32[]{:S(2)}, u32[]{:S(2)}) collective-permute-start(bf16[2,72,432]{2,1,0:T(8,128)(2,1)S(1)} %get-tuple-element.47), channel_id=1, source_target_pairs={{0,64},{32,96},{64,128},{96,160},{128,192},{160,224},{192,0},{224,... | collective-permute-start | bytes 373256 | tf_op jit(solution)/shard_map/ppermute | solution.py:39
  61.6 3.4 %collective-permute-done.6.low_hbm = bf16[2,72,432]{2,1,0:T(8,128)(2,1)S(1)} collective-permute-done((bf16[2,72,432]{2,1,0:T(8,128)(2,1)S(1)}, bf16[2,72,432]{2,1,0:T(8,128)(2,1)S(1)}, u32[]{:S(2)}, u32[]{:S(2)}) %collective-permute-start.6) | collective-permute-done | bytes 124448 | tf_op jit(solution)/shard_map/ppermute | solution.py:39
  65.0 5.1 %collective-permute-start.9 = (bf16[256,1536]{1,0:T(8,128)(2,1)S(1)}, bf16[256,1536]{1,0:T(8,128)(2,1)S(1)}, u32[]{:S(2)}, u32[]{:S(2)}) collective-permute-start(bf16[256,1536]{1,0:T(8,128)(2,1)S(1)} %get-tuple-element.36.own_hbm), channel_id=1, source_target_pairs={{0,16},{16,0},{1,17},{17,1},{2,18},{18,2},{3,19},{19,3},{4,20},{20... | collective-permute-start | bytes 2359304 | tf_op jit(solution)/shard_map/ppermute | solution.py:34
  70.1 0.0 collective-permute-done.7.high_hbm
  70.1 0.0 copy-start.15
  70.1 0.0 collective-permute-done.5.up_hbm
  70.1 0.0 copy-start.12
  70.1 0.0 collective-permute-done.8.down_hbm
  70.1 0.0 collective-permute-done.4.side_hbm
  70.1 4.1 %collective-permute-start.10 = (bf16[256,1536]{1,0:T(8,128)(2,1)S(1)}, bf16[256,1536]{1,0:T(8,128)(2,1)S(1)}, u32[]{:S(2)}, u32[]{:S(2)}) collective-permute-start(bf16[256,1536]{1,0:T(8,128)(2,1)S(1)} %collective-permute-done.4.side_hbm), channel_id=1, source_target_pairs={{0,16},{16,0},{1,17},{17,1},{2,18},{18,2},{3,19},{19,3},{4,20},{20... | collective-permute-start | bytes 2359304 | tf_op jit(solution)/shard_map/ppermute | solution.py:34
  74.3 0.0 collective-permute-done.9.core_hbm
  74.3 1.9 %collective-permute-done.10.both_hbm = bf16[256,1536]{1,0:T(8,128)(2,1)S(1)} collective-permute-done((bf16[256,1536]{1,0:T(8,128)(2,1)S(1)}, bf16[256,1536]{1,0:T(8,128)(2,1)S(1)}, u32[]{:S(2)}, u32[]{:S(2)}) %collective-permute-start.10) | collective-permute-done | bytes 786464 | tf_op jit(solution)/shard_map/ppermute | solution.py:34
  76.2 0.0 copy-done.12
  76.2 0.0 copy-done.13
  76.2 0.0 copy-done.9
  76.2 0.0 copy-done.10
  76.2 0.0 copy-start.11
  76.2 0.9 copy-done.11
  77.1 13.0 %shard_map.108 = (bf16[128,32,128]{2,1,0:T(8,128)(2,1)}, bf16[512,1152]{1,0:T(8,128)(2,1)}, bf16[512,1152]{1,0:T(8,128)(2,1)}) custom-call(s32[3]{0:T(128)} %copy-done.6, bf16[4,72,432]{2,1,0:T(8,128)(2,1)} %copy-done.2, bf16[4,72,432]{2,1,0:T(8,128)(2,1)} %copy-done.12, bf16[2,72,432]{2,1,0:T(8,128)(2,1)} %copy-done.14, bf16[2,72,432]{2,1,0:T(8,128)(2,1)} %copy-done.15, ...), custom_call_target="tpu_custom_call" | custom-call | flops 3057647616 | bytes 7548940 | tf_op jit(solution)/shard_map/pallas_call | solution.py:323
  90.2 14.3 %all-to-all-start.1 = ((bf16[128,32,128]{2,1,0:T(8,128)(2,1)}), bf16[128,32,128]{2,1,0:T(8,128)(2,1)S(1)}, u32[]{:S(2)}, u32[]{:S(2)}) async-start(bf16[128,32,128]{2,1,0:T(8,128)(2,1)} %get-tuple-element.38), calls=%async_computation.1 | async-start | bytes 2097152 | tf_op jit(solution)/shard_map/all_to_all | solution.py:419
  104.5 2.6 %collective-permute-start.11 = (bf16[512,1152]{1,0:T(8,128)(2,1)}, bf16[512,1152]{1,0:T(8,128)(2,1)S(1)}, u32[]{:S(2)}, u32[]{:S(2)}) collective-permute-start(bf16[512,1152]{1,0:T(8,128)(2,1)} %get-tuple-element.40), channel_id=1, source_target_pairs={{0,16},{16,0},{1,17},{17,1},{2,18},{18,2},{3,19},{19,3},{4,20},{20... | collective-permute-start | bytes 3538952 | tf_op jit(solution)/shard_map/ppermute | solution.py:34
  107.0 2.7 %collective-permute-done.11.got_ref = bf16[512,1152]{1,0:T(8,128)(2,1)S(1)} collective-permute-done((bf16[512,1152]{1,0:T(8,128)(2,1)}, bf16[512,1152]{1,0:T(8,128)(2,1)S(1)}, u32[]{:S(2)}, u32[]{:S(2)}) %collective-permute-start.11) | collective-permute-done | bytes 1179680 | tf_op jit(solution)/shard_map/ppermute | solution.py:34
  109.7 1.3 copy-done.1
  111.0 0.3 shard_map.109
  111.2 1.9 %collective-permute-start.12 = (bf16[256,1152]{1,0:T(8,128)(2,1)S(1)}, bf16[256,1152]{1,0:T(8,128)(2,1)S(1)}, u32[]{:S(2)}, u32[]{:S(2)}) collective-permute-start(bf16[256,1152]{1,0:T(8,128)(2,1)S(1)} %get-tuple-element.42), channel_id=1, source_target_pairs={{0,8},{8,0},{1,9},{9,1},{2,10},{10,2},{3,11},{11,3},{4,12},{12,4},... | collective-permute-start | bytes 1769480 | tf_op jit(solution)/shard_map/ppermute | solution.py:34
  113.2 21.7 %collective-permute-done.12.refs_1_ = bf16[256,1152]{1,0:T(8,128)(2,1)S(1)} collective-permute-done((bf16[256,1152]{1,0:T(8,128)(2,1)S(1)}, bf16[256,1152]{1,0:T(8,128)(2,1)S(1)}, u32[]{:S(2)}, u32[]{:S(2)}) %collective-permute-start.12) | collective-permute-done | bytes 589856 | tf_op jit(solution)/shard_map/ppermute | solution.py:34
  134.8 0.9 shard_map.110.back_ref
  135.7 0.0 all-to-all-done.1.parts_ref
  135.7 0.2 shard_map.111
  135.9 24.5 %all_to_all.15.pieces_ref = bf16[16,16,1408]{2,1,0:T(8,128)(2,1)S(1)} all-to-all(bf16[16,16,1408]{2,1,0:T(8,128)(2,1)S(1)} %bitcast.18), channel_id=1, replica_groups=mesh['xh'=2,'z'=8,'c'=2,'xl'=2,'y'=8] {'xl','y'}, dimensions={0} | all-to-all | bytes 1441792 | tf_op jit(solution)/shard_map/all_to_all | solution.py:421
  160.4 0.6 shard_map.112
  161.1 5.0 %collective-permute-start.13 = (f32[2,36,432]{2,1,0:T(8,128)S(1)}, f32[2,36,432]{2,1,0:T(8,128)S(1)}, u32[]{:S(2)}, u32[]{:S(2)}) collective-permute-start(f32[2,36,432]{2,1,0:T(8,128)S(1)} %get-tuple-element.44), channel_id=1, source_target_pairs={{0,16},{16,0},{1,17},{17,1},{2,18},{18,2},{3,19},{19,3},{4,20},{20... | collective-permute-start | bytes 373256 | tf_op jit(solution)/shard_map/ppermute | solution.py:34
  166.8 0.1 pad_maximum_fusion.decay_ref
  166.9 0.9 slice.12
  167.8 0.0 collective-permute-done.13.core_ref
  167.8 1.5 shard_map.113
  (18 shorter events, 0.1 us)
Async XLA Ops:
  0.6 33.5 %copy-start = (bf16[128,2304]{1,0:T(8,128)(2,1)S(1)}, bf16[128,2304]{1,0:T(8,128)(2,1)}, u32[]{:S(2)}) copy-start(bf16[128,2304]{1,0:T(8,128)(2,1)} %param.10) | copy-start | bytes 1769476
  2.8 8.9 %copy-start.3 = (f32[36,1728]{1,0:T(8,128)S(1)}, f32[36,1728]{1,0:T(8,128)}, u32[]{:S(2)}) copy-start(f32[36,1728]{1,0:T(8,128)} %master_ref.1) | copy-start | bytes 746500
  2.8 41.4 %all-to-all-start = ((bf16[16,16,1792]{2,1,0:T(8,128)(2,1)}), bf16[16,16,1792]{2,1,0:T(8,128)(2,1)S(1)}, u32[]{:S(2)}, u32[]{:S(2)}) async-start(bf16[16,16,1792]{2,1,0:T(8,128)(2,1)} %bitcast.19), calls=%async_computation | async-start | bytes 1835008 | tf_op jit(solution)/shard_map/all_to_all | solution.py:368
  11.8 34.3 %copy-start.6 = (s32[3]{0:T(128)}, s32[3]{0:T(128)S(1)}, u32[]{:S(2)}) copy-start(s32[3]{0:T(128)S(1)} %pad_add_fusion.spot_ref) | copy-start | bytes 40
  12.6 4.6 %collective-permute-start = (bf16[36,432]{1,0:T(8,128)(2,1)S(1)}, bf16[36,432]{1,0:T(8,128)(2,1)S(1)}, u32[]{:S(2)}, u32[]{:S(2)}) collective-permute-start(bf16[36,432]{1,0:T(8,128)(2,1)S(1)} %get-tuple-element.26), channel_id=1, source_target_pairs={{0,16},{16,0},{1,17},{17,1},{2,18},{18,2},{3,19},{19,3},{4,20},{20... | collective-permute-start | bytes 93320 | tf_op jit(solution)/shard_map/ppermute | solution.py:34
  17.8 16.6 %collective-permute-start.1 = (bf16[72,432]{1,0:T(8,128)(2,1)S(1)}, bf16[72,432]{1,0:T(8,128)(2,1)S(1)}, u32[]{:S(2)}, u32[]{:S(2)}) collective-permute-start(bf16[72,432]{1,0:T(8,128)(2,1)S(1)} %shard_map.104.own_ref), channel_id=1, source_target_pairs={{0,128},{32,160},{64,192},{96,224},{128,0},{160,32},{192,64},{224,... | collective-permute-start | bytes 186632 | tf_op jit(solution)/shard_map/ppermute | solution.py:39
  27.6 7.5 %collective-permute-start.2 = (bf16[72,432]{1,0:T(8,128)(2,1)S(1)}, bf16[72,432]{1,0:T(8,128)(2,1)S(1)}, u32[]{:S(2)}, u32[]{:S(2)}) collective-permute-start(bf16[72,432]{1,0:T(8,128)(2,1)S(1)} %shard_map.104.own_ref), channel_id=1, source_target_pairs={{0,256},{256,0},{1,257},{257,1},{2,258},{258,2},{3,259},{259,3},{4... | collective-permute-start | bytes 186632 | tf_op jit(solution)/shard_map/ppermute | solution.py:34
  31.9 11.7 %collective-permute-start.3 = (bf16[72,432]{1,0:T(8,128)(2,1)S(1)}, bf16[72,432]{1,0:T(8,128)(2,1)S(1)}, u32[]{:S(2)}, u32[]{:S(2)}) collective-permute-start(bf16[72,432]{1,0:T(8,128)(2,1)S(1)} %shard_map.104.own_ref), channel_id=1, source_target_pairs={{0,384},{32,416},{64,448},{96,480},{128,256},{160,288},{192,320},{... | collective-permute-start | bytes 186632 | tf_op jit(solution)/shard_map/ppermute | solution.py:49
  44.2 32.0 %copy-start.2 = (bf16[4,72,432]{2,1,0:T(8,128)(2,1)}, bf16[4,72,432]{2,1,0:T(8,128)(2,1)S(1)}, u32[]{:S(2)}) copy-start(bf16[4,72,432]{2,1,0:T(8,128)(2,1)S(1)} %shard_map.105.near_hbm) | copy-start | bytes 746500
  46.1 30.1 %copy-start.8 = (bf16[256,1536]{1,0:T(8,128)(2,1)}, bf16[256,1536]{1,0:T(8,128)(2,1)S(1)}, u32[]{:S(2)}) copy-start(bf16[256,1536]{1,0:T(8,128)(2,1)S(1)} %get-tuple-element.36.own_hbm) | copy-start | bytes 2359300
  46.1 24.1 %collective-permute-start.4 = (bf16[256,1536]{1,0:T(8,128)(2,1)S(1)}, bf16[256,1536]{1,0:T(8,128)(2,1)S(1)}, u32[]{:S(2)}, u32[]{:S(2)}) collective-permute-start(bf16[256,1536]{1,0:T(8,128)(2,1)S(1)} %get-tuple-element.29), channel_id=1, source_target_pairs={{0,8},{8,0},{1,9},{9,1},{2,10},{10,2},{3,11},{11,3},{4,12},{12,4},... | collective-permute-start | bytes 2359304 | tf_op jit(solution)/shard_map/ppermute | solution.py:34
  49.0 21.1 %collective-permute-start.5 = (bf16[4,72,432]{2,1,0:T(8,128)(2,1)S(1)}, bf16[4,72,432]{2,1,0:T(8,128)(2,1)S(1)}, u32[]{:S(2)}, u32[]{:S(2)}) collective-permute-start(bf16[4,72,432]{2,1,0:T(8,128)(2,1)S(1)} %shard_map.105.near_hbm), channel_id=1, source_target_pairs={{0,224},{32,0},{64,32},{96,64},{128,96},{160,128},{192,160},{224,1... | collective-permute-start | bytes 746504 | tf_op jit(solution)/shard_map/ppermute | solution.py:39
  50.9 19.2 %collective-permute-start.8 = (bf16[4,72,432]{2,1,0:T(8,128)(2,1)S(1)}, bf16[4,72,432]{2,1,0:T(8,128)(2,1)S(1)}, u32[]{:S(2)}, u32[]{:S(2)}) collective-permute-start(bf16[4,72,432]{2,1,0:T(8,128)(2,1)S(1)} %shard_map.105.near_hbm), channel_id=1, source_target_pairs={{0,32},{32,64},{64,96},{96,128},{128,160},{160,192},{192,224},{224... | collective-permute-start | bytes 746504 | tf_op jit(solution)/shard_map/ppermute | solution.py:39
  54.3 10.7 %collective-permute-start.6 = (bf16[2,72,432]{2,1,0:T(8,128)(2,1)S(1)}, bf16[2,72,432]{2,1,0:T(8,128)(2,1)S(1)}, u32[]{:S(2)}, u32[]{:S(2)}) collective-permute-start(bf16[2,72,432]{2,1,0:T(8,128)(2,1)S(1)} %get-tuple-element.48), channel_id=1, source_target_pairs={{0,192},{32,224},{64,0},{96,32},{128,64},{160,96},{192,128},{224,1... | collective-permute-start | bytes 373256 | tf_op jit(solution)/shard_map/ppermute | solution.py:39
  58.7 11.4 %collective-permute-start.7 = (bf16[2,72,432]{2,1,0:T(8,128)(2,1)S(1)}, bf16[2,72,432]{2,1,0:T(8,128)(2,1)S(1)}, u32[]{:S(2)}, u32[]{:S(2)}) collective-permute-start(bf16[2,72,432]{2,1,0:T(8,128)(2,1)S(1)} %get-tuple-element.47), channel_id=1, source_target_pairs={{0,64},{32,96},{64,128},{96,160},{128,192},{160,224},{192,0},{224,... | collective-permute-start | bytes 373256 | tf_op jit(solution)/shard_map/ppermute | solution.py:39
  65.0 11.2 %copy-start.14 = (bf16[2,72,432]{2,1,0:T(8,128)(2,1)}, bf16[2,72,432]{2,1,0:T(8,128)(2,1)S(1)}, u32[]{:S(2)}) copy-start(bf16[2,72,432]{2,1,0:T(8,128)(2,1)S(1)} %collective-permute-done.6.low_hbm) | copy-start | bytes 373252
  65.0 9.3 %collective-permute-start.9 = (bf16[256,1536]{1,0:T(8,128)(2,1)S(1)}, bf16[256,1536]{1,0:T(8,128)(2,1)S(1)}, u32[]{:S(2)}, u32[]{:S(2)}) collective-permute-start(bf16[256,1536]{1,0:T(8,128)(2,1)S(1)} %get-tuple-element.36.own_hbm), channel_id=1, source_target_pairs={{0,16},{16,0},{1,17},{17,1},{2,18},{18,2},{3,19},{19,3},{4,20},{20... | collective-permute-start | bytes 2359304 | tf_op jit(solution)/shard_map/ppermute | solution.py:34
  70.1 4.2 %copy-start.15 = (bf16[2,72,432]{2,1,0:T(8,128)(2,1)}, bf16[2,72,432]{2,1,0:T(8,128)(2,1)S(1)}, u32[]{:S(2)}) copy-start(bf16[2,72,432]{2,1,0:T(8,128)(2,1)S(1)} %collective-permute-done.7.high_hbm) | copy-start | bytes 373252
  70.1 6.1 %copy-start.12 = (bf16[4,72,432]{2,1,0:T(8,128)(2,1)}, bf16[4,72,432]{2,1,0:T(8,128)(2,1)S(1)}, u32[]{:S(2)}) copy-start(bf16[4,72,432]{2,1,0:T(8,128)(2,1)S(1)} %collective-permute-done.5.up_hbm) | copy-start | bytes 746500
  70.1 6.1 %copy-start.13 = (bf16[4,72,432]{2,1,0:T(8,128)(2,1)}, bf16[4,72,432]{2,1,0:T(8,128)(2,1)S(1)}, u32[]{:S(2)}) copy-start(bf16[4,72,432]{2,1,0:T(8,128)(2,1)S(1)} %collective-permute-done.8.down_hbm) | copy-start | bytes 746500
  70.1 6.1 %copy-start.9 = (bf16[256,1536]{1,0:T(8,128)(2,1)}, bf16[256,1536]{1,0:T(8,128)(2,1)S(1)}, u32[]{:S(2)}) copy-start(bf16[256,1536]{1,0:T(8,128)(2,1)S(1)} %collective-permute-done.4.side_hbm) | copy-start | bytes 2359300
  70.1 6.0 %collective-permute-start.10 = (bf16[256,1536]{1,0:T(8,128)(2,1)S(1)}, bf16[256,1536]{1,0:T(8,128)(2,1)S(1)}, u32[]{:S(2)}, u32[]{:S(2)}) collective-permute-start(bf16[256,1536]{1,0:T(8,128)(2,1)S(1)} %collective-permute-done.4.side_hbm), channel_id=1, source_target_pairs={{0,16},{16,0},{1,17},{17,1},{2,18},{18,2},{3,19},{19,3},{4,20},{20... | collective-permute-start | bytes 2359304 | tf_op jit(solution)/shard_map/ppermute | solution.py:34
  74.3 1.9 %copy-start.10 = (bf16[256,1536]{1,0:T(8,128)(2,1)}, bf16[256,1536]{1,0:T(8,128)(2,1)S(1)}, u32[]{:S(2)}) copy-start(bf16[256,1536]{1,0:T(8,128)(2,1)S(1)} %collective-permute-done.9.core_hbm) | copy-start | bytes 2359300
  76.2 0.9 copy-start.11
  90.2 45.5 %all-to-all-start.1 = ((bf16[128,32,128]{2,1,0:T(8,128)(2,1)}), bf16[128,32,128]{2,1,0:T(8,128)(2,1)S(1)}, u32[]{:S(2)}, u32[]{:S(2)}) async-start(bf16[128,32,128]{2,1,0:T(8,128)(2,1)} %get-tuple-element.38), calls=%async_computation.1 | async-start | bytes 2097152 | tf_op jit(solution)/shard_map/all_to_all | solution.py:419
  104.5 5.2 %collective-permute-start.11 = (bf16[512,1152]{1,0:T(8,128)(2,1)}, bf16[512,1152]{1,0:T(8,128)(2,1)S(1)}, u32[]{:S(2)}, u32[]{:S(2)}) collective-permute-start(bf16[512,1152]{1,0:T(8,128)(2,1)} %get-tuple-element.40), channel_id=1, source_target_pairs={{0,16},{16,0},{1,17},{17,1},{2,18},{18,2},{3,19},{19,3},{4,20},{20... | collective-permute-start | bytes 3538952 | tf_op jit(solution)/shard_map/ppermute | solution.py:34
  109.7 1.3 copy-start.1
  111.2 23.6 %collective-permute-start.12 = (bf16[256,1152]{1,0:T(8,128)(2,1)S(1)}, bf16[256,1152]{1,0:T(8,128)(2,1)S(1)}, u32[]{:S(2)}, u32[]{:S(2)}) collective-permute-start(bf16[256,1152]{1,0:T(8,128)(2,1)S(1)} %get-tuple-element.42), channel_id=1, source_target_pairs={{0,8},{8,0},{1,9},{9,1},{2,10},{10,2},{3,11},{11,3},{4,12},{12,4},... | collective-permute-start | bytes 1769480 | tf_op jit(solution)/shard_map/ppermute | solution.py:34
  135.9 24.5 %copy-start.7 = (s32[3]{0:T(128)S(1)}, s32[3]{0:T(128)}, u32[]{:S(2)}) copy-start(s32[3]{0:T(128)} %copy-done.6) | copy-start | bytes 40
  160.4 7.4 %copy-start.4 = (f32[36,1728]{1,0:T(8,128)S(1)}, f32[36,1728]{1,0:T(8,128)}, u32[]{:S(2)}) copy-start(f32[36,1728]{1,0:T(8,128)} %slow_ref.1) | copy-start | bytes 746500
  160.4 7.4 %copy-start.5 = (f32[36,1728]{1,0:T(8,128)S(1)}, f32[36,1728]{1,0:T(8,128)}, u32[]{:S(2)}) copy-start(f32[36,1728]{1,0:T(8,128)} %fast_ref.1) | copy-start | bytes 746500
  161.1 6.7 %collective-permute-start.13 = (f32[2,36,432]{2,1,0:T(8,128)S(1)}, f32[2,36,432]{2,1,0:T(8,128)S(1)}, u32[]{:S(2)}, u32[]{:S(2)}) collective-permute-start(f32[2,36,432]{2,1,0:T(8,128)S(1)} %get-tuple-element.44), channel_id=1, source_target_pairs={{0,16},{16,0},{1,17},{17,1},{2,18},{18,2},{3,19},{19,3},{4,20},{20... | collective-permute-start | bytes 373256 | tf_op jit(solution)/shard_map/ppermute | solution.py:34

commit v10 on v9

--- a/solution.py
+++ b/solution.py
@@ -140,7 +140,7 @@
         scores = jnp.where(same, scores, -1e30)
         top = jnp.max(scores, axis=-1, keepdims=True)
         expo = jnp.exp(scores - top)
-        attention = expo / jnp.sum(expo, axis=-1, keepdims=True)
+        attention = expo * (1.0 / jnp.sum(expo, axis=-1, keepdims=True))
         prob_grad = dot(own_out, values, ((1,), (1,)))
         row_dot = jnp.sum(attention * prob_grad, axis=-1, keepdims=True)
         score_grad = (attention * (prob_grad - row_dot)).astype(BF16)
@@ -180,21 +180,21 @@
 
 def main_kernel(
     spot_ref, near_hbm, up_hbm, low_hbm, high_hbm, down_hbm, own_hbm, core_hbm, side_hbm, both_hbm, packed_hbm, inner_hbm, outer_hbm,
-    raw_ref, own_ref, core_ref, side_ref, both_ref, weight_ref, packed_ref, parts_ref, total_ref, in_sems, out_sems,
+    raw_ref, token_ref, weight_ref, packed_ref, parts_ref, total_ref, grads_ref, in_sems, out_sems,
 ):
-    tokens = own_ref.shape[0]
+    tokens = own_hbm.shape[0]
     model_width, cols = total_ref.shape
     quarter = cols // 3
     lows = [lax.rem(spot_ref[1] + ahead, 4) for ahead in range(4)]
     half = raw_ref.shape[1] // 2
-    tokens_in = ((own_hbm, own_ref), (core_hbm, core_ref), (side_hbm, side_ref), (both_hbm, both_ref))
+    sources = (own_hbm, core_hbm, side_hbm, both_hbm)
     pairs = (
         (near_hbm, raw_ref.at[lows[0]]),
         (up_hbm, raw_ref.at[lows[1]]),
         (low_hbm, raw_ref.at[lows[2], pl.ds(0, half)]),
         (high_hbm, raw_ref.at[lows[2], pl.ds(half, half)]),
         (down_hbm, raw_ref.at[lows[3]]),
-    ) + tokens_in
+    ) + tuple((source, token_ref.at[pl.ds(i * tokens, tokens)]) for i, source in enumerate(sources))
     loads = [pltpu.make_async_copy(source, target, in_sems.at[i]) for i, (source, target) in enumerate(pairs)]
     for load in loads:
         load.start()
@@ -202,34 +202,23 @@
     col = lax.broadcasted_iota(jnp.int32, (tokens, tokens), 1)
     same = lax.rem(row, 16) == lax.rem(col, 16)
     lane = lax.broadcasted_iota(jnp.int32, (tokens, quarter), 1)
-    stores = []
     for load in loads[:5]:
         load.wait()
     blocks = [raw_ref[low, group].astype(F32) for group in range(4) for low in range(4)]
     weight_ref[...] = jnp.concatenate(blocks, axis=0).astype(BF16)
-    places = ((inner_hbm, 0, 1), (outer_hbm, 0, 0), (inner_hbm, 1, 0), (outer_hbm, 1, 1))
-    for index, (target, place, skip) in enumerate(places):
-        ref = tokens_in[index][1]
-        loads[index + 5].wait()
-        projected = dot(ref[:, :model_width], weight_ref[...], ((1,), (0,)))
+    for load in loads[5:]:
+        load.wait()
+    projected_all = dot(token_ref[:, :model_width], weight_ref[...], ((1,), (0,)))
+    for index, skip in enumerate((1, 0, 0, 1)):
+        here = slice(index * tokens, (index + 1) * tokens)
+        projected = projected_all[here]
         projected = projected.astype(BF16).astype(F32)
-        cot = ref[:, model_width:].astype(F32)
-        out_grad = cot[:, skip * quarter : (skip + 1) * quarter]
-        grads = attend_block(projected, out_grad, same, lane).astype(BF16)
-        part = dot(ref[:, :model_width], grads, ((0,), (0,)))
-        if index == 0:
-            total_ref[...] = part
-        else:
-            total_ref[...] += part
-        parts_ref[index] = dot(grads, weight_ref[...], ((1,), (1,))).astype(BF16)
-        stores.append(
-            pltpu.make_async_copy(
-                parts_ref.at[index], target.at[pl.ds(place * tokens, tokens)], out_sems.at[index]
-            )
-        )
-        stores[-1].start()
+        out_grad = token_ref[here, model_width + skip * quarter : model_width + (skip + 1) * quarter].astype(F32)
+        grads_ref[here, :] = attend_block(projected, out_grad, same, lane).astype(BF16)
+    total_ref[...] = dot(token_ref[:, :model_width], grads_ref[...], ((0,), (0,)))
     height = model_width // 16
     pieces = packed_ref.shape[0] // 16
+    stores = []
     for owner in range(16):
         tiles = tiles_of(total_ref[owner * height : (owner + 1) * height, :])
         each = len(tiles) // pieces
@@ -239,6 +228,12 @@
             part = pl.ds((owner - 3) * pieces, 4 * pieces)
             stores.append(pltpu.make_async_copy(packed_ref.at[part], packed_hbm.at[part], out_sems.at[4 + owner // 4]))
             stores[-1].start()
+    for index, (target, place) in enumerate(((inner_hbm, 0), (outer_hbm, 0), (inner_hbm, 1), (outer_hbm, 1))):
+        parts_ref[index] = dot(grads_ref[index * tokens : (index + 1) * tokens, :], weight_ref[...], ((1,), (1,))).astype(BF16)
+        stores.append(
+            pltpu.make_async_copy(parts_ref.at[index], target.at[pl.ds(place * tokens, tokens)], out_sems.at[index])
+        )
+        stores[-1].start()
     for store in stores:
         store.wait()
 
@@ -396,14 +391,12 @@
         flops=6 * 4 * patches * width * cols,
         scratch=[
             pltpu.VMEM((4, 4, pair_rows, cols), BF16),
-            pltpu.VMEM((patches, broad), BF16),
-            pltpu.VMEM((patches, broad), BF16),
-            pltpu.VMEM((patches, broad), BF16),
-            pltpu.VMEM((patches, broad), BF16),
+            pltpu.VMEM((4 * patches, broad), BF16),
             pltpu.VMEM((width, cols), BF16),
             pltpu.VMEM((pieces, 32, 128), BF16),
             pltpu.VMEM((4, patches, width), BF16),
             pltpu.VMEM((width, cols), F32),
+            pltpu.VMEM((4 * patches, cols), BF16),
             pltpu.SemaphoreType.DMA((9,)),
             pltpu.SemaphoreType.DMA((8,)),
         ],

time: 170 us -> 168 us (0.988)
  Pallas kernels: 22.5 us -> 20.5 us
    pallas_call x11, Pallas kernels: 22.5 us -> 20.5 us  [call(): pl.pallas_call(kernel, out_shape=shapes, in_specs=specs, out_specs=[pl.Bl...]
where the time goes in v10:
time: 168 us; the launch traced here: 167 us
  starting transfers between devices  77.2 us (46%)
  waiting for transfers between devices  39 us (23%)
  blocking collectives  24.5 us (15%)
  Pallas kernels  20.5 us (12%)
  local copies, waits for them, and re-layouts  3.11 us (2%)
  between operations  2.49 us (1%)
    ppermute x8, starting transfers between devices, swap(): return lax.ppermute(value, axis, [(0, 1), (1, 0)])  29.7 us
    ppermute x8, waiting for transfers between devices, swap(): return lax.ppermute(value, axis, [(0, 1), (1, 0)])  27 us
    all_to_all x1, blocking collectives, on_device(): lax.all_to_all(joint.reshape(n_seq, patches // n_seq, width + 256), SEQ,...  24.5 us
    ppermute x5, starting transfers between devices, shift(): lax.ppermute(value, 'z', [(i, (i + away) % count) for i in range(count)])  22.3 us
    pallas_call x11, Pallas kernels, call(): pl.pallas_call(kernel, out_shape=shapes, in_specs=specs, out_specs=[pl.Bl...  20.5 us
    all_to_all x1, starting transfers between devices, on_device(): parts = lax.all_to_all(packed, ROWS + ('y',), 0, 0, tiled=True)  14.3 us
    all_to_all x1, starting transfers between devices, on_device(): lax.all_to_all(packed.reshape(n_seq, patches // n_seq, width + loose), SE...  8.83 us
    ppermute x1, waiting for transfers between devices, both_turn(): return lax.ppermute(value, ('xh', 'z'), pairs)  8.6 us
  transfers between devices with their start and end apart: 16, of which 7 were waited for; matrix products, arithmetic and copies ran while one was open for 1% of the time, Pallas kernels for 2%

profile of v10, /device:TPU:1, one launch (start us, length us, event | category | flops | bytes accessed | tf_op | source)
XLA Modules:
  0.0 167.3 jit_solution(14648347030090556963)
XLA Ops:
  0.6 0.0 copy-start
  0.6 2.2 %shard_map.106 = bf16[256,1792]{1,0:T(8,128)(2,1)} custom-call(bf16[256,1152]{1,0:T(8,128)(2,1)} %bitcast.20, bf16[576,256]{1,0:T(8,128)(2,1)} %bitcast.22), custom_call_target="tpu_custom_call" | custom-call | bytes 1802240 | tf_op jit(solution)/shard_map/pallas_call | solution.py:318
  2.8 0.0 copy-start.3
  2.8 8.8 %all-to-all-start = ((bf16[16,16,1792]{2,1,0:T(8,128)(2,1)}), bf16[16,16,1792]{2,1,0:T(8,128)(2,1)S(1)}, u32[]{:S(2)}, u32[]{:S(2)}) async-start(bf16[16,16,1792]{2,1,0:T(8,128)(2,1)} %bitcast.19), calls=%async_computation | async-start | bytes 1835008 | tf_op jit(solution)/shard_map/all_to_all | solution.py:363
  11.7 0.1 pad_add_fusion.spot_ref
  11.7 0.0 copy-done.3
  11.8 0.9 shard_map.103
  12.6 3.7 %collective-permute-start = (bf16[36,432]{1,0:T(8,128)(2,1)S(1)}, bf16[36,432]{1,0:T(8,128)(2,1)S(1)}, u32[]{:S(2)}, u32[]{:S(2)}) collective-permute-start(bf16[36,432]{1,0:T(8,128)(2,1)S(1)} %get-tuple-element.26), channel_id=1, source_target_pairs={{0,16},{16,0},{1,17},{17,1},{2,18},{18,2},{3,19},{19,3},{4,20},{20... | collective-permute-start | bytes 93320 | tf_op jit(solution)/shard_map/ppermute | solution.py:34
  17.0 0.1 sine_convert_fusion
  17.1 0.1 collective-permute-done.theirs_ref
  17.2 0.6 shard_map.104.own_ref
  17.8 9.8 %collective-permute-start.1 = (bf16[72,432]{1,0:T(8,128)(2,1)S(1)}, bf16[72,432]{1,0:T(8,128)(2,1)S(1)}, u32[]{:S(2)}, u32[]{:S(2)}) collective-permute-start(bf16[72,432]{1,0:T(8,128)(2,1)S(1)} %shard_map.104.own_ref), channel_id=1, source_target_pairs={{0,128},{32,160},{64,192},{96,224},{128,0},{160,32},{192,64},{224,... | collective-permute-start | bytes 186632 | tf_op jit(solution)/shard_map/ppermute | solution.py:39
  27.6 4.4 %collective-permute-start.2 = (bf16[72,432]{1,0:T(8,128)(2,1)S(1)}, bf16[72,432]{1,0:T(8,128)(2,1)S(1)}, u32[]{:S(2)}, u32[]{:S(2)}) collective-permute-start(bf16[72,432]{1,0:T(8,128)(2,1)S(1)} %shard_map.104.own_ref), channel_id=1, source_target_pairs={{0,256},{256,0},{1,257},{257,1},{2,258},{258,2},{3,259},{259,3},{4... | collective-permute-start | bytes 186632 | tf_op jit(solution)/shard_map/ppermute | solution.py:34
  31.9 2.2 %collective-permute-start.3 = (bf16[72,432]{1,0:T(8,128)(2,1)S(1)}, bf16[72,432]{1,0:T(8,128)(2,1)S(1)}, u32[]{:S(2)}, u32[]{:S(2)}) collective-permute-start(bf16[72,432]{1,0:T(8,128)(2,1)S(1)} %shard_map.104.own_ref), channel_id=1, source_target_pairs={{0,384},{32,416},{64,448},{96,480},{128,256},{160,288},{192,320},{... | collective-permute-start | bytes 186632 | tf_op jit(solution)/shard_map/ppermute | solution.py:49
  34.1 0.0 copy-done
  34.1 0.2 fusion.mod_ref
  34.3 0.0 collective-permute-done.1.far_ref
  34.3 0.7 collective-permute-done.2.across_ref
  35.0 8.6 %collective-permute-done.3.both_ref = bf16[72,432]{1,0:T(8,128)(2,1)S(1)} collective-permute-done((bf16[72,432]{1,0:T(8,128)(2,1)S(1)}, bf16[72,432]{1,0:T(8,128)(2,1)S(1)}, u32[]{:S(2)}, u32[]{:S(2)}) %collective-permute-start.3) | collective-permute-done | bytes 62240 | tf_op jit(solution)/shard_map/ppermute | solution.py:49
  43.6 0.6 shard_map.105.near_hbm
  44.2 0.0 copy-start.2
  44.2 0.0 all-to-all-done
  44.2 1.8 %shard_map.107 = (bf16[256,1536]{1,0:T(8,128)(2,1)S(1)}, bf16[256,1536]{1,0:T(8,128)(2,1)S(1)}) custom-call(s32[3]{0:T(128)S(1)} %pad_add_fusion.spot_ref, bf16[256,1792]{1,0:T(8,128)(2,1)S(1)} %bitcast.16, f32[1,2304]{1,0:T(1,128)S(1)} %fusion.mod_ref), custom_call_target="tpu_custom_call" | custom-call | bytes 2499596 | tf_op jit(solution)/shard_map/pallas_call | solution.py:318
  46.0 0.0 copy-done.6
  46.1 0.0 copy-start.8
  46.1 2.9 %collective-permute-start.4 = (bf16[256,1536]{1,0:T(8,128)(2,1)S(1)}, bf16[256,1536]{1,0:T(8,128)(2,1)S(1)}, u32[]{:S(2)}, u32[]{:S(2)}) collective-permute-start(bf16[256,1536]{1,0:T(8,128)(2,1)S(1)} %get-tuple-element.29), channel_id=1, source_target_pairs={{0,8},{8,0},{1,9},{9,1},{2,10},{10,2},{3,11},{11,3},{4,12},{12,4},... | collective-permute-start | bytes 2359304 | tf_op jit(solution)/shard_map/ppermute | solution.py:34
  49.0 1.9 %collective-permute-start.5 = (bf16[4,72,432]{2,1,0:T(8,128)(2,1)S(1)}, bf16[4,72,432]{2,1,0:T(8,128)(2,1)S(1)}, u32[]{:S(2)}, u32[]{:S(2)}) collective-permute-start(bf16[4,72,432]{2,1,0:T(8,128)(2,1)S(1)} %shard_map.105.near_hbm), channel_id=1, source_target_pairs={{0,224},{32,0},{64,32},{96,64},{128,96},{160,128},{192,160},{224,1... | collective-permute-start | bytes 746504 | tf_op jit(solution)/shard_map/ppermute | solution.py:39
  50.9 3.4 %collective-permute-start.8 = (bf16[4,72,432]{2,1,0:T(8,128)(2,1)S(1)}, bf16[4,72,432]{2,1,0:T(8,128)(2,1)S(1)}, u32[]{:S(2)}, u32[]{:S(2)}) collective-permute-start(bf16[4,72,432]{2,1,0:T(8,128)(2,1)S(1)} %shard_map.105.near_hbm), channel_id=1, source_target_pairs={{0,32},{32,64},{64,96},{96,128},{128,160},{160,192},{192,224},{224... | collective-permute-start | bytes 746504 | tf_op jit(solution)/shard_map/ppermute | solution.py:39
  54.3 4.3 %collective-permute-start.6 = (bf16[2,72,432]{2,1,0:T(8,128)(2,1)S(1)}, bf16[2,72,432]{2,1,0:T(8,128)(2,1)S(1)}, u32[]{:S(2)}, u32[]{:S(2)}) collective-permute-start(bf16[2,72,432]{2,1,0:T(8,128)(2,1)S(1)} %get-tuple-element.48), channel_id=1, source_target_pairs={{0,192},{32,224},{64,0},{96,32},{128,64},{160,96},{192,128},{224,1... | collective-permute-start | bytes 373256 | tf_op jit(solution)/shard_map/ppermute | solution.py:39
  58.7 2.9 %collective-permute-start.7 = (bf16[2,72,432]{2,1,0:T(8,128)(2,1)S(1)}, bf16[2,72,432]{2,1,0:T(8,128)(2,1)S(1)}, u32[]{:S(2)}, u32[]{:S(2)}) collective-permute-start(bf16[2,72,432]{2,1,0:T(8,128)(2,1)S(1)} %get-tuple-element.47), channel_id=1, source_target_pairs={{0,64},{32,96},{64,128},{96,160},{128,192},{160,224},{192,0},{224,... | collective-permute-start | bytes 373256 | tf_op jit(solution)/shard_map/ppermute | solution.py:39
  61.6 3.4 %collective-permute-done.6.low_hbm = bf16[2,72,432]{2,1,0:T(8,128)(2,1)S(1)} collective-permute-done((bf16[2,72,432]{2,1,0:T(8,128)(2,1)S(1)}, bf16[2,72,432]{2,1,0:T(8,128)(2,1)S(1)}, u32[]{:S(2)}, u32[]{:S(2)}) %collective-permute-start.6) | collective-permute-done | bytes 124448 | tf_op jit(solution)/shard_map/ppermute | solution.py:39
  65.0 5.1 %collective-permute-start.9 = (bf16[256,1536]{1,0:T(8,128)(2,1)S(1)}, bf16[256,1536]{1,0:T(8,128)(2,1)S(1)}, u32[]{:S(2)}, u32[]{:S(2)}) collective-permute-start(bf16[256,1536]{1,0:T(8,128)(2,1)S(1)} %get-tuple-element.36.own_hbm), channel_id=1, source_target_pairs={{0,16},{16,0},{1,17},{17,1},{2,18},{18,2},{3,19},{19,3},{4,20},{20... | collective-permute-start | bytes 2359304 | tf_op jit(solution)/shard_map/ppermute | solution.py:34
  70.1 0.0 collective-permute-done.7.high_hbm
  70.1 0.0 copy-start.15
  70.1 0.0 collective-permute-done.5.up_hbm
  70.1 0.0 copy-start.12
  70.1 0.0 collective-permute-done.8.down_hbm
  70.1 0.0 copy-start.13
  70.1 0.0 collective-permute-done.4.side_hbm
  70.1 4.1 %collective-permute-start.10 = (bf16[256,1536]{1,0:T(8,128)(2,1)S(1)}, bf16[256,1536]{1,0:T(8,128)(2,1)S(1)}, u32[]{:S(2)}, u32[]{:S(2)}) collective-permute-start(bf16[256,1536]{1,0:T(8,128)(2,1)S(1)} %collective-permute-done.4.side_hbm), channel_id=1, source_target_pairs={{0,16},{16,0},{1,17},{17,1},{2,18},{18,2},{3,19},{19,3},{4,20},{20... | collective-permute-start | bytes 2359304 | tf_op jit(solution)/shard_map/ppermute | solution.py:34
  74.3 0.0 collective-permute-done.9.core_hbm
  74.3 1.9 %collective-permute-done.10.both_hbm = bf16[256,1536]{1,0:T(8,128)(2,1)S(1)} collective-permute-done((bf16[256,1536]{1,0:T(8,128)(2,1)S(1)}, bf16[256,1536]{1,0:T(8,128)(2,1)S(1)}, u32[]{:S(2)}, u32[]{:S(2)}) %collective-permute-start.10) | collective-permute-done | bytes 786464 | tf_op jit(solution)/shard_map/ppermute | solution.py:34
  76.2 0.0 copy-done.8
  76.2 0.9 copy-done.11
  77.1 11.1 %shard_map.108 = (bf16[128,32,128]{2,1,0:T(8,128)(2,1)}, bf16[512,1152]{1,0:T(8,128)(2,1)}, bf16[512,1152]{1,0:T(8,128)(2,1)}) custom-call(s32[3]{0:T(128)} %copy-done.6, bf16[4,72,432]{2,1,0:T(8,128)(2,1)} %copy-done.2, bf16[4,72,432]{2,1,0:T(8,128)(2,1)} %copy-done.12, bf16[2,72,432]{2,1,0:T(8,128)(2,1)} %copy-done.14, bf16[2,72,432]{2,1,0:T(8,128)(2,1)} %copy-done.15, ...), custom_call_target="tpu_custom_call" | custom-call | flops 3057647616 | bytes 7548940 | tf_op jit(solution)/shard_map/pallas_call | solution.py:318
  88.2 14.3 %all-to-all-start.1 = ((bf16[128,32,128]{2,1,0:T(8,128)(2,1)}), bf16[128,32,128]{2,1,0:T(8,128)(2,1)S(1)}, u32[]{:S(2)}, u32[]{:S(2)}) async-start(bf16[128,32,128]{2,1,0:T(8,128)(2,1)} %get-tuple-element.38), calls=%async_computation.1 | async-start | bytes 2097152 | tf_op jit(solution)/shard_map/all_to_all | solution.py:412
  102.5 2.6 %collective-permute-start.11 = (bf16[512,1152]{1,0:T(8,128)(2,1)}, bf16[512,1152]{1,0:T(8,128)(2,1)S(1)}, u32[]{:S(2)}, u32[]{:S(2)}) collective-permute-start(bf16[512,1152]{1,0:T(8,128)(2,1)} %get-tuple-element.40), channel_id=1, source_target_pairs={{0,16},{16,0},{1,17},{17,1},{2,18},{18,2},{3,19},{19,3},{4,20},{20... | collective-permute-start | bytes 3538952 | tf_op jit(solution)/shard_map/ppermute | solution.py:34
  105.1 2.7 %collective-permute-done.11.got_ref = bf16[512,1152]{1,0:T(8,128)(2,1)S(1)} collective-permute-done((bf16[512,1152]{1,0:T(8,128)(2,1)}, bf16[512,1152]{1,0:T(8,128)(2,1)S(1)}, u32[]{:S(2)}, u32[]{:S(2)}) %collective-permute-start.11) | collective-permute-done | bytes 1179680 | tf_op jit(solution)/shard_map/ppermute | solution.py:34
  107.7 1.3 copy-done.1
  109.0 0.3 shard_map.109
  109.3 1.9 %collective-permute-start.12 = (bf16[256,1152]{1,0:T(8,128)(2,1)S(1)}, bf16[256,1152]{1,0:T(8,128)(2,1)S(1)}, u32[]{:S(2)}, u32[]{:S(2)}) collective-permute-start(bf16[256,1152]{1,0:T(8,128)(2,1)S(1)} %get-tuple-element.42), channel_id=1, source_target_pairs={{0,8},{8,0},{1,9},{9,1},{2,10},{10,2},{3,11},{11,3},{4,12},{12,4},... | collective-permute-start | bytes 1769480 | tf_op jit(solution)/shard_map/ppermute | solution.py:34
  111.2 21.7 %collective-permute-done.12.refs_1_ = bf16[256,1152]{1,0:T(8,128)(2,1)S(1)} collective-permute-done((bf16[256,1152]{1,0:T(8,128)(2,1)S(1)}, bf16[256,1152]{1,0:T(8,128)(2,1)S(1)}, u32[]{:S(2)}, u32[]{:S(2)}) %collective-permute-start.12) | collective-permute-done | bytes 589856 | tf_op jit(solution)/shard_map/ppermute | solution.py:34
  132.9 0.9 shard_map.110.back_ref
  133.7 0.0 all-to-all-done.1.parts_ref
  133.7 0.2 shard_map.111
  134.0 0.0 copy-start.7
  134.0 24.5 %all_to_all.15.pieces_ref = bf16[16,16,1408]{2,1,0:T(8,128)(2,1)S(1)} all-to-all(bf16[16,16,1408]{2,1,0:T(8,128)(2,1)S(1)} %bitcast.18), channel_id=1, replica_groups=mesh['xh'=2,'z'=8,'c'=2,'xl'=2,'y'=8] {'xl','y'}, dimensions={0} | all-to-all | bytes 1441792 | tf_op jit(solution)/shard_map/all_to_all | solution.py:414
  158.5 0.6 shard_map.112
  159.1 5.0 %collective-permute-start.13 = (f32[2,36,432]{2,1,0:T(8,128)S(1)}, f32[2,36,432]{2,1,0:T(8,128)S(1)}, u32[]{:S(2)}, u32[]{:S(2)}) collective-permute-start(f32[2,36,432]{2,1,0:T(8,128)S(1)} %get-tuple-element.44), channel_id=1, source_target_pairs={{0,16},{16,0},{1,17},{17,1},{2,18},{18,2},{3,19},{19,3},{4,20},{20... | collective-permute-start | bytes 373256 | tf_op jit(solution)/shard_map/ppermute | solution.py:34
  164.9 0.1 pad_maximum_fusion.decay_ref
  164.9 0.9 slice.12
  165.8 0.0 collective-permute-done.13.core_ref
  165.8 0.0 copy-done.4
  165.8 1.5 shard_map.113
  (18 shorter events, 0.1 us)
Async XLA Ops:
  0.6 33.5 %copy-start = (bf16[128,2304]{1,0:T(8,128)(2,1)S(1)}, bf16[128,2304]{1,0:T(8,128)(2,1)}, u32[]{:S(2)}) copy-start(bf16[128,2304]{1,0:T(8,128)(2,1)} %param.10) | copy-start | bytes 1769476
  2.8 8.9 %copy-start.3 = (f32[36,1728]{1,0:T(8,128)S(1)}, f32[36,1728]{1,0:T(8,128)}, u32[]{:S(2)}) copy-start(f32[36,1728]{1,0:T(8,128)} %master_ref.1) | copy-start | bytes 746500
  2.8 41.4 %all-to-all-start = ((bf16[16,16,1792]{2,1,0:T(8,128)(2,1)}), bf16[16,16,1792]{2,1,0:T(8,128)(2,1)S(1)}, u32[]{:S(2)}, u32[]{:S(2)}) async-start(bf16[16,16,1792]{2,1,0:T(8,128)(2,1)} %bitcast.19), calls=%async_computation | async-start | bytes 1835008 | tf_op jit(solution)/shard_map/all_to_all | solution.py:363
  11.8 34.3 %copy-start.6 = (s32[3]{0:T(128)}, s32[3]{0:T(128)S(1)}, u32[]{:S(2)}) copy-start(s32[3]{0:T(128)S(1)} %pad_add_fusion.spot_ref) | copy-start | bytes 40
  12.6 4.6 %collective-permute-start = (bf16[36,432]{1,0:T(8,128)(2,1)S(1)}, bf16[36,432]{1,0:T(8,128)(2,1)S(1)}, u32[]{:S(2)}, u32[]{:S(2)}) collective-permute-start(bf16[36,432]{1,0:T(8,128)(2,1)S(1)} %get-tuple-element.26), channel_id=1, source_target_pairs={{0,16},{16,0},{1,17},{17,1},{2,18},{18,2},{3,19},{19,3},{4,20},{20... | collective-permute-start | bytes 93320 | tf_op jit(solution)/shard_map/ppermute | solution.py:34
  17.8 16.6 %collective-permute-start.1 = (bf16[72,432]{1,0:T(8,128)(2,1)S(1)}, bf16[72,432]{1,0:T(8,128)(2,1)S(1)}, u32[]{:S(2)}, u32[]{:S(2)}) collective-permute-start(bf16[72,432]{1,0:T(8,128)(2,1)S(1)} %shard_map.104.own_ref), channel_id=1, source_target_pairs={{0,128},{32,160},{64,192},{96,224},{128,0},{160,32},{192,64},{224,... | collective-permute-start | bytes 186632 | tf_op jit(solution)/shard_map/ppermute | solution.py:39
  27.6 7.5 %collective-permute-start.2 = (bf16[72,432]{1,0:T(8,128)(2,1)S(1)}, bf16[72,432]{1,0:T(8,128)(2,1)S(1)}, u32[]{:S(2)}, u32[]{:S(2)}) collective-permute-start(bf16[72,432]{1,0:T(8,128)(2,1)S(1)} %shard_map.104.own_ref), channel_id=1, source_target_pairs={{0,256},{256,0},{1,257},{257,1},{2,258},{258,2},{3,259},{259,3},{4... | collective-permute-start | bytes 186632 | tf_op jit(solution)/shard_map/ppermute | solution.py:34
  31.9 11.7 %collective-permute-start.3 = (bf16[72,432]{1,0:T(8,128)(2,1)S(1)}, bf16[72,432]{1,0:T(8,128)(2,1)S(1)}, u32[]{:S(2)}, u32[]{:S(2)}) collective-permute-start(bf16[72,432]{1,0:T(8,128)(2,1)S(1)} %shard_map.104.own_ref), channel_id=1, source_target_pairs={{0,384},{32,416},{64,448},{96,480},{128,256},{160,288},{192,320},{... | collective-permute-start | bytes 186632 | tf_op jit(solution)/shard_map/ppermute | solution.py:49
  44.2 32.0 %copy-start.2 = (bf16[4,72,432]{2,1,0:T(8,128)(2,1)}, bf16[4,72,432]{2,1,0:T(8,128)(2,1)S(1)}, u32[]{:S(2)}) copy-start(bf16[4,72,432]{2,1,0:T(8,128)(2,1)S(1)} %shard_map.105.near_hbm) | copy-start | bytes 746500
  46.1 30.1 %copy-start.8 = (bf16[256,1536]{1,0:T(8,128)(2,1)}, bf16[256,1536]{1,0:T(8,128)(2,1)S(1)}, u32[]{:S(2)}) copy-start(bf16[256,1536]{1,0:T(8,128)(2,1)S(1)} %get-tuple-element.36.own_hbm) | copy-start | bytes 2359300
  46.1 24.1 %collective-permute-start.4 = (bf16[256,1536]{1,0:T(8,128)(2,1)S(1)}, bf16[256,1536]{1,0:T(8,128)(2,1)S(1)}, u32[]{:S(2)}, u32[]{:S(2)}) collective-permute-start(bf16[256,1536]{1,0:T(8,128)(2,1)S(1)} %get-tuple-element.29), channel_id=1, source_target_pairs={{0,8},{8,0},{1,9},{9,1},{2,10},{10,2},{3,11},{11,3},{4,12},{12,4},... | collective-permute-start | bytes 2359304 | tf_op jit(solution)/shard_map/ppermute | solution.py:34
  49.0 21.1 %collective-permute-start.5 = (bf16[4,72,432]{2,1,0:T(8,128)(2,1)S(1)}, bf16[4,72,432]{2,1,0:T(8,128)(2,1)S(1)}, u32[]{:S(2)}, u32[]{:S(2)}) collective-permute-start(bf16[4,72,432]{2,1,0:T(8,128)(2,1)S(1)} %shard_map.105.near_hbm), channel_id=1, source_target_pairs={{0,224},{32,0},{64,32},{96,64},{128,96},{160,128},{192,160},{224,1... | collective-permute-start | bytes 746504 | tf_op jit(solution)/shard_map/ppermute | solution.py:39
  50.9 19.2 %collective-permute-start.8 = (bf16[4,72,432]{2,1,0:T(8,128)(2,1)S(1)}, bf16[4,72,432]{2,1,0:T(8,128)(2,1)S(1)}, u32[]{:S(2)}, u32[]{:S(2)}) collective-permute-start(bf16[4,72,432]{2,1,0:T(8,128)(2,1)S(1)} %shard_map.105.near_hbm), channel_id=1, source_target_pairs={{0,32},{32,64},{64,96},{96,128},{128,160},{160,192},{192,224},{224... | collective-permute-start | bytes 746504 | tf_op jit(solution)/shard_map/ppermute | solution.py:39
  54.3 10.7 %collective-permute-start.6 = (bf16[2,72,432]{2,1,0:T(8,128)(2,1)S(1)}, bf16[2,72,432]{2,1,0:T(8,128)(2,1)S(1)}, u32[]{:S(2)}, u32[]{:S(2)}) collective-permute-start(bf16[2,72,432]{2,1,0:T(8,128)(2,1)S(1)} %get-tuple-element.48), channel_id=1, source_target_pairs={{0,192},{32,224},{64,0},{96,32},{128,64},{160,96},{192,128},{224,1... | collective-permute-start | bytes 373256 | tf_op jit(solution)/shard_map/ppermute | solution.py:39
  58.7 11.4 %collective-permute-start.7 = (bf16[2,72,432]{2,1,0:T(8,128)(2,1)S(1)}, bf16[2,72,432]{2,1,0:T(8,128)(2,1)S(1)}, u32[]{:S(2)}, u32[]{:S(2)}) collective-permute-start(bf16[2,72,432]{2,1,0:T(8,128)(2,1)S(1)} %get-tuple-element.47), channel_id=1, source_target_pairs={{0,64},{32,96},{64,128},{96,160},{128,192},{160,224},{192,0},{224,... | collective-permute-start | bytes 373256 | tf_op jit(solution)/shard_map/ppermute | solution.py:39
  65.0 11.2 %copy-start.14 = (bf16[2,72,432]{2,1,0:T(8,128)(2,1)}, bf16[2,72,432]{2,1,0:T(8,128)(2,1)S(1)}, u32[]{:S(2)}) copy-start(bf16[2,72,432]{2,1,0:T(8,128)(2,1)S(1)} %collective-permute-done.6.low_hbm) | copy-start | bytes 373252
  65.0 9.3 %collective-permute-start.9 = (bf16[256,1536]{1,0:T(8,128)(2,1)S(1)}, bf16[256,1536]{1,0:T(8,128)(2,1)S(1)}, u32[]{:S(2)}, u32[]{:S(2)}) collective-permute-start(bf16[256,1536]{1,0:T(8,128)(2,1)S(1)} %get-tuple-element.36.own_hbm), channel_id=1, source_target_pairs={{0,16},{16,0},{1,17},{17,1},{2,18},{18,2},{3,19},{19,3},{4,20},{20... | collective-permute-start | bytes 2359304 | tf_op jit(solution)/shard_map/ppermute | solution.py:34
  70.1 4.2 %copy-start.15 = (bf16[2,72,432]{2,1,0:T(8,128)(2,1)}, bf16[2,72,432]{2,1,0:T(8,128)(2,1)S(1)}, u32[]{:S(2)}) copy-start(bf16[2,72,432]{2,1,0:T(8,128)(2,1)S(1)} %collective-permute-done.7.high_hbm) | copy-start | bytes 373252
  70.1 6.1 %copy-start.12 = (bf16[4,72,432]{2,1,0:T(8,128)(2,1)}, bf16[4,72,432]{2,1,0:T(8,128)(2,1)S(1)}, u32[]{:S(2)}) copy-start(bf16[4,72,432]{2,1,0:T(8,128)(2,1)S(1)} %collective-permute-done.5.up_hbm) | copy-start | bytes 746500
  70.1 6.1 %copy-start.13 = (bf16[4,72,432]{2,1,0:T(8,128)(2,1)}, bf16[4,72,432]{2,1,0:T(8,128)(2,1)S(1)}, u32[]{:S(2)}) copy-start(bf16[4,72,432]{2,1,0:T(8,128)(2,1)S(1)} %collective-permute-done.8.down_hbm) | copy-start | bytes 746500
  70.1 6.1 %copy-start.9 = (bf16[256,1536]{1,0:T(8,128)(2,1)}, bf16[256,1536]{1,0:T(8,128)(2,1)S(1)}, u32[]{:S(2)}) copy-start(bf16[256,1536]{1,0:T(8,128)(2,1)S(1)} %collective-permute-done.4.side_hbm) | copy-start | bytes 2359300
  70.1 6.0 %collective-permute-start.10 = (bf16[256,1536]{1,0:T(8,128)(2,1)S(1)}, bf16[256,1536]{1,0:T(8,128)(2,1)S(1)}, u32[]{:S(2)}, u32[]{:S(2)}) collective-permute-start(bf16[256,1536]{1,0:T(8,128)(2,1)S(1)} %collective-permute-done.4.side_hbm), channel_id=1, source_target_pairs={{0,16},{16,0},{1,17},{17,1},{2,18},{18,2},{3,19},{19,3},{4,20},{20... | collective-permute-start | bytes 2359304 | tf_op jit(solution)/shard_map/ppermute | solution.py:34
  74.3 1.9 %copy-start.10 = (bf16[256,1536]{1,0:T(8,128)(2,1)}, bf16[256,1536]{1,0:T(8,128)(2,1)S(1)}, u32[]{:S(2)}) copy-start(bf16[256,1536]{1,0:T(8,128)(2,1)S(1)} %collective-permute-done.9.core_hbm) | copy-start | bytes 2359300
  76.2 0.9 copy-start.11
  88.2 45.5 %all-to-all-start.1 = ((bf16[128,32,128]{2,1,0:T(8,128)(2,1)}), bf16[128,32,128]{2,1,0:T(8,128)(2,1)S(1)}, u32[]{:S(2)}, u32[]{:S(2)}) async-start(bf16[128,32,128]{2,1,0:T(8,128)(2,1)} %get-tuple-element.38), calls=%async_computation.1 | async-start | bytes 2097152 | tf_op jit(solution)/shard_map/all_to_all | solution.py:412
  102.5 5.2 %collective-permute-start.11 = (bf16[512,1152]{1,0:T(8,128)(2,1)}, bf16[512,1152]{1,0:T(8,128)(2,1)S(1)}, u32[]{:S(2)}, u32[]{:S(2)}) collective-permute-start(bf16[512,1152]{1,0:T(8,128)(2,1)} %get-tuple-element.40), channel_id=1, source_target_pairs={{0,16},{16,0},{1,17},{17,1},{2,18},{18,2},{3,19},{19,3},{4,20},{20... | collective-permute-start | bytes 3538952 | tf_op jit(solution)/shard_map/ppermute | solution.py:34
  107.7 1.3 copy-start.1
  109.3 23.6 %collective-permute-start.12 = (bf16[256,1152]{1,0:T(8,128)(2,1)S(1)}, bf16[256,1152]{1,0:T(8,128)(2,1)S(1)}, u32[]{:S(2)}, u32[]{:S(2)}) collective-permute-start(bf16[256,1152]{1,0:T(8,128)(2,1)S(1)} %get-tuple-element.42), channel_id=1, source_target_pairs={{0,8},{8,0},{1,9},{9,1},{2,10},{10,2},{3,11},{11,3},{4,12},{12,4},... | collective-permute-start | bytes 1769480 | tf_op jit(solution)/shard_map/ppermute | solution.py:34
  134.0 24.5 %copy-start.7 = (s32[3]{0:T(128)S(1)}, s32[3]{0:T(128)}, u32[]{:S(2)}) copy-start(s32[3]{0:T(128)} %copy-done.6) | copy-start | bytes 40
  158.5 7.4 %copy-start.4 = (f32[36,1728]{1,0:T(8,128)S(1)}, f32[36,1728]{1,0:T(8,128)}, u32[]{:S(2)}) copy-start(f32[36,1728]{1,0:T(8,128)} %slow_ref.1) | copy-start | bytes 746500
  158.5 7.4 %copy-start.5 = (f32[36,1728]{1,0:T(8,128)S(1)}, f32[36,1728]{1,0:T(8,128)}, u32[]{:S(2)}) copy-start(f32[36,1728]{1,0:T(8,128)} %fast_ref.1) | copy-start | bytes 746500
  159.1 6.7 %collective-permute-start.13 = (f32[2,36,432]{2,1,0:T(8,128)S(1)}, f32[2,36,432]{2,1,0:T(8,128)S(1)}, u32[]{:S(2)}, u32[]{:S(2)}) collective-permute-start(f32[2,36,432]{2,1,0:T(8,128)S(1)} %get-tuple-element.44), channel_id=1, source_target_pairs={{0,16},{16,0},{1,17},{17,1},{2,18},{18,2},{3,19},{19,3},{4,20},{20... | collective-permute-start | bytes 373256 | tf_op jit(solution)/shard_map/ppermute | solution.py:34

commit v11 on v10

--- a/solution.py
+++ b/solution.py
@@ -206,9 +206,13 @@
         load.wait()
     blocks = [raw_ref[low, group].astype(F32) for group in range(4) for low in range(4)]
     weight_ref[...] = jnp.concatenate(blocks, axis=0).astype(BF16)
-    for load in loads[5:]:
-        load.wait()
-    projected_all = dot(token_ref[:, :model_width], weight_ref[...], ((1,), (0,)))
+    halves = []
+    for side in range(2):
+        for load in loads[5 + 2 * side : 7 + 2 * side]:
+            load.wait()
+        rows = token_ref[2 * side * tokens : 2 * (side + 1) * tokens, :model_width]
+        halves.append(dot(rows, weight_ref[...], ((1,), (0,))))
+    projected_all = jnp.concatenate(halves, axis=0)
     for index, skip in enumerate((1, 0, 0, 1)):
         here = slice(index * tokens, (index + 1) * tokens)
         projected = projected_all[here]
@@ -262,12 +266,14 @@
     out_ref[...] = jnp.concatenate([upper, lower], axis=0).astype(BF16)
 
 
-def quad_kernel(spot_ref, own_ref, far_ref, across_ref, both_ref, out_ref):
+def quad_kernel(spot_ref, own_ref, far_ref, across_ref, both_ref, out_ref, lower_ref, upper_ref):
     place = spot_ref[2]
     out_ref[place] = own_ref[...]
     out_ref[place + 1 - 2 * lax.rem(place, 2)] = far_ref[...]
     out_ref[lax.rem(place + 2, 4)] = across_ref[...]
     out_ref[3 - place] = both_ref[...]
+    lower_ref[...] = out_ref[:2]
+    upper_ref[...] = out_ref[2:]
 
 
 def payload_kernel(parts_ref, back_ref, out_ref):
@@ -365,19 +371,21 @@
 
     mine, theirs = call(columns_kernel, [((own_rows, cols), BF16)] * 2, spots, master, smem=1)
     pair = call(pair_kernel, [((pair_rows, cols), BF16)], spots, mine, swap(theirs, "c"), smem=1)
-    quad = call(
-        quad_kernel,
-        [((4, pair_rows, cols), BF16)],
-        spots, pair, half_turn(pair), swap(pair, "xh"), both_turn(pair),
-        smem=1,
-    )
-    quad, tokens = lax.optimization_barrier((quad, tokens))
+    turned, opposite, diagonal = half_turn(pair), swap(pair, "xh"), both_turn(pair)
+    turned, opposite, diagonal, tokens = lax.optimization_barrier((turned, opposite, diagonal, tokens))
 
     modulation = modulate_table(timesteps, ada_weight)
     broad = lanes(width + 2 * quarter)
     to_core, to_side = call(norm_kernel, [((patches, broad), BF16)] * 2, spots, tokens, modulation, smem=1)
     from_side = swap(to_side, "xl")
-    up, low, high, down = shift(quad, -1), shift(quad[:2], -2), shift(quad[2:], 2), shift(quad, 1)
+    pair, turned, opposite, diagonal, to_core = lax.optimization_barrier((pair, turned, opposite, diagonal, to_core))
+    quad, lower, upper = call(
+        quad_kernel,
+        [((4, pair_rows, cols), BF16), ((2, pair_rows, cols), BF16), ((2, pair_rows, cols), BF16)],
+        spots, pair, turned, opposite, diagonal,
+        smem=1,
+    )
+    up, low, high, down = shift(quad, -1), shift(lower, -2), shift(upper, 2), shift(quad, 1)
     to_core, low = lax.optimization_barrier((to_core, low))
     from_core = swap(to_core, "c")
     from_side, up, low, high, down = lax.optimization_barrier((from_side, up, low, high, down))

time: 168 us -> 168 us (level)
  no operation moved by 1% of the time
where the time goes in v11:
time: 168 us; the launch traced here: 167 us
  starting transfers between devices  77.2 us (46%)
  waiting for transfers between devices  39.1 us (23%)
  blocking collectives  24.5 us (15%)
  Pallas kernels  20.6 us (12%)
  local copies, waits for them, and re-layouts  3.09 us (2%)
  between operations  2.48 us (1%)
    ppermute x8, starting transfers between devices, swap(): return lax.ppermute(value, axis, [(0, 1), (1, 0)])  29.7 us
    ppermute x8, waiting for transfers between devices, swap(): return lax.ppermute(value, axis, [(0, 1), (1, 0)])  27 us
    all_to_all x1, blocking collectives, on_device(): lax.all_to_all(joint.reshape(n_seq, patches // n_seq, width + 256), SEQ,...  24.5 us
    ppermute x5, starting transfers between devices, shift(): lax.ppermute(value, 'z', [(i, (i + away) % count) for i in range(count)])  22.3 us
    pallas_call x11, Pallas kernels, call(): pl.pallas_call(kernel, out_shape=shapes, in_specs=specs, out_specs=[pl.Bl...  20.6 us
    all_to_all x1, starting transfers between devices, on_device(): parts = lax.all_to_all(packed, ROWS + ('y',), 0, 0, tiled=True)  14.3 us
    all_to_all x1, starting transfers between devices, on_device(): lax.all_to_all(packed.reshape(n_seq, patches // n_seq, width + loose), SE...  8.83 us
    ppermute x1, waiting for transfers between devices, both_turn(): return lax.ppermute(value, ('xh', 'z'), pairs)  8.6 us
  transfers between devices with their start and end apart: 16, of which 7 were waited for; matrix products, arithmetic and copies ran while one was open for 1% of the time, Pallas kernels for 2%

profile of v11, /device:TPU:1, one launch (start us, length us, event | category | flops | bytes accessed | tf_op | source)
XLA Modules:
  0.0 167.4 jit_solution(4268756370159942136)
XLA Ops:
  0.6 0.0 copy-start
  0.6 2.2 %shard_map.105 = bf16[256,1792]{1,0:T(8,128)(2,1)} custom-call(bf16[256,1152]{1,0:T(8,128)(2,1)} %bitcast.20, bf16[576,256]{1,0:T(8,128)(2,1)} %bitcast.22), custom_call_target="tpu_custom_call" | custom-call | bytes 1802240 | tf_op jit(solution)/shard_map/pallas_call | solution.py:324
  2.8 0.0 copy-start.2
  2.8 8.8 %all-to-all-start = ((bf16[16,16,1792]{2,1,0:T(8,128)(2,1)}), bf16[16,16,1792]{2,1,0:T(8,128)(2,1)S(1)}, u32[]{:S(2)}, u32[]{:S(2)}) async-start(bf16[16,16,1792]{2,1,0:T(8,128)(2,1)} %bitcast.19), calls=%async_computation | async-start | bytes 1835008 | tf_op jit(solution)/shard_map/all_to_all | solution.py:369
  11.7 0.1 pad_add_fusion.spot_ref
  11.7 0.0 copy-done.2
  11.8 0.9 shard_map.103
  12.6 3.7 %collective-permute-start = (bf16[36,432]{1,0:T(8,128)(2,1)S(1)}, bf16[36,432]{1,0:T(8,128)(2,1)S(1)}, u32[]{:S(2)}, u32[]{:S(2)}) collective-permute-start(bf16[36,432]{1,0:T(8,128)(2,1)S(1)} %get-tuple-element.36), channel_id=1, source_target_pairs={{0,16},{16,0},{1,17},{17,1},{2,18},{18,2},{3,19},{19,3},{4,20},{20... | collective-permute-start | bytes 93320 | tf_op jit(solution)/shard_map/ppermute | solution.py:34
  17.0 0.1 sine_convert_fusion
  17.1 0.1 collective-permute-done.theirs_ref
  17.2 0.6 shard_map.104.own_ref
  17.8 9.8 %collective-permute-start.1 = (bf16[72,432]{1,0:T(8,128)(2,1)S(1)}, bf16[72,432]{1,0:T(8,128)(2,1)S(1)}, u32[]{:S(2)}, u32[]{:S(2)}) collective-permute-start(bf16[72,432]{1,0:T(8,128)(2,1)S(1)} %shard_map.104.own_ref), channel_id=1, source_target_pairs={{0,128},{32,160},{64,192},{96,224},{128,0},{160,32},{192,64},{224,... | collective-permute-start | bytes 186632 | tf_op jit(solution)/shard_map/ppermute | solution.py:39
  27.6 4.4 %collective-permute-start.2 = (bf16[72,432]{1,0:T(8,128)(2,1)S(1)}, bf16[72,432]{1,0:T(8,128)(2,1)S(1)}, u32[]{:S(2)}, u32[]{:S(2)}) collective-permute-start(bf16[72,432]{1,0:T(8,128)(2,1)S(1)} %shard_map.104.own_ref), channel_id=1, source_target_pairs={{0,256},{256,0},{1,257},{257,1},{2,258},{258,2},{3,259},{259,3},{4... | collective-permute-start | bytes 186632 | tf_op jit(solution)/shard_map/ppermute | solution.py:34
  31.9 2.2 %collective-permute-start.3 = (bf16[72,432]{1,0:T(8,128)(2,1)S(1)}, bf16[72,432]{1,0:T(8,128)(2,1)S(1)}, u32[]{:S(2)}, u32[]{:S(2)}) collective-permute-start(bf16[72,432]{1,0:T(8,128)(2,1)S(1)} %shard_map.104.own_ref), channel_id=1, source_target_pairs={{0,384},{32,416},{64,448},{96,480},{128,256},{160,288},{192,320},{... | collective-permute-start | bytes 186632 | tf_op jit(solution)/shard_map/ppermute | solution.py:49
  34.1 0.0 copy-done
  34.1 0.2 fusion.mod_ref
  34.3 0.0 collective-permute-done.1.far_ref
  34.3 0.7 collective-permute-done.2.across_ref
  35.0 8.6 %collective-permute-done.3.both_ref = bf16[72,432]{1,0:T(8,128)(2,1)S(1)} collective-permute-done((bf16[72,432]{1,0:T(8,128)(2,1)S(1)}, bf16[72,432]{1,0:T(8,128)(2,1)S(1)}, u32[]{:S(2)}, u32[]{:S(2)}) %collective-permute-start.3) | collective-permute-done | bytes 62240 | tf_op jit(solution)/shard_map/ppermute | solution.py:49
  43.6 0.0 all-to-all-done
  43.6 1.8 %shard_map.106 = (bf16[256,1536]{1,0:T(8,128)(2,1)S(1)}, bf16[256,1536]{1,0:T(8,128)(2,1)S(1)}) custom-call(s32[3]{0:T(128)S(1)} %pad_add_fusion.spot_ref, bf16[256,1792]{1,0:T(8,128)(2,1)S(1)} %bitcast.16, f32[1,2304]{1,0:T(1,128)S(1)} %fusion.mod_ref), custom_call_target="tpu_custom_call" | custom-call | bytes 2499596 | tf_op jit(solution)/shard_map/pallas_call | solution.py:324
  45.4 0.0 copy-start.7
  45.5 2.9 %collective-permute-start.4 = (bf16[256,1536]{1,0:T(8,128)(2,1)S(1)}, bf16[256,1536]{1,0:T(8,128)(2,1)S(1)}, u32[]{:S(2)}, u32[]{:S(2)}) collective-permute-start(bf16[256,1536]{1,0:T(8,128)(2,1)S(1)} %get-tuple-element.47), channel_id=1, source_target_pairs={{0,8},{8,0},{1,9},{9,1},{2,10},{10,2},{3,11},{11,3},{4,12},{12,4},... | collective-permute-start | bytes 2359304 | tf_op jit(solution)/shard_map/ppermute | solution.py:34
  48.4 0.6 shard_map.107
  49.0 0.0 copy-start.8
  49.0 1.9 %collective-permute-start.5 = (bf16[4,72,432]{2,1,0:T(8,128)(2,1)S(1)}, bf16[4,72,432]{2,1,0:T(8,128)(2,1)S(1)}, u32[]{:S(2)}, u32[]{:S(2)}) collective-permute-start(bf16[4,72,432]{2,1,0:T(8,128)(2,1)S(1)} %get-tuple-element.46.near_hbm), channel_id=1, source_target_pairs={{0,224},{32,0},{64,32},{96,64},{128,96},{160,128},{192,160},{224,1... | collective-permute-start | bytes 746504 | tf_op jit(solution)/shard_map/ppermute | solution.py:39
  50.9 3.4 %collective-permute-start.8 = (bf16[4,72,432]{2,1,0:T(8,128)(2,1)S(1)}, bf16[4,72,432]{2,1,0:T(8,128)(2,1)S(1)}, u32[]{:S(2)}, u32[]{:S(2)}) collective-permute-start(bf16[4,72,432]{2,1,0:T(8,128)(2,1)S(1)} %get-tuple-element.46.near_hbm), channel_id=1, source_target_pairs={{0,32},{32,64},{64,96},{96,128},{128,160},{160,192},{192,224},{224... | collective-permute-start | bytes 746504 | tf_op jit(solution)/shard_map/ppermute | solution.py:39
  54.3 4.3 %collective-permute-start.6 = (bf16[2,72,432]{2,1,0:T(8,128)(2,1)S(1)}, bf16[2,72,432]{2,1,0:T(8,128)(2,1)S(1)}, u32[]{:S(2)}, u32[]{:S(2)}) collective-permute-start(bf16[2,72,432]{2,1,0:T(8,128)(2,1)S(1)} %get-tuple-element.49), channel_id=1, source_target_pairs={{0,192},{32,224},{64,0},{96,32},{128,64},{160,96},{192,128},{224,1... | collective-permute-start | bytes 373256 | tf_op jit(solution)/shard_map/ppermute | solution.py:39
  58.7 2.9 %collective-permute-start.7 = (bf16[2,72,432]{2,1,0:T(8,128)(2,1)S(1)}, bf16[2,72,432]{2,1,0:T(8,128)(2,1)S(1)}, u32[]{:S(2)}, u32[]{:S(2)}) collective-permute-start(bf16[2,72,432]{2,1,0:T(8,128)(2,1)S(1)} %get-tuple-element.51), channel_id=1, source_target_pairs={{0,64},{32,96},{64,128},{96,160},{128,192},{160,224},{192,0},{224,... | collective-permute-start | bytes 373256 | tf_op jit(solution)/shard_map/ppermute | solution.py:39
  61.5 3.5 %collective-permute-done.6.low_hbm = bf16[2,72,432]{2,1,0:T(8,128)(2,1)S(1)} collective-permute-done((bf16[2,72,432]{2,1,0:T(8,128)(2,1)S(1)}, bf16[2,72,432]{2,1,0:T(8,128)(2,1)S(1)}, u32[]{:S(2)}, u32[]{:S(2)}) %collective-permute-start.6) | collective-permute-done | bytes 124448 | tf_op jit(solution)/shard_map/ppermute | solution.py:39
  65.0 5.0 %collective-permute-start.9 = (bf16[256,1536]{1,0:T(8,128)(2,1)S(1)}, bf16[256,1536]{1,0:T(8,128)(2,1)S(1)}, u32[]{:S(2)}, u32[]{:S(2)}) collective-permute-start(bf16[256,1536]{1,0:T(8,128)(2,1)S(1)} %get-tuple-element.56.own_hbm), channel_id=1, source_target_pairs={{0,16},{16,0},{1,17},{17,1},{2,18},{18,2},{3,19},{19,3},{4,20},{20... | collective-permute-start | bytes 2359304 | tf_op jit(solution)/shard_map/ppermute | solution.py:34
  70.0 0.0 collective-permute-done.7.high_hbm
  70.1 0.0 copy-start.15
  70.1 0.0 collective-permute-done.5.up_hbm
  70.1 0.0 copy-start.12
  70.1 0.0 collective-permute-done.8.down_hbm
  70.1 0.0 copy-start.13
  70.1 0.0 collective-permute-done.4.side_hbm
  70.1 0.0 copy-start.9
  70.1 4.1 %collective-permute-start.10 = (bf16[256,1536]{1,0:T(8,128)(2,1)S(1)}, bf16[256,1536]{1,0:T(8,128)(2,1)S(1)}, u32[]{:S(2)}, u32[]{:S(2)}) collective-permute-start(bf16[256,1536]{1,0:T(8,128)(2,1)S(1)} %collective-permute-done.4.side_hbm), channel_id=1, source_target_pairs={{0,16},{16,0},{1,17},{17,1},{2,18},{18,2},{3,19},{19,3},{4,20},{20... | collective-permute-start | bytes 2359304 | tf_op jit(solution)/shard_map/ppermute | solution.py:34
  74.3 0.0 collective-permute-done.9.core_hbm
  74.3 1.9 %collective-permute-done.10.both_hbm = bf16[256,1536]{1,0:T(8,128)(2,1)S(1)} collective-permute-done((bf16[256,1536]{1,0:T(8,128)(2,1)S(1)}, bf16[256,1536]{1,0:T(8,128)(2,1)S(1)}, u32[]{:S(2)}, u32[]{:S(2)}) %collective-permute-start.10) | collective-permute-done | bytes 786464 | tf_op jit(solution)/shard_map/ppermute | solution.py:34
  76.2 0.0 copy-done.7
  76.2 0.0 copy-done.14
  76.2 0.9 copy-done.11
  77.1 11.1 %shard_map.108 = (bf16[128,32,128]{2,1,0:T(8,128)(2,1)}, bf16[512,1152]{1,0:T(8,128)(2,1)}, bf16[512,1152]{1,0:T(8,128)(2,1)}) custom-call(s32[3]{0:T(128)} %copy-done.5, bf16[4,72,432]{2,1,0:T(8,128)(2,1)} %copy-done.8, bf16[4,72,432]{2,1,0:T(8,128)(2,1)} %copy-done.12, bf16[2,72,432]{2,1,0:T(8,128)(2,1)} %copy-done.14, bf16[2,72,432]{2,1,0:T(8,128)(2,1)} %copy-done.15, ...), custom_call_target="tpu_custom_call" | custom-call | flops 3057647616 | bytes 7548940 | tf_op jit(solution)/shard_map/pallas_call | solution.py:324
  88.2 14.3 %all-to-all-start.1 = ((bf16[128,32,128]{2,1,0:T(8,128)(2,1)}), bf16[128,32,128]{2,1,0:T(8,128)(2,1)S(1)}, u32[]{:S(2)}, u32[]{:S(2)}) async-start(bf16[128,32,128]{2,1,0:T(8,128)(2,1)} %get-tuple-element.58), calls=%async_computation.1 | async-start | bytes 2097152 | tf_op jit(solution)/shard_map/all_to_all | solution.py:420
  102.5 2.6 %collective-permute-start.11 = (bf16[512,1152]{1,0:T(8,128)(2,1)}, bf16[512,1152]{1,0:T(8,128)(2,1)S(1)}, u32[]{:S(2)}, u32[]{:S(2)}) collective-permute-start(bf16[512,1152]{1,0:T(8,128)(2,1)} %get-tuple-element.60), channel_id=1, source_target_pairs={{0,16},{16,0},{1,17},{17,1},{2,18},{18,2},{3,19},{19,3},{4,20},{20... | collective-permute-start | bytes 3538952 | tf_op jit(solution)/shard_map/ppermute | solution.py:34
  105.1 2.7 %collective-permute-done.11.got_ref = bf16[512,1152]{1,0:T(8,128)(2,1)S(1)} collective-permute-done((bf16[512,1152]{1,0:T(8,128)(2,1)}, bf16[512,1152]{1,0:T(8,128)(2,1)S(1)}, u32[]{:S(2)}, u32[]{:S(2)}) %collective-permute-start.11) | collective-permute-done | bytes 1179680 | tf_op jit(solution)/shard_map/ppermute | solution.py:34
  107.8 1.3 copy-done.1
  109.0 0.3 shard_map.109
  109.3 1.9 %collective-permute-start.12 = (bf16[256,1152]{1,0:T(8,128)(2,1)S(1)}, bf16[256,1152]{1,0:T(8,128)(2,1)S(1)}, u32[]{:S(2)}, u32[]{:S(2)}) collective-permute-start(bf16[256,1152]{1,0:T(8,128)(2,1)S(1)} %get-tuple-element.62), channel_id=1, source_target_pairs={{0,8},{8,0},{1,9},{9,1},{2,10},{10,2},{3,11},{11,3},{4,12},{12,4},... | collective-permute-start | bytes 1769480 | tf_op jit(solution)/shard_map/ppermute | solution.py:34
  111.2 21.7 %collective-permute-done.12.refs_1_ = bf16[256,1152]{1,0:T(8,128)(2,1)S(1)} collective-permute-done((bf16[256,1152]{1,0:T(8,128)(2,1)S(1)}, bf16[256,1152]{1,0:T(8,128)(2,1)S(1)}, u32[]{:S(2)}, u32[]{:S(2)}) %collective-permute-start.12) | collective-permute-done | bytes 589856 | tf_op jit(solution)/shard_map/ppermute | solution.py:34
  132.9 0.9 shard_map.110.back_ref
  133.8 0.0 all-to-all-done.1.parts_ref
  133.8 0.2 shard_map.111
  134.0 24.5 %all_to_all.15.pieces_ref = bf16[16,16,1408]{2,1,0:T(8,128)(2,1)S(1)} all-to-all(bf16[16,16,1408]{2,1,0:T(8,128)(2,1)S(1)} %bitcast.18), channel_id=1, replica_groups=mesh['xh'=2,'z'=8,'c'=2,'xl'=2,'y'=8] {'xl','y'}, dimensions={0} | all-to-all | bytes 1441792 | tf_op jit(solution)/shard_map/all_to_all | solution.py:422
  158.5 0.6 shard_map.112
  159.1 5.0 %collective-permute-start.13 = (f32[2,36,432]{2,1,0:T(8,128)S(1)}, f32[2,36,432]{2,1,0:T(8,128)S(1)}, u32[]{:S(2)}, u32[]{:S(2)}) collective-permute-start(f32[2,36,432]{2,1,0:T(8,128)S(1)} %get-tuple-element.64), channel_id=1, source_target_pairs={{0,16},{16,0},{1,17},{17,1},{2,18},{18,2},{3,19},{19,3},{4,20},{20... | collective-permute-start | bytes 373256 | tf_op jit(solution)/shard_map/ppermute | solution.py:34
  164.9 0.1 pad_maximum_fusion.decay_ref
  165.0 0.9 slice.4
  165.8 0.0 collective-permute-done.13.core_ref
  165.9 0.0 copy-done.3
  165.9 1.5 shard_map.113
  (17 shorter events, 0.0 us)
Async XLA Ops:
  0.6 33.5 %copy-start = (bf16[128,2304]{1,0:T(8,128)(2,1)S(1)}, bf16[128,2304]{1,0:T(8,128)(2,1)}, u32[]{:S(2)}) copy-start(bf16[128,2304]{1,0:T(8,128)(2,1)} %param.10) | copy-start | bytes 1769476
  2.8 8.9 %copy-start.2 = (f32[36,1728]{1,0:T(8,128)S(1)}, f32[36,1728]{1,0:T(8,128)}, u32[]{:S(2)}) copy-start(f32[36,1728]{1,0:T(8,128)} %master_ref.1) | copy-start | bytes 746500
  2.8 40.8 %all-to-all-start = ((bf16[16,16,1792]{2,1,0:T(8,128)(2,1)}), bf16[16,16,1792]{2,1,0:T(8,128)(2,1)S(1)}, u32[]{:S(2)}, u32[]{:S(2)}) async-start(bf16[16,16,1792]{2,1,0:T(8,128)(2,1)} %bitcast.19), calls=%async_computation | async-start | bytes 1835008 | tf_op jit(solution)/shard_map/all_to_all | solution.py:369
  11.8 64.4 %copy-start.5 = (s32[3]{0:T(128)}, s32[3]{0:T(128)S(1)}, u32[]{:S(2)}) copy-start(s32[3]{0:T(128)S(1)} %pad_add_fusion.spot_ref) | copy-start | bytes 40
  12.6 4.6 %collective-permute-start = (bf16[36,432]{1,0:T(8,128)(2,1)S(1)}, bf16[36,432]{1,0:T(8,128)(2,1)S(1)}, u32[]{:S(2)}, u32[]{:S(2)}) collective-permute-start(bf16[36,432]{1,0:T(8,128)(2,1)S(1)} %get-tuple-element.36), channel_id=1, source_target_pairs={{0,16},{16,0},{1,17},{17,1},{2,18},{18,2},{3,19},{19,3},{4,20},{20... | collective-permute-start | bytes 93320 | tf_op jit(solution)/shard_map/ppermute | solution.py:34
  17.8 16.6 %collective-permute-start.1 = (bf16[72,432]{1,0:T(8,128)(2,1)S(1)}, bf16[72,432]{1,0:T(8,128)(2,1)S(1)}, u32[]{:S(2)}, u32[]{:S(2)}) collective-permute-start(bf16[72,432]{1,0:T(8,128)(2,1)S(1)} %shard_map.104.own_ref), channel_id=1, source_target_pairs={{0,128},{32,160},{64,192},{96,224},{128,0},{160,32},{192,64},{224,... | collective-permute-start | bytes 186632 | tf_op jit(solution)/shard_map/ppermute | solution.py:39
  27.6 7.5 %collective-permute-start.2 = (bf16[72,432]{1,0:T(8,128)(2,1)S(1)}, bf16[72,432]{1,0:T(8,128)(2,1)S(1)}, u32[]{:S(2)}, u32[]{:S(2)}) collective-permute-start(bf16[72,432]{1,0:T(8,128)(2,1)S(1)} %shard_map.104.own_ref), channel_id=1, source_target_pairs={{0,256},{256,0},{1,257},{257,1},{2,258},{258,2},{3,259},{259,3},{4... | collective-permute-start | bytes 186632 | tf_op jit(solution)/shard_map/ppermute | solution.py:34
  31.9 11.7 %collective-permute-start.3 = (bf16[72,432]{1,0:T(8,128)(2,1)S(1)}, bf16[72,432]{1,0:T(8,128)(2,1)S(1)}, u32[]{:S(2)}, u32[]{:S(2)}) collective-permute-start(bf16[72,432]{1,0:T(8,128)(2,1)S(1)} %shard_map.104.own_ref), channel_id=1, source_target_pairs={{0,384},{32,416},{64,448},{96,480},{128,256},{160,288},{192,320},{... | collective-permute-start | bytes 186632 | tf_op jit(solution)/shard_map/ppermute | solution.py:49
  45.4 30.7 %copy-start.7 = (bf16[256,1536]{1,0:T(8,128)(2,1)}, bf16[256,1536]{1,0:T(8,128)(2,1)S(1)}, u32[]{:S(2)}) copy-start(bf16[256,1536]{1,0:T(8,128)(2,1)S(1)} %get-tuple-element.56.own_hbm) | copy-start | bytes 2359300
  45.5 24.7 %collective-permute-start.4 = (bf16[256,1536]{1,0:T(8,128)(2,1)S(1)}, bf16[256,1536]{1,0:T(8,128)(2,1)S(1)}, u32[]{:S(2)}, u32[]{:S(2)}) collective-permute-start(bf16[256,1536]{1,0:T(8,128)(2,1)S(1)} %get-tuple-element.47), channel_id=1, source_target_pairs={{0,8},{8,0},{1,9},{9,1},{2,10},{10,2},{3,11},{11,3},{4,12},{12,4},... | collective-permute-start | bytes 2359304 | tf_op jit(solution)/shard_map/ppermute | solution.py:34
  49.0 27.2 %copy-start.8 = (bf16[4,72,432]{2,1,0:T(8,128)(2,1)}, bf16[4,72,432]{2,1,0:T(8,128)(2,1)S(1)}, u32[]{:S(2)}) copy-start(bf16[4,72,432]{2,1,0:T(8,128)(2,1)S(1)} %get-tuple-element.46.near_hbm) | copy-start | bytes 746500
  49.0 21.1 %collective-permute-start.5 = (bf16[4,72,432]{2,1,0:T(8,128)(2,1)S(1)}, bf16[4,72,432]{2,1,0:T(8,128)(2,1)S(1)}, u32[]{:S(2)}, u32[]{:S(2)}) collective-permute-start(bf16[4,72,432]{2,1,0:T(8,128)(2,1)S(1)} %get-tuple-element.46.near_hbm), channel_id=1, source_target_pairs={{0,224},{32,0},{64,32},{96,64},{128,96},{160,128},{192,160},{224,1... | collective-permute-start | bytes 746504 | tf_op jit(solution)/shard_map/ppermute | solution.py:39
  50.9 19.2 %collective-permute-start.8 = (bf16[4,72,432]{2,1,0:T(8,128)(2,1)S(1)}, bf16[4,72,432]{2,1,0:T(8,128)(2,1)S(1)}, u32[]{:S(2)}, u32[]{:S(2)}) collective-permute-start(bf16[4,72,432]{2,1,0:T(8,128)(2,1)S(1)} %get-tuple-element.46.near_hbm), channel_id=1, source_target_pairs={{0,32},{32,64},{64,96},{96,128},{128,160},{160,192},{192,224},{224... | collective-permute-start | bytes 746504 | tf_op jit(solution)/shard_map/ppermute | solution.py:39
  54.3 10.7 %collective-permute-start.6 = (bf16[2,72,432]{2,1,0:T(8,128)(2,1)S(1)}, bf16[2,72,432]{2,1,0:T(8,128)(2,1)S(1)}, u32[]{:S(2)}, u32[]{:S(2)}) collective-permute-start(bf16[2,72,432]{2,1,0:T(8,128)(2,1)S(1)} %get-tuple-element.49), channel_id=1, source_target_pairs={{0,192},{32,224},{64,0},{96,32},{128,64},{160,96},{192,128},{224,1... | collective-permute-start | bytes 373256 | tf_op jit(solution)/shard_map/ppermute | solution.py:39
  58.7 11.4 %collective-permute-start.7 = (bf16[2,72,432]{2,1,0:T(8,128)(2,1)S(1)}, bf16[2,72,432]{2,1,0:T(8,128)(2,1)S(1)}, u32[]{:S(2)}, u32[]{:S(2)}) collective-permute-start(bf16[2,72,432]{2,1,0:T(8,128)(2,1)S(1)} %get-tuple-element.51), channel_id=1, source_target_pairs={{0,64},{32,96},{64,128},{96,160},{128,192},{160,224},{192,0},{224,... | collective-permute-start | bytes 373256 | tf_op jit(solution)/shard_map/ppermute | solution.py:39
  65.0 11.2 %copy-start.14 = (bf16[2,72,432]{2,1,0:T(8,128)(2,1)}, bf16[2,72,432]{2,1,0:T(8,128)(2,1)S(1)}, u32[]{:S(2)}) copy-start(bf16[2,72,432]{2,1,0:T(8,128)(2,1)S(1)} %collective-permute-done.6.low_hbm) | copy-start | bytes 373252
  65.0 9.3 %collective-permute-start.9 = (bf16[256,1536]{1,0:T(8,128)(2,1)S(1)}, bf16[256,1536]{1,0:T(8,128)(2,1)S(1)}, u32[]{:S(2)}, u32[]{:S(2)}) collective-permute-start(bf16[256,1536]{1,0:T(8,128)(2,1)S(1)} %get-tuple-element.56.own_hbm), channel_id=1, source_target_pairs={{0,16},{16,0},{1,17},{17,1},{2,18},{18,2},{3,19},{19,3},{4,20},{20... | collective-permute-start | bytes 2359304 | tf_op jit(solution)/shard_map/ppermute | solution.py:34
  70.1 6.1 %copy-start.15 = (bf16[2,72,432]{2,1,0:T(8,128)(2,1)}, bf16[2,72,432]{2,1,0:T(8,128)(2,1)S(1)}, u32[]{:S(2)}) copy-start(bf16[2,72,432]{2,1,0:T(8,128)(2,1)S(1)} %collective-permute-done.7.high_hbm) | copy-start | bytes 373252
  70.1 6.1 %copy-start.12 = (bf16[4,72,432]{2,1,0:T(8,128)(2,1)}, bf16[4,72,432]{2,1,0:T(8,128)(2,1)S(1)}, u32[]{:S(2)}) copy-start(bf16[4,72,432]{2,1,0:T(8,128)(2,1)S(1)} %collective-permute-done.5.up_hbm) | copy-start | bytes 746500
  70.1 6.1 %copy-start.13 = (bf16[4,72,432]{2,1,0:T(8,128)(2,1)}, bf16[4,72,432]{2,1,0:T(8,128)(2,1)S(1)}, u32[]{:S(2)}) copy-start(bf16[4,72,432]{2,1,0:T(8,128)(2,1)S(1)} %collective-permute-done.8.down_hbm) | copy-start | bytes 746500
  70.1 6.1 %copy-start.9 = (bf16[256,1536]{1,0:T(8,128)(2,1)}, bf16[256,1536]{1,0:T(8,128)(2,1)S(1)}, u32[]{:S(2)}) copy-start(bf16[256,1536]{1,0:T(8,128)(2,1)S(1)} %collective-permute-done.4.side_hbm) | copy-start | bytes 2359300
  70.1 6.0 %collective-permute-start.10 = (bf16[256,1536]{1,0:T(8,128)(2,1)S(1)}, bf16[256,1536]{1,0:T(8,128)(2,1)S(1)}, u32[]{:S(2)}, u32[]{:S(2)}) collective-permute-start(bf16[256,1536]{1,0:T(8,128)(2,1)S(1)} %collective-permute-done.4.side_hbm), channel_id=1, source_target_pairs={{0,16},{16,0},{1,17},{17,1},{2,18},{18,2},{3,19},{19,3},{4,20},{20... | collective-permute-start | bytes 2359304 | tf_op jit(solution)/shard_map/ppermute | solution.py:34
  74.3 1.9 %copy-start.10 = (bf16[256,1536]{1,0:T(8,128)(2,1)}, bf16[256,1536]{1,0:T(8,128)(2,1)S(1)}, u32[]{:S(2)}) copy-start(bf16[256,1536]{1,0:T(8,128)(2,1)S(1)} %collective-permute-done.9.core_hbm) | copy-start | bytes 2359300
  76.2 0.9 copy-start.11
  88.2 45.5 %all-to-all-start.1 = ((bf16[128,32,128]{2,1,0:T(8,128)(2,1)}), bf16[128,32,128]{2,1,0:T(8,128)(2,1)S(1)}, u32[]{:S(2)}, u32[]{:S(2)}) async-start(bf16[128,32,128]{2,1,0:T(8,128)(2,1)} %get-tuple-element.58), calls=%async_computation.1 | async-start | bytes 2097152 | tf_op jit(solution)/shard_map/all_to_all | solution.py:420
  102.5 5.2 %collective-permute-start.11 = (bf16[512,1152]{1,0:T(8,128)(2,1)}, bf16[512,1152]{1,0:T(8,128)(2,1)S(1)}, u32[]{:S(2)}, u32[]{:S(2)}) collective-permute-start(bf16[512,1152]{1,0:T(8,128)(2,1)} %get-tuple-element.60), channel_id=1, source_target_pairs={{0,16},{16,0},{1,17},{17,1},{2,18},{18,2},{3,19},{19,3},{4,20},{20... | collective-permute-start | bytes 3538952 | tf_op jit(solution)/shard_map/ppermute | solution.py:34
  107.8 1.3 copy-start.1
  109.3 23.6 %collective-permute-start.12 = (bf16[256,1152]{1,0:T(8,128)(2,1)S(1)}, bf16[256,1152]{1,0:T(8,128)(2,1)S(1)}, u32[]{:S(2)}, u32[]{:S(2)}) collective-permute-start(bf16[256,1152]{1,0:T(8,128)(2,1)S(1)} %get-tuple-element.62), channel_id=1, source_target_pairs={{0,8},{8,0},{1,9},{9,1},{2,10},{10,2},{3,11},{11,3},{4,12},{12,4},... | collective-permute-start | bytes 1769480 | tf_op jit(solution)/shard_map/ppermute | solution.py:34
  134.0 24.5 %copy-start.6 = (s32[3]{0:T(128)S(1)}, s32[3]{0:T(128)}, u32[]{:S(2)}) copy-start(s32[3]{0:T(128)} %copy-done.5) | copy-start | bytes 40
  158.5 7.4 %copy-start.3 = (f32[36,1728]{1,0:T(8,128)S(1)}, f32[36,1728]{1,0:T(8,128)}, u32[]{:S(2)}) copy-start(f32[36,1728]{1,0:T(8,128)} %slow_ref.1) | copy-start | bytes 746500
  158.5 7.4 %copy-start.4 = (f32[36,1728]{1,0:T(8,128)S(1)}, f32[36,1728]{1,0:T(8,128)}, u32[]{:S(2)}) copy-start(f32[36,1728]{1,0:T(8,128)} %fast_ref.1) | copy-start | bytes 746500
  159.1 6.7 %collective-permute-start.13 = (f32[2,36,432]{2,1,0:T(8,128)S(1)}, f32[2,36,432]{2,1,0:T(8,128)S(1)}, u32[]{:S(2)}, u32[]{:S(2)}) collective-permute-start(f32[2,36,432]{2,1,0:T(8,128)S(1)} %get-tuple-element.64), channel_id=1, source_target_pairs={{0,16},{16,0},{1,17},{17,1},{2,18},{18,2},{3,19},{19,3},{4,20},{20... | collective-permute-start | bytes 373256 | tf_op jit(solution)/shard_map/ppermute | solution.py:34

commit v12 on v11

--- a/solution.py
+++ b/solution.py
@@ -227,11 +227,11 @@
         tiles = tiles_of(total_ref[owner * height : (owner + 1) * height, :])
         each = len(tiles) // pieces
         for piece in range(pieces):
-            packed_ref[owner * pieces + piece] = jnp.concatenate(tiles[each * piece : each * piece + each], axis=0).astype(BF16)
-        if owner % 4 == 3:
-            part = pl.ds((owner - 3) * pieces, 4 * pieces)
-            stores.append(pltpu.make_async_copy(packed_ref.at[part], packed_hbm.at[part], out_sems.at[4 + owner // 4]))
-            stores[-1].start()
+            packed_ref[piece * 16 + owner] = jnp.concatenate(tiles[each * piece : each * piece + each], axis=0).astype(BF16)
+    for group in range(4):
+        part = pl.ds(group * 4 * pieces, 4 * pieces)
+        stores.append(pltpu.make_async_copy(packed_ref.at[part], packed_hbm.at[part], out_sems.at[4 + group]))
+        stores[-1].start()
     for index, (target, place) in enumerate(((inner_hbm, 0), (outer_hbm, 0), (inner_hbm, 1), (outer_hbm, 1))):
         parts_ref[index] = dot(grads_ref[index * tokens : (index + 1) * tokens, :], weight_ref[...], ((1,), (1,))).astype(BF16)
         stores.append(
@@ -417,7 +417,7 @@
     part, give = call(add_kernel, [((patches, width), BF16)] * 2, near, swap(far, "c"))
     back = call(norm_back_kernel, [((patches, width), BF16)], tokens, modulation, part, swap(give, "xl"))
 
-    parts = lax.all_to_all(packed, ROWS + ("y",), 0, 0, tiled=True)
+    parts = lax.all_to_all(packed, ("y",) + ROWS, 0, 0, tiled=True)
     joint = call(payload_kernel, [((patches, width + 256), BF16)], parts, back)
     joint = lax.all_to_all(joint.reshape(n_seq, patches // n_seq, width + 256), SEQ, 0, 0, tiled=True)
     own_grad, other_grad = call(rows_kernel, [((2, own_rows, cols), F32)] * 2, spots, joint, smem=1)

time: 168 us -> 169 us (level)
  no operation moved by 1% of the time
where the time goes in v12:
time: 169 us; the launch traced here: 168 us
  starting transfers between devices  77.1 us (46%)
  waiting for transfers between devices  39.3 us (23%)
  blocking collectives  25.1 us (15%)
  Pallas kernels  20.6 us (12%)
  local copies, waits for them, and re-layouts  3.09 us (2%)
  between operations  2.48 us (1%)
    ppermute x8, starting transfers between devices, swap(): return lax.ppermute(value, axis, [(0, 1), (1, 0)])  29.5 us
    ppermute x8, waiting for transfers between devices, swap(): return lax.ppermute(value, axis, [(0, 1), (1, 0)])  27.2 us
    all_to_all x1, blocking collectives, on_device(): lax.all_to_all(joint.reshape(n_seq, patches // n_seq, width + 256), SEQ,...  25.1 us
    ppermute x5, starting transfers between devices, shift(): lax.ppermute(value, 'z', [(i, (i + away) % count) for i in range(count)])  22.3 us
    pallas_call x11, Pallas kernels, call(): pl.pallas_call(kernel, out_shape=shapes, in_specs=specs, out_specs=[pl.Bl...  20.6 us
    all_to_all x1, starting transfers between devices, on_device(): parts = lax.all_to_all(packed, ('y',) + ROWS, 0, 0, tiled=True)  14.3 us
    all_to_all x1, starting transfers between devices, on_device(): lax.all_to_all(packed.reshape(n_seq, patches // n_seq, width + loose), SE...  8.83 us
    ppermute x1, waiting for transfers between devices, both_turn(): return lax.ppermute(value, ('xh', 'z'), pairs)  8.6 us
  transfers between devices with their start and end apart: 16, of which 7 were waited for; matrix products, arithmetic and copies ran while one was open for 1% of the time, Pallas kernels for 2%

profile of v12, /device:TPU:1, one launch (start us, length us, event | category | flops | bytes accessed | tf_op | source)
XLA Modules:
  0.0 168.0 jit_solution(17808293400572469246)
XLA Ops:
  0.6 0.0 copy-start
  0.6 2.2 %shard_map.105 = bf16[256,1792]{1,0:T(8,128)(2,1)} custom-call(bf16[256,1152]{1,0:T(8,128)(2,1)} %bitcast.20, bf16[576,256]{1,0:T(8,128)(2,1)} %bitcast.22), custom_call_target="tpu_custom_call" | custom-call | bytes 1802240 | tf_op jit(solution)/shard_map/pallas_call | solution.py:324
  2.8 0.0 copy-start.2
  2.8 8.8 %all-to-all-start = ((bf16[16,16,1792]{2,1,0:T(8,128)(2,1)}), bf16[16,16,1792]{2,1,0:T(8,128)(2,1)S(1)}, u32[]{:S(2)}, u32[]{:S(2)}) async-start(bf16[16,16,1792]{2,1,0:T(8,128)(2,1)} %bitcast.19), calls=%async_computation | async-start | bytes 1835008 | tf_op jit(solution)/shard_map/all_to_all | solution.py:369
  11.7 0.1 pad_add_fusion.spot_ref
  11.7 0.0 copy-done.2
  11.8 0.9 shard_map.103
  12.6 3.7 %collective-permute-start = (bf16[36,432]{1,0:T(8,128)(2,1)S(1)}, bf16[36,432]{1,0:T(8,128)(2,1)S(1)}, u32[]{:S(2)}, u32[]{:S(2)}) collective-permute-start(bf16[36,432]{1,0:T(8,128)(2,1)S(1)} %get-tuple-element.36), channel_id=1, source_target_pairs={{0,16},{16,0},{1,17},{17,1},{2,18},{18,2},{3,19},{19,3},{4,20},{20... | collective-permute-start | bytes 93320 | tf_op jit(solution)/shard_map/ppermute | solution.py:34
  17.0 0.1 sine_convert_fusion
  17.1 0.1 collective-permute-done.theirs_ref
  17.2 0.6 shard_map.104.own_ref
  17.8 9.8 %collective-permute-start.1 = (bf16[72,432]{1,0:T(8,128)(2,1)S(1)}, bf16[72,432]{1,0:T(8,128)(2,1)S(1)}, u32[]{:S(2)}, u32[]{:S(2)}) collective-permute-start(bf16[72,432]{1,0:T(8,128)(2,1)S(1)} %shard_map.104.own_ref), channel_id=1, source_target_pairs={{0,128},{32,160},{64,192},{96,224},{128,0},{160,32},{192,64},{224,... | collective-permute-start | bytes 186632 | tf_op jit(solution)/shard_map/ppermute | solution.py:39
  27.6 4.4 %collective-permute-start.2 = (bf16[72,432]{1,0:T(8,128)(2,1)S(1)}, bf16[72,432]{1,0:T(8,128)(2,1)S(1)}, u32[]{:S(2)}, u32[]{:S(2)}) collective-permute-start(bf16[72,432]{1,0:T(8,128)(2,1)S(1)} %shard_map.104.own_ref), channel_id=1, source_target_pairs={{0,256},{256,0},{1,257},{257,1},{2,258},{258,2},{3,259},{259,3},{4... | collective-permute-start | bytes 186632 | tf_op jit(solution)/shard_map/ppermute | solution.py:34
  31.9 2.2 %collective-permute-start.3 = (bf16[72,432]{1,0:T(8,128)(2,1)S(1)}, bf16[72,432]{1,0:T(8,128)(2,1)S(1)}, u32[]{:S(2)}, u32[]{:S(2)}) collective-permute-start(bf16[72,432]{1,0:T(8,128)(2,1)S(1)} %shard_map.104.own_ref), channel_id=1, source_target_pairs={{0,384},{32,416},{64,448},{96,480},{128,256},{160,288},{192,320},{... | collective-permute-start | bytes 186632 | tf_op jit(solution)/shard_map/ppermute | solution.py:49
  34.1 0.0 copy-done
  34.1 0.2 fusion.mod_ref
  34.3 0.0 collective-permute-done.1.far_ref
  34.3 0.7 collective-permute-done.2.across_ref
  35.0 8.6 %collective-permute-done.3.both_ref = bf16[72,432]{1,0:T(8,128)(2,1)S(1)} collective-permute-done((bf16[72,432]{1,0:T(8,128)(2,1)S(1)}, bf16[72,432]{1,0:T(8,128)(2,1)S(1)}, u32[]{:S(2)}, u32[]{:S(2)}) %collective-permute-start.3) | collective-permute-done | bytes 62240 | tf_op jit(solution)/shard_map/ppermute | solution.py:49
  43.6 0.0 all-to-all-done
  43.6 1.8 %shard_map.106 = (bf16[256,1536]{1,0:T(8,128)(2,1)S(1)}, bf16[256,1536]{1,0:T(8,128)(2,1)S(1)}) custom-call(s32[3]{0:T(128)S(1)} %pad_add_fusion.spot_ref, bf16[256,1792]{1,0:T(8,128)(2,1)S(1)} %bitcast.16, f32[1,2304]{1,0:T(1,128)S(1)} %fusion.mod_ref), custom_call_target="tpu_custom_call" | custom-call | bytes 2499596 | tf_op jit(solution)/shard_map/pallas_call | solution.py:324
  45.4 0.0 copy-start.7
  45.5 2.9 %collective-permute-start.4 = (bf16[256,1536]{1,0:T(8,128)(2,1)S(1)}, bf16[256,1536]{1,0:T(8,128)(2,1)S(1)}, u32[]{:S(2)}, u32[]{:S(2)}) collective-permute-start(bf16[256,1536]{1,0:T(8,128)(2,1)S(1)} %get-tuple-element.47), channel_id=1, source_target_pairs={{0,8},{8,0},{1,9},{9,1},{2,10},{10,2},{3,11},{11,3},{4,12},{12,4},... | collective-permute-start | bytes 2359304 | tf_op jit(solution)/shard_map/ppermute | solution.py:34
  48.4 0.6 shard_map.107
  49.0 0.0 copy-start.8
  49.0 1.9 %collective-permute-start.5 = (bf16[4,72,432]{2,1,0:T(8,128)(2,1)S(1)}, bf16[4,72,432]{2,1,0:T(8,128)(2,1)S(1)}, u32[]{:S(2)}, u32[]{:S(2)}) collective-permute-start(bf16[4,72,432]{2,1,0:T(8,128)(2,1)S(1)} %get-tuple-element.46.near_hbm), channel_id=1, source_target_pairs={{0,224},{32,0},{64,32},{96,64},{128,96},{160,128},{192,160},{224,1... | collective-permute-start | bytes 746504 | tf_op jit(solution)/shard_map/ppermute | solution.py:39
  50.9 3.4 %collective-permute-start.8 = (bf16[4,72,432]{2,1,0:T(8,128)(2,1)S(1)}, bf16[4,72,432]{2,1,0:T(8,128)(2,1)S(1)}, u32[]{:S(2)}, u32[]{:S(2)}) collective-permute-start(bf16[4,72,432]{2,1,0:T(8,128)(2,1)S(1)} %get-tuple-element.46.near_hbm), channel_id=1, source_target_pairs={{0,32},{32,64},{64,96},{96,128},{128,160},{160,192},{192,224},{224... | collective-permute-start | bytes 746504 | tf_op jit(solution)/shard_map/ppermute | solution.py:39
  54.3 4.3 %collective-permute-start.6 = (bf16[2,72,432]{2,1,0:T(8,128)(2,1)S(1)}, bf16[2,72,432]{2,1,0:T(8,128)(2,1)S(1)}, u32[]{:S(2)}, u32[]{:S(2)}) collective-permute-start(bf16[2,72,432]{2,1,0:T(8,128)(2,1)S(1)} %get-tuple-element.49), channel_id=1, source_target_pairs={{0,192},{32,224},{64,0},{96,32},{128,64},{160,96},{192,128},{224,1... | collective-permute-start | bytes 373256 | tf_op jit(solution)/shard_map/ppermute | solution.py:39
  58.7 2.9 %collective-permute-start.7 = (bf16[2,72,432]{2,1,0:T(8,128)(2,1)S(1)}, bf16[2,72,432]{2,1,0:T(8,128)(2,1)S(1)}, u32[]{:S(2)}, u32[]{:S(2)}) collective-permute-start(bf16[2,72,432]{2,1,0:T(8,128)(2,1)S(1)} %get-tuple-element.51), channel_id=1, source_target_pairs={{0,64},{32,96},{64,128},{96,160},{128,192},{160,224},{192,0},{224,... | collective-permute-start | bytes 373256 | tf_op jit(solution)/shard_map/ppermute | solution.py:39
  61.5 3.5 %collective-permute-done.6.low_hbm = bf16[2,72,432]{2,1,0:T(8,128)(2,1)S(1)} collective-permute-done((bf16[2,72,432]{2,1,0:T(8,128)(2,1)S(1)}, bf16[2,72,432]{2,1,0:T(8,128)(2,1)S(1)}, u32[]{:S(2)}, u32[]{:S(2)}) %collective-permute-start.6) | collective-permute-done | bytes 124448 | tf_op jit(solution)/shard_map/ppermute | solution.py:39
  65.0 5.0 %collective-permute-start.9 = (bf16[256,1536]{1,0:T(8,128)(2,1)S(1)}, bf16[256,1536]{1,0:T(8,128)(2,1)S(1)}, u32[]{:S(2)}, u32[]{:S(2)}) collective-permute-start(bf16[256,1536]{1,0:T(8,128)(2,1)S(1)} %get-tuple-element.56.own_hbm), channel_id=1, source_target_pairs={{0,16},{16,0},{1,17},{17,1},{2,18},{18,2},{3,19},{19,3},{4,20},{20... | collective-permute-start | bytes 2359304 | tf_op jit(solution)/shard_map/ppermute | solution.py:34
  70.0 0.0 collective-permute-done.7.high_hbm
  70.1 0.0 copy-start.15
  70.1 0.0 collective-permute-done.5.up_hbm
  70.1 0.0 copy-start.12
  70.1 0.0 collective-permute-done.8.down_hbm
  70.1 0.0 copy-start.13
  70.1 0.0 collective-permute-done.4.side_hbm
  70.1 0.0 copy-start.9
  70.1 4.1 %collective-permute-start.10 = (bf16[256,1536]{1,0:T(8,128)(2,1)S(1)}, bf16[256,1536]{1,0:T(8,128)(2,1)S(1)}, u32[]{:S(2)}, u32[]{:S(2)}) collective-permute-start(bf16[256,1536]{1,0:T(8,128)(2,1)S(1)} %collective-permute-done.4.side_hbm), channel_id=1, source_target_pairs={{0,16},{16,0},{1,17},{17,1},{2,18},{18,2},{3,19},{19,3},{4,20},{20... | collective-permute-start | bytes 2359304 | tf_op jit(solution)/shard_map/ppermute | solution.py:34
  74.3 0.0 collective-permute-done.9.core_hbm
  74.3 0.0 copy-start.10
  74.3 1.9 %collective-permute-done.10.both_hbm = bf16[256,1536]{1,0:T(8,128)(2,1)S(1)} collective-permute-done((bf16[256,1536]{1,0:T(8,128)(2,1)S(1)}, bf16[256,1536]{1,0:T(8,128)(2,1)S(1)}, u32[]{:S(2)}, u32[]{:S(2)}) %collective-permute-start.10) | collective-permute-done | bytes 786464 | tf_op jit(solution)/shard_map/ppermute | solution.py:34
  76.2 0.0 copy-done.8
  76.2 0.9 copy-done.11
  77.1 11.1 %shard_map.108 = (bf16[128,32,128]{2,1,0:T(8,128)(2,1)}, bf16[512,1152]{1,0:T(8,128)(2,1)}, bf16[512,1152]{1,0:T(8,128)(2,1)}) custom-call(s32[3]{0:T(128)} %copy-done.5, bf16[4,72,432]{2,1,0:T(8,128)(2,1)} %copy-done.8, bf16[4,72,432]{2,1,0:T(8,128)(2,1)} %copy-done.12, bf16[2,72,432]{2,1,0:T(8,128)(2,1)} %copy-done.14, bf16[2,72,432]{2,1,0:T(8,128)(2,1)} %copy-done.15, ...), custom_call_target="tpu_custom_call" | custom-call | flops 3057647616 | bytes 7548940 | tf_op jit(solution)/shard_map/pallas_call | solution.py:324
  88.2 14.3 %all-to-all-start.1 = ((bf16[128,32,128]{2,1,0:T(8,128)(2,1)}), bf16[128,32,128]{2,1,0:T(8,128)(2,1)S(1)}, u32[]{:S(2)}, u32[]{:S(2)}) async-start(bf16[128,32,128]{2,1,0:T(8,128)(2,1)} %get-tuple-element.58), calls=%async_computation.1 | async-start | bytes 2097152 | tf_op jit(solution)/shard_map/all_to_all | solution.py:420
  102.5 2.6 %collective-permute-start.11 = (bf16[512,1152]{1,0:T(8,128)(2,1)}, bf16[512,1152]{1,0:T(8,128)(2,1)S(1)}, u32[]{:S(2)}, u32[]{:S(2)}) collective-permute-start(bf16[512,1152]{1,0:T(8,128)(2,1)} %get-tuple-element.60), channel_id=1, source_target_pairs={{0,16},{16,0},{1,17},{17,1},{2,18},{18,2},{3,19},{19,3},{4,20},{20... | collective-permute-start | bytes 3538952 | tf_op jit(solution)/shard_map/ppermute | solution.py:34
  105.1 2.7 %collective-permute-done.11.got_ref = bf16[512,1152]{1,0:T(8,128)(2,1)S(1)} collective-permute-done((bf16[512,1152]{1,0:T(8,128)(2,1)}, bf16[512,1152]{1,0:T(8,128)(2,1)S(1)}, u32[]{:S(2)}, u32[]{:S(2)}) %collective-permute-start.11) | collective-permute-done | bytes 1179680 | tf_op jit(solution)/shard_map/ppermute | solution.py:34
  107.7 1.3 copy-done.1
  109.0 0.3 shard_map.109
  109.3 1.9 %collective-permute-start.12 = (bf16[256,1152]{1,0:T(8,128)(2,1)S(1)}, bf16[256,1152]{1,0:T(8,128)(2,1)S(1)}, u32[]{:S(2)}, u32[]{:S(2)}) collective-permute-start(bf16[256,1152]{1,0:T(8,128)(2,1)S(1)} %get-tuple-element.62), channel_id=1, source_target_pairs={{0,8},{8,0},{1,9},{9,1},{2,10},{10,2},{3,11},{11,3},{4,12},{12,4},... | collective-permute-start | bytes 1769480 | tf_op jit(solution)/shard_map/ppermute | solution.py:34
  111.2 21.8 %collective-permute-done.12.refs_1_ = bf16[256,1152]{1,0:T(8,128)(2,1)S(1)} collective-permute-done((bf16[256,1152]{1,0:T(8,128)(2,1)S(1)}, bf16[256,1152]{1,0:T(8,128)(2,1)S(1)}, u32[]{:S(2)}, u32[]{:S(2)}) %collective-permute-start.12) | collective-permute-done | bytes 589856 | tf_op jit(solution)/shard_map/ppermute | solution.py:34
  133.0 0.9 shard_map.110.back_ref
  133.9 0.0 all-to-all-done.1.parts_ref
  133.9 0.2 shard_map.111
  134.2 25.1 %all_to_all.15.pieces_ref = bf16[16,16,1408]{2,1,0:T(8,128)(2,1)S(1)} all-to-all(bf16[16,16,1408]{2,1,0:T(8,128)(2,1)S(1)} %bitcast.18), channel_id=1, replica_groups=mesh['xh'=2,'z'=8,'c'=2,'xl'=2,'y'=8] {'xl','y'}, dimensions={0} | all-to-all | bytes 1441792 | tf_op jit(solution)/shard_map/all_to_all | solution.py:422
  159.2 0.0 copy-done.6
  159.2 0.6 shard_map.112
  159.9 4.9 %collective-permute-start.13 = (f32[2,36,432]{2,1,0:T(8,128)S(1)}, f32[2,36,432]{2,1,0:T(8,128)S(1)}, u32[]{:S(2)}, u32[]{:S(2)}) collective-permute-start(f32[2,36,432]{2,1,0:T(8,128)S(1)} %get-tuple-element.64), channel_id=1, source_target_pairs={{0,16},{16,0},{1,17},{17,1},{2,18},{18,2},{3,19},{19,3},{4,20},{20... | collective-permute-start | bytes 373256 | tf_op jit(solution)/shard_map/ppermute | solution.py:34
  165.5 0.1 pad_maximum_fusion.decay_ref
  165.6 0.9 slice.4
  166.5 0.0 collective-permute-done.13.core_ref
  166.5 1.5 shard_map.113
  (17 shorter events, 0.0 us)
Async XLA Ops:
  0.6 33.5 %copy-start = (bf16[128,2304]{1,0:T(8,128)(2,1)S(1)}, bf16[128,2304]{1,0:T(8,128)(2,1)}, u32[]{:S(2)}) copy-start(bf16[128,2304]{1,0:T(8,128)(2,1)} %param.10) | copy-start | bytes 1769476
  2.8 8.9 %copy-start.2 = (f32[36,1728]{1,0:T(8,128)S(1)}, f32[36,1728]{1,0:T(8,128)}, u32[]{:S(2)}) copy-start(f32[36,1728]{1,0:T(8,128)} %master_ref.1) | copy-start | bytes 746500
  2.8 40.8 %all-to-all-start = ((bf16[16,16,1792]{2,1,0:T(8,128)(2,1)}), bf16[16,16,1792]{2,1,0:T(8,128)(2,1)S(1)}, u32[]{:S(2)}, u32[]{:S(2)}) async-start(bf16[16,16,1792]{2,1,0:T(8,128)(2,1)} %bitcast.19), calls=%async_computation | async-start | bytes 1835008 | tf_op jit(solution)/shard_map/all_to_all | solution.py:369
  11.8 64.4 %copy-start.5 = (s32[3]{0:T(128)}, s32[3]{0:T(128)S(1)}, u32[]{:S(2)}) copy-start(s32[3]{0:T(128)S(1)} %pad_add_fusion.spot_ref) | copy-start | bytes 40
  12.6 4.6 %collective-permute-start = (bf16[36,432]{1,0:T(8,128)(2,1)S(1)}, bf16[36,432]{1,0:T(8,128)(2,1)S(1)}, u32[]{:S(2)}, u32[]{:S(2)}) collective-permute-start(bf16[36,432]{1,0:T(8,128)(2,1)S(1)} %get-tuple-element.36), channel_id=1, source_target_pairs={{0,16},{16,0},{1,17},{17,1},{2,18},{18,2},{3,19},{19,3},{4,20},{20... | collective-permute-start | bytes 93320 | tf_op jit(solution)/shard_map/ppermute | solution.py:34
  17.8 16.6 %collective-permute-start.1 = (bf16[72,432]{1,0:T(8,128)(2,1)S(1)}, bf16[72,432]{1,0:T(8,128)(2,1)S(1)}, u32[]{:S(2)}, u32[]{:S(2)}) collective-permute-start(bf16[72,432]{1,0:T(8,128)(2,1)S(1)} %shard_map.104.own_ref), channel_id=1, source_target_pairs={{0,128},{32,160},{64,192},{96,224},{128,0},{160,32},{192,64},{224,... | collective-permute-start | bytes 186632 | tf_op jit(solution)/shard_map/ppermute | solution.py:39
  27.6 7.5 %collective-permute-start.2 = (bf16[72,432]{1,0:T(8,128)(2,1)S(1)}, bf16[72,432]{1,0:T(8,128)(2,1)S(1)}, u32[]{:S(2)}, u32[]{:S(2)}) collective-permute-start(bf16[72,432]{1,0:T(8,128)(2,1)S(1)} %shard_map.104.own_ref), channel_id=1, source_target_pairs={{0,256},{256,0},{1,257},{257,1},{2,258},{258,2},{3,259},{259,3},{4... | collective-permute-start | bytes 186632 | tf_op jit(solution)/shard_map/ppermute | solution.py:34
  31.9 11.7 %collective-permute-start.3 = (bf16[72,432]{1,0:T(8,128)(2,1)S(1)}, bf16[72,432]{1,0:T(8,128)(2,1)S(1)}, u32[]{:S(2)}, u32[]{:S(2)}) collective-permute-start(bf16[72,432]{1,0:T(8,128)(2,1)S(1)} %shard_map.104.own_ref), channel_id=1, source_target_pairs={{0,384},{32,416},{64,448},{96,480},{128,256},{160,288},{192,320},{... | collective-permute-start | bytes 186632 | tf_op jit(solution)/shard_map/ppermute | solution.py:49
  45.4 30.7 %copy-start.7 = (bf16[256,1536]{1,0:T(8,128)(2,1)}, bf16[256,1536]{1,0:T(8,128)(2,1)S(1)}, u32[]{:S(2)}) copy-start(bf16[256,1536]{1,0:T(8,128)(2,1)S(1)} %get-tuple-element.56.own_hbm) | copy-start | bytes 2359300
  45.5 24.7 %collective-permute-start.4 = (bf16[256,1536]{1,0:T(8,128)(2,1)S(1)}, bf16[256,1536]{1,0:T(8,128)(2,1)S(1)}, u32[]{:S(2)}, u32[]{:S(2)}) collective-permute-start(bf16[256,1536]{1,0:T(8,128)(2,1)S(1)} %get-tuple-element.47), channel_id=1, source_target_pairs={{0,8},{8,0},{1,9},{9,1},{2,10},{10,2},{3,11},{11,3},{4,12},{12,4},... | collective-permute-start | bytes 2359304 | tf_op jit(solution)/shard_map/ppermute | solution.py:34
  49.0 27.2 %copy-start.8 = (bf16[4,72,432]{2,1,0:T(8,128)(2,1)}, bf16[4,72,432]{2,1,0:T(8,128)(2,1)S(1)}, u32[]{:S(2)}) copy-start(bf16[4,72,432]{2,1,0:T(8,128)(2,1)S(1)} %get-tuple-element.46.near_hbm) | copy-start | bytes 746500
  49.0 21.1 %collective-permute-start.5 = (bf16[4,72,432]{2,1,0:T(8,128)(2,1)S(1)}, bf16[4,72,432]{2,1,0:T(8,128)(2,1)S(1)}, u32[]{:S(2)}, u32[]{:S(2)}) collective-permute-start(bf16[4,72,432]{2,1,0:T(8,128)(2,1)S(1)} %get-tuple-element.46.near_hbm), channel_id=1, source_target_pairs={{0,224},{32,0},{64,32},{96,64},{128,96},{160,128},{192,160},{224,1... | collective-permute-start | bytes 746504 | tf_op jit(solution)/shard_map/ppermute | solution.py:39
  50.9 19.2 %collective-permute-start.8 = (bf16[4,72,432]{2,1,0:T(8,128)(2,1)S(1)}, bf16[4,72,432]{2,1,0:T(8,128)(2,1)S(1)}, u32[]{:S(2)}, u32[]{:S(2)}) collective-permute-start(bf16[4,72,432]{2,1,0:T(8,128)(2,1)S(1)} %get-tuple-element.46.near_hbm), channel_id=1, source_target_pairs={{0,32},{32,64},{64,96},{96,128},{128,160},{160,192},{192,224},{224... | collective-permute-start | bytes 746504 | tf_op jit(solution)/shard_map/ppermute | solution.py:39
  54.3 10.7 %collective-permute-start.6 = (bf16[2,72,432]{2,1,0:T(8,128)(2,1)S(1)}, bf16[2,72,432]{2,1,0:T(8,128)(2,1)S(1)}, u32[]{:S(2)}, u32[]{:S(2)}) collective-permute-start(bf16[2,72,432]{2,1,0:T(8,128)(2,1)S(1)} %get-tuple-element.49), channel_id=1, source_target_pairs={{0,192},{32,224},{64,0},{96,32},{128,64},{160,96},{192,128},{224,1... | collective-permute-start | bytes 373256 | tf_op jit(solution)/shard_map/ppermute | solution.py:39
  58.7 11.4 %collective-permute-start.7 = (bf16[2,72,432]{2,1,0:T(8,128)(2,1)S(1)}, bf16[2,72,432]{2,1,0:T(8,128)(2,1)S(1)}, u32[]{:S(2)}, u32[]{:S(2)}) collective-permute-start(bf16[2,72,432]{2,1,0:T(8,128)(2,1)S(1)} %get-tuple-element.51), channel_id=1, source_target_pairs={{0,64},{32,96},{64,128},{96,160},{128,192},{160,224},{192,0},{224,... | collective-permute-start | bytes 373256 | tf_op jit(solution)/shard_map/ppermute | solution.py:39
  65.0 11.2 %copy-start.14 = (bf16[2,72,432]{2,1,0:T(8,128)(2,1)}, bf16[2,72,432]{2,1,0:T(8,128)(2,1)S(1)}, u32[]{:S(2)}) copy-start(bf16[2,72,432]{2,1,0:T(8,128)(2,1)S(1)} %collective-permute-done.6.low_hbm) | copy-start | bytes 373252
  65.0 9.3 %collective-permute-start.9 = (bf16[256,1536]{1,0:T(8,128)(2,1)S(1)}, bf16[256,1536]{1,0:T(8,128)(2,1)S(1)}, u32[]{:S(2)}, u32[]{:S(2)}) collective-permute-start(bf16[256,1536]{1,0:T(8,128)(2,1)S(1)} %get-tuple-element.56.own_hbm), channel_id=1, source_target_pairs={{0,16},{16,0},{1,17},{17,1},{2,18},{18,2},{3,19},{19,3},{4,20},{20... | collective-permute-start | bytes 2359304 | tf_op jit(solution)/shard_map/ppermute | solution.py:34
  70.1 6.1 %copy-start.15 = (bf16[2,72,432]{2,1,0:T(8,128)(2,1)}, bf16[2,72,432]{2,1,0:T(8,128)(2,1)S(1)}, u32[]{:S(2)}) copy-start(bf16[2,72,432]{2,1,0:T(8,128)(2,1)S(1)} %collective-permute-done.7.high_hbm) | copy-start | bytes 373252
  70.1 6.1 %copy-start.12 = (bf16[4,72,432]{2,1,0:T(8,128)(2,1)}, bf16[4,72,432]{2,1,0:T(8,128)(2,1)S(1)}, u32[]{:S(2)}) copy-start(bf16[4,72,432]{2,1,0:T(8,128)(2,1)S(1)} %collective-permute-done.5.up_hbm) | copy-start | bytes 746500
  70.1 6.1 %copy-start.13 = (bf16[4,72,432]{2,1,0:T(8,128)(2,1)}, bf16[4,72,432]{2,1,0:T(8,128)(2,1)S(1)}, u32[]{:S(2)}) copy-start(bf16[4,72,432]{2,1,0:T(8,128)(2,1)S(1)} %collective-permute-done.8.down_hbm) | copy-start | bytes 746500
  70.1 6.1 %copy-start.9 = (bf16[256,1536]{1,0:T(8,128)(2,1)}, bf16[256,1536]{1,0:T(8,128)(2,1)S(1)}, u32[]{:S(2)}) copy-start(bf16[256,1536]{1,0:T(8,128)(2,1)S(1)} %collective-permute-done.4.side_hbm) | copy-start | bytes 2359300
  70.1 6.0 %collective-permute-start.10 = (bf16[256,1536]{1,0:T(8,128)(2,1)S(1)}, bf16[256,1536]{1,0:T(8,128)(2,1)S(1)}, u32[]{:S(2)}, u32[]{:S(2)}) collective-permute-start(bf16[256,1536]{1,0:T(8,128)(2,1)S(1)} %collective-permute-done.4.side_hbm), channel_id=1, source_target_pairs={{0,16},{16,0},{1,17},{17,1},{2,18},{18,2},{3,19},{19,3},{4,20},{20... | collective-permute-start | bytes 2359304 | tf_op jit(solution)/shard_map/ppermute | solution.py:34
  74.3 1.9 %copy-start.10 = (bf16[256,1536]{1,0:T(8,128)(2,1)}, bf16[256,1536]{1,0:T(8,128)(2,1)S(1)}, u32[]{:S(2)}) copy-start(bf16[256,1536]{1,0:T(8,128)(2,1)S(1)} %collective-permute-done.9.core_hbm) | copy-start | bytes 2359300
  76.2 0.9 copy-start.11
  88.2 45.7 %all-to-all-start.1 = ((bf16[128,32,128]{2,1,0:T(8,128)(2,1)}), bf16[128,32,128]{2,1,0:T(8,128)(2,1)S(1)}, u32[]{:S(2)}, u32[]{:S(2)}) async-start(bf16[128,32,128]{2,1,0:T(8,128)(2,1)} %get-tuple-element.58), calls=%async_computation.1 | async-start | bytes 2097152 | tf_op jit(solution)/shard_map/all_to_all | solution.py:420
  102.5 5.2 %collective-permute-start.11 = (bf16[512,1152]{1,0:T(8,128)(2,1)}, bf16[512,1152]{1,0:T(8,128)(2,1)S(1)}, u32[]{:S(2)}, u32[]{:S(2)}) collective-permute-start(bf16[512,1152]{1,0:T(8,128)(2,1)} %get-tuple-element.60), channel_id=1, source_target_pairs={{0,16},{16,0},{1,17},{17,1},{2,18},{18,2},{3,19},{19,3},{4,20},{20... | collective-permute-start | bytes 3538952 | tf_op jit(solution)/shard_map/ppermute | solution.py:34
  107.7 1.3 copy-start.1
  109.3 23.8 %collective-permute-start.12 = (bf16[256,1152]{1,0:T(8,128)(2,1)S(1)}, bf16[256,1152]{1,0:T(8,128)(2,1)S(1)}, u32[]{:S(2)}, u32[]{:S(2)}) collective-permute-start(bf16[256,1152]{1,0:T(8,128)(2,1)S(1)} %get-tuple-element.62), channel_id=1, source_target_pairs={{0,8},{8,0},{1,9},{9,1},{2,10},{10,2},{3,11},{11,3},{4,12},{12,4},... | collective-permute-start | bytes 1769480 | tf_op jit(solution)/shard_map/ppermute | solution.py:34
  134.1 25.1 %copy-start.6 = (s32[3]{0:T(128)S(1)}, s32[3]{0:T(128)}, u32[]{:S(2)}) copy-start(s32[3]{0:T(128)} %copy-done.5) | copy-start | bytes 40
  159.2 7.2 %copy-start.3 = (f32[36,1728]{1,0:T(8,128)S(1)}, f32[36,1728]{1,0:T(8,128)}, u32[]{:S(2)}) copy-start(f32[36,1728]{1,0:T(8,128)} %slow_ref.1) | copy-start | bytes 746500
  159.2 7.2 %copy-start.4 = (f32[36,1728]{1,0:T(8,128)S(1)}, f32[36,1728]{1,0:T(8,128)}, u32[]{:S(2)}) copy-start(f32[36,1728]{1,0:T(8,128)} %fast_ref.1) | copy-start | bytes 746500
  159.9 6.6 %collective-permute-start.13 = (f32[2,36,432]{2,1,0:T(8,128)S(1)}, f32[2,36,432]{2,1,0:T(8,128)S(1)}, u32[]{:S(2)}, u32[]{:S(2)}) collective-permute-start(f32[2,36,432]{2,1,0:T(8,128)S(1)} %get-tuple-element.64), channel_id=1, source_target_pairs={{0,16},{16,0},{1,17},{17,1},{2,18},{18,2},{3,19},{19,3},{4,20},{20... | collective-permute-start | bytes 373256 | tf_op jit(solution)/shard_map/ppermute | solution.py:34

commit v13 on v11

--- a/solution.py
+++ b/solution.py
@@ -242,10 +242,19 @@
         store.wait()
 
 
-def add_kernel(near_ref, got_ref, own_ref, side_ref):
+def add_kernel(near_hbm, got_hbm, own_ref, side_ref, near_ref, got_ref, sems):
     half = own_ref.shape[0]
-    side_ref[...] = (near_ref[half:].astype(F32) + got_ref[half:].astype(F32)).astype(BF16)
-    own_ref[...] = (near_ref[:half].astype(F32) + got_ref[:half].astype(F32)).astype(BF16)
+    pairs = [(side_ref, pl.ds(half, half)), (own_ref, pl.ds(0, half))]
+    loads = []
+    for index, (_, rows) in enumerate(pairs):
+        loads.append(pltpu.make_async_copy(near_hbm.at[rows], near_ref.at[rows], sems.at[2 * index]))
+        loads.append(pltpu.make_async_copy(got_hbm.at[rows], got_ref.at[rows], sems.at[2 * index + 1]))
+    for load in loads:
+        load.start()
+    for index, (target, rows) in enumerate(pairs):
+        loads[2 * index].wait()
+        loads[2 * index + 1].wait()
+        target[...] = (near_ref[rows, :].astype(F32) + got_ref[rows, :].astype(F32)).astype(BF16)
 
 
 def columns_kernel(spot_ref, master_ref, mine_ref, theirs_ref):
@@ -414,7 +423,14 @@
         hbm_out=(0, 1, 2),
     )
 
-    part, give = call(add_kernel, [((patches, width), BF16)] * 2, near, swap(far, "c"))
+    part, give = call(
+        add_kernel,
+        [((patches, width), BF16)] * 2,
+        near, swap(far, "c"),
+        scratch=[pltpu.VMEM((2 * patches, width), BF16)] * 2 + [pltpu.SemaphoreType.DMA((4,))],
+        mib=56,
+        hbm_in=True,
+    )
     back = call(norm_back_kernel, [((patches, width), BF16)], tokens, modulation, part, swap(give, "xl"))
 
     parts = lax.all_to_all(packed, ROWS + ("y",), 0, 0, tiled=True)

time: 168 us -> 171 us (1.018)
  Pallas kernels: 20.6 us -> 23 us
    pallas_call x11, Pallas kernels: 20.6 us -> 23 us  [call(): pl.pallas_call(kernel, out_shape=shapes, in_specs=specs, out_specs=[pl.Bl...]
  transfers between devices with their start and end apart: 16 -> 16, of which waited for: 7 -> 7; matrix products, arithmetic and copies ran while one was open for 1% -> 1% of each run, Pallas kernels for 2% -> 3%
where the time goes in v13:
time: 171 us; the launch traced here: 170 us
  starting transfers between devices  76.7 us (45%)
  waiting for transfers between devices  38.1 us (22%)
  blocking collectives  25.4 us (15%)
  Pallas kernels  23 us (13%)
  local copies, waits for them, and re-layouts  3.9 us (2%)
  between operations  2.49 us (1%)
    ppermute x8, starting transfers between devices, swap(): return lax.ppermute(value, axis, [(0, 1), (1, 0)])  29.2 us
    ppermute x8, waiting for transfers between devices, swap(): return lax.ppermute(value, axis, [(0, 1), (1, 0)])  26.1 us
    all_to_all x1, blocking collectives, on_device(): lax.all_to_all(joint.reshape(n_seq, patches // n_seq, width + 256), SEQ,...  25.4 us
    pallas_call x11, Pallas kernels, call(): pl.pallas_call(kernel, out_shape=shapes, in_specs=specs, out_specs=[pl.Bl...  23 us
    ppermute x5, starting transfers between devices, shift(): lax.ppermute(value, 'z', [(i, (i + away) % count) for i in range(count)])  22.3 us
    all_to_all x1, starting transfers between devices, on_device(): parts = lax.all_to_all(packed, ROWS + ('y',), 0, 0, tiled=True)  14.3 us
    all_to_all x1, starting transfers between devices, on_device(): lax.all_to_all(packed.reshape(n_seq, patches // n_seq, width + loose), SE...  8.83 us
    ppermute x1, waiting for transfers between devices, both_turn(): return lax.ppermute(value, ('xh', 'z'), pairs)  8.6 us
  transfers between devices with their start and end apart: 16, of which 7 were waited for; matrix products, arithmetic and copies ran while one was open for 1% of the time, Pallas kernels for 3%

profile of v13, /device:TPU:1, one launch (start us, length us, event | category | flops | bytes accessed | tf_op | source)
XLA Modules:
  0.0 170.1 jit_solution(11122736437008872036)
XLA Ops:
  0.6 0.0 copy-start
  0.6 2.2 %shard_map.105 = bf16[256,1792]{1,0:T(8,128)(2,1)} custom-call(bf16[256,1152]{1,0:T(8,128)(2,1)} %bitcast.20, bf16[576,256]{1,0:T(8,128)(2,1)} %bitcast.22), custom_call_target="tpu_custom_call" | custom-call | bytes 1802240 | tf_op jit(solution)/shard_map/pallas_call | solution.py:333
  2.8 0.0 copy-start.2
  2.8 8.8 %all-to-all-start = ((bf16[16,16,1792]{2,1,0:T(8,128)(2,1)}), bf16[16,16,1792]{2,1,0:T(8,128)(2,1)S(1)}, u32[]{:S(2)}, u32[]{:S(2)}) async-start(bf16[16,16,1792]{2,1,0:T(8,128)(2,1)} %bitcast.19), calls=%async_computation | async-start | bytes 1835008 | tf_op jit(solution)/shard_map/all_to_all | solution.py:378
  11.7 0.1 pad_add_fusion.spot_ref
  11.8 0.9 shard_map.103
  12.6 3.7 %collective-permute-start = (bf16[36,432]{1,0:T(8,128)(2,1)S(1)}, bf16[36,432]{1,0:T(8,128)(2,1)S(1)}, u32[]{:S(2)}, u32[]{:S(2)}) collective-permute-start(bf16[36,432]{1,0:T(8,128)(2,1)S(1)} %get-tuple-element.36), channel_id=1, source_target_pairs={{0,16},{16,0},{1,17},{17,1},{2,18},{18,2},{3,19},{19,3},{4,20},{20... | collective-permute-start | bytes 93320 | tf_op jit(solution)/shard_map/ppermute | solution.py:34
  17.0 0.1 sine_convert_fusion
  17.1 0.1 collective-permute-done.theirs_ref
  17.2 0.6 shard_map.104.own_ref
  17.8 9.8 %collective-permute-start.1 = (bf16[72,432]{1,0:T(8,128)(2,1)S(1)}, bf16[72,432]{1,0:T(8,128)(2,1)S(1)}, u32[]{:S(2)}, u32[]{:S(2)}) collective-permute-start(bf16[72,432]{1,0:T(8,128)(2,1)S(1)} %shard_map.104.own_ref), channel_id=1, source_target_pairs={{0,128},{32,160},{64,192},{96,224},{128,0},{160,32},{192,64},{224,... | collective-permute-start | bytes 186632 | tf_op jit(solution)/shard_map/ppermute | solution.py:39
  27.6 4.4 %collective-permute-start.2 = (bf16[72,432]{1,0:T(8,128)(2,1)S(1)}, bf16[72,432]{1,0:T(8,128)(2,1)S(1)}, u32[]{:S(2)}, u32[]{:S(2)}) collective-permute-start(bf16[72,432]{1,0:T(8,128)(2,1)S(1)} %shard_map.104.own_ref), channel_id=1, source_target_pairs={{0,256},{256,0},{1,257},{257,1},{2,258},{258,2},{3,259},{259,3},{4... | collective-permute-start | bytes 186632 | tf_op jit(solution)/shard_map/ppermute | solution.py:34
  31.9 2.2 %collective-permute-start.3 = (bf16[72,432]{1,0:T(8,128)(2,1)S(1)}, bf16[72,432]{1,0:T(8,128)(2,1)S(1)}, u32[]{:S(2)}, u32[]{:S(2)}) collective-permute-start(bf16[72,432]{1,0:T(8,128)(2,1)S(1)} %shard_map.104.own_ref), channel_id=1, source_target_pairs={{0,384},{32,416},{64,448},{96,480},{128,256},{160,288},{192,320},{... | collective-permute-start | bytes 186632 | tf_op jit(solution)/shard_map/ppermute | solution.py:49
  34.1 0.2 fusion.mod_ref
  34.4 0.0 collective-permute-done.1.far_ref
  34.4 0.7 collective-permute-done.2.across_ref
  35.0 8.6 %collective-permute-done.3.both_ref = bf16[72,432]{1,0:T(8,128)(2,1)S(1)} collective-permute-done((bf16[72,432]{1,0:T(8,128)(2,1)S(1)}, bf16[72,432]{1,0:T(8,128)(2,1)S(1)}, u32[]{:S(2)}, u32[]{:S(2)}) %collective-permute-start.3) | collective-permute-done | bytes 62240 | tf_op jit(solution)/shard_map/ppermute | solution.py:49
  43.6 0.0 all-to-all-done
  43.6 1.8 %shard_map.106 = (bf16[256,1536]{1,0:T(8,128)(2,1)S(1)}, bf16[256,1536]{1,0:T(8,128)(2,1)S(1)}) custom-call(s32[3]{0:T(128)S(1)} %pad_add_fusion.spot_ref, bf16[256,1792]{1,0:T(8,128)(2,1)S(1)} %bitcast.16, f32[1,2304]{1,0:T(1,128)S(1)} %fusion.mod_ref), custom_call_target="tpu_custom_call" | custom-call | bytes 2499596 | tf_op jit(solution)/shard_map/pallas_call | solution.py:333
  45.5 2.9 %collective-permute-start.4 = (bf16[256,1536]{1,0:T(8,128)(2,1)S(1)}, bf16[256,1536]{1,0:T(8,128)(2,1)S(1)}, u32[]{:S(2)}, u32[]{:S(2)}) collective-permute-start(bf16[256,1536]{1,0:T(8,128)(2,1)S(1)} %get-tuple-element.47), channel_id=1, source_target_pairs={{0,8},{8,0},{1,9},{9,1},{2,10},{10,2},{3,11},{11,3},{4,12},{12,4},... | collective-permute-start | bytes 2359304 | tf_op jit(solution)/shard_map/ppermute | solution.py:34
  48.4 0.6 shard_map.107
  49.0 0.0 copy-start.8
  49.0 1.9 %collective-permute-start.5 = (bf16[4,72,432]{2,1,0:T(8,128)(2,1)S(1)}, bf16[4,72,432]{2,1,0:T(8,128)(2,1)S(1)}, u32[]{:S(2)}, u32[]{:S(2)}) collective-permute-start(bf16[4,72,432]{2,1,0:T(8,128)(2,1)S(1)} %get-tuple-element.46.near_hbm), channel_id=1, source_target_pairs={{0,224},{32,0},{64,32},{96,64},{128,96},{160,128},{192,160},{224,1... | collective-permute-start | bytes 746504 | tf_op jit(solution)/shard_map/ppermute | solution.py:39
  50.9 3.4 %collective-permute-start.8 = (bf16[4,72,432]{2,1,0:T(8,128)(2,1)S(1)}, bf16[4,72,432]{2,1,0:T(8,128)(2,1)S(1)}, u32[]{:S(2)}, u32[]{:S(2)}) collective-permute-start(bf16[4,72,432]{2,1,0:T(8,128)(2,1)S(1)} %get-tuple-element.46.near_hbm), channel_id=1, source_target_pairs={{0,32},{32,64},{64,96},{96,128},{128,160},{160,192},{192,224},{224... | collective-permute-start | bytes 746504 | tf_op jit(solution)/shard_map/ppermute | solution.py:39
  54.3 4.3 %collective-permute-start.6 = (bf16[2,72,432]{2,1,0:T(8,128)(2,1)S(1)}, bf16[2,72,432]{2,1,0:T(8,128)(2,1)S(1)}, u32[]{:S(2)}, u32[]{:S(2)}) collective-permute-start(bf16[2,72,432]{2,1,0:T(8,128)(2,1)S(1)} %get-tuple-element.49), channel_id=1, source_target_pairs={{0,192},{32,224},{64,0},{96,32},{128,64},{160,96},{192,128},{224,1... | collective-permute-start | bytes 373256 | tf_op jit(solution)/shard_map/ppermute | solution.py:39
  58.7 2.9 %collective-permute-start.7 = (bf16[2,72,432]{2,1,0:T(8,128)(2,1)S(1)}, bf16[2,72,432]{2,1,0:T(8,128)(2,1)S(1)}, u32[]{:S(2)}, u32[]{:S(2)}) collective-permute-start(bf16[2,72,432]{2,1,0:T(8,128)(2,1)S(1)} %get-tuple-element.51), channel_id=1, source_target_pairs={{0,64},{32,96},{64,128},{96,160},{128,192},{160,224},{192,0},{224,... | collective-permute-start | bytes 373256 | tf_op jit(solution)/shard_map/ppermute | solution.py:39
  61.6 3.5 %collective-permute-done.6.low_hbm = bf16[2,72,432]{2,1,0:T(8,128)(2,1)S(1)} collective-permute-done((bf16[2,72,432]{2,1,0:T(8,128)(2,1)S(1)}, bf16[2,72,432]{2,1,0:T(8,128)(2,1)S(1)}, u32[]{:S(2)}, u32[]{:S(2)}) %collective-permute-start.6) | collective-permute-done | bytes 124448 | tf_op jit(solution)/shard_map/ppermute | solution.py:39
  65.0 5.0 %collective-permute-start.9 = (bf16[256,1536]{1,0:T(8,128)(2,1)S(1)}, bf16[256,1536]{1,0:T(8,128)(2,1)S(1)}, u32[]{:S(2)}, u32[]{:S(2)}) collective-permute-start(bf16[256,1536]{1,0:T(8,128)(2,1)S(1)} %get-tuple-element.56.own_hbm), channel_id=1, source_target_pairs={{0,16},{16,0},{1,17},{17,1},{2,18},{18,2},{3,19},{19,3},{4,20},{20... | collective-permute-start | bytes 2359304 | tf_op jit(solution)/shard_map/ppermute | solution.py:34
  70.1 0.0 collective-permute-done.7.high_hbm
  70.1 0.0 copy-start.16
  70.1 0.0 collective-permute-done.5.up_hbm
  70.1 0.0 collective-permute-done.8.down_hbm
  70.1 0.0 collective-permute-done.4.side_hbm
  70.1 4.1 %collective-permute-start.10 = (bf16[256,1536]{1,0:T(8,128)(2,1)S(1)}, bf16[256,1536]{1,0:T(8,128)(2,1)S(1)}, u32[]{:S(2)}, u32[]{:S(2)}) collective-permute-start(bf16[256,1536]{1,0:T(8,128)(2,1)S(1)} %collective-permute-done.4.side_hbm), channel_id=1, source_target_pairs={{0,16},{16,0},{1,17},{17,1},{2,18},{18,2},{3,19},{19,3},{4,20},{20... | collective-permute-start | bytes 2359304 | tf_op jit(solution)/shard_map/ppermute | solution.py:34
  74.3 0.0 collective-permute-done.9.core_hbm
  74.3 1.9 %collective-permute-done.10.both_hbm = bf16[256,1536]{1,0:T(8,128)(2,1)S(1)} collective-permute-done((bf16[256,1536]{1,0:T(8,128)(2,1)S(1)}, bf16[256,1536]{1,0:T(8,128)(2,1)S(1)}, u32[]{:S(2)}, u32[]{:S(2)}) %collective-permute-start.10) | collective-permute-done | bytes 786464 | tf_op jit(solution)/shard_map/ppermute | solution.py:34
  76.2 0.0 copy-done.15
  76.2 0.0 copy-done.16
  76.2 0.0 copy-done.13
  76.2 0.0 copy-done.14
  76.2 0.0 copy-done.10
  76.2 0.0 copy-done.11
  76.2 0.0 copy-start.12
  76.2 0.9 copy-done.12
  77.1 11.1 %shard_map.108 = (bf16[128,32,128]{2,1,0:T(8,128)(2,1)}, bf16[512,1152]{1,0:T(8,128)(2,1)}, bf16[512,1152]{1,0:T(8,128)(2,1)}) custom-call(s32[3]{0:T(128)} %copy-done.5, bf16[4,72,432]{2,1,0:T(8,128)(2,1)} %copy-done.8, bf16[4,72,432]{2,1,0:T(8,128)(2,1)} %copy-done.13, bf16[2,72,432]{2,1,0:T(8,128)(2,1)} %copy-done.15, bf16[2,72,432]{2,1,0:T(8,128)(2,1)} %copy-done.16, ...), custom_call_target="tpu_custom_call" | custom-call | flops 3057647616 | bytes 7548940 | tf_op jit(solution)/shard_map/pallas_call | solution.py:333
  88.3 14.3 %all-to-all-start.1 = ((bf16[128,32,128]{2,1,0:T(8,128)(2,1)}), bf16[128,32,128]{2,1,0:T(8,128)(2,1)S(1)}, u32[]{:S(2)}, u32[]{:S(2)}) async-start(bf16[128,32,128]{2,1,0:T(8,128)(2,1)} %get-tuple-element.58), calls=%async_computation.1 | async-start | bytes 2097152 | tf_op jit(solution)/shard_map/all_to_all | solution.py:436
  102.6 2.6 %collective-permute-start.11 = (bf16[512,1152]{1,0:T(8,128)(2,1)}, bf16[512,1152]{1,0:T(8,128)(2,1)S(1)}, u32[]{:S(2)}, u32[]{:S(2)}) collective-permute-start(bf16[512,1152]{1,0:T(8,128)(2,1)} %get-tuple-element.60), channel_id=1, source_target_pairs={{0,16},{16,0},{1,17},{17,1},{2,18},{18,2},{3,19},{19,3},{4,20},{20... | collective-permute-start | bytes 3538952 | tf_op jit(solution)/shard_map/ppermute | solution.py:34
  105.1 2.7 %collective-permute-done.11.got_hbm = bf16[512,1152]{1,0:T(8,128)(2,1)S(1)} collective-permute-done((bf16[512,1152]{1,0:T(8,128)(2,1)}, bf16[512,1152]{1,0:T(8,128)(2,1)S(1)}, u32[]{:S(2)}, u32[]{:S(2)}) %collective-permute-start.11) | collective-permute-done | bytes 1179680 | tf_op jit(solution)/shard_map/ppermute | solution.py:34
  107.8 1.0 copy-done.9
  108.8 2.6 %shard_map.109 = (bf16[256,1152]{1,0:T(8,128)(2,1)}, bf16[256,1152]{1,0:T(8,128)(2,1)}) custom-call(bf16[512,1152]{1,0:T(8,128)(2,1)} %get-tuple-element.59.near_hbm, bf16[512,1152]{1,0:T(8,128)(2,1)} %copy-done.9), custom_call_target="tpu_custom_call" | custom-call | bytes 3538944 | tf_op jit(solution)/shard_map/pallas_call | solution.py:333
  111.5 1.9 %collective-permute-start.12 = (bf16[256,1152]{1,0:T(8,128)(2,1)}, bf16[256,1152]{1,0:T(8,128)(2,1)S(1)}, u32[]{:S(2)}, u32[]{:S(2)}) collective-permute-start(bf16[256,1152]{1,0:T(8,128)(2,1)} %get-tuple-element.62), channel_id=1, source_target_pairs={{0,8},{8,0},{1,9},{9,1},{2,10},{10,2},{3,11},{11,3},{4,12},{12,4},... | collective-permute-start | bytes 1769480 | tf_op jit(solution)/shard_map/ppermute | solution.py:34
  113.4 20.7 %collective-permute-done.12.refs_1_ = bf16[256,1152]{1,0:T(8,128)(2,1)S(1)} collective-permute-done((bf16[256,1152]{1,0:T(8,128)(2,1)}, bf16[256,1152]{1,0:T(8,128)(2,1)S(1)}, u32[]{:S(2)}, u32[]{:S(2)}) %collective-permute-start.12) | collective-permute-done | bytes 589856 | tf_op jit(solution)/shard_map/ppermute | solution.py:34
  134.1 1.1 copy-done.1
  135.2 0.9 shard_map.110.back_ref
  136.0 0.0 all-to-all-done.1.parts_ref
  136.0 0.2 shard_map.111
  136.3 0.0 copy-start.6
  136.3 25.4 %all_to_all.15.pieces_ref = bf16[16,16,1408]{2,1,0:T(8,128)(2,1)S(1)} all-to-all(bf16[16,16,1408]{2,1,0:T(8,128)(2,1)S(1)} %bitcast.18), channel_id=1, replica_groups=mesh['xh'=2,'z'=8,'c'=2,'xl'=2,'y'=8] {'xl','y'}, dimensions={0} | all-to-all | bytes 1441792 | tf_op jit(solution)/shard_map/all_to_all | solution.py:438
  161.7 0.6 shard_map.112
  162.3 4.5 %collective-permute-start.13 = (f32[2,36,432]{2,1,0:T(8,128)S(1)}, f32[2,36,432]{2,1,0:T(8,128)S(1)}, u32[]{:S(2)}, u32[]{:S(2)}) collective-permute-start(f32[2,36,432]{2,1,0:T(8,128)S(1)} %get-tuple-element.64), channel_id=1, source_target_pairs={{0,16},{16,0},{1,17},{17,1},{2,18},{18,2},{3,19},{19,3},{4,20},{20... | collective-permute-start | bytes 373256 | tf_op jit(solution)/shard_map/ppermute | solution.py:34
  167.6 0.1 pad_maximum_fusion.decay_ref
  167.7 0.9 slice.4
  168.6 0.0 collective-permute-done.13.core_ref
  168.6 1.5 shard_map.113
  (19 shorter events, 0.0 us)
Async XLA Ops:
  0.6 33.5 %copy-start = (bf16[128,2304]{1,0:T(8,128)(2,1)S(1)}, bf16[128,2304]{1,0:T(8,128)(2,1)}, u32[]{:S(2)}) copy-start(bf16[128,2304]{1,0:T(8,128)(2,1)} %param.10) | copy-start | bytes 1769476
  2.8 8.9 %copy-start.2 = (f32[36,1728]{1,0:T(8,128)S(1)}, f32[36,1728]{1,0:T(8,128)}, u32[]{:S(2)}) copy-start(f32[36,1728]{1,0:T(8,128)} %master_ref.1) | copy-start | bytes 746500
  2.8 40.8 %all-to-all-start = ((bf16[16,16,1792]{2,1,0:T(8,128)(2,1)}), bf16[16,16,1792]{2,1,0:T(8,128)(2,1)S(1)}, u32[]{:S(2)}, u32[]{:S(2)}) async-start(bf16[16,16,1792]{2,1,0:T(8,128)(2,1)} %bitcast.19), calls=%async_computation | async-start | bytes 1835008 | tf_op jit(solution)/shard_map/all_to_all | solution.py:378
  11.8 64.4 %copy-start.5 = (s32[3]{0:T(128)}, s32[3]{0:T(128)S(1)}, u32[]{:S(2)}) copy-start(s32[3]{0:T(128)S(1)} %pad_add_fusion.spot_ref) | copy-start | bytes 40
  12.6 4.6 %collective-permute-start = (bf16[36,432]{1,0:T(8,128)(2,1)S(1)}, bf16[36,432]{1,0:T(8,128)(2,1)S(1)}, u32[]{:S(2)}, u32[]{:S(2)}) collective-permute-start(bf16[36,432]{1,0:T(8,128)(2,1)S(1)} %get-tuple-element.36), channel_id=1, source_target_pairs={{0,16},{16,0},{1,17},{17,1},{2,18},{18,2},{3,19},{19,3},{4,20},{20... | collective-permute-start | bytes 93320 | tf_op jit(solution)/shard_map/ppermute | solution.py:34
  17.8 16.6 %collective-permute-start.1 = (bf16[72,432]{1,0:T(8,128)(2,1)S(1)}, bf16[72,432]{1,0:T(8,128)(2,1)S(1)}, u32[]{:S(2)}, u32[]{:S(2)}) collective-permute-start(bf16[72,432]{1,0:T(8,128)(2,1)S(1)} %shard_map.104.own_ref), channel_id=1, source_target_pairs={{0,128},{32,160},{64,192},{96,224},{128,0},{160,32},{192,64},{224,... | collective-permute-start | bytes 186632 | tf_op jit(solution)/shard_map/ppermute | solution.py:39
  27.6 7.5 %collective-permute-start.2 = (bf16[72,432]{1,0:T(8,128)(2,1)S(1)}, bf16[72,432]{1,0:T(8,128)(2,1)S(1)}, u32[]{:S(2)}, u32[]{:S(2)}) collective-permute-start(bf16[72,432]{1,0:T(8,128)(2,1)S(1)} %shard_map.104.own_ref), channel_id=1, source_target_pairs={{0,256},{256,0},{1,257},{257,1},{2,258},{258,2},{3,259},{259,3},{4... | collective-permute-start | bytes 186632 | tf_op jit(solution)/shard_map/ppermute | solution.py:34
  31.9 11.7 %collective-permute-start.3 = (bf16[72,432]{1,0:T(8,128)(2,1)S(1)}, bf16[72,432]{1,0:T(8,128)(2,1)S(1)}, u32[]{:S(2)}, u32[]{:S(2)}) collective-permute-start(bf16[72,432]{1,0:T(8,128)(2,1)S(1)} %shard_map.104.own_ref), channel_id=1, source_target_pairs={{0,384},{32,416},{64,448},{96,480},{128,256},{160,288},{192,320},{... | collective-permute-start | bytes 186632 | tf_op jit(solution)/shard_map/ppermute | solution.py:49
  45.5 30.7 %copy-start.7 = (bf16[256,1536]{1,0:T(8,128)(2,1)}, bf16[256,1536]{1,0:T(8,128)(2,1)S(1)}, u32[]{:S(2)}) copy-start(bf16[256,1536]{1,0:T(8,128)(2,1)S(1)} %get-tuple-element.56.own_hbm) | copy-start | bytes 2359300
  45.5 24.7 %collective-permute-start.4 = (bf16[256,1536]{1,0:T(8,128)(2,1)S(1)}, bf16[256,1536]{1,0:T(8,128)(2,1)S(1)}, u32[]{:S(2)}, u32[]{:S(2)}) collective-permute-start(bf16[256,1536]{1,0:T(8,128)(2,1)S(1)} %get-tuple-element.47), channel_id=1, source_target_pairs={{0,8},{8,0},{1,9},{9,1},{2,10},{10,2},{3,11},{11,3},{4,12},{12,4},... | collective-permute-start | bytes 2359304 | tf_op jit(solution)/shard_map/ppermute | solution.py:34
  49.0 27.2 %copy-start.8 = (bf16[4,72,432]{2,1,0:T(8,128)(2,1)}, bf16[4,72,432]{2,1,0:T(8,128)(2,1)S(1)}, u32[]{:S(2)}) copy-start(bf16[4,72,432]{2,1,0:T(8,128)(2,1)S(1)} %get-tuple-element.46.near_hbm) | copy-start | bytes 746500
  49.0 21.1 %collective-permute-start.5 = (bf16[4,72,432]{2,1,0:T(8,128)(2,1)S(1)}, bf16[4,72,432]{2,1,0:T(8,128)(2,1)S(1)}, u32[]{:S(2)}, u32[]{:S(2)}) collective-permute-start(bf16[4,72,432]{2,1,0:T(8,128)(2,1)S(1)} %get-tuple-element.46.near_hbm), channel_id=1, source_target_pairs={{0,224},{32,0},{64,32},{96,64},{128,96},{160,128},{192,160},{224,1... | collective-permute-start | bytes 746504 | tf_op jit(solution)/shard_map/ppermute | solution.py:39
  50.9 19.2 %collective-permute-start.8 = (bf16[4,72,432]{2,1,0:T(8,128)(2,1)S(1)}, bf16[4,72,432]{2,1,0:T(8,128)(2,1)S(1)}, u32[]{:S(2)}, u32[]{:S(2)}) collective-permute-start(bf16[4,72,432]{2,1,0:T(8,128)(2,1)S(1)} %get-tuple-element.46.near_hbm), channel_id=1, source_target_pairs={{0,32},{32,64},{64,96},{96,128},{128,160},{160,192},{192,224},{224... | collective-permute-start | bytes 746504 | tf_op jit(solution)/shard_map/ppermute | solution.py:39
  54.3 10.7 %collective-permute-start.6 = (bf16[2,72,432]{2,1,0:T(8,128)(2,1)S(1)}, bf16[2,72,432]{2,1,0:T(8,128)(2,1)S(1)}, u32[]{:S(2)}, u32[]{:S(2)}) collective-permute-start(bf16[2,72,432]{2,1,0:T(8,128)(2,1)S(1)} %get-tuple-element.49), channel_id=1, source_target_pairs={{0,192},{32,224},{64,0},{96,32},{128,64},{160,96},{192,128},{224,1... | collective-permute-start | bytes 373256 | tf_op jit(solution)/shard_map/ppermute | solution.py:39
  58.7 11.4 %collective-permute-start.7 = (bf16[2,72,432]{2,1,0:T(8,128)(2,1)S(1)}, bf16[2,72,432]{2,1,0:T(8,128)(2,1)S(1)}, u32[]{:S(2)}, u32[]{:S(2)}) collective-permute-start(bf16[2,72,432]{2,1,0:T(8,128)(2,1)S(1)} %get-tuple-element.51), channel_id=1, source_target_pairs={{0,64},{32,96},{64,128},{96,160},{128,192},{160,224},{192,0},{224,... | collective-permute-start | bytes 373256 | tf_op jit(solution)/shard_map/ppermute | solution.py:39
  65.0 11.2 %copy-start.15 = (bf16[2,72,432]{2,1,0:T(8,128)(2,1)}, bf16[2,72,432]{2,1,0:T(8,128)(2,1)S(1)}, u32[]{:S(2)}) copy-start(bf16[2,72,432]{2,1,0:T(8,128)(2,1)S(1)} %collective-permute-done.6.low_hbm) | copy-start | bytes 373252
  65.0 9.3 %collective-permute-start.9 = (bf16[256,1536]{1,0:T(8,128)(2,1)S(1)}, bf16[256,1536]{1,0:T(8,128)(2,1)S(1)}, u32[]{:S(2)}, u32[]{:S(2)}) collective-permute-start(bf16[256,1536]{1,0:T(8,128)(2,1)S(1)} %get-tuple-element.56.own_hbm), channel_id=1, source_target_pairs={{0,16},{16,0},{1,17},{17,1},{2,18},{18,2},{3,19},{19,3},{4,20},{20... | collective-permute-start | bytes 2359304 | tf_op jit(solution)/shard_map/ppermute | solution.py:34
  70.1 6.1 %copy-start.16 = (bf16[2,72,432]{2,1,0:T(8,128)(2,1)}, bf16[2,72,432]{2,1,0:T(8,128)(2,1)S(1)}, u32[]{:S(2)}) copy-start(bf16[2,72,432]{2,1,0:T(8,128)(2,1)S(1)} %collective-permute-done.7.high_hbm) | copy-start | bytes 373252
  70.1 6.1 %copy-start.13 = (bf16[4,72,432]{2,1,0:T(8,128)(2,1)}, bf16[4,72,432]{2,1,0:T(8,128)(2,1)S(1)}, u32[]{:S(2)}) copy-start(bf16[4,72,432]{2,1,0:T(8,128)(2,1)S(1)} %collective-permute-done.5.up_hbm) | copy-start | bytes 746500
  70.1 6.1 %copy-start.14 = (bf16[4,72,432]{2,1,0:T(8,128)(2,1)}, bf16[4,72,432]{2,1,0:T(8,128)(2,1)S(1)}, u32[]{:S(2)}) copy-start(bf16[4,72,432]{2,1,0:T(8,128)(2,1)S(1)} %collective-permute-done.8.down_hbm) | copy-start | bytes 746500
  70.1 6.1 %copy-start.10 = (bf16[256,1536]{1,0:T(8,128)(2,1)}, bf16[256,1536]{1,0:T(8,128)(2,1)S(1)}, u32[]{:S(2)}) copy-start(bf16[256,1536]{1,0:T(8,128)(2,1)S(1)} %collective-permute-done.4.side_hbm) | copy-start | bytes 2359300
  70.1 6.0 %collective-permute-start.10 = (bf16[256,1536]{1,0:T(8,128)(2,1)S(1)}, bf16[256,1536]{1,0:T(8,128)(2,1)S(1)}, u32[]{:S(2)}, u32[]{:S(2)}) collective-permute-start(bf16[256,1536]{1,0:T(8,128)(2,1)S(1)} %collective-permute-done.4.side_hbm), channel_id=1, source_target_pairs={{0,16},{16,0},{1,17},{17,1},{2,18},{18,2},{3,19},{19,3},{4,20},{20... | collective-permute-start | bytes 2359304 | tf_op jit(solution)/shard_map/ppermute | solution.py:34
  74.3 1.9 %copy-start.11 = (bf16[256,1536]{1,0:T(8,128)(2,1)}, bf16[256,1536]{1,0:T(8,128)(2,1)S(1)}, u32[]{:S(2)}) copy-start(bf16[256,1536]{1,0:T(8,128)(2,1)S(1)} %collective-permute-done.9.core_hbm) | copy-start | bytes 2359300
  76.2 0.9 copy-start.12
  88.3 47.8 %all-to-all-start.1 = ((bf16[128,32,128]{2,1,0:T(8,128)(2,1)}), bf16[128,32,128]{2,1,0:T(8,128)(2,1)S(1)}, u32[]{:S(2)}, u32[]{:S(2)}) async-start(bf16[128,32,128]{2,1,0:T(8,128)(2,1)} %get-tuple-element.58), calls=%async_computation.1 | async-start | bytes 2097152 | tf_op jit(solution)/shard_map/all_to_all | solution.py:436
  102.6 5.2 %collective-permute-start.11 = (bf16[512,1152]{1,0:T(8,128)(2,1)}, bf16[512,1152]{1,0:T(8,128)(2,1)S(1)}, u32[]{:S(2)}, u32[]{:S(2)}) collective-permute-start(bf16[512,1152]{1,0:T(8,128)(2,1)} %get-tuple-element.60), channel_id=1, source_target_pairs={{0,16},{16,0},{1,17},{17,1},{2,18},{18,2},{3,19},{19,3},{4,20},{20... | collective-permute-start | bytes 3538952 | tf_op jit(solution)/shard_map/ppermute | solution.py:34
  107.8 1.0 copy-start.9
  111.5 22.6 %collective-permute-start.12 = (bf16[256,1152]{1,0:T(8,128)(2,1)}, bf16[256,1152]{1,0:T(8,128)(2,1)S(1)}, u32[]{:S(2)}, u32[]{:S(2)}) collective-permute-start(bf16[256,1152]{1,0:T(8,128)(2,1)} %get-tuple-element.62), channel_id=1, source_target_pairs={{0,8},{8,0},{1,9},{9,1},{2,10},{10,2},{3,11},{11,3},{4,12},{12,4},... | collective-permute-start | bytes 1769480 | tf_op jit(solution)/shard_map/ppermute | solution.py:34
  134.1 1.1 copy-start.1
  136.3 25.4 %copy-start.6 = (s32[3]{0:T(128)S(1)}, s32[3]{0:T(128)}, u32[]{:S(2)}) copy-start(s32[3]{0:T(128)} %copy-done.5) | copy-start | bytes 40
  161.7 6.9 %copy-start.3 = (f32[36,1728]{1,0:T(8,128)S(1)}, f32[36,1728]{1,0:T(8,128)}, u32[]{:S(2)}) copy-start(f32[36,1728]{1,0:T(8,128)} %slow_ref.1) | copy-start | bytes 746500
  161.7 6.9 %copy-start.4 = (f32[36,1728]{1,0:T(8,128)S(1)}, f32[36,1728]{1,0:T(8,128)}, u32[]{:S(2)}) copy-start(f32[36,1728]{1,0:T(8,128)} %fast_ref.1) | copy-start | bytes 746500
  162.3 6.3 %collective-permute-start.13 = (f32[2,36,432]{2,1,0:T(8,128)S(1)}, f32[2,36,432]{2,1,0:T(8,128)S(1)}, u32[]{:S(2)}, u32[]{:S(2)}) collective-permute-start(f32[2,36,432]{2,1,0:T(8,128)S(1)} %get-tuple-element.64), channel_id=1, source_target_pairs={{0,16},{16,0},{1,17},{17,1},{2,18},{18,2},{3,19},{19,3},{4,20},{20... | collective-permute-start | bytes 373256 | tf_op jit(solution)/shard_map/ppermute | solution.py:34
